TPU v7x, 32 devices: a whole 2x2x4 slice. The times are simulated.
32 devices in a mesh: group: 8 (over y, x, core), expert: 4 (over z).
Axes of the slice: x: 2, y: 2, z: 4, core: 2. Of those that a mesh axis runs over, the one named last changes fastest.
Arguments:
- inputs: bfloat16 [8192, 1024], P(('group', 'expert')), may hold values from -6 to 6
- gain_one: float32 [1024], replicated, may hold values from 0.5 to 1.5
- query_matrix: bfloat16 [1024, 1024], replicated, may hold values from -0.1875 to 0.1875
- key_matrix: bfloat16 [1024, 512], replicated, may hold values from -0.1875 to 0.1875
- value_matrix: bfloat16 [1024, 512], replicated, may hold values from -0.1875 to 0.1875
- w_attn_out: bfloat16 [1024, 1024], replicated, may hold values from -0.75 to 0.75
- gain_two: float32 [1024], replicated, may hold values from 0.5 to 1.5
- w_router: bfloat16 [1024, 16], replicated, may hold values from -0.09375 to 0.09375
- expert_in: bfloat16 [16, 1024, 1024], P('expert'), may hold values from -0.1875 to 0.1875
- expert_out: bfloat16 [16, 512, 1024], P('expert'), may hold values from -0.75 to 0.75
- lengths: int32 [32], P(('group', 'expert')), may hold values from 85 to 256, as said below
- routes: int32 [8192, 8], P(('group', 'expert')), may hold values from 0 to 15, all different within a row
- ranks: int32 [8192, 8], P(('group', 'expert')), may hold values from 0 to 2047, as said below
- cotangent: bfloat16 [8192, 1024], P(('group', 'expert')), may hold values from -6 to 6
Outputs:
- output: float32 [8192, 1024], P(('group', 'expert'))
- grad_inputs: float32 [8192, 1024], P(('group', 'expert'))
- grad_gain_one: float32 [1024], P('group')
- grad_w_query: float32 [1024, 1024], P('group')
- grad_w_key: float32 [1024, 512], P('group')
- grad_w_value: float32 [1024, 512], P('group')
- grad_w_attn_out: float32 [1024, 1024], P('group')
- grad_gain_two: float32 [1024], P('group')
- grad_w_router: float32 [1024, 16], P('group')
- grad_expert_in: float32 [16, 1024, 1024], P('expert')
- grad_expert_out: float32 [16, 512, 1024], P('expert')
Inputs may be any that keep to these rules, and one draw needn't show every extreme that they name: `lengths`: some slot holds exactly 256 tokens and some exactly 85. `routes`: each row names 8 different experts. `ranks`: the rows of one slot hold each of 0 to 2047 once.
All inputs are finite; a program needn't handle non-finite values.
Results may differ from a plain program's by a relative error of at most 0.012.
The roundings to bfloat16 on the way count: a program that leaves them out, or rounds other values in their place, can miss the bound.
Values may be sent and summed in bfloat16 or wider, within the bound.
No kernel may reach another device: no remote copies, remote signals or barrier semaphores. Data moves between devices by JAX's collectives and lax.ppermute only.
A program may use at most 192 MiB of HBM per device.

v0:
```python
import jax
import jax.numpy as jnp
from jax import lax
from jax.sharding import PartitionSpec as P

QUERY_HEADS = 16
KEY_VALUE_HEADS = 8
HEAD_DIMENSION = 64


EPS = 1e-05


def norm_forward(values, gain_vec):
    inverse = lax.rsqrt(jnp.mean(values * values, -1, keepdims=True) + EPS)
    return (values * inverse * gain_vec, inverse)


def norm_backward(values, inverse, gain_vec, upstream):
    scaled = upstream * gain_vec
    grad_gain = jnp.sum(upstream * values * inverse, 0)
    grad_values = inverse * scaled - values * inverse**3 * jnp.mean(
        scaled * values, -1, keepdims=True
    )
    return (grad_values, grad_gain)


def place_pairs(seq_length, route_rows, rank_rows, expert_count, capacity):
    sequence_rows, route_count = route_rows.shape
    pair_total = sequence_rows * route_count
    flat_route = route_rows.reshape(-1)
    flat_rank = rank_rows.reshape(-1)
    counter = jnp.arange(pair_total, dtype=jnp.int32)
    valid_pair = counter // route_count < seq_length
    rank_order = jnp.zeros((pair_total,), jnp.int32).at[flat_rank].set(counter)
    ranked_route = flat_route[rank_order]
    ranked_valid = valid_pair[rank_order]
    hit_table = (
        (ranked_route[:, None] == jnp.arange(expert_count, dtype=jnp.int32)[None, :])
        & ranked_valid[:, None]
    ).astype(jnp.int32)
    earlier = jnp.cumsum(hit_table, 0) - hit_table
    ranked_place = jnp.sum(earlier * hit_table, 1)
    slot_place = ranked_place[flat_rank]
    kept_pair = valid_pair & (slot_place < capacity)
    slot_index = jnp.where(kept_pair, flat_route * capacity + slot_place, expert_count * capacity)
    slot_token = (
        jnp.zeros((expert_count * capacity,), jnp.int32)
        .at[slot_index]
        .set(counter // route_count, mode="drop")
    )
    slot_used = jnp.zeros((expert_count * capacity,), jnp.int32).at[slot_index].set(1, mode="drop")
    return (kept_pair, slot_index, slot_token, slot_used)


def split_heads(query_rows, rows_of_key, rows_of_value):
    sequence_rows = query_rows.shape[0]
    groups_per_head = QUERY_HEADS // KEY_VALUE_HEADS
    heads_of_query = query_rows.reshape(
        sequence_rows, KEY_VALUE_HEADS, groups_per_head, HEAD_DIMENSION
    ).transpose(1, 2, 0, 3)
    heads_of_key = rows_of_key.reshape(sequence_rows, KEY_VALUE_HEADS, HEAD_DIMENSION).transpose(
        1, 0, 2
    )
    heads_of_value = rows_of_value.reshape(
        sequence_rows, KEY_VALUE_HEADS, HEAD_DIMENSION
    ).transpose(1, 0, 2)
    return (heads_of_query, heads_of_key, heads_of_value)


def head_scores(query_head, key_head, allowed):
    scores = jnp.einsum(
        "gqd,kd->gqk", query_head, key_head, preferred_element_type=jnp.float32
    ) * HEAD_DIMENSION ** (-0.5)
    return jnp.where(allowed, scores, -1e30)


def attend_forward(query_rows, rows_of_key, rows_of_value, allowed):
    sequence_rows = query_rows.shape[0]
    heads_of_query, heads_of_key, heads_of_value = split_heads(
        query_rows, rows_of_key, rows_of_value
    )

    def one_head(entry):
        query_head, key_head, value_head = entry
        scores = head_scores(query_head, key_head, allowed)
        row_max = jnp.max(scores, -1, keepdims=True)
        shifted_exp = jnp.exp(scores - row_max)
        row_total = jnp.sum(shifted_exp, -1, keepdims=True)
        attn_probs = (shifted_exp / row_total).astype(jnp.bfloat16)
        attn_mixed = jnp.einsum(
            "gqk,kd->gqd", attn_probs, value_head, preferred_element_type=jnp.float32
        )
        return (attn_mixed.astype(jnp.bfloat16), (row_max + jnp.log(row_total))[..., 0])

    mixed_heads, log_totals = lax.map(one_head, (heads_of_query, heads_of_key, heads_of_value))
    return (
        mixed_heads.transpose(2, 0, 1, 3).reshape(sequence_rows, QUERY_HEADS * HEAD_DIMENSION),
        log_totals,
    )


def attend_backward(query_rows, rows_of_key, rows_of_value, mixed_gradient, log_totals, allowed):
    sequence_rows = query_rows.shape[0]
    groups_per_head = QUERY_HEADS // KEY_VALUE_HEADS
    heads_of_query, heads_of_key, heads_of_value = split_heads(
        query_rows, rows_of_key, rows_of_value
    )
    heads_gradient = mixed_gradient.reshape(
        sequence_rows, KEY_VALUE_HEADS, groups_per_head, HEAD_DIMENSION
    ).transpose(1, 2, 0, 3)
    score_scale = HEAD_DIMENSION ** (-0.5)

    def one_head(entry):
        query_head, key_head, value_head, grad_head, log_head = entry
        attn_probs = jnp.exp(head_scores(query_head, key_head, allowed) - log_head[..., None])
        grad_probs = jnp.einsum(
            "gqd,kd->gqk", grad_head, value_head, preferred_element_type=jnp.float32
        )
        inner_sum = jnp.sum(grad_probs * attn_probs, -1, keepdims=True)
        grad_scores = (attn_probs * (grad_probs - inner_sum)).astype(jnp.bfloat16)
        grad_query = (
            jnp.einsum("gqk,kd->gqd", grad_scores, key_head, preferred_element_type=jnp.float32)
            * score_scale
        )
        key_gradient = (
            jnp.einsum("gqk,gqd->kd", grad_scores, query_head, preferred_element_type=jnp.float32)
            * score_scale
        )
        value_gradient = jnp.einsum(
            "gqk,gqd->kd",
            attn_probs.astype(jnp.bfloat16),
            grad_head,
            preferred_element_type=jnp.float32,
        )
        return (
            grad_query.astype(jnp.bfloat16),
            key_gradient.astype(jnp.bfloat16),
            value_gradient.astype(jnp.bfloat16),
        )

    grad_query, key_gradient, value_gradient = lax.map(
        one_head, (heads_of_query, heads_of_key, heads_of_value, heads_gradient, log_totals)
    )
    return (
        grad_query.transpose(2, 0, 1, 3).reshape(sequence_rows, QUERY_HEADS * HEAD_DIMENSION),
        key_gradient.transpose(1, 0, 2).reshape(sequence_rows, KEY_VALUE_HEADS * HEAD_DIMENSION),
        value_gradient.transpose(1, 0, 2).reshape(sequence_rows, KEY_VALUE_HEADS * HEAD_DIMENSION),
    )


def expert_pre(arrived, expert_in):
    return jnp.einsum("secd,edf->secf", arrived, expert_in, preferred_element_type=jnp.float32)


def expert_hidden(pre_act, half_width):
    gate_part = pre_act[..., :half_width]
    up_part = pre_act[..., half_width:]
    sigmoid_g = jax.nn.sigmoid(gate_part)
    silu_gate = gate_part * sigmoid_g
    return (gate_part, up_part, sigmoid_g, silu_gate, (silu_gate * up_part).astype(jnp.bfloat16))


def on_device(
    inputs,
    gain_one,
    query_matrix,
    key_matrix,
    value_matrix,
    w_attn_out,
    gain_two,
    w_router,
    expert_in,
    expert_out,
    lengths,
    routes,
    ranks,
    cotangent,
):
    sequence_rows, model_width = inputs.shape
    route_count = routes.shape[1]
    expert_count = w_router.shape[1]
    local_count = expert_in.shape[0]
    half_width = expert_out.shape[1]
    owner_count = lax.axis_size("expert")
    capacity = (5 * sequence_rows * route_count + 4 * expert_count - 1) // (4 * expert_count)
    slot_total = expert_count * capacity
    seq_length = lengths[0]
    kept_pair, slot_index, slot_token, slot_used = place_pairs(
        seq_length, routes, ranks, expert_count, capacity
    )
    kept_float = kept_pair.reshape(sequence_rows, route_count).astype(jnp.float32)
    safe_index = jnp.minimum(slot_index, slot_total - 1)
    positions = jnp.arange(sequence_rows, dtype=jnp.int32)
    allowed = (positions[None, :] <= positions[:, None]) & (positions[None, :] < seq_length)
    inputs_f = inputs.astype(jnp.float32)
    first_normalized, inverse_one = norm_forward(inputs_f, gain_one)
    first_normalized = first_normalized.astype(jnp.bfloat16)
    query_rows = jnp.dot(first_normalized, query_matrix, preferred_element_type=jnp.float32).astype(
        jnp.bfloat16
    )
    rows_of_key = jnp.dot(first_normalized, key_matrix, preferred_element_type=jnp.float32).astype(
        jnp.bfloat16
    )
    rows_of_value = jnp.dot(
        first_normalized, value_matrix, preferred_element_type=jnp.float32
    ).astype(jnp.bfloat16)
    attn_mixed, log_totals = attend_forward(query_rows, rows_of_key, rows_of_value, allowed)
    residual = inputs_f + jnp.dot(attn_mixed, w_attn_out, preferred_element_type=jnp.float32)
    normed_two, inverse_two = norm_forward(residual, gain_two)
    normed_two = normed_two.astype(jnp.bfloat16)
    logits = jnp.dot(normed_two, w_router, preferred_element_type=jnp.float32)
    route_table = routes[:, :, None] == jnp.arange(expert_count, dtype=jnp.int32)[None, None, :]
    chosen = jnp.sum(jnp.where(route_table, logits[:, None, :], 0.0), -1)
    gate_values = jax.nn.softmax(chosen, axis=-1)
    pair_weight = gate_values * kept_float
    sent_rows = (normed_two[slot_token] * slot_used[:, None].astype(jnp.bfloat16)).reshape(
        owner_count, local_count, capacity, model_width
    )
    arrived = lax.all_to_all(sent_rows, "expert", split_axis=0, concat_axis=0, tiled=True)
    pre_act = expert_pre(arrived, expert_in)
    hidden = expert_hidden(pre_act, half_width)[4]
    result = jnp.einsum(
        "secf,efd->secd", hidden, expert_out, preferred_element_type=jnp.float32
    ).astype(jnp.bfloat16)
    returned = lax.all_to_all(result, "expert", split_axis=0, concat_axis=0, tiled=True)
    outcome = (returned, arrived, pre_act)
    returned = outcome[0].reshape(slot_total, model_width)
    arrived = outcome[1]
    pair_rows = returned[safe_index].reshape(sequence_rows, route_count, model_width)
    output = residual + jnp.sum(pair_weight[..., None] * pair_rows.astype(jnp.float32), 1)
    upstream = cotangent.astype(jnp.float32)
    grad_gate = kept_float * jnp.sum(pair_rows.astype(jnp.float32) * upstream[:, None, :], -1)
    slot_gate = (
        jnp.zeros((slot_total,), jnp.float32)
        .at[slot_index]
        .set(pair_weight.reshape(-1), mode="drop")
    )
    grad_sent = (
        (slot_gate[:, None] * upstream[slot_token])
        .astype(jnp.bfloat16)
        .reshape(owner_count, local_count, capacity, model_width)
    )
    grad_arrived = lax.all_to_all(grad_sent, "expert", split_axis=0, concat_axis=0, tiled=True)
    pre_act = outcome[2]
    gate_part, up_part, sigmoid_g, silu_gate, hidden = expert_hidden(pre_act, half_width)
    grad_down = jnp.einsum(
        "secf,secd->efd", hidden, grad_arrived, preferred_element_type=jnp.float32
    )
    grad_hidden = jnp.einsum(
        "secd,efd->secf", grad_arrived, expert_out, preferred_element_type=jnp.float32
    )
    grad_pre = jnp.concatenate(
        [
            grad_hidden * up_part * sigmoid_g * (1.0 + gate_part * (1.0 - sigmoid_g)),
            grad_hidden * silu_gate,
        ],
        -1,
    ).astype(jnp.bfloat16)
    grad_in_weight = jnp.einsum(
        "secd,secf->edf", arrived, grad_pre, preferred_element_type=jnp.float32
    )
    grad_rows = jnp.einsum(
        "secf,edf->secd", grad_pre, expert_in, preferred_element_type=jnp.float32
    ).astype(jnp.bfloat16)
    grad_back = lax.all_to_all(
        grad_rows, "expert", split_axis=0, concat_axis=0, tiled=True
    ).reshape(slot_total, model_width)
    grad_normed = jnp.sum(
        grad_back[safe_index].reshape(sequence_rows, route_count, model_width).astype(jnp.float32)
        * kept_float[..., None],
        1,
    )
    gate_mean = jnp.sum(gate_values * grad_gate, -1, keepdims=True)
    grad_chosen = gate_values * (grad_gate - gate_mean)
    grad_logits = jnp.sum(jnp.where(route_table, grad_chosen[..., None], 0.0), 1).astype(
        jnp.bfloat16
    )
    grad_normed = grad_normed + jnp.einsum(
        "te,de->td", grad_logits, w_router, preferred_element_type=jnp.float32
    )
    grad_router = jnp.einsum(
        "td,te->de", normed_two, grad_logits, preferred_element_type=jnp.float32
    )
    grad_residual, grad_gain_two = norm_backward(residual, inverse_two, gain_two, grad_normed)
    grad_residual = grad_residual + upstream
    grad_branch = grad_residual.astype(jnp.bfloat16)
    grad_attn_out = jnp.einsum(
        "tc,td->cd", attn_mixed, grad_branch, preferred_element_type=jnp.float32
    )
    mixed_gradient = jnp.einsum(
        "td,cd->tc", grad_branch, w_attn_out, preferred_element_type=jnp.float32
    ).astype(jnp.bfloat16)
    grad_queries, grad_keys, grad_values = attend_backward(
        query_rows, rows_of_key, rows_of_value, mixed_gradient, log_totals, allowed
    )
    grad_query_w = jnp.einsum(
        "td,tc->dc", first_normalized, grad_queries, preferred_element_type=jnp.float32
    )
    grad_key_w = jnp.einsum(
        "td,tc->dc", first_normalized, grad_keys, preferred_element_type=jnp.float32
    )
    grad_value_w = jnp.einsum(
        "td,tc->dc", first_normalized, grad_values, preferred_element_type=jnp.float32
    )
    grad_normed_one = jnp.einsum(
        "tc,dc->td", grad_queries, query_matrix, preferred_element_type=jnp.float32
    )
    grad_normed_one = grad_normed_one + jnp.einsum(
        "tc,dc->td", grad_keys, key_matrix, preferred_element_type=jnp.float32
    )
    grad_normed_one = grad_normed_one + jnp.einsum(
        "tc,dc->td", grad_values, value_matrix, preferred_element_type=jnp.float32
    )
    grad_from_norm, grad_gain_one = norm_backward(inputs_f, inverse_one, gain_one, grad_normed_one)
    grad_inputs = grad_residual + grad_from_norm
    summed = lax.psum(
        (
            grad_gain_one,
            grad_query_w,
            grad_key_w,
            grad_value_w,
            grad_attn_out,
            grad_gain_two,
            grad_router,
        ),
        "expert",
    )
    shares = (
        lax.psum_scatter(summed[0], "group", scatter_dimension=0, tiled=True),
        lax.psum_scatter(summed[1], "group", scatter_dimension=0, tiled=True),
        lax.psum_scatter(summed[2], "group", scatter_dimension=0, tiled=True),
        lax.psum_scatter(summed[3], "group", scatter_dimension=0, tiled=True),
        lax.psum_scatter(summed[4], "group", scatter_dimension=0, tiled=True),
        lax.psum_scatter(summed[5], "group", scatter_dimension=0, tiled=True),
        lax.psum_scatter(summed[6], "group", scatter_dimension=0, tiled=True),
    )
    expert_parts = (
        lax.psum_scatter(grad_in_weight, "group", scatter_dimension=1, tiled=True),
        lax.psum_scatter(grad_down, "group", scatter_dimension=2, tiled=True),
    )
    expert_full = (
        lax.all_gather(expert_parts[0], "group", axis=1, tiled=True),
        lax.all_gather(expert_parts[1], "group", axis=2, tiled=True),
    )
    return (
        output,
        grad_inputs,
        shares[0],
        shares[1],
        shares[2],
        shares[3],
        shares[4],
        shares[5],
        shares[6],
        expert_full[0],
        expert_full[1],
    )


def solution(mesh):
    placed = (
        P(("group", "expert"), None),
        P(),
        P(),
        P(),
        P(),
        P(),
        P(),
        P(),
        P("expert", None, None),
        P("expert", None, None),
        P(("group", "expert")),
        P(("group", "expert"), None),
        P(("group", "expert"), None),
        P(("group", "expert"), None),
    )
    return jax.shard_map(
        on_device,
        mesh=mesh,
        in_specs=placed,
        out_specs=(
            P(("group", "expert"), None),
            P(("group", "expert"), None),
            P("group"),
            P("group", None),
            P("group", None),
            P("group", None),
            P("group", None),
            P("group"),
            P("group", None),
            P("expert", None, None),
            P("expert", None, None),
        ),
        check_vma=False,
    )
```

profile of v0, /device:TPU:0, one launch (start us, length us, event | category | flops | bytes accessed | tf_op | source)
XLA Modules:
  0.0 1219.8 jit_solution(9526622951367553430)
XLA Ops:
  20.0 23.3 %while.28 = (s32[]{:T(128)}, bf16[8,2,256,64]{2,3,1,0:T(8,128)(2,1)S(1)}, f32[8,2,256]{2,1,0:T(2,128)}, bf16[8,2,256,64]{2,3,1,0:T(8,128)(2,1)}, bf16[8,256,64]{...) while((s32[]{:T(128)}, ...), condition=%wide.region_4.5_spmd.clone, body=%wide.region_1.0_spmd.clone.sunk | while | flops 34766336 | bytes 1919329 | solution.py:96
  46.9 8.0 scatter_custom_fusion
  55.0 11.8 gather_fusion
  66.8 13.1 %gather_fusion.1 = pred[2048]{0:T(1024)(128)(4,1)S(1)} fusion(pred[2048]{0:T(1024)(128)(4,1)S(1)} %broadcast_compare_fusion.1, s32[2048]{0:T(1024)S(1)} %fusion.110), kind=kCustom, calls=%fused_computation.1 | custom fusion | bytes 12288 | tf_op jit(solution)/shard_map/gather | solution.py:37
  80.0 4.5 reduce-window.6
  85.3 11.8 gather_fusion.2
  97.8 8.2 scatter_custom_fusion.1
  106.0 8.1 scatter_custom_fusion.2
  115.6 8.8 gather_fusion.3
  124.4 5.3 broadcast_multiply_fusion
  129.7 6.3 all-to-all-start
  137.1 8.8 gather_fusion.5
  147.6 8.4 scatter_custom_fusion.3
  156.1 7.0 multiply_convert_fusion.1
  163.1 89.0 %all-to-all-done = bf16[4,4,160,1024]{3,2,1,0:T(8,128)(2,1)} async-done(((bf16[4,4,160,1024]{3,2,1,0:T(8,128)(2,1)}), bf16[4,4,160,1024]{3,2,1,0:T(8,128)(2,1)}, u32[]{:S(2)}, u32[]{:S(2)}) %all-to-all-start) | async-done | bytes 5242912 | tf_op jit(solution)/shard_map/all_to_all | solution.py:220
  252.1 5.1 all-to-all-start.2
  257.2 12.3 %fusion.76 = f32[4,4,160,1024]{3,2,0,1:T(8,128)} fusion(bf16[4,1024,1024]{2,1,0:T(8,128)(2,1)} %param.26, bf16[4,4,160,1024]{3,2,1,0:T(8,128)(2,1)} %all-to-all-done), kind=kOutput, calls=%fused_computation.111 | convolution fusion | flops 5368709120 | bytes 24117248 | tf_op jit(solution)/shard_map/secd,edf->secf/dot_general | solution.py:153
  269.5 102.8 %all-to-all-done.2 = bf16[4,4,160,1024]{3,2,1,0:T(8,128)(2,1)} async-done(((bf16[4,4,160,1024]{3,2,1,0:T(8,128)(2,1)}), bf16[4,4,160,1024]{3,2,1,0:T(8,128)(2,1)}, u32[]{:S(2)}, u32[]{:S(2)}) %all-to-all-start.2) | async-done | bytes 5242912 | tf_op jit(solution)/shard_map/all_to_all | solution.py:244
  372.4 11.2 fusion.64
  385.1 8.2 fusion.81
  393.3 10.1 convert_bitcast_fusion
  403.4 3.4 copy.110
  406.8 5.1 all-to-all-start.3
  412.0 13.6 %convolution_bitcast_fusion.2 = f32[4,1024,1024]{2,1,0:T(8,128)} fusion(bf16[4,4,160,1024]{3,2,1,0:T(8,128)(2,1)} %all-to-all-done, bf16[4,4,160,512]{3,2,0,1:T(8,128)(2,1)} %get-tuple-element.208, bf16[4,4,160,512]{3,2,0,1:T(8,128)(2,1)} %get-tuple-element.207), kind=kOutput, calls=%fused_computation.81 | convolution fusion | flops 5379194880 | bytes 27262976 | tf_op jit(solution)/shard_map/secd,secf->edf/dot_general | solution.py:260
  425.7 6.1 convert_bitcast_fusion.1
  431.8 3.2 copy.107
  435.0 92.2 %all-to-all-done.3 = bf16[4,4,160,1024]{3,2,1,0:T(8,128)(2,1)} async-done(((bf16[4,4,160,1024]{3,2,1,0:T(8,128)(2,1)}), bf16[4,4,160,1024]{3,2,1,0:T(8,128)(2,1)}, u32[]{:S(2)}, u32[]{:S(2)}) %all-to-all-start.3) | async-done | bytes 5242912 | tf_op jit(solution)/shard_map/all_to_all | solution.py:266
  527.1 5.0 all-to-all-start.1
  536.2 14.5 %gather_fusion.6 = bf16[2048,1024]{1,0:T(8,128)(2,1)} fusion(bf16[2560,1024]{1,0:T(8,128)(2,1)} %bitcast.30, s32[2048]{0:T(1024)} %broadcast_clamp_fusion), kind=kCustom, calls=%fused_computation.6 | custom fusion | bytes 8396800 | tf_op jit(solution)/shard_map/gather | solution.py:270
  550.7 96.7 %all-to-all-done.1 = bf16[4,4,160,1024]{3,2,1,0:T(8,128)(2,1)} async-done(((bf16[4,4,160,1024]{3,2,1,0:T(8,128)(2,1)}), bf16[4,4,160,1024]{3,2,1,0:T(8,128)(2,1)}, u32[]{:S(2)}, u32[]{:S(2)}) %all-to-all-start.1) | async-done | bytes 5242912 | tf_op jit(solution)/shard_map/all_to_all | solution.py:226
  647.3 14.5 %gather_fusion.4 = bf16[2048,1024]{1,0:T(8,128)(2,1)} fusion(bf16[2560,1024]{1,0:T(8,128)(2,1)} %bitcast.22, s32[2048]{0:T(1024)} %broadcast_clamp_fusion), kind=kCustom, calls=%fused_computation.4 | custom fusion | bytes 8396800 | tf_op jit(solution)/shard_map/gather | solution.py:230
  661.9 6.1 fusion.56
  670.6 4.8 fusion.57
  680.3 54.5 %while.29 = (s32[]{:T(128)}, bf16[8,2,256,64]{2,3,1,0:T(8,128)(2,1)S(1)}, bf16[8,256,64]{1,2,0:T(8,128)(2,1)}, bf16[8,256,64]{1,2,0:T(8,128)(2,1)S(1)}, bf16[8,2...) while((s32[]{:T(128)}, ...), condition=%wide.region_24.25_spmd.clone, body=%wide.region_22.24_spmd.clone.sunk | while | flops 85310976 | bytes 4570489 | solution.py:142
  734.8 3.1 fusion.130
  743.1 4.1 fusion.97
  749.7 28.7 %reduce-scatter.14.cloned.1.call-done = f32[128,512]{1,0:T(8,128)} async-done(((f32[1024,512]{1,0:T(8,128)}), f32[128,512]{1,0:T(8,128)}) %reduce-scatter.14.cloned.1.call-update) | async-done | bytes 262160 | tf_op jit(solution)/shard_map/reduce_scatter | solution.py:332
  778.4 44.4 %reduce-scatter.16.cloned.1.call-done = f32[128,512]{1,0:T(8,128)} async-done(((f32[1024,512]{1,0:T(8,128)}), f32[128,512]{1,0:T(8,128)}) %reduce-scatter.16.cloned.1.call-update) | async-done | bytes 262160 | tf_op jit(solution)/shard_map/reduce_scatter | solution.py:333
  822.7 55.0 %reduce-scatter.12.cloned.1.call-done = f32[128,1024]{1,0:T(8,128)} async-done(((f32[1024,1024]{1,0:T(8,128)}), f32[128,1024]{1,0:T(8,128)}) %reduce-scatter.12.cloned.1.call-update) | async-done | bytes 524304 | tf_op jit(solution)/shard_map/reduce_scatter | solution.py:331
  877.7 54.5 %reduce-scatter.18.cloned.1.call-done = f32[128,1024]{1,0:T(8,128)} async-done(((f32[1024,1024]{1,0:T(8,128)}), f32[128,1024]{1,0:T(8,128)}) %reduce-scatter.18.cloned.1.call-update) | async-done | bytes 524304 | tf_op jit(solution)/shard_map/reduce_scatter | solution.py:334
  939.5 13.0 %all-reduce.2 = (f32[1024]{0:T(1024)S(1)}, f32[1024]{0:T(1024)S(1)}) all-reduce(f32[1024]{0:T(1024)S(1)} %get-tuple-element.152, f32[1024]{0:T(1024)S(1)} %get-tuple-element.150), channel_id=2, replica_groups=mesh['group'=8,'expert'=4] {'group'}, use_global_device_ids=true, to_apply=%region_28.29.clone | all-reduce | flops 2048 | bytes 16384
  955.4 12.1 reduce-scatter.20.cloned.1.call-done
  967.6 12.7 %all-reduce.3 = (f32[128]{0:T(128)}, f32[128]{0:T(128)}, f32[128,16]{0,1:T(8,128)}) all-reduce(f32[128]{0:T(128)S(1)} %dynamic-slice.1, f32[128]{0:T(128)S(1)} %dynamic-slice.3, f32[128,16]{0,1:T(8,128)} %reduce-scatter.20.cloned.1.call-done), channel_id=1, replica_groups=mesh['group'=8,'expert'=4] {'expert'}, use_global_device_ids=true, to_apply=%region_27.28 | all-reduce | flops 2304 | bytes 18432 | tf_op jit(solution)/shard_map/psum | solution.py:317
  980.3 45.2 %all-gather.5.cloned.1.call-done = f32[4,512,1024]{2,1,0:T(8,128)} async-done(((f32[4,512,128]{2,1,0:T(8,128)}), f32[4,512,1024]{2,1,0:T(8,128)}) %all-gather.5.cloned.1.call-update) | async-done | bytes 8388624 | tf_op jit(solution)/shard_map/all_gather | solution.py:344
  1025.5 91.8 %all-gather.3.cloned.1.call-done = f32[4,1024,1024]{2,1,0:T(8,128)} async-done(((f32[4,128,1024]{2,1,0:T(8,128)}), f32[4,1024,1024]{2,1,0:T(8,128)}) %all-gather.3.cloned.1.call-update) | async-done | bytes 16777232 | tf_op jit(solution)/shard_map/all_gather | solution.py:343
  1117.3 72.7 %all-reduce.7.cloned.1.call-done = (f32[128,1024]{1,0:T(8,128)}, f32[128,512]{1,0:T(8,128)}, f32[128,512]{1,0:T(8,128)}, f32[128,1024]{1,0:T(8,128)}) async-done(((f32[128,1024]{1,0:T(8,128)}, f32[128,512]{1,0:T(8,128)}, f32[128,512]{1,0:T(8,128)}, f32[128,1024]{1,0:T(8,128)}), (f32[128,1024]{1,0:T(8,128)}, f32[128,512]{1,0:T(8,128)}, f32[128,512]{1,0:T(8,128)}, ...) | async-done | bytes 1572880 | tf_op jit(solution)/shard_map/psum | solution.py:317
  1197.2 12.1 copy.178
  1209.4 3.4 copy.179
  (282 shorter events, 136.0 us)
Async XLA Ops:
  7.2 36.1 %copy-start = (bf16[1024,1024]{1,0:T(8,128)(2,1)S(1)}, bf16[1024,1024]{1,0:T(8,128)(2,1)}, u32[]{:S(2)}) copy-start(bf16[1024,1024]{1,0:T(8,128)(2,1)} %param.23) | copy-start | bytes 6291460
  7.2 7.7 copy-start.3
  7.2 7.7 copy-start.17
  11.3 8.6 copy-start.23
  43.3 23.5 %copy-start.8 = (bf16[8,2,256,64]{2,3,1,0:T(8,128)(2,1)}, bf16[8,2,256,64]{2,3,1,0:T(8,128)(2,1)S(1)}, u32[]{:S(2)}) copy-start(bf16[8,2,256,64]{2,3,1,0:T(8,128)(2,1)S(1)} %get-tuple-element.103) | copy-start | bytes 1572868
  43.3 23.5 %copy-start.11 = (bf16[8,256,64]{1,2,0:T(8,128)(2,1)}, bf16[8,256,64]{1,2,0:T(8,128)(2,1)S(1)}, u32[]{:S(2)}) copy-start(bf16[8,256,64]{1,2,0:T(8,128)(2,1)S(1)} %get-tuple-element.454) | copy-start | bytes 786436
  43.3 23.5 %copy-start.19 = (pred[256]{0:T(512)(128)(4,1)}, pred[256]{0:T(512)(128)(4,1)S(1)}, u32[]{:S(2)}) copy-start(pred[256]{0:T(512)(128)(4,1)S(1)} %get-tuple-element.475) | copy-start | bytes 772
  45.6 68.6 %copy-start.28 = (f32[256]{0:T(256)}, f32[256]{0:T(256)S(1)}, u32[]{:S(2)}) copy-start(f32[256]{0:T(256)S(1)} %get-tuple-element.215) | copy-start | bytes 3076
  79.9 34.3 %copy-start.21 = (f32[1024]{0:T(1024)S(1)}, f32[1024]{0:T(1024)}, u32[]{:S(2)}) copy-start(f32[1024]{0:T(1024)} %param.24) | copy-start | bytes 12292
  115.6 8.8 copy-start.1
  129.7 122.4 %all-to-all-start = ((bf16[4,4,160,1024]{3,2,1,0:T(8,128)(2,1)}), bf16[4,4,160,1024]{3,2,1,0:T(8,128)(2,1)}, u32[]{:S(2)}, u32[]{:S(2)}) async-start(bf16[4,4,160,1024]{3,2,1,0:T(8,128)(2,1)} %broadcast_multiply_fusion), calls=%async_computation | async-start | bytes 10485760 | tf_op jit(solution)/shard_map/all_to_all | solution.py:220
  137.1 8.8 copy-start.14
  137.1 10.1 copy-start.16
  147.3 386.2 %copy-start.25 = (f32[256]{0:T(256)}, f32[256]{0:T(256)S(1)}, u32[]{:S(2)}) copy-start(f32[256]{0:T(256)S(1)} %reduce_max.18) | copy-start | bytes 3076
  147.3 386.1 %copy-start.27 = (f32[256]{0:T(256)}, f32[256]{0:T(256)S(1)}, u32[]{:S(2)}) copy-start(f32[256]{0:T(256)S(1)} %fusion.116) | copy-start | bytes 3076
  252.1 120.3 %all-to-all-start.2 = ((bf16[4,4,160,1024]{3,2,1,0:T(8,128)(2,1)}), bf16[4,4,160,1024]{3,2,1,0:T(8,128)(2,1)}, u32[]{:S(2)}, u32[]{:S(2)}) async-start(bf16[4,4,160,1024]{3,2,1,0:T(8,128)(2,1)} %multiply_convert_fusion.1), calls=%async_computation.2 | async-start | bytes 10485760 | tf_op jit(solution)/shard_map/all_to_all | solution.py:244
  257.2 491.0 %reduce-scatter.10.cloned.1.call-start = ((), (), s32[]{:S(2)}) async-start(), calls=%async_computation.13 | async-start | bytes 9437184 | tf_op jit(solution)/shard_map/reduce_scatter | solution.py:340
  383.6 1.5 copy-start.33
  406.8 120.3 %all-to-all-start.3 = ((bf16[4,4,160,1024]{3,2,1,0:T(8,128)(2,1)}), bf16[4,4,160,1024]{3,2,1,0:T(8,128)(2,1)}, u32[]{:S(2)}, u32[]{:S(2)}) async-start(bf16[4,4,160,1024]{3,2,1,0:T(8,128)(2,1)} %copy.110), calls=%async_computation.3 | async-start | bytes 10485760 | tf_op jit(solution)/shard_map/all_to_all | solution.py:266
  412.0 337.0 %reduce-scatter.8.cloned.1.call-start = ((), (), s32[]{:S(2)}) async-start(), calls=%async_computation.11 | async-start | bytes 18874368 | tf_op jit(solution)/shard_map/reduce_scatter | solution.py:339
  527.1 120.2 %all-to-all-start.1 = ((bf16[4,4,160,1024]{3,2,1,0:T(8,128)(2,1)}), bf16[4,4,160,1024]{3,2,1,0:T(8,128)(2,1)}, u32[]{:S(2)}, u32[]{:S(2)}) async-start(bf16[4,4,160,1024]{3,2,1,0:T(8,128)(2,1)} %copy.107), calls=%async_computation.1 | async-start | bytes 10485760 | tf_op jit(solution)/shard_map/all_to_all | solution.py:226
  532.2 246.2 %reduce-scatter.14.cloned.1.call-start = ((), (), s32[]{:S(2)}) async-start(), calls=%async_computation.16 | async-start | bytes 2359296 | tf_op jit(solution)/shard_map/reduce_scatter | solution.py:332
  668.0 7.4 copy-start.6
  668.0 7.4 copy-start.15
  668.0 7.5 copy-start.22
  668.0 7.5 copy-start.29
  668.0 8.1 copy-start.31
  669.0 7.0 copy-start.9
  669.0 7.0 copy-start.10
  676.1 4.2 copy-start.20
  680.3 54.5 %copy-start.4 = (bf16[256,1024]{1,0:T(8,128)(2,1)S(1)}, bf16[256,1024]{1,0:T(8,128)(2,1)}, u32[]{:S(2)}) copy-start(bf16[256,1024]{1,0:T(8,128)(2,1)} %param.18) | copy-start | bytes 1572868
  680.3 54.5 %copy-start.18 = (f32[1024]{0:T(1024)S(1)}, f32[1024]{0:T(1024)}, u32[]{:S(2)}) copy-start(f32[1024]{0:T(1024)} %param.19) | copy-start | bytes 12292
  680.3 54.5 %copy-start.24 = (f32[256]{0:T(256)S(1)}, f32[256]{0:T(256)}, u32[]{:S(2)}) copy-start(f32[256]{0:T(256)} %copy-done.23) | copy-start | bytes 3076
  734.8 8.0 copy-start.7
  737.9 84.8 %reduce-scatter.16.cloned.1.call-start = ((), (), s32[]{:S(2)}) async-start(), calls=%async_computation.17 | async-start | bytes 2359296 | tf_op jit(solution)/shard_map/reduce_scatter | solution.py:333
  739.9 137.8 %reduce-scatter.12.cloned.1.call-start = ((), (), s32[]{:S(2)}) async-start(), calls=%async_computation.15 | async-start | bytes 4718592 | tf_op jit(solution)/shard_map/reduce_scatter | solution.py:331
  742.8 4.5 copy-start.2
  742.8 189.4 %reduce-scatter.18.cloned.1.call-start = ((), (), s32[]{:S(2)}) async-start(), calls=%async_computation.18 | async-start | bytes 4718592 | tf_op jit(solution)/shard_map/reduce_scatter | solution.py:334
  747.2 185.1 %copy-start.32 = (u32[32]{0:T(128)S(1)}, u32[32]{0:T(128)}, u32[]{:S(2)}) copy-start(u32[32]{0:T(128)} %constant.144) | copy-start | bytes 388
  747.2 220.3 %reduce-scatter.20.cloned.1.call-start = ((), (), s32[]{:S(2)}) async-start(), calls=%async_computation.19 | async-start | bytes 73728 | tf_op jit(solution)/shard_map/reduce_scatter | solution.py:336
  748.1 188.0 %copy-start.13 = (bf16[8,256,64]{1,2,0:T(8,128)(2,1)S(1)}, bf16[8,256,64]{1,2,0:T(8,128)(2,1)}, u32[]{:S(2)}) copy-start(bf16[8,256,64]{1,2,0:T(8,128)(2,1)} %get-tuple-element.106) | copy-start | bytes 786436
  748.1 277.3 %all-gather.5.cloned.1.call-start = ((), (), s32[]{:S(2)}) async-start(), calls=%async_computation.14 | async-start | bytes 9437184 | tf_op jit(solution)/shard_map/all_gather | solution.py:344
  748.9 368.4 %all-gather.3.cloned.1.call-start = ((), (), s32[]{:S(2)}) async-start(), calls=%async_computation.12 | async-start | bytes 18874368 | tf_op jit(solution)/shard_map/all_gather | solution.py:343
  749.6 440.4 %all-reduce.7.cloned.1.call-start = ((), (), s32[]{:S(2)}) async-start(), calls=%async_computation.20 | async-start | bytes 3145728 | tf_op jit(solution)/shard_map/psum | solution.py:317
  933.5 4.4 copy-start.12
  933.5 19.1 %copy-start.30 = (f32[256]{0:T(256)S(1)}, f32[256]{0:T(256)}, u32[]{:S(2)}) copy-start(f32[256]{0:T(256)} %get-tuple-element.212) | copy-start | bytes 3076
  1195.2 14.1 %slice-start = ((s8[8388608]{0:T(1024)(128)(4,1)}), s8[4194304]{0:T(1024)(128)(4,1)S(1)}, s32[]{:S(2)}) async-start(s8[8388608]{0:T(1024)(128)(4,1)} %bitcast.256), calls=%async_computation.21 | async-start | bytes 8388608
  1197.2 12.1 slice-start.1
  (2 other events, 1.8 us)
Sparse Core Ops, SparseCore 0:
  393.4 70.2 reduce-scatter.9
  468.3 115.9 reduce-scatter.7
  738.1 40.2 reduce-scatter.13
  781.5 41.1 reduce-scatter.15
  826.3 51.3 reduce-scatter.11
  880.9 51.2 reduce-scatter.17
  936.1 31.4 reduce-scatter.19
  969.4 55.9 all-gather.4
  1027.4 89.8 all-gather.2
  1119.7 70.2 all-reduce.6
where the time goes:
time: 1230 us; the launch traced here: 1220 us
  waiting for transfers between devices  787 us (64%)
  local copies, waits for them, and re-layouts  163 us (13%)
  matrix products  155 us (13%)
  other arithmetic  50.7 us (4%)
  blocking collectives  25.7 us (2%)
  starting transfers between devices  22.4 us (2%)
  between operations  16.5 us (1%)
    all_to_all x1, waiting for transfers between devices, on_device(): lax.all_to_all(grad_sent, 'expert', split_axis=0, concat_axis=0, tiled=True)  103 us
    all_to_all x1, waiting for transfers between devices, on_device(): lax.all_to_all(result, 'expert', split_axis=0, concat_axis=0, tiled=True)  96.7 us
    all_to_all x1, waiting for transfers between devices, on_device(): lax.all_to_all(grad_rows, 'expert', split_axis=0, concat_axis=0, tiled=True)  92.2 us
    all_gather x1, waiting for transfers between devices, on_device(): lax.all_gather(expert_parts[0], 'group', axis=1, tiled=True)  91.8 us
    all_to_all x1, waiting for transfers between devices, on_device(): lax.all_to_all(sent_rows, 'expert', split_axis=0, concat_axis=0, tiled=True)  89 us
    psum x1, waiting for transfers between devices, on_device(): lax.psum((grad_gain_one, grad_query_w, grad_key_w, grad_value_w, grad_att...  72.7 us
    reduce_scatter x1, waiting for transfers between devices, on_device(): lax.psum_scatter(summed[1], 'group', scatter_dimension=0, tiled=True)  55 us
    reduce_scatter x1, waiting for transfers between devices, on_device(): lax.psum_scatter(summed[4], 'group', scatter_dimension=0, tiled=True)  54.5 us
  transfers between devices with their start and end apart: 14, of which 12 were waited for; matrix products, arithmetic and copies ran while one was open for 17% of the time, Pallas kernels for 0%

commit v1 on v0

v1 whole, which is shorter than its diff:
```python
import functools

import jax
import jax.numpy as jnp
from jax import lax
from jax.experimental import pallas as pl
from jax.experimental.pallas import tpu as pltpu
from jax.sharding import PartitionSpec as P

QUERY_HEADS = 16
KEY_VALUE_HEADS = 8
HEAD_DIMENSION = 64
PAIR = 2 * HEAD_DIMENSION
EPS = 1e-05
UNROUTED = 1 << 20
LANES = 128
SCALE = HEAD_DIMENSION ** (-0.5)

bf16 = jnp.bfloat16
f32 = jnp.float32
VMEM = pl.BlockSpec(memory_space=pltpu.VMEM)
SMEM = pl.BlockSpec(memory_space=pltpu.SMEM)
LIMIT = 56 * 1024 * 1024


def mm(left, right, dims=((1,), (0,))):
    return lax.dot_general(left, right, (dims, ((), ())), preferred_element_type=f32)


def call(kernel, outs, *args, smem=0, scratch=(), flops=0, name=None):
    outs = [jax.ShapeDtypeStruct(s, d) for s, d in outs]
    moved = sum(a.size * a.dtype.itemsize for a in args) + sum(
        o.size * o.dtype.itemsize for o in outs
    )
    return pl.pallas_call(
        kernel,
        out_shape=outs,
        in_specs=[SMEM] * smem + [VMEM] * (len(args) - smem),
        out_specs=[VMEM] * len(outs),
        scratch_shapes=list(scratch),
        compiler_params=pltpu.CompilerParams(vmem_limit_bytes=LIMIT),
        cost_estimate=pl.CostEstimate(flops=flops, bytes_accessed=moved, transcendentals=0),
        name=name,
    )(*args)


def low_lanes(rows):
    return lax.broadcasted_iota(jnp.int32, (rows, PAIR), 1) < HEAD_DIMENSION


def stack_heads(pair, low):
    pair = pair.astype(f32)
    return jnp.concatenate([jnp.where(low, pair, 0.0), jnp.where(low, 0.0, pair)], 0).astype(bf16)


def allowed_keys(rows, length):
    shape = (2 * rows, rows)
    query = lax.broadcasted_iota(jnp.int32, shape, 0)
    query = jnp.where(query >= rows, query - rows, query)
    key = lax.broadcasted_iota(jnp.int32, shape, 1)
    return (key <= query) & (key < length)


def dense_forward(
    len_ref, x_ref, g1_ref, wq_ref, wk_ref, wv_ref, wo_ref, g2_ref, wr_ref, table_ref,
    n1_ref, q_ref, kk_ref, vv_ref, lse_ref, mixed_ref, res_ref, n2_ref, gate_ref,
):
    rows = x_ref.shape[0]
    x = x_ref[...].astype(f32)
    inverse = lax.rsqrt(jnp.mean(x * x, -1, keepdims=True) + EPS)
    n1 = (x * inverse * g1_ref[...]).astype(bf16)
    n1_ref[...] = n1
    q_ref[...] = mm(n1, wq_ref[...]).astype(bf16)
    low = low_lanes(rows)
    for weight_ref, twice_ref in ((wk_ref, kk_ref), (wv_ref, vv_ref)):
        both = mm(n1, weight_ref[...])
        for j in range(KEY_VALUE_HEADS // 2):
            block = both[:, j * PAIR : (j + 1) * PAIR]
            rolled = pltpu.roll(block, HEAD_DIMENSION, 1)
            twice_ref[:, 2 * j * PAIR : (2 * j + 1) * PAIR] = jnp.where(low, block, rolled).astype(bf16)
            twice_ref[:, (2 * j + 1) * PAIR : (2 * j + 2) * PAIR] = jnp.where(low, rolled, block).astype(bf16)
    allowed = allowed_keys(rows, len_ref[0])
    lane = lax.broadcasted_iota(jnp.int32, (rows, LANES), 1)
    totals = jnp.zeros((rows, LANES), f32)
    for h in range(KEY_VALUE_HEADS):
        cols = slice(h * PAIR, (h + 1) * PAIR)
        scores = mm(stack_heads(q_ref[:, cols], low), kk_ref[:, cols], ((1,), (1,))) * SCALE
        scores = jnp.where(allowed, scores, -1e30)
        top = jnp.max(scores, -1, keepdims=True)
        raised = jnp.exp(scores - top)
        total = jnp.sum(raised, -1, keepdims=True)
        probs = (raised / total).astype(bf16)
        mixed = mm(probs, vv_ref[:, cols])
        mixed_ref[:, cols] = jnp.where(low, mixed[:rows], mixed[rows:]).astype(bf16)
        logs = top + jnp.log(total)
        totals = jnp.where(lane == 2 * h, logs[:rows], totals)
        totals = jnp.where(lane == 2 * h + 1, logs[rows:], totals)
    lse_ref[...] = totals
    residual = x + mm(mixed_ref[...], wo_ref[...])
    res_ref[...] = residual
    inverse = lax.rsqrt(jnp.mean(residual * residual, -1, keepdims=True) + EPS)
    n2 = (residual * inverse * g2_ref[...]).astype(bf16)
    n2_ref[...] = n2
    logits = mm(wr_ref[...], n2, ((1,), (1,)))
    routed = table_ref[...] < UNROUTED
    top = jnp.max(jnp.where(routed, logits, -jnp.inf), 0, keepdims=True)
    raised = jnp.where(routed, jnp.exp(jnp.where(routed, logits - top, 0.0)), 0.0)
    total = jnp.sum(raised, 0, keepdims=True)
    gate_ref[...] = raised / jnp.where(total > 0.0, total, 1.0)


def place_kernel(local, capacity, id_ref, *refs):
    tables, (row_ref, col_ref) = refs[:-2], refs[-2:]
    rows = tables[0].shape[1]
    first = id_ref[0] * local
    mine = [table[pl.ds(first + j, 1), :] for table in tables for j in range(local)]
    count = len(mine)
    packed = jnp.concatenate(mine + [jnp.zeros((LANES - count, rows), jnp.int32)], 0).astype(f32)
    columns = packed.T
    places = []
    for i in range(count):
        row = mine[i].astype(f32)
        before = jnp.sum(jnp.where(columns[:, i : i + 1] < row, 1.0, 0.0), 0, keepdims=True)
        places.append(jnp.where((row < UNROUTED) & (before < capacity), before, -1.0))
    for i in range(count):
        d, j = divmod(i, local)
        row_ref[j, d : d + 1, :] = places[i].astype(jnp.int32)
    full = jnp.concatenate(places + [jnp.zeros((LANES - count, rows), f32)], 0)
    col_ref[...] = full.T.astype(jnp.int32)


def expert_kernel(index, local, capacity, owners, id_ref, *refs):
    place_ref = refs[0]
    gates = refs[1 : 1 + owners]
    tokens = refs[1 + owners : 1 + 2 * owners]
    grads = refs[1 + 2 * owners : 1 + 3 * owners]
    (win_ref, wout_ref, keep_ref, send_ref, wret_ref, grow_ref, gg_ref,
     sent, crow, weight, slope, silu, hidden, gret, gpre, acc) = refs[1 + 3 * owners :]
    width = win_ref.shape[1]
    half = wout_ref.shape[1]
    seq = tokens[0].shape[0]
    row = id_ref[0] * local + index
    core = id_ref[1]
    place = lax.broadcasted_iota(jnp.int32, (capacity, seq), 0)
    for d in range(owners):
        span = slice(d * capacity, (d + 1) * capacity)
        hit = place == place_ref[0, d : d + 1, :]
        one = jnp.where(hit, 1.0, 0.0).astype(bf16)
        sent[span, :] = mm(one, tokens[d][...]).astype(bf16)
        crow[span, :] = mm(one, grads[d][...]).astype(bf16)
        weight[span, :] = jnp.sum(jnp.where(hit, gates[d][pl.ds(row, 1), :], 0.0), 1, keepdims=True)
    tile = 256
    for t in range(0, half, tile):
        gate = mm(sent[...], win_ref[0, :, t : t + tile])
        up = mm(sent[...], win_ref[0, :, half + t : half + t + tile])
        sig = jax.nn.sigmoid(gate)
        act = gate * sig
        silu[:, t : t + tile] = act
        slope[:, t : t + tile] = up * sig * (1.0 + gate * (1.0 - sig))
        hidden[:, t : t + tile] = (act * up).astype(bf16)
    dots = jnp.zeros((owners * capacity, 1), f32)
    for t in range(0, width, tile):
        cols = slice(t, t + tile)
        returned = mm(hidden[...], wout_ref[0, :, cols]).astype(bf16).astype(f32)
        upstream = crow[:, cols].astype(f32)
        dots = dots + jnp.sum(returned * upstream, 1, keepdims=True)
        wret_ref[:, cols] = (weight[...] * returned).astype(bf16)
        gret[:, cols] = (weight[...] * upstream).astype(bf16)
    for d in range(owners):
        hit = place == place_ref[0, d : d + 1, :]
        part = dots[d * capacity : (d + 1) * capacity]
        gg_ref[d : d + 1, :] = jnp.sum(jnp.where(hit, part, 0.0), 0, keepdims=True)
    for t in range(0, half, tile):
        ghid = mm(gret[...], wout_ref[0, t : t + tile, :], ((1,), (1,)))
        gpre[:, t : t + tile] = (ghid * slope[:, t : t + tile]).astype(bf16)
        gpre[:, half + t : half + t + tile] = (ghid * silu[:, t : t + tile]).astype(bf16)
    for t in range(0, width, tile):
        grow_ref[:, t : t + tile] = mm(gpre[...], win_ref[0, t : t + tile, :], ((1,), (1,))).astype(bf16)
    pieces = 2 * keep_ref.shape[0]
    base = 0
    for left, right in ((sent, gpre), (hidden, gret)):
        size = left.shape[1]
        step = size // pieces
        for t in range(0, width, tile):
            acc[:size, t : t + tile] = mm(left[...], right[:, t : t + tile], ((0,), (0,)))
        for q in range(pieces // 2):
            lo = pl.multiple_of((2 * q + core) * step, step)
            hi = pl.multiple_of((2 * q + 1 - core) * step, step)
            keep_ref[q, base : base + step, :] = acc[pl.ds(lo, step), :].astype(bf16)
            send_ref[q, base : base + step, :] = acc[pl.ds(hi, step), :].astype(bf16)
        base += step


def combine_kernel(local, capacity, owners, col_ref, *refs):
    rows_in = refs[:local]
    parts = refs[local : local + owners]
    seq = col_ref.shape[0]
    lane = lax.broadcasted_iota(jnp.int32, (seq, local * capacity), 1)
    for d in range(owners):
        hit = None
        for j in range(local):
            col = col_ref[:, d * local + j : d * local + j + 1]
            same = lane == jnp.where(col < 0, -1, col + j * capacity)
            hit = same if hit is None else hit | same
        one = jnp.where(hit, 1.0, 0.0).astype(bf16)
        span = slice(d * capacity, (d + 1) * capacity)
        stacked = jnp.concatenate([r[span, :] for r in rows_in], 0)
        parts[d][...] = mm(one, stacked).astype(parts[d].dtype)


def dense_backward(owners, local, id_ref, len_ref, *refs):
    parts = refs[:owners]
    ggs = refs[owners : 2 * owners]
    (gate_ref, x_ref, cot_ref, res_ref, n1_ref, n2_ref, q_ref, kk_ref, vv_ref, lse_ref, mixed_ref,
     wq_ref, wk_ref, wv_ref, wo_ref, wr_ref, g1_ref, g2_ref,
     gin_ref, keep_ref, send_ref, gg_all, gmix, gq, gk, gv, acc) = refs[2 * owners :]
    rows, width = x_ref.shape
    core = id_ref[1]
    pieces = 2 * keep_ref.shape[0]
    step = width // pieces

    def put(offset, size):
        for q in range(pieces // 2):
            lo = pl.multiple_of((2 * q + core) * step, step)
            hi = pl.multiple_of((2 * q + 1 - core) * step, step)
            keep_ref[q, :, offset : offset + size] = acc[pl.ds(lo, step), :size].astype(bf16)
            send_ref[q, :, offset : offset + size] = acc[pl.ds(hi, step), :size].astype(bf16)

    def weight_gradient(left, right, offset):
        size = right.shape[1]
        tile = 256
        for t in range(0, size, tile):
            acc[:, t : t + tile] = mm(left[...], right[:, t : t + tile], ((0,), (0,)))
        put(offset, size)

    for d in range(owners):
        owner = lax.rem(id_ref[0] + d, owners)
        for j in range(local):
            gg_all[pl.ds(owner * local + j, 1), :] = ggs[d][j : j + 1, :]
    gates = gate_ref[...]
    grad_gates = gg_all[...]
    mean = jnp.sum(gates * grad_gates, 0, keepdims=True)
    glog = (gates * (grad_gates - mean)).astype(bf16)
    grad = parts[0][...]
    for part in parts[1:]:
        grad = grad + part[...].astype(f32)
    grad = grad + mm(glog, wr_ref[...], ((0,), (0,)))
    grouter = mm(glog, n2_ref[...])
    residual = res_ref[...]
    inverse = lax.rsqrt(jnp.mean(residual * residual, -1, keepdims=True) + EPS)
    ggain_two = jnp.sum(grad * residual * inverse, 0, keepdims=True)
    scaled = grad * g2_ref[...]
    gres = cot_ref[...].astype(f32) + inverse * scaled - residual * inverse**3 * jnp.mean(
        scaled * residual, -1, keepdims=True
    )
    branch = gres.astype(bf16)
    gmix[...] = mm(branch, wo_ref[...], ((1,), (1,))).astype(bf16)
    gin_ref[...] = gres
    gq[...] = branch
    col = wq_ref.shape[1] + wk_ref.shape[1] + wv_ref.shape[1]
    weight_gradient(mixed_ref, gq, col)
    low = low_lanes(rows)
    allowed = allowed_keys(rows, len_ref[0])
    held = None
    for h in range(KEY_VALUE_HEADS):
        cols = slice(h * PAIR, (h + 1) * PAIR)
        queries = stack_heads(q_ref[:, cols], low)
        upstream = stack_heads(gmix[:, cols], low)
        scores = mm(queries, kk_ref[:, cols], ((1,), (1,))) * SCALE
        logs = jnp.concatenate([lse_ref[:, 2 * h : 2 * h + 1], lse_ref[:, 2 * h + 1 : 2 * h + 2]], 0)
        probs = jnp.exp(jnp.where(allowed, scores, -1e30) - logs)
        gprobs = mm(upstream, vv_ref[:, cols], ((1,), (1,)))
        inner = jnp.sum(gprobs * probs, -1, keepdims=True)
        gscores = (probs * (gprobs - inner)).astype(bf16)
        gqueries = mm(gscores, kk_ref[:, cols]) * SCALE
        gq[:, cols] = jnp.where(low, gqueries[:rows], gqueries[rows:]).astype(bf16)
        gkey = mm(gscores, queries, ((0,), (0,))) * SCALE
        gvalue = mm(probs.astype(bf16), upstream, ((0,), (0,)))
        gkey = gkey + pltpu.roll(gkey, HEAD_DIMENSION, 1)
        gvalue = gvalue + pltpu.roll(gvalue, HEAD_DIMENSION, 1)
        if h % 2 == 0:
            held = (gkey, gvalue)
        else:
            both = slice((h // 2) * PAIR, (h // 2 + 1) * PAIR)
            gk[:, both] = jnp.where(low, held[0], gkey).astype(bf16)
            gv[:, both] = jnp.where(low, held[1], gvalue).astype(bf16)
    weight_gradient(n1_ref, gq, 0)
    weight_gradient(n1_ref, gk, wq_ref.shape[1])
    weight_gradient(n1_ref, gv, wq_ref.shape[1] + wk_ref.shape[1])
    grad = mm(gq[...], wq_ref[...], ((1,), (1,)))
    grad = grad + mm(gk[...], wk_ref[...], ((1,), (1,)))
    grad = grad + mm(gv[...], wv_ref[...], ((1,), (1,)))
    x = x_ref[...].astype(f32)
    inverse = lax.rsqrt(jnp.mean(x * x, -1, keepdims=True) + EPS)
    ggain_one = jnp.sum(grad * x * inverse, 0, keepdims=True)
    scaled = grad * g1_ref[...]
    gin_ref[...] = gin_ref[...] + inverse * scaled - x * inverse**3 * jnp.mean(
        scaled * x, -1, keepdims=True
    )
    small = jnp.concatenate(
        [grouter, ggain_one, ggain_two, jnp.zeros((LANES - 2 - grouter.shape[0], width), f32)], 0
    )
    acc[:, :LANES] = small.T
    put(col + width, LANES)


def on_device(
    inputs, gain_one, query_matrix, key_matrix, value_matrix, w_attn_out, gain_two, w_router,
    expert_in, expert_out, lengths, routes, ranks, cotangent,
):
    seq, width = inputs.shape
    picks = routes.shape[1]
    experts = w_router.shape[1]
    local = expert_in.shape[0]
    half = expert_out.shape[1]
    owners = lax.axis_size("expert")
    groups = lax.axis_size("group")
    bits = groups.bit_length() - 1
    capacity = (5 * seq * picks + 4 * experts - 1) // (4 * experts)
    places = owners * capacity
    z = lax.axis_index("expert").astype(jnp.int32)
    g = lax.axis_index("group").astype(jnp.int32)
    ids = jnp.stack([z, g % 2])

    def shift(x, d):
        return lax.ppermute(x, "expert", [(i, (i + d) % owners) for i in range(owners)])

    def gather(x):
        return [x] + [shift(x, d) for d in range(1, owners)]

    def scatter(parts):
        return [parts[0]] + [shift(parts[d], -d) for d in range(1, owners)]

    def exchange(x, bit):
        return lax.ppermute(x, "group", [(i, i ^ (1 << bit)) for i in range(groups)])

    expert_ids = jnp.arange(experts, dtype=jnp.int32)
    valid = jnp.arange(seq, dtype=jnp.int32) < lengths[0]
    hits = (routes.T[None] == expert_ids[:, None, None]) & valid[None, None, :]
    table = jnp.min(jnp.where(hits, ranks.T[None], UNROUTED), 1)
    tables = gather(table)
    cots = gather(cotangent)
    gain_one = gain_one.reshape(1, width)
    gain_two = gain_two.reshape(1, width)
    router = w_router.T

    n1, q, kk, vv, lse, mixed, residual, n2, gates = call(
        dense_forward,
        [((seq, width), bf16)] * 4
        + [((seq, LANES), f32), ((seq, width), bf16), ((seq, width), f32), ((seq, width), bf16), ((experts, seq), f32)],
        lengths, inputs, gain_one, query_matrix, key_matrix, value_matrix, w_attn_out, gain_two, router, table,
        smem=1, flops=2 * seq * width * width * 4, name="dense_forward",
    )
    tokens = gather(n2)
    gate_tables = gather(gates)
    row_places, col_places = call(
        functools.partial(place_kernel, local, capacity),
        [((local, owners, seq), jnp.int32), ((seq, LANES), jnp.int32)],
        ids, *tables, smem=1, name="places",
    )

    piece = (width + half) // groups

    def run_expert(j):
        args = [row_places] + gate_tables + tokens + cots + [expert_in, expert_out]
        outs = [
            ((groups // 2, piece, width), bf16),
            ((groups // 2, piece, width), bf16),
            ((places, width), bf16),
            ((places, width), bf16),
            ((owners, seq), f32),
        ]
        picked = [pl.BlockSpec((1, owners, seq), lambda i: (j, 0, 0))]
        picked += [VMEM] * (3 * owners)
        picked += [
            pl.BlockSpec((1, width, 2 * half), lambda i: (j, 0, 0)),
            pl.BlockSpec((1, half, width), lambda i: (j, 0, 0)),
        ]
        return pl.pallas_call(
            functools.partial(expert_kernel, j, local, capacity, owners),
            grid=(1,),
            out_shape=[jax.ShapeDtypeStruct(s, d) for s, d in outs],
            in_specs=[SMEM] + picked,
            out_specs=[VMEM] * len(outs),
            scratch_shapes=[
                pltpu.VMEM((places, width), bf16),
                pltpu.VMEM((places, width), bf16),
                pltpu.VMEM((places, 1), f32),
                pltpu.VMEM((places, half), f32),
                pltpu.VMEM((places, half), f32),
                pltpu.VMEM((places, half), bf16),
                pltpu.VMEM((places, width), bf16),
                pltpu.VMEM((places, 2 * half), bf16),
                pltpu.VMEM((width, width), f32),
            ],
            compiler_params=pltpu.CompilerParams(vmem_limit_bytes=LIMIT),
            cost_estimate=pl.CostEstimate(
                flops=18 * places * width * half, bytes_accessed=20 << 20, transcendentals=0
            ),
            name=f"expert{j}",
        )(ids, *args)

    def reduce_group(keep, send, order):
        total = keep.astype(f32) + exchange(send, 0).astype(f32)
        done = []
        cut = total.shape[-1] // (2 * LANES) * LANES
        for cols, way in ((slice(0, cut), order), (slice(cut, None), order[::-1])):
            part = total[..., cols]
            part = part.reshape((2,) * (bits - 1) + part.shape[1:])
            left = list(range(bits - 1, 0, -1))
            for bit in way:
                axis = left.index(bit)
                left.pop(axis)
                mine = (g >> bit) & 1
                out = lax.dynamic_index_in_dim(part, 1 - mine, axis, keepdims=False).astype(bf16)
                own = lax.dynamic_index_in_dim(part, mine, axis, keepdims=False)
                part = own + exchange(out, bit).astype(f32)
            done.append(part)
        return done

    def gather_group(halves, order):
        wide = []
        for part, way in zip(halves, (order[::-1], order)):
            part = part.astype(bf16)
            left = []
            for bit in (*way, 0):
                at = len([b for b in left if b > bit])
                other = exchange(part, bit)
                mine = (g >> bit) & 1
                part = jnp.where(
                    mine == 0, jnp.stack([part, other], at), jnp.stack([other, part], at)
                )
                left = sorted(left + [bit], reverse=True)
            wide.append(part.reshape((groups,) + part.shape[-2:]))
        return jnp.concatenate(wide, -1)

    order = tuple(range(1, bits))
    returned, grad_rows, dots, full_in, full_out = [], [], [], [], []
    for j in range(local):
        keep, send, wret, grow, gg = run_expert(j)
        returned.append(wret)
        grad_rows.append(grow)
        dots.append(gg)
        whole = gather_group(reduce_group(keep, send, order), order)
        rows_in = width // groups
        full_in.append(whole[:, :rows_in].reshape(width, 2 * half).astype(f32))
        full_out.append(whole[:, rows_in:].reshape(half, width).astype(f32))

    def combine(rows, name):
        return call(
            functools.partial(combine_kernel, local, capacity, owners),
            [((seq, width), f32)] + [((seq, width), bf16)] * (owners - 1),
            col_places, *rows, flops=2 * seq * owners * local * capacity * width, name=name,
        )

    grad_parts = scatter(combine(grad_rows, "combine_grad"))
    dots = jnp.stack(dots, 1)
    dots = scatter([dots[d] for d in range(owners)])
    out_parts = scatter(combine(returned, "combine_out"))
    output = residual
    for part in out_parts:
        output = output + part.astype(f32)

    columns = 2 * width + key_matrix.shape[1] + value_matrix.shape[1] + LANES
    grad_inputs, keep, send = call(
        functools.partial(dense_backward, owners, local),
        [((seq, width), f32)] + [((groups // 2, width // groups, columns), bf16)] * 2,
        ids, lengths, *grad_parts, *dots, gates, inputs, cotangent, residual, n1, n2, q, kk, vv, lse, mixed,
        query_matrix, key_matrix, value_matrix, w_attn_out, router, gain_one, gain_two,
        smem=2, flops=2 * seq * width * width * 8, name="dense_backward",
        scratch=[
            pltpu.VMEM((experts, seq), f32),
            pltpu.VMEM((seq, width), bf16),
            pltpu.VMEM((seq, width), bf16),
            pltpu.VMEM((seq, key_matrix.shape[1]), bf16),
            pltpu.VMEM((seq, value_matrix.shape[1]), bf16),
            pltpu.VMEM((width, width), f32),
        ],
    )
    dense = jnp.concatenate(reduce_group(keep, send, order), -1)
    dense = dense.reshape((owners, dense.shape[0] // owners, columns)).astype(bf16)
    own = lax.dynamic_index_in_dim(dense, z, 0, keepdims=False).astype(f32)
    for d in range(1, owners):
        out = lax.dynamic_index_in_dim(dense, (z + d) % owners, 0, keepdims=False)
        own = own + shift(out, d).astype(f32)
    blocks = gather(own.astype(bf16))
    stacked = jnp.stack(blocks[::-1])
    dense = jnp.roll(stacked, z + 1, 0).reshape(-1, columns).astype(f32)
    sizes = (width, key_matrix.shape[1], value_matrix.shape[1], width, experts, 1, 1)
    cuts = []
    at = 0
    for size in sizes:
        cuts.append(dense[:, at : at + size])
        at += size
    return (
        output,
        grad_inputs,
        cuts[5].reshape(-1),
        cuts[0],
        cuts[1],
        cuts[2],
        cuts[3],
        cuts[6].reshape(-1),
        cuts[4],
        jnp.stack(full_in),
        jnp.stack(full_out),
    )


def solution(mesh):
    tokens = P(("group", "expert"), None)
    experts = P("expert", None, None)
    shares = P("group", None)
    return jax.shard_map(
        on_device,
        mesh=mesh,
        in_specs=(
            tokens, P(), P(), P(), P(), P(), P(), P(), experts, experts,
            P(("group", "expert")), tokens, tokens, tokens,
        ),
        out_specs=(
            tokens, tokens, P("group"), shares, shares, shares, shares, P("group"), shares,
            experts, experts,
        ),
        check_vma=False,
    )
```

time: 1230 us -> 487 us (0.40)
  waiting for transfers between devices: 787 us -> 248 us
  matrix products: 155 us -> 0 us
  local copies, waits for them, and re-layouts: 163 us -> 11.4 us
  Pallas kernels: 0 us -> 94.7 us
  starting transfers between devices: 22.4 us -> 95.8 us
  blocking collectives: 25.7 us -> 0 us
  other arithmetic: 50.7 us -> 29.3 us
  between operations: 16.5 us -> 3.07 us
    all_to_all x4 -> x0, waiting for transfers between devices: 381 us -> none  [the longest x1 103 us: on_device(): lax.all_to_all(grad_sent, 'expert', split_axis=0, concat_axis=0, tiled=True)]
    ppermute x0 -> x76, waiting for transfers between devices: none -> 248 us  [the longest x27 158 us: shift(): lax.ppermute(x, 'expert', [(i, (i + d) % owners) for i in range(owners)])]
    reduce_scatter x7 -> x0, waiting for transfers between devices: 195 us -> none  [the longest x1 55 us: on_device(): lax.psum_scatter(summed[1], 'group', scatter_dimension=0, tiled=True)]
    dot_general x77 -> x0, matrix products: 155 us -> none  [the longest x16 18.2 us: head_scores(): jnp.einsum('gqd,kd->gqk', query_head, key_head, preferred_element_type=jn...]
    all_gather x2 -> x0, waiting for transfers between devices: 137 us -> none  [the longest x1 91.8 us: on_device(): lax.all_gather(expert_parts[0], 'group', axis=1, tiled=True)]
    ppermute x0 -> x76, starting transfers between devices: none -> 95.8 us  [the longest x27 48.2 us: shift(): lax.ppermute(x, 'expert', [(i, (i + d) % owners) for i in range(owners)])]
    pallas_call x0 -> x9, Pallas kernels: none -> 94.7 us  [the longest x4 53.3 us: run_expert(): pl.pallas_call(functools.partial(expert_kernel, j, local, capacity, owner...]
    gather x7 -> x0, local copies, waits for them, and re-layouts: 83.2 us -> none  [the longest x1 14.5 us: on_device(): returned[safe_index].reshape(sequence_rows, route_count, model_width)]
  transfers between devices with their start and end apart: 14 -> 76, of which waited for: 12 -> 39; matrix products, arithmetic and copies ran while one was open for 17% -> 6% of each run, Pallas kernels for 0% -> 17%
where the time goes in v1:
time: 487 us; the launch traced here: 483 us
  waiting for transfers between devices  248 us (51%)
  starting transfers between devices  95.8 us (20%)
  Pallas kernels  94.7 us (19%)
  other arithmetic  29.3 us (6%)
  local copies, waits for them, and re-layouts  11.4 us (2%)
    ppermute x27, waiting for transfers between devices, shift(): lax.ppermute(x, 'expert', [(i, (i + d) % owners) for i in range(owners)])  158 us
    ppermute x49, waiting for transfers between devices, exchange(): return lax.ppermute(x, 'group', [(i, i ^ 1 << bit) for i in range(groups)])  90.5 us
    pallas_call x4, Pallas kernels, run_expert(): pl.pallas_call(functools.partial(expert_kernel, j, local, capacity, owner...  53.3 us
    ppermute x27, starting transfers between devices, shift(): lax.ppermute(x, 'expert', [(i, (i + d) % owners) for i in range(owners)])  48.2 us
    ppermute x49, starting transfers between devices, exchange(): return lax.ppermute(x, 'group', [(i, i ^ 1 << bit) for i in range(groups)])  47.6 us
    pallas_call x5, Pallas kernels, call(): pl.pallas_call(kernel, out_shape=outs, in_specs=[SMEM] * smem + [VMEM] *...  41.4 us
  transfers between devices with their start and end apart: 76, of which 39 were waited for; matrix products, arithmetic and copies ran while one was open for 6% of the time, Pallas kernels for 17%

profile of v1, /device:TPU:0, one launch (start us, length us, event | category | flops | bytes accessed | tf_op | source)
XLA Modules:
  0.0 482.7 jit_solution(31618299386240168)
XLA Ops:
  0.6 5.1 %collective-permute-start.11 = (bf16[256,1024]{1,0:T(8,128)(2,1)}, bf16[256,1024]{1,0:T(8,128)(2,1)S(1)}, u32[]{:S(2)}, u32[]{:S(2)}) collective-permute-start(bf16[256,1024]{1,0:T(8,128)(2,1)} %refs_10_.1), channel_id=1, source_target_pairs={{0,3},{1,0},{2,1},{3,2},{4,7},{5,4},{6,5},{7,6},{8,11},{9,8},{10,9... | collective-permute-start | bytes 1572872 | tf_op jit(solution)/shard_map/ppermute | solution.py:326
  9.3 8.4 %dense_forward.1 = (bf16[256,1024]{1,0:T(8,128)(2,1)}, bf16[256,1024]{1,0:T(8,128)(2,1)}, bf16[256,1024]{1,0:T(8,128)(2,1)}, bf16[256,1024]{1,0:T(8,128)(2,1)}, ...) custom-call(s32[1]{0:T(128)} %copy.187.len_ref, ...), custom_call_target="tpu_custom_call" | custom-call | flops 2147483648 | bytes 11214852 | tf_op jit(solution)/shard_map/dense_forward/pallas_call | solution.py:35
  17.7 2.4 collective-permute-start.5
  23.2 2.3 collective-permute-start.9
  25.6 19.7 %collective-permute-done.4.refs_3_ = f32[16,256]{1,0:T(8,128)S(1)} collective-permute-done((f32[16,256]{1,0:T(8,128)}, f32[16,256]{1,0:T(8,128)S(1)}, u32[]{:S(2)}, u32[]{:S(2)}) %collective-permute-start.4) | collective-permute-done | bytes 16416 | tf_op jit(solution)/shard_map/ppermute | solution.py:326
  45.3 2.2 collective-permute-start.6
  48.1 2.3 places.1
  50.4 31.0 %collective-permute-done.10.refs_11_ = bf16[256,1024]{1,0:T(8,128)(2,1)S(1)} collective-permute-done((bf16[256,1024]{1,0:T(8,128)(2,1)S(1)}, bf16[256,1024]{1,0:T(8,128)(2,1)S(1)}, u32[]{:S(2)}, u32[]{:S(2)}) %collective-permute-start.10) | collective-permute-done | bytes 524320 | tf_op jit(solution)/shard_map/ppermute | solution.py:326
  81.4 22.1 %collective-permute-done.7.refs_7_ = bf16[256,1024]{1,0:T(8,128)(2,1)} collective-permute-done((bf16[256,1024]{1,0:T(8,128)(2,1)}, bf16[256,1024]{1,0:T(8,128)(2,1)}, u32[]{:S(2)}, u32[]{:S(2)}) %collective-permute-start.7) | collective-permute-done | bytes 524320 | tf_op jit(solution)/shard_map/ppermute | solution.py:326
  103.6 13.1 %expert3.1 = (bf16[4,192,1024]{2,1,0:T(8,128)(2,1)}, bf16[4,192,1024]{2,1,0:T(8,128)(2,1)}, bf16[640,1024]{1,0:T(8,128)(2,1)}, bf16[640,1024]{1,0:T(8,128)(2,1)}, f32[4,256]{1,0:T(4,128)}) custom-call(s32[2]{0:T(128)} %pad_add_fusion.id_ref, s32[4,4,256]{2,1,0:T(4,128)} %get-tuple-element.55.refs_0_, f32[16,256]{1,0:T(8,128)} %get-tuple-element.56.refs_1_.refs_8_, ...), custom_call_target="tpu_custom_call" | custom-call | flops 6039797760 | bytes 20971520 | tf_op jit(solution)/shard_map/expert3/pallas_call | solution.py:379
  116.8 13.3 %expert2.1 = (bf16[4,192,1024]{2,1,0:T(8,128)(2,1)}, bf16[4,192,1024]{2,1,0:T(8,128)(2,1)}, bf16[640,1024]{1,0:T(8,128)(2,1)}, bf16[640,1024]{1,0:T(8,128)(2,1)}, f32[4,256]{1,0:T(4,128)}) custom-call(s32[2]{0:T(128)} %pad_add_fusion.id_ref, s32[4,4,256]{2,1,0:T(4,128)} %get-tuple-element.55.refs_0_, f32[16,256]{1,0:T(8,128)} %get-tuple-element.56.refs_1_.refs_8_, ...), custom_call_target="tpu_custom_call" | custom-call | flops 6039797760 | bytes 20971520 | tf_op jit(solution)/shard_map/expert2/pallas_call | solution.py:379
  130.1 13.3 %expert1.1 = (bf16[4,192,1024]{2,1,0:T(8,128)(2,1)}, bf16[4,192,1024]{2,1,0:T(8,128)(2,1)}, bf16[640,1024]{1,0:T(8,128)(2,1)}, bf16[640,1024]{1,0:T(8,128)(2,1)}, f32[4,256]{1,0:T(4,128)}) custom-call(s32[2]{0:T(128)} %pad_add_fusion.id_ref, s32[4,4,256]{2,1,0:T(4,128)} %get-tuple-element.55.refs_0_, f32[16,256]{1,0:T(8,128)} %get-tuple-element.56.refs_1_.refs_8_, ...), custom_call_target="tpu_custom_call" | custom-call | flops 6039797760 | bytes 20971520 | tf_op jit(solution)/shard_map/expert1/pallas_call | solution.py:379
  143.4 13.6 %expert0.1 = (bf16[4,192,1024]{2,1,0:T(8,128)(2,1)}, bf16[4,192,1024]{2,1,0:T(8,128)(2,1)}, bf16[640,1024]{1,0:T(8,128)(2,1)}, bf16[640,1024]{1,0:T(8,128)(2,1)}, f32[4,256]{1,0:T(4,128)}) custom-call(s32[2]{0:T(128)} %pad_add_fusion.id_ref, s32[4,4,256]{2,1,0:T(4,128)} %get-tuple-element.55.refs_0_, f32[16,256]{1,0:T(8,128)} %get-tuple-element.56.refs_1_.refs_8_, ...), custom_call_target="tpu_custom_call" | custom-call | flops 6039797760 | bytes 20971520 | tf_op jit(solution)/shard_map/expert0/pallas_call | solution.py:379
  157.0 5.9 %combine_grad.1 = (f32[256,1024]{1,0:T(8,128)}, bf16[256,1024]{1,0:T(8,128)(2,1)}, bf16[256,1024]{1,0:T(8,128)(2,1)}, bf16[256,1024]{1,0:T(8,128)(2,1)}) custom-call(s32[256,128]{1,0:T(8,128)} %get-tuple-element.54.col_ref, bf16[640,1024]{1,0:T(8,128)(2,1)} %get-tuple-element.66.refs_0_, bf16[640,1024]{1,0:T(8,128)(2,1)} %get-tuple-element.67.refs_1_, ...), custom_call_target="tpu_custom_call" | custom-call | flops 1342177280 | bytes 7995392 | tf_op jit(solution)/shard_map/combine_grad/pallas_call | solution.py:35
  164.2 2.1 collective-permute-start.17
  167.1 33.6 %collective-permute-done.20.refs_7_ = f32[4,256]{1,0:T(4,128)S(1)} collective-permute-done((f32[4,256]{1,0:T(4,128)S(1)}, f32[4,256]{1,0:T(4,128)S(1)}, u32[]{:S(2)}, u32[]{:S(2)}) %collective-permute-start.20) | collective-permute-done | bytes 4128 | tf_op jit(solution)/shard_map/ppermute | solution.py:326
  200.8 11.7 %collective-permute-start.19 = (f32[4,256]{1,0:T(4,128)S(1)}, f32[4,256]{1,0:T(4,128)S(1)}, u32[]{:S(2)}, u32[]{:S(2)}) collective-permute-start(f32[4,256]{1,0:T(4,128)S(1)} %get-tuple-element.161), channel_id=1, source_target_pairs={{0,2},{1,3},{2,0},{3,1},{4,6},{5,7},{6,4},{7,5},{8,10},{9,11},{10,... | collective-permute-start | bytes 12296 | tf_op jit(solution)/shard_map/ppermute | solution.py:326
  214.5 5.8 %combine_out.1 = (f32[256,1024]{1,0:T(8,128)}, bf16[256,1024]{1,0:T(8,128)(2,1)}, bf16[256,1024]{1,0:T(8,128)(2,1)}, bf16[256,1024]{1,0:T(8,128)(2,1)}) custom-call(s32[256,128]{1,0:T(8,128)} %get-tuple-element.54.col_ref, bf16[640,1024]{1,0:T(8,128)(2,1)} %get-tuple-element.58.refs_0_, bf16[640,1024]{1,0:T(8,128)(2,1)} %get-tuple-element.59.refs_1_, ...), custom_call_target="tpu_custom_call" | custom-call | flops 1342177280 | bytes 7995392 | tf_op jit(solution)/shard_map/combine_out/pallas_call | solution.py:35
  220.4 4.0 collective-permute-start.12
  225.4 19.0 %dense_backward.1 = (f32[256,1024]{1,0:T(8,128)}, bf16[4,128,3200]{2,1,0:T(8,128)(2,1)}, bf16[4,128,3200]{2,1,0:T(8,128)(2,1)}) custom-call(s32[2]{0:T(128)} %pad_add_fusion.id_ref, s32[1]{0:T(128)} %copy.187.len_ref, f32[256,1024]{1,0:T(8,128)} %get-tuple-element.70.refs_0_, bf16[256,1024]{1,0:T(8,128)(2,1)} %copy-done.16, bf16[256,1024]{1,0:T(8,128)(2,1)} %copy-done.17, ...), custom_call_target="tpu_custom_call" | custom-call | flops 4294967296 | bytes 21962764 | tf_op jit(solution)/shard_map/dense_backward/pallas_call | solution.py:35
  244.9 23.4 %collective-permute-done.13 = bf16[256,1024]{1,0:T(8,128)(2,1)} collective-permute-done((bf16[256,1024]{1,0:T(8,128)(2,1)}, bf16[256,1024]{1,0:T(8,128)(2,1)}, u32[]{:S(2)}, u32[]{:S(2)}) %collective-permute-start.13) | collective-permute-done | bytes 524320 | tf_op jit(solution)/shard_map/ppermute | solution.py:326
  268.7 2.7 convert_add_fusion.5
  281.8 3.0 collective-permute-done.71
  286.4 6.8 %collective-permute-done.60 = bf16[2,192,512]{2,1,0:T(8,128)(2,1)S(1)} collective-permute-done((bf16[2,192,512]{2,1,0:T(8,128)(2,1)S(1)}, bf16[2,192,512]{2,1,0:T(8,128)(2,1)S(1)}, u32[]{:S(2)}, u32[]{:S(2)}) %collective-permute-start.60) | collective-permute-done | bytes 393248 | tf_op jit(solution)/shard_map/ppermute | solution.py:335
  297.3 4.3 collective-permute-done.49
  303.2 2.0 collective-permute-done.44
  307.0 3.0 collective-permute-done.38
  311.6 2.0 collective-permute-done.33
  315.4 2.5 collective-permute-done.72
  342.7 1.9 collective-permute-done.40
  344.7 3.1 collective-permute-done.35
  350.3 2.1 collective-permute-start.58
  352.6 7.4 %collective-permute-done.74 = bf16[2,192,512]{2,1,0:T(8,128)(2,1)S(1)} collective-permute-done((bf16[2,192,512]{2,1,0:T(8,128)(2,1)S(1)}, bf16[2,192,512]{2,1,0:T(8,128)(2,1)S(1)}, u32[]{:S(2)}, u32[]{:S(2)}) %collective-permute-start.74) | collective-permute-done | bytes 393248 | tf_op jit(solution)/shard_map/ppermute | solution.py:335
  362.1 6.4 %collective-permute-done.63 = bf16[2,192,512]{2,1,0:T(8,128)(2,1)S(1)} collective-permute-done((bf16[2,192,512]{2,1,0:T(8,128)(2,1)S(1)}, bf16[2,192,512]{2,1,0:T(8,128)(2,1)S(1)}, u32[]{:S(2)}, u32[]{:S(2)}) %collective-permute-start.63) | collective-permute-done | bytes 393248 | tf_op jit(solution)/shard_map/ppermute | solution.py:335
  370.7 9.1 %collective-permute-done.36 = bf16[2,192,512]{2,1,0:T(8,128)(2,1)S(1)} collective-permute-done((bf16[2,192,512]{2,1,0:T(8,128)(2,1)S(1)}, bf16[2,192,512]{2,1,0:T(8,128)(2,1)S(1)}, u32[]{:S(2)}, u32[]{:S(2)}) %collective-permute-start.36) | collective-permute-done | bytes 393248 | tf_op jit(solution)/shard_map/ppermute | solution.py:335
  393.1 3.6 convert_add_fusion
  398.7 6.3 %maximum_convert_fusion = f32[4,1024,1024]{2,1,0:T(8,128)} fusion(bf16[1,1024,1024]{2,1,0:T(8,128)(2,1)S(1)} %bitcast.340, bf16[1,1024,1024]{2,1,0:T(8,128)(2,1)S(1)} %bitcast.341, bf16[1,1024,1024]{2,1,0:T(8,128)(2,1)S(1)} %bitcast.342, bf16[1,1024,1024]{2,1,0:T(8,128)(2,1)S(1)} %bitcast.343), kind=kLoop, calls=%fused_computation | loop fusion | flops 16777216 | bytes 25165824 | tf_op jit(solution)/shard_map/stack | solution.py:505
  406.2 10.7 %collective-permute-done.22 = bf16[2,128,1536]{2,1,0:T(8,128)(2,1)S(1)} collective-permute-done((bf16[2,128,1536]{2,1,0:T(8,128)(2,1)S(1)}, bf16[2,128,1536]{2,1,0:T(8,128)(2,1)S(1)}, u32[]{:S(2)}, u32[]{:S(2)}) %collective-permute-start.22) | collective-permute-done | bytes 786464 | tf_op jit(solution)/shard_map/ppermute | solution.py:335
  417.7 9.7 %collective-permute-done.24 = bf16[2,128,1664]{2,1,0:T(8,128)(2,1)S(1)} collective-permute-done((bf16[2,128,1664]{2,1,0:T(8,128)(2,1)S(1)}, bf16[2,128,1664]{2,1,0:T(8,128)(2,1)S(1)}, u32[]{:S(2)}, u32[]{:S(2)}) %collective-permute-start.24) | collective-permute-done | bytes 852000 | tf_op jit(solution)/shard_map/ppermute | solution.py:335
  428.2 6.5 %collective-permute-done.23 = bf16[128,1536]{1,0:T(8,128)(2,1)S(1)} collective-permute-done((bf16[128,1536]{1,0:T(8,128)(2,1)S(1)}, bf16[128,1536]{1,0:T(8,128)(2,1)S(1)}, u32[]{:S(2)}, u32[]{:S(2)}) %collective-permute-start.23) | collective-permute-done | bytes 393248 | tf_op jit(solution)/shard_map/ppermute | solution.py:335
  434.7 2.5 collective-permute-done.25
  437.4 2.5 collective-permute-start.26
  441.3 2.6 collective-permute-start.27
  444.2 3.2 collective-permute-done.26
  448.1 8.4 %collective-permute-done.27 = bf16[32,3200]{1,0:T(8,128)(2,1)S(1)} collective-permute-done((bf16[32,3200]{1,0:T(8,128)(2,1)S(1)}, bf16[32,3200]{1,0:T(8,128)(2,1)S(1)}, u32[]{:S(2)}, u32[]{:S(2)}) %collective-permute-start.27) | collective-permute-done | bytes 204832 | tf_op jit(solution)/shard_map/ppermute | solution.py:326
  456.6 3.4 collective-permute-start.29
  460.0 3.7 maximum_convert_fusion.1
  464.4 14.1 %collective-permute-done.30 = bf16[32,3200]{1,0:T(8,128)(2,1)S(1)} collective-permute-done((bf16[32,3200]{1,0:T(8,128)(2,1)S(1)}, bf16[32,3200]{1,0:T(8,128)(2,1)S(1)}, u32[]{:S(2)}, u32[]{:S(2)}) %collective-permute-start.30) | collective-permute-done | bytes 204832 | tf_op jit(solution)/shard_map/ppermute | solution.py:326
  (315 shorter events, 91.9 us)
Async XLA Ops:
  0.6 44.7 %collective-permute-start.11 = (bf16[256,1024]{1,0:T(8,128)(2,1)}, bf16[256,1024]{1,0:T(8,128)(2,1)S(1)}, u32[]{:S(2)}, u32[]{:S(2)}) collective-permute-start(bf16[256,1024]{1,0:T(8,128)(2,1)} %refs_10_.1), channel_id=1, source_target_pairs={{0,3},{1,0},{2,1},{3,2},{4,7},{5,4},{6,5},{7,6},{8,11},{9,8},{10,9... | collective-permute-start | bytes 1572872 | tf_op jit(solution)/shard_map/ppermute | solution.py:326
  7.2 12.9 %collective-permute-start.2 = (s32[16,256]{1,0:T(8,128)S(1)}, s32[16,256]{1,0:T(8,128)S(1)}, u32[]{:S(2)}, u32[]{:S(2)}) collective-permute-start(s32[16,256]{1,0:T(8,128)S(1)} %select_reduce_fusion.table_ref.refs_0_), channel_id=1, source_target_pairs={{0,3},{1,0},{2,1},{3,2},{4,7},{5,4},{6,5},{7,6},{8,11},{9,8},{10,9... | collective-permute-start | bytes 49160 | tf_op jit(solution)/shard_map/ppermute | solution.py:326
  7.7 13.4 %collective-permute-start.1 = (s32[16,256]{1,0:T(8,128)S(1)}, s32[16,256]{1,0:T(8,128)S(1)}, u32[]{:S(2)}, u32[]{:S(2)}) collective-permute-start(s32[16,256]{1,0:T(8,128)S(1)} %select_reduce_fusion.table_ref.refs_0_), channel_id=1, source_target_pairs={{0,2},{1,3},{2,0},{3,1},{4,6},{5,7},{6,4},{7,5},{8,10},{9,11},{10,... | collective-permute-start | bytes 49160 | tf_op jit(solution)/shard_map/ppermute | solution.py:326
  7.7 15.1 %collective-permute-start = (s32[16,256]{1,0:T(8,128)S(1)}, s32[16,256]{1,0:T(8,128)S(1)}, u32[]{:S(2)}, u32[]{:S(2)}) collective-permute-start(s32[16,256]{1,0:T(8,128)S(1)} %select_reduce_fusion.table_ref.refs_0_), channel_id=1, source_target_pairs={{0,1},{1,2},{2,3},{3,0},{4,5},{5,6},{6,7},{7,4},{8,9},{9,10},{10,1... | collective-permute-start | bytes 49160 | tf_op jit(solution)/shard_map/ppermute | solution.py:326
  20.1 25.1 %collective-permute-start.4 = (f32[16,256]{1,0:T(8,128)}, f32[16,256]{1,0:T(8,128)S(1)}, u32[]{:S(2)}, u32[]{:S(2)}) collective-permute-start(f32[16,256]{1,0:T(8,128)} %get-tuple-element.56.refs_1_.refs_8_), channel_id=1, source_target_pairs={{0,2},{1,3},{2,0},{3,1},{4,6},{5,7},{6,4},{7,5},{8,10},{9,11},{10,... | collective-permute-start | bytes 49160 | tf_op jit(solution)/shard_map/ppermute | solution.py:326
  21.1 24.1 %collective-permute-start.3 = (f32[16,256]{1,0:T(8,128)}, f32[16,256]{1,0:T(8,128)S(1)}, u32[]{:S(2)}, u32[]{:S(2)}) collective-permute-start(f32[16,256]{1,0:T(8,128)} %get-tuple-element.56.refs_1_.refs_8_), channel_id=1, source_target_pairs={{0,1},{1,2},{2,3},{3,0},{4,5},{5,6},{6,7},{7,4},{8,9},{9,10},{10,1... | collective-permute-start | bytes 49160 | tf_op jit(solution)/shard_map/ppermute | solution.py:326
  22.8 58.6 %collective-permute-start.10 = (bf16[256,1024]{1,0:T(8,128)(2,1)S(1)}, bf16[256,1024]{1,0:T(8,128)(2,1)S(1)}, u32[]{:S(2)}, u32[]{:S(2)}) collective-permute-start(bf16[256,1024]{1,0:T(8,128)(2,1)S(1)} %copy-done.15), channel_id=1, source_target_pairs={{0,2},{1,3},{2,0},{3,1},{4,6},{5,7},{6,4},{7,5},{8,10},{9,11},{10,... | collective-permute-start | bytes 1572872 | tf_op jit(solution)/shard_map/ppermute | solution.py:326
  23.2 58.2 %collective-permute-start.9 = (bf16[256,1024]{1,0:T(8,128)(2,1)S(1)}, bf16[256,1024]{1,0:T(8,128)(2,1)S(1)}, u32[]{:S(2)}, u32[]{:S(2)}) collective-permute-start(bf16[256,1024]{1,0:T(8,128)(2,1)S(1)} %copy-done.15), channel_id=1, source_target_pairs={{0,1},{1,2},{2,3},{3,0},{4,5},{5,6},{6,7},{7,4},{8,9},{9,10},{10,1... | collective-permute-start | bytes 1572872 | tf_op jit(solution)/shard_map/ppermute | solution.py:326
  45.2 36.2 %collective-permute-start.8 = (bf16[256,1024]{1,0:T(8,128)(2,1)}, bf16[256,1024]{1,0:T(8,128)(2,1)S(1)}, u32[]{:S(2)}, u32[]{:S(2)}) collective-permute-start(bf16[256,1024]{1,0:T(8,128)(2,1)} %get-tuple-element.57.refs_5_.refs_13_), channel_id=1, source_target_pairs={{0,3},{1,0},{2,1},{3,2},{4,7},{5,4},{6,5},{7,6},{8,11},{9,8},{10,9... | collective-permute-start | bytes 1572872 | tf_op jit(solution)/shard_map/ppermute | solution.py:326
  45.2 58.3 %collective-permute-start.7 = (bf16[256,1024]{1,0:T(8,128)(2,1)}, bf16[256,1024]{1,0:T(8,128)(2,1)}, u32[]{:S(2)}, u32[]{:S(2)}) collective-permute-start(bf16[256,1024]{1,0:T(8,128)(2,1)} %get-tuple-element.57.refs_5_.refs_13_), channel_id=1, source_target_pairs={{0,2},{1,3},{2,0},{3,1},{4,6},{5,7},{6,4},{7,5},{8,10},{9,11},{10,... | collective-permute-start | bytes 1572872 | tf_op jit(solution)/shard_map/ppermute | solution.py:326
  45.3 58.2 %collective-permute-start.6 = (bf16[256,1024]{1,0:T(8,128)(2,1)}, bf16[256,1024]{1,0:T(8,128)(2,1)}, u32[]{:S(2)}, u32[]{:S(2)}) collective-permute-start(bf16[256,1024]{1,0:T(8,128)(2,1)} %get-tuple-element.57.refs_5_.refs_13_), channel_id=1, source_target_pairs={{0,1},{1,2},{2,3},{3,0},{4,5},{5,6},{6,7},{7,4},{8,9},{9,10},{10,1... | collective-permute-start | bytes 1572872 | tf_op jit(solution)/shard_map/ppermute | solution.py:326
  116.7 154.8 %collective-permute-start.65 = (bf16[4,192,1024]{2,1,0:T(8,128)(2,1)}, bf16[4,192,1024]{2,1,0:T(8,128)(2,1)S(1)}, u32[]{:S(2)}, u32[]{:S(2)}) collective-permute-start(bf16[4,192,1024]{2,1,0:T(8,128)(2,1)} %get-tuple-element.94), channel_id=1, source_target_pairs={{0,4},{4,0},{8,12},{12,8},{16,20},{20,16},{24,28},{28,24},{1,5},{5... | collective-permute-start | bytes 4718600 | tf_op jit(solution)/shard_map/ppermute | solution.py:335
  162.9 61.5 %collective-permute-start.15 = (bf16[256,1024]{1,0:T(8,128)(2,1)}, bf16[256,1024]{1,0:T(8,128)(2,1)S(1)}, u32[]{:S(2)}, u32[]{:S(2)}) collective-permute-start(bf16[256,1024]{1,0:T(8,128)(2,1)} %get-tuple-element.71), channel_id=1, source_target_pairs={{0,3},{1,0},{2,1},{3,2},{4,7},{5,4},{6,5},{7,6},{8,11},{9,8},{10,9... | collective-permute-start | bytes 1572872 | tf_op jit(solution)/shard_map/ppermute | solution.py:326
  162.9 61.5 %collective-permute-start.16 = (bf16[256,1024]{1,0:T(8,128)(2,1)}, bf16[256,1024]{1,0:T(8,128)(2,1)S(1)}, u32[]{:S(2)}, u32[]{:S(2)}) collective-permute-start(bf16[256,1024]{1,0:T(8,128)(2,1)} %get-tuple-element.72), channel_id=1, source_target_pairs={{0,2},{1,3},{2,0},{3,1},{4,6},{5,7},{6,4},{7,5},{8,10},{9,11},{10,... | collective-permute-start | bytes 1572872 | tf_op jit(solution)/shard_map/ppermute | solution.py:326
  164.2 61.0 %collective-permute-start.17 = (bf16[256,1024]{1,0:T(8,128)(2,1)}, bf16[256,1024]{1,0:T(8,128)(2,1)}, u32[]{:S(2)}, u32[]{:S(2)}) collective-permute-start(bf16[256,1024]{1,0:T(8,128)(2,1)} %get-tuple-element.73), channel_id=1, source_target_pairs={{0,1},{1,2},{2,3},{3,0},{4,5},{5,6},{6,7},{7,4},{8,9},{9,10},{10,1... | collective-permute-start | bytes 1572872 | tf_op jit(solution)/shard_map/ppermute | solution.py:326
  166.9 33.9 %collective-permute-start.20 = (f32[4,256]{1,0:T(4,128)S(1)}, f32[4,256]{1,0:T(4,128)S(1)}, u32[]{:S(2)}, u32[]{:S(2)}) collective-permute-start(f32[4,256]{1,0:T(4,128)S(1)} %get-tuple-element.160), channel_id=1, source_target_pairs={{0,1},{1,2},{2,3},{3,0},{4,5},{5,6},{6,7},{7,4},{8,9},{9,10},{10,1... | collective-permute-start | bytes 12296 | tf_op jit(solution)/shard_map/ppermute | solution.py:326
  200.8 13.3 %collective-permute-start.19 = (f32[4,256]{1,0:T(4,128)S(1)}, f32[4,256]{1,0:T(4,128)S(1)}, u32[]{:S(2)}, u32[]{:S(2)}) collective-permute-start(f32[4,256]{1,0:T(4,128)S(1)} %get-tuple-element.161), channel_id=1, source_target_pairs={{0,2},{1,3},{2,0},{3,1},{4,6},{5,7},{6,4},{7,5},{8,10},{9,11},{10,... | collective-permute-start | bytes 12296 | tf_op jit(solution)/shard_map/ppermute | solution.py:326
  220.4 24.0 %collective-permute-start.12 = (bf16[256,1024]{1,0:T(8,128)(2,1)}, bf16[256,1024]{1,0:T(8,128)(2,1)S(1)}, u32[]{:S(2)}, u32[]{:S(2)}) collective-permute-start(bf16[256,1024]{1,0:T(8,128)(2,1)} %get-tuple-element.63), channel_id=1, source_target_pairs={{0,3},{1,0},{2,1},{3,2},{4,7},{5,4},{6,5},{7,6},{8,11},{9,8},{10,9... | collective-permute-start | bytes 1572872 | tf_op jit(solution)/shard_map/ppermute | solution.py:326
  224.4 43.9 %collective-permute-start.13 = (bf16[256,1024]{1,0:T(8,128)(2,1)}, bf16[256,1024]{1,0:T(8,128)(2,1)}, u32[]{:S(2)}, u32[]{:S(2)}) collective-permute-start(bf16[256,1024]{1,0:T(8,128)(2,1)} %get-tuple-element.64), channel_id=1, source_target_pairs={{0,2},{1,3},{2,0},{3,1},{4,6},{5,7},{6,4},{7,5},{8,10},{9,11},{10,... | collective-permute-start | bytes 1572872 | tf_op jit(solution)/shard_map/ppermute | solution.py:326
  224.4 43.8 %collective-permute-start.14 = (bf16[256,1024]{1,0:T(8,128)(2,1)}, bf16[256,1024]{1,0:T(8,128)(2,1)}, u32[]{:S(2)}, u32[]{:S(2)}) collective-permute-start(bf16[256,1024]{1,0:T(8,128)(2,1)} %get-tuple-element.65), channel_id=1, source_target_pairs={{0,1},{1,2},{2,3},{3,0},{4,5},{5,6},{6,7},{7,4},{8,9},{9,10},{10,1... | collective-permute-start | bytes 1572872 | tf_op jit(solution)/shard_map/ppermute | solution.py:326
  225.2 49.1 %collective-permute-start.54 = (bf16[4,192,1024]{2,1,0:T(8,128)(2,1)}, bf16[4,192,1024]{2,1,0:T(8,128)(2,1)S(1)}, u32[]{:S(2)}, u32[]{:S(2)}) collective-permute-start(bf16[4,192,1024]{2,1,0:T(8,128)(2,1)} %get-tuple-element.92), channel_id=1, source_target_pairs={{0,4},{4,0},{8,12},{12,8},{16,20},{20,16},{24,28},{28,24},{1,5},{5... | collective-permute-start | bytes 4718600 | tf_op jit(solution)/shard_map/ppermute | solution.py:335
  244.4 32.7 %collective-permute-start.43 = (bf16[4,192,1024]{2,1,0:T(8,128)(2,1)}, bf16[4,192,1024]{2,1,0:T(8,128)(2,1)S(1)}, u32[]{:S(2)}, u32[]{:S(2)}) collective-permute-start(bf16[4,192,1024]{2,1,0:T(8,128)(2,1)} %get-tuple-element.90), channel_id=1, source_target_pairs={{0,4},{4,0},{8,12},{12,8},{16,20},{20,16},{24,28},{28,24},{1,5},{5... | collective-permute-start | bytes 4718600 | tf_op jit(solution)/shard_map/ppermute | solution.py:335
  268.2 11.2 %collective-permute-start.32 = (bf16[4,192,1024]{2,1,0:T(8,128)(2,1)}, bf16[4,192,1024]{2,1,0:T(8,128)(2,1)S(1)}, u32[]{:S(2)}, u32[]{:S(2)}) collective-permute-start(bf16[4,192,1024]{2,1,0:T(8,128)(2,1)} %get-tuple-element.88), channel_id=1, source_target_pairs={{0,4},{4,0},{8,12},{12,8},{16,20},{20,16},{24,28},{28,24},{1,5},{5... | collective-permute-start | bytes 4718600 | tf_op jit(solution)/shard_map/ppermute | solution.py:335
  268.2 123.2 %collective-permute-start.21 = (bf16[4,128,3200]{2,1,0:T(8,128)(2,1)}, bf16[4,128,3200]{2,1,0:T(8,128)(2,1)S(1)}, u32[]{:S(2)}, u32[]{:S(2)}) collective-permute-start(bf16[4,128,3200]{2,1,0:T(8,128)(2,1)} %get-tuple-element.86), channel_id=1, source_target_pairs={{0,4},{4,0},{8,12},{12,8},{16,20},{20,16},{24,28},{28,24},{1,5},{5... | collective-permute-start | bytes 9830408 | tf_op jit(solution)/shard_map/ppermute | solution.py:335
  272.7 12.0 %collective-permute-start.71 = (bf16[2,192,512]{2,1,0:T(8,128)(2,1)S(1)}, bf16[2,192,512]{2,1,0:T(8,128)(2,1)S(1)}, u32[]{:S(2)}, u32[]{:S(2)}) collective-permute-start(bf16[2,192,512]{2,1,0:T(8,128)(2,1)S(1)} %fusion.18), channel_id=1, source_target_pairs={{0,16},{4,20},{8,24},{12,28},{16,0},{20,4},{24,8},{28,12},{1,17},{... | collective-permute-start | bytes 1179656 | tf_op jit(solution)/shard_map/ppermute | solution.py:335
  274.3 20.4 %collective-permute-start.66 = (bf16[2,192,512]{2,1,0:T(8,128)(2,1)S(1)}, bf16[2,192,512]{2,1,0:T(8,128)(2,1)S(1)}, u32[]{:S(2)}, u32[]{:S(2)}) collective-permute-start(bf16[2,192,512]{2,1,0:T(8,128)(2,1)S(1)} %fusion.22), channel_id=1, source_target_pairs={{0,8},{4,12},{8,0},{12,4},{16,24},{20,28},{24,16},{28,20},{1,9},{5... | collective-permute-start | bytes 1179656 | tf_op jit(solution)/shard_map/ppermute | solution.py:335
  277.1 16.0 %collective-permute-start.60 = (bf16[2,192,512]{2,1,0:T(8,128)(2,1)S(1)}, bf16[2,192,512]{2,1,0:T(8,128)(2,1)S(1)}, u32[]{:S(2)}, u32[]{:S(2)}) collective-permute-start(bf16[2,192,512]{2,1,0:T(8,128)(2,1)S(1)} %fusion.17), channel_id=1, source_target_pairs={{0,16},{4,20},{8,24},{12,28},{16,0},{20,4},{24,8},{28,12},{1,17},{... | collective-permute-start | bytes 1179656 | tf_op jit(solution)/shard_map/ppermute | solution.py:335
  279.5 17.0 %collective-permute-start.55 = (bf16[2,192,512]{2,1,0:T(8,128)(2,1)S(1)}, bf16[2,192,512]{2,1,0:T(8,128)(2,1)S(1)}, u32[]{:S(2)}, u32[]{:S(2)}) collective-permute-start(bf16[2,192,512]{2,1,0:T(8,128)(2,1)S(1)} %fusion.21), channel_id=1, source_target_pairs={{0,8},{4,12},{8,0},{12,4},{16,24},{20,28},{24,16},{28,20},{1,9},{5... | collective-permute-start | bytes 1179656 | tf_op jit(solution)/shard_map/ppermute | solution.py:335
  284.7 16.9 %collective-permute-start.49 = (bf16[2,192,512]{2,1,0:T(8,128)(2,1)S(1)}, bf16[2,192,512]{2,1,0:T(8,128)(2,1)S(1)}, u32[]{:S(2)}, u32[]{:S(2)}) collective-permute-start(bf16[2,192,512]{2,1,0:T(8,128)(2,1)S(1)} %fusion.16), channel_id=1, source_target_pairs={{0,16},{4,20},{8,24},{12,28},{16,0},{20,4},{24,8},{28,12},{1,17},{... | collective-permute-start | bytes 1179656 | tf_op jit(solution)/shard_map/ppermute | solution.py:335
  293.2 12.1 %collective-permute-start.44 = (bf16[2,192,512]{2,1,0:T(8,128)(2,1)S(1)}, bf16[2,192,512]{2,1,0:T(8,128)(2,1)S(1)}, u32[]{:S(2)}, u32[]{:S(2)}) collective-permute-start(bf16[2,192,512]{2,1,0:T(8,128)(2,1)S(1)} %fusion.20), channel_id=1, source_target_pairs={{0,8},{4,12},{8,0},{12,4},{16,24},{20,28},{24,16},{28,20},{1,9},{5... | collective-permute-start | bytes 1179656 | tf_op jit(solution)/shard_map/ppermute | solution.py:335
  294.8 15.2 %collective-permute-start.38 = (bf16[2,192,512]{2,1,0:T(8,128)(2,1)S(1)}, bf16[2,192,512]{2,1,0:T(8,128)(2,1)S(1)}, u32[]{:S(2)}, u32[]{:S(2)}) collective-permute-start(bf16[2,192,512]{2,1,0:T(8,128)(2,1)S(1)} %fusion.15), channel_id=1, source_target_pairs={{0,16},{4,20},{8,24},{12,28},{16,0},{20,4},{24,8},{28,12},{1,17},{... | collective-permute-start | bytes 1179656 | tf_op jit(solution)/shard_map/ppermute | solution.py:335
  296.5 17.1 %collective-permute-start.33 = (bf16[2,192,512]{2,1,0:T(8,128)(2,1)S(1)}, bf16[2,192,512]{2,1,0:T(8,128)(2,1)S(1)}, u32[]{:S(2)}, u32[]{:S(2)}) collective-permute-start(bf16[2,192,512]{2,1,0:T(8,128)(2,1)S(1)} %fusion.19), channel_id=1, source_target_pairs={{0,8},{4,12},{8,0},{12,4},{16,24},{20,28},{24,16},{28,20},{1,9},{5... | collective-permute-start | bytes 1179656 | tf_op jit(solution)/shard_map/ppermute | solution.py:335
  301.6 16.3 %collective-permute-start.72 = (bf16[192,512]{1,0:T(8,128)(2,1)S(1)}, bf16[192,512]{1,0:T(8,128)(2,1)S(1)}, u32[]{:S(2)}, u32[]{:S(2)}) collective-permute-start(bf16[192,512]{1,0:T(8,128)(2,1)S(1)} %fusion.40), channel_id=1, source_target_pairs={{0,8},{4,12},{8,0},{12,4},{16,24},{20,28},{24,16},{28,20},{1,9},{5... | collective-permute-start | bytes 589832 | tf_op jit(solution)/shard_map/ppermute | solution.py:335
  305.2 14.2 %collective-permute-start.67 = (bf16[192,512]{1,0:T(8,128)(2,1)S(1)}, bf16[192,512]{1,0:T(8,128)(2,1)S(1)}, u32[]{:S(2)}, u32[]{:S(2)}) collective-permute-start(bf16[192,512]{1,0:T(8,128)(2,1)S(1)} %fusion.39), channel_id=1, source_target_pairs={{0,16},{4,20},{8,24},{12,28},{16,0},{20,4},{24,8},{28,12},{1,17},{... | collective-permute-start | bytes 589832 | tf_op jit(solution)/shard_map/ppermute | solution.py:335
  310.0 12.1 %collective-permute-start.61 = (bf16[192,512]{1,0:T(8,128)(2,1)S(1)}, bf16[192,512]{1,0:T(8,128)(2,1)S(1)}, u32[]{:S(2)}, u32[]{:S(2)}) collective-permute-start(bf16[192,512]{1,0:T(8,128)(2,1)S(1)} %fusion.38), channel_id=1, source_target_pairs={{0,8},{4,12},{8,0},{12,4},{16,24},{20,28},{24,16},{28,20},{1,9},{5... | collective-permute-start | bytes 589832 | tf_op jit(solution)/shard_map/ppermute | solution.py:335
  347.9 12.1 %collective-permute-start.74 = (bf16[2,192,512]{2,1,0:T(8,128)(2,1)S(1)}, bf16[2,192,512]{2,1,0:T(8,128)(2,1)S(1)}, u32[]{:S(2)}, u32[]{:S(2)}) collective-permute-start(bf16[2,192,512]{2,1,0:T(8,128)(2,1)S(1)} %maximum_select_fusion.31), channel_id=1, source_target_pairs={{0,16},{4,20},{8,24},{12,28},{16,0},{20,4},{24,8},{28,12},{1,17},{... | collective-permute-start | bytes 1179656 | tf_op jit(solution)/shard_map/ppermute | solution.py:335
  349.6 12.1 %collective-permute-start.69 = (bf16[2,192,512]{2,1,0:T(8,128)(2,1)S(1)}, bf16[2,192,512]{2,1,0:T(8,128)(2,1)S(1)}, u32[]{:S(2)}, u32[]{:S(2)}) collective-permute-start(bf16[2,192,512]{2,1,0:T(8,128)(2,1)S(1)} %maximum_select_fusion.30), channel_id=1, source_target_pairs={{0,8},{4,12},{8,0},{12,4},{16,24},{20,28},{24,16},{28,20},{1,9},{5... | collective-permute-start | bytes 1179656 | tf_op jit(solution)/shard_map/ppermute | solution.py:335
  349.7 18.8 %collective-permute-start.63 = (bf16[2,192,512]{2,1,0:T(8,128)(2,1)S(1)}, bf16[2,192,512]{2,1,0:T(8,128)(2,1)S(1)}, u32[]{:S(2)}, u32[]{:S(2)}) collective-permute-start(bf16[2,192,512]{2,1,0:T(8,128)(2,1)S(1)} %maximum_select_fusion.28), channel_id=1, source_target_pairs={{0,16},{4,20},{8,24},{12,28},{16,0},{20,4},{24,8},{28,12},{1,17},{... | collective-permute-start | bytes 1179656 | tf_op jit(solution)/shard_map/ppermute | solution.py:335
  350.3 20.1 %collective-permute-start.58 = (bf16[2,192,512]{2,1,0:T(8,128)(2,1)S(1)}, bf16[2,192,512]{2,1,0:T(8,128)(2,1)S(1)}, u32[]{:S(2)}, u32[]{:S(2)}) collective-permute-start(bf16[2,192,512]{2,1,0:T(8,128)(2,1)S(1)} %maximum_select_fusion.26), channel_id=1, source_target_pairs={{0,8},{4,12},{8,0},{12,4},{16,24},{20,28},{24,16},{28,20},{1,9},{5... | collective-permute-start | bytes 1179656 | tf_op jit(solution)/shard_map/ppermute | solution.py:335
  360.1 20.2 %collective-permute-start.52 = (bf16[2,192,512]{2,1,0:T(8,128)(2,1)S(1)}, bf16[2,192,512]{2,1,0:T(8,128)(2,1)S(1)}, u32[]{:S(2)}, u32[]{:S(2)}) collective-permute-start(bf16[2,192,512]{2,1,0:T(8,128)(2,1)S(1)} %maximum_select_fusion.25), channel_id=1, source_target_pairs={{0,16},{4,20},{8,24},{12,28},{16,0},{20,4},{24,8},{28,12},{1,17},{... | collective-permute-start | bytes 1179656 | tf_op jit(solution)/shard_map/ppermute | solution.py:335
  361.7 19.4 %collective-permute-start.47 = (bf16[2,192,512]{2,1,0:T(8,128)(2,1)S(1)}, bf16[2,192,512]{2,1,0:T(8,128)(2,1)S(1)}, u32[]{:S(2)}, u32[]{:S(2)}) collective-permute-start(bf16[2,192,512]{2,1,0:T(8,128)(2,1)S(1)} %maximum_select_fusion.23), channel_id=1, source_target_pairs={{0,8},{4,12},{8,0},{12,4},{16,24},{20,28},{24,16},{28,20},{1,9},{5... | collective-permute-start | bytes 1179656 | tf_op jit(solution)/shard_map/ppermute | solution.py:335
  368.5 12.9 %collective-permute-start.41 = (bf16[2,192,512]{2,1,0:T(8,128)(2,1)S(1)}, bf16[2,192,512]{2,1,0:T(8,128)(2,1)S(1)}, u32[]{:S(2)}, u32[]{:S(2)}) collective-permute-start(bf16[2,192,512]{2,1,0:T(8,128)(2,1)S(1)} %maximum_select_fusion.22), channel_id=1, source_target_pairs={{0,16},{4,20},{8,24},{12,28},{16,0},{20,4},{24,8},{28,12},{1,17},{... | collective-permute-start | bytes 1179656 | tf_op jit(solution)/shard_map/ppermute | solution.py:335
  397.2 19.6 %collective-permute-start.22 = (bf16[2,128,1536]{2,1,0:T(8,128)(2,1)S(1)}, bf16[2,128,1536]{2,1,0:T(8,128)(2,1)S(1)}, u32[]{:S(2)}, u32[]{:S(2)}) collective-permute-start(bf16[2,128,1536]{2,1,0:T(8,128)(2,1)S(1)} %fusion.6), channel_id=1, source_target_pairs={{0,8},{4,12},{8,0},{12,4},{16,24},{20,28},{24,16},{28,20},{1,9},{5... | collective-permute-start | bytes 2359304 | tf_op jit(solution)/shard_map/ppermute | solution.py:335
  405.5 21.9 %collective-permute-start.24 = (bf16[2,128,1664]{2,1,0:T(8,128)(2,1)S(1)}, bf16[2,128,1664]{2,1,0:T(8,128)(2,1)S(1)}, u32[]{:S(2)}, u32[]{:S(2)}) collective-permute-start(bf16[2,128,1664]{2,1,0:T(8,128)(2,1)S(1)} %fusion.4), channel_id=1, source_target_pairs={{0,16},{4,20},{8,24},{12,28},{16,0},{20,4},{24,8},{28,12},{1,17},{... | collective-permute-start | bytes 2555912 | tf_op jit(solution)/shard_map/ppermute | solution.py:335
  417.1 17.6 %collective-permute-start.23 = (bf16[128,1536]{1,0:T(8,128)(2,1)S(1)}, bf16[128,1536]{1,0:T(8,128)(2,1)S(1)}, u32[]{:S(2)}, u32[]{:S(2)}) collective-permute-start(bf16[128,1536]{1,0:T(8,128)(2,1)S(1)} %fusion.14), channel_id=1, source_target_pairs={{0,16},{4,20},{8,24},{12,28},{16,0},{20,4},{24,8},{28,12},{1,17},{... | collective-permute-start | bytes 1179656 | tf_op jit(solution)/shard_map/ppermute | solution.py:335
  441.3 15.2 %collective-permute-start.27 = (bf16[32,3200]{1,0:T(8,128)(2,1)S(1)}, bf16[32,3200]{1,0:T(8,128)(2,1)S(1)}, u32[]{:S(2)}, u32[]{:S(2)}) collective-permute-start(bf16[32,3200]{1,0:T(8,128)(2,1)S(1)} %get-tuple-element.155), channel_id=1, source_target_pairs={{0,2},{1,3},{2,0},{3,1},{4,6},{5,7},{6,4},{7,5},{8,10},{9,11},{10,... | collective-permute-start | bytes 614408 | tf_op jit(solution)/shard_map/ppermute | solution.py:326
  463.8 14.8 %collective-permute-start.31 = (bf16[32,3200]{1,0:T(8,128)(2,1)S(1)}, bf16[32,3200]{1,0:T(8,128)(2,1)S(1)}, u32[]{:S(2)}, u32[]{:S(2)}) collective-permute-start(bf16[32,3200]{1,0:T(8,128)(2,1)S(1)} %fusion.13), channel_id=1, source_target_pairs={{0,1},{1,2},{2,3},{3,0},{4,5},{5,6},{6,7},{7,4},{8,9},{9,10},{10,1... | collective-permute-start | bytes 614408 | tf_op jit(solution)/shard_map/ppermute | solution.py:326
  463.8 14.7 %collective-permute-start.30 = (bf16[32,3200]{1,0:T(8,128)(2,1)S(1)}, bf16[32,3200]{1,0:T(8,128)(2,1)S(1)}, u32[]{:S(2)}, u32[]{:S(2)}) collective-permute-start(bf16[32,3200]{1,0:T(8,128)(2,1)S(1)} %fusion.13), channel_id=1, source_target_pairs={{0,2},{1,3},{2,0},{3,1},{4,6},{5,7},{6,4},{7,5},{8,10},{9,11},{10,... | collective-permute-start | bytes 614408 | tf_op jit(solution)/shard_map/ppermute | solution.py:326
  (56 other events, 767.7 us)

commit v2 on v1

v2 whole, which is shorter than its diff:
```python
import functools

import jax
import jax.numpy as jnp
from jax import lax
from jax.experimental import pallas as pl
from jax.experimental.pallas import tpu as pltpu
from jax.sharding import PartitionSpec as P

QUERY_HEADS = 16
KEY_VALUE_HEADS = 8
HEAD_DIMENSION = 64
PAIR = 2 * HEAD_DIMENSION
EPS = 1e-05
UNROUTED = 1 << 20
LANES = 128
SCALE = HEAD_DIMENSION ** (-0.5)

bf16 = jnp.bfloat16
f32 = jnp.float32
VMEM = pl.BlockSpec(memory_space=pltpu.VMEM)
SMEM = pl.BlockSpec(memory_space=pltpu.SMEM)
ANY = pl.BlockSpec(memory_space=pl.ANY)
COST = 3600000


def mm(left, right, dims=((1,), (0,))):
    return lax.dot_general(left, right, (dims, ((), ())), preferred_element_type=f32)


def call(kernel, outs, *args, smem=0, deps=(), specs=None, out_specs=None, grid=None, prefetch=0, scratch=(), vmem=56, alias=None, us=4, name=None):
    outs = [(pltpu.HBM if vmem > 32 else jax.ShapeDtypeStruct)(s, d) for s, d in outs]
    taken = len(args)

    def body(*refs):
        kernel(*refs[:taken], *refs[taken + len(deps) :])

    in_specs = (specs or [SMEM] * smem + [VMEM] * (taken - smem)) + [ANY] * len(deps)
    out_specs = out_specs or [VMEM] * len(outs)
    if prefetch:
        placed = dict(
            grid_spec=pltpu.PrefetchScalarGridSpec(
                num_scalar_prefetch=prefetch, grid=grid, in_specs=in_specs, out_specs=out_specs, scratch_shapes=list(scratch)
            )
        )
    else:
        placed = dict(in_specs=in_specs, out_specs=out_specs, scratch_shapes=list(scratch))
        if grid:
            placed["grid"] = grid
    return pl.pallas_call(
        body,
        out_shape=outs,
        compiler_params=pltpu.CompilerParams(vmem_limit_bytes=vmem * 1024 * 1024),
        cost_estimate=pl.CostEstimate(flops=0, bytes_accessed=us * COST, transcendentals=0),
        input_output_aliases=alias or {},
        name=name,
        **placed,
    )(*args, *deps)


def low_lanes(rows):
    return lax.broadcasted_iota(jnp.int32, (rows, PAIR), 1) < HEAD_DIMENSION


def stack_heads(pair, low):
    pair = pair.astype(f32)
    return jnp.concatenate([jnp.where(low, pair, 0.0), jnp.where(low, 0.0, pair)], 0).astype(bf16)


def allowed_keys(rows, length):
    shape = (2 * rows, rows)
    query = lax.broadcasted_iota(jnp.int32, shape, 0)
    query = jnp.where(query >= rows, query - rows, query)
    key = lax.broadcasted_iota(jnp.int32, shape, 1)
    return (key <= query) & (key < length)


def pack_rows(field, blocks):
    per = field.shape[0] // blocks
    return jnp.concatenate([field[c * per : (c + 1) * per] for c in range(blocks)], 1)


def places_and_ranks(length, routes_ref, ranks_ref, experts, capacity):
    picks, rows = routes_ref.shape
    expert = lax.broadcasted_iota(jnp.int32, (LANES, rows), 0)
    table = jnp.full((LANES, rows), UNROUTED, jnp.int32)
    for k in range(picks):
        table = jnp.where(expert == routes_ref[k : k + 1, :], ranks_ref[k : k + 1, :], table)
    token = lax.broadcasted_iota(jnp.int32, (LANES, rows), 1)
    table = jnp.where(token < length, table, UNROUTED).astype(f32)
    columns = table.T
    places = []
    for e in range(experts):
        row = table[e : e + 1]
        before = jnp.sum(jnp.where(columns[:, e : e + 1] < row, 1.0, 0.0), 0, keepdims=True)
        places.append(jnp.where((row < UNROUTED) & (before < capacity), before, -1.0))
    return jnp.concatenate(places, 0), table[:experts] < UNROUTED


def dense_forward(
    capacity, len_ref, x_ref, g1_ref, wq_ref, wk_ref, wv_ref, wo_ref, g2_ref, wr_ref, routes_ref, ranks_ref,
    n1_ref, q_ref, kk_ref, vv_ref, lse_ref, mixed_ref, res_ref, pack_ref, gate_ref,
):
    rows = x_ref.shape[0]
    x = x_ref[...].astype(f32)
    inverse = lax.rsqrt(jnp.mean(x * x, -1, keepdims=True) + EPS)
    n1 = (x * inverse * g1_ref[...]).astype(bf16)
    n1_ref[...] = n1
    q_ref[...] = mm(n1, wq_ref[...]).astype(bf16)
    low = low_lanes(rows)
    for weight_ref, twice_ref in ((wk_ref, kk_ref), (wv_ref, vv_ref)):
        both = mm(n1, weight_ref[...])
        for j in range(KEY_VALUE_HEADS // 2):
            block = both[:, j * PAIR : (j + 1) * PAIR]
            rolled = pltpu.roll(block, HEAD_DIMENSION, 1)
            twice_ref[:, 2 * j * PAIR : (2 * j + 1) * PAIR] = jnp.where(low, block, rolled).astype(bf16)
            twice_ref[:, (2 * j + 1) * PAIR : (2 * j + 2) * PAIR] = jnp.where(low, rolled, block).astype(bf16)
    allowed = allowed_keys(rows, len_ref[0])
    lane = lax.broadcasted_iota(jnp.int32, (rows, LANES), 1)
    totals = jnp.zeros((rows, LANES), f32)
    for h in range(KEY_VALUE_HEADS):
        cols = slice(h * PAIR, (h + 1) * PAIR)
        scores = mm(stack_heads(q_ref[:, cols], low), kk_ref[:, cols], ((1,), (1,))) * SCALE
        scores = jnp.where(allowed, scores, -1e30)
        top = jnp.max(scores, -1, keepdims=True)
        raised = jnp.exp(scores - top)
        total = jnp.sum(raised, -1, keepdims=True)
        probs = (raised / total).astype(bf16)
        mixed = mm(probs, vv_ref[:, cols])
        mixed_ref[:, cols] = jnp.where(low, mixed[:rows], mixed[rows:]).astype(bf16)
        logs = top + jnp.log(total)
        totals = jnp.where(lane == 2 * h, logs[:rows], totals)
        totals = jnp.where(lane == 2 * h + 1, logs[rows:], totals)
    lse_ref[...] = totals
    residual = x + mm(mixed_ref[...], wo_ref[...])
    res_ref[...] = residual
    inverse = lax.rsqrt(jnp.mean(residual * residual, -1, keepdims=True) + EPS)
    n2 = (residual * inverse * g2_ref[...]).astype(bf16)
    pack_ref[:rows, :] = n2
    logits = mm(wr_ref[...], n2, ((1,), (1,)))
    places, routed = places_and_ranks(len_ref[0], routes_ref, ranks_ref, wr_ref.shape[0], capacity)
    top = jnp.max(jnp.where(routed, logits, -jnp.inf), 0, keepdims=True)
    raised = jnp.where(routed, jnp.exp(jnp.where(routed, logits - top, 0.0)), 0.0)
    total = jnp.sum(raised, 0, keepdims=True)
    gates = raised / jnp.where(total > 0.0, total, 1.0)
    gate_ref[...] = gates
    high = gates.astype(bf16).astype(f32)
    blocks = x_ref.shape[1] // rows
    fields = [pack_rows(field, blocks) for field in (places, high, gates - high)]
    fill = pack_ref.shape[0] - rows - sum(field.shape[0] for field in fields)
    if fill:
        fields.append(jnp.zeros((fill, x_ref.shape[1]), f32))
    pack_ref[rows:, :] = jnp.concatenate(fields, 0).astype(bf16)


def unpack(pack_ref, expert, experts, seq):
    extra, width = pack_ref.shape[0] - seq, pack_ref.shape[1]
    per = experts * seq // width
    at = expert // per
    row = expert - at * per
    block = pack_ref[seq:, pl.ds(pl.multiple_of(at * seq, seq), seq)].astype(f32)
    index = lax.broadcasted_iota(jnp.int32, (extra, seq), 0)
    place = jnp.sum(jnp.where(index == row, block, 0.0), 0, keepdims=True)
    gate = jnp.sum(
        jnp.where((index == per + row) | (index == 2 * per + row), block, 0.0), 0, keepdims=True
    )
    return place, gate


def expert_forward(local, capacity, owners, id_ref, *refs):
    tokens = refs[:owners]
    (win_ref, wout_ref, sent_ref, hidden_ref, slope_ref, silu_ref, wret_ref, weight) = refs[owners:]
    width, half = win_ref.shape[1], wout_ref.shape[1]
    seq = width // local
    expert = id_ref[0] * local + pl.program_id(0)
    place = lax.broadcasted_iota(jnp.int32, (capacity, seq), 0).astype(f32)
    for d in range(owners):
        span = slice(d * capacity, (d + 1) * capacity)
        row, gate = unpack(tokens[d], expert, owners * local, seq)
        hit = place == row
        one = jnp.where(hit, 1.0, 0.0).astype(bf16)
        sent_ref[0, span, :] = mm(one, tokens[d][:seq, :]).astype(bf16)
        weight[span, :] = jnp.sum(jnp.where(hit, gate, 0.0), 1, keepdims=True)
    tile = 256
    for t in range(0, half, tile):
        gate = mm(sent_ref[0], win_ref[0, :, t : t + tile])
        up = mm(sent_ref[0], win_ref[0, :, half + t : half + t + tile])
        sig = jax.nn.sigmoid(gate)
        act = gate * sig
        silu_ref[0, :, t : t + tile] = act
        slope_ref[0, :, t : t + tile] = up * sig * (1.0 + gate * (1.0 - sig))
        hidden_ref[0, :, t : t + tile] = (act * up).astype(bf16)
    for t in range(0, width, tile):
        cols = slice(t, t + tile)
        returned = mm(hidden_ref[0], wout_ref[0, :, cols]).astype(bf16).astype(f32)
        wret_ref[0, :, cols] = (weight[...] * returned).astype(bf16)


def expert_backward(local, capacity, owners, id_ref, *refs):
    tokens, cots = refs[:owners], refs[owners : 2 * owners]
    (sent_ref, hidden_ref, slope_ref, silu_ref, win_ref, wout_ref,
     sums_ref, grow_ref, gg_ref, crow, weight, gret, gpre) = refs[2 * owners :]
    width, half = win_ref.shape[1], wout_ref.shape[1]
    seq = cots[0].shape[0]
    expert = id_ref[0] * local + pl.program_id(0)
    place = lax.broadcasted_iota(jnp.int32, (capacity, seq), 0).astype(f32)
    places = []
    for d in range(owners):
        span = slice(d * capacity, (d + 1) * capacity)
        row, gate = unpack(tokens[d], expert, owners * local, seq)
        places.append(row)
        hit = place == row
        one = jnp.where(hit, 1.0, 0.0).astype(bf16)
        weight[span, :] = jnp.sum(jnp.where(hit, gate, 0.0), 1, keepdims=True)
        rows = mm(one, cots[d][...])
        crow[span, :] = rows.astype(bf16)
        gret[span, :] = (weight[span, :] * rows).astype(bf16)
    tile = 256
    dots = jnp.zeros((owners * capacity, 1), f32)
    for t in range(0, half, tile):
        cols = slice(t, t + tile)
        ghid = mm(crow[...], wout_ref[0, cols, :], ((1,), (1,)))
        dots = dots + jnp.sum(ghid * hidden_ref[0, :, cols].astype(f32), 1, keepdims=True)
        ghid = ghid * weight[...]
        gpre[:, cols] = (ghid * slope_ref[0, :, cols]).astype(bf16)
        gpre[:, half + t : half + t + tile] = (ghid * silu_ref[0, :, cols]).astype(bf16)
    for d in range(owners):
        part = dots[d * capacity : (d + 1) * capacity]
        gg_ref[0, d : d + 1, :] = jnp.sum(jnp.where(place == places[d], part, 0.0), 0, keepdims=True)
    for t in range(0, width, tile):
        grow_ref[0, :, t : t + tile] = mm(gpre[...], win_ref[0, t : t + tile, :], ((1,), (1,))).astype(bf16)
    pieces = sums_ref.shape[0]
    base = 0
    for left, right in ((sent_ref, gpre), (hidden_ref, gret)):
        size = left.shape[2]
        step = size // pieces
        for t in range(0, width, tile):
            made = mm(left[0], right[:, t : t + tile], ((0,), (0,))).astype(bf16)
            for q in range(pieces):
                sums_ref[q, base : base + step, t : t + tile] = made[q * step : (q + 1) * step]
        base += step


def combine_kernel(local, capacity, owners, counts, id_ref, *refs):
    tokens = refs[:owners]
    rest = refs[owners:]
    rows_in = [(r, i) for r in rest[: counts[0]] for i in range(r.shape[0])]
    dots = [(r, i) for r in rest[counts[0] : counts[0] + counts[1]] for i in range(r.shape[0])]
    part_ref, columns = rest[-2:]
    width = part_ref.shape[2]
    seq = width // local
    d = pl.program_id(0)

    @pl.when(d == 0)
    def _():
        first = id_ref[0] * local
        for t in range(owners):
            table = [unpack(tokens[t], first + j, owners * local, seq)[0] for j in range(local)]
            table.append(jnp.zeros((LANES - local, seq), f32))
            columns[t] = jnp.concatenate(table, 0).T.astype(jnp.int32)

    lane = lax.broadcasted_iota(jnp.int32, (seq, local * capacity), 1)
    hit = None
    for j in range(local):
        col = columns[d, :, j : j + 1]
        same = lane == jnp.where(col < 0, -1, col + j * capacity)
        hit = same if hit is None else hit | same
    one = jnp.where(hit, 1.0, 0.0).astype(bf16)
    stacked = jnp.concatenate([r[i] for r, i in rows_in], 0)
    part_ref[0, :seq, :] = mm(one, stacked).astype(bf16)
    if dots:
        line = jnp.concatenate([r[i, pl.ds(d, 1), :] for r, i in dots], 1)
        high = line.astype(bf16).astype(f32)
        index = lax.broadcasted_iota(jnp.int32, (part_ref.shape[1] - seq, width), 0)
        mine = jnp.where(index == id_ref[0], high, 0.0)
        mine = jnp.where(index == owners + id_ref[0], line - high, mine)
        part_ref[0, seq:, :] = mine.astype(bf16)


def halve_kernel(id_ref, keep_ref, recv_ref, keep_go_ref, recv_go_ref, own_ref, send_ref):
    own_ref[...] = keep_ref[...].astype(f32) + recv_ref[...].astype(f32)
    send_ref[...] = (keep_go_ref[...].astype(f32) + recv_go_ref[...].astype(f32)).astype(bf16)


def last_kernel(keep_ref, recv_ref, out_ref):
    out_ref[...] = (keep_ref[...].astype(f32) + recv_ref[...].astype(f32)).astype(bf16)


def nothing_kernel(*refs):
    pass


def add_kernel(base_ref, parts_ref, out_ref):
    total = base_ref[...]
    for i in range(parts_ref.shape[0]):
        total = total + parts_ref[i].astype(f32)
    out_ref[...] = total


def sum_kernel(in_ref, out_ref):
    total = in_ref[0].astype(f32)
    for i in range(1, in_ref.shape[0]):
        total = total + in_ref[i].astype(f32)
    out_ref[...] = total.astype(out_ref.dtype)


def widen_kernel(in_ref, first_ref, second_ref):
    count, rows, _ = first_ref.shape
    size = in_ref.shape[1] // count
    for j in range(count):
        first_ref[j] = in_ref[0, j * size : j * size + rows, :].astype(f32)
        second_ref[j] = in_ref[0, j * size + rows : (j + 1) * size, :].astype(f32)


def finish_kernel(owners, id_ref, *refs):
    blocks, outs, ordered = refs[:owners], refs[owners:-1], refs[-1]
    size = blocks[0].shape[0]
    for d in range(owners):
        ordered[lax.rem(id_ref[0] + owners - d, owners)] = blocks[d][...].astype(f32)
    for i in range(owners):
        col = 0
        for out in outs:
            cols = out.shape[1]
            out[i * size : (i + 1) * size, :] = ordered[i, :, col : col + cols]
            col += cols


def dense_backward(owners, local, id_ref, len_ref, *refs):
    (part_ref, gate_ref, x_ref, cot_ref, res_ref, n1_ref, pack_ref, q_ref, kk_ref, vv_ref, lse_ref, mixed_ref,
     wq_ref, wk_ref, wv_ref, wo_ref, wr_ref, g1_ref, g2_ref,
     gin_ref, keep_ref, send_ref, gg_all, gmix, gq, gk, gv, acc) = refs
    rows, width = x_ref.shape
    core = id_ref[1]
    pieces = 2 * keep_ref.shape[0]
    step = width // pieces

    def put(offset, size):
        for q in range(pieces // 2):
            lo = pl.multiple_of((2 * q + core) * step, step)
            hi = pl.multiple_of((2 * q + 1 - core) * step, step)
            keep_ref[q, :, offset : offset + size] = acc[pl.ds(lo, step), :size].astype(bf16)
            send_ref[q, :, offset : offset + size] = acc[pl.ds(hi, step), :size].astype(bf16)

    def weight_gradient(left, right, offset):
        size = right.shape[1]
        tile = 256
        for t in range(0, size, tile):
            acc[:, t : t + tile] = mm(left[...], right[:, t : t + tile], ((0,), (0,)))
        put(offset, size)

    tail = part_ref[0, rows:, :].astype(f32)
    for owner in range(1, owners):
        tail = tail + part_ref[owner, rows:, :].astype(f32)
    lines = tail[:owners] + tail[owners : 2 * owners]
    for owner in range(owners):
        for j in range(local):
            gg_all[owner * local + j : owner * local + j + 1, :] = lines[owner : owner + 1, j * rows : (j + 1) * rows]
    gates = gate_ref[...]
    grad_gates = gg_all[...]
    mean = jnp.sum(gates * grad_gates, 0, keepdims=True)
    glog = (gates * (grad_gates - mean)).astype(bf16)
    grad = part_ref[0, :rows, :].astype(f32)
    for owner in range(1, owners):
        grad = grad + part_ref[owner, :rows, :].astype(f32)
    grad = grad + mm(glog, wr_ref[...], ((0,), (0,)))
    grouter = mm(glog, pack_ref[:rows, :])
    residual = res_ref[...]
    inverse = lax.rsqrt(jnp.mean(residual * residual, -1, keepdims=True) + EPS)
    ggain_two = jnp.sum(grad * residual * inverse, 0, keepdims=True)
    scaled = grad * g2_ref[...]
    gres = cot_ref[...].astype(f32) + inverse * scaled - residual * inverse**3 * jnp.mean(
        scaled * residual, -1, keepdims=True
    )
    branch = gres.astype(bf16)
    gmix[...] = mm(branch, wo_ref[...], ((1,), (1,))).astype(bf16)
    gin_ref[...] = gres
    gq[...] = branch
    col = wq_ref.shape[1] + wk_ref.shape[1] + wv_ref.shape[1]
    weight_gradient(mixed_ref, gq, col)
    low = low_lanes(rows)
    allowed = allowed_keys(rows, len_ref[0])
    held = None
    for h in range(KEY_VALUE_HEADS):
        cols = slice(h * PAIR, (h + 1) * PAIR)
        queries = stack_heads(q_ref[:, cols], low)
        upstream = stack_heads(gmix[:, cols], low)
        scores = mm(queries, kk_ref[:, cols], ((1,), (1,))) * SCALE
        logs = jnp.concatenate([lse_ref[:, 2 * h : 2 * h + 1], lse_ref[:, 2 * h + 1 : 2 * h + 2]], 0)
        probs = jnp.exp(jnp.where(allowed, scores, -1e30) - logs)
        gprobs = mm(upstream, vv_ref[:, cols], ((1,), (1,)))
        inner = jnp.sum(gprobs * probs, -1, keepdims=True)
        gscores = (probs * (gprobs - inner)).astype(bf16)
        gqueries = mm(gscores, kk_ref[:, cols]) * SCALE
        gq[:, cols] = jnp.where(low, gqueries[:rows], gqueries[rows:]).astype(bf16)
        gkey = mm(gscores, queries, ((0,), (0,))) * SCALE
        gvalue = mm(probs.astype(bf16), upstream, ((0,), (0,)))
        gkey = gkey + pltpu.roll(gkey, HEAD_DIMENSION, 1)
        gvalue = gvalue + pltpu.roll(gvalue, HEAD_DIMENSION, 1)
        if h % 2 == 0:
            held = (gkey, gvalue)
        else:
            both = slice((h // 2) * PAIR, (h // 2 + 1) * PAIR)
            gk[:, both] = jnp.where(low, held[0], gkey).astype(bf16)
            gv[:, both] = jnp.where(low, held[1], gvalue).astype(bf16)
    weight_gradient(n1_ref, gq, 0)
    weight_gradient(n1_ref, gk, wq_ref.shape[1])
    weight_gradient(n1_ref, gv, wq_ref.shape[1] + wk_ref.shape[1])
    grad = mm(gq[...], wq_ref[...], ((1,), (1,)))
    grad = grad + mm(gk[...], wk_ref[...], ((1,), (1,)))
    grad = grad + mm(gv[...], wv_ref[...], ((1,), (1,)))
    x = x_ref[...].astype(f32)
    inverse = lax.rsqrt(jnp.mean(x * x, -1, keepdims=True) + EPS)
    ggain_one = jnp.sum(grad * x * inverse, 0, keepdims=True)
    scaled = grad * g1_ref[...]
    gin_ref[...] = gin_ref[...] + inverse * scaled - x * inverse**3 * jnp.mean(
        scaled * x, -1, keepdims=True
    )
    small = jnp.concatenate(
        [grouter, ggain_one, ggain_two, jnp.zeros((LANES - 2 - grouter.shape[0], width), f32)], 0
    )
    acc[:, :LANES] = small.T
    put(col + width, LANES)


def on_device(
    inputs, gain_one, query_matrix, key_matrix, value_matrix, w_attn_out, gain_two, w_router,
    expert_in, expert_out, lengths, routes, ranks, cotangent,
):
    seq, width = inputs.shape
    picks = routes.shape[1]
    experts = w_router.shape[1]
    local = expert_in.shape[0]
    half = expert_out.shape[1]
    owners = lax.axis_size("expert")
    groups = lax.axis_size("group")
    steps = groups.bit_length() - 2
    capacity = (5 * seq * picks + 4 * experts - 1) // (4 * experts)
    places = owners * capacity
    z = lax.axis_index("expert").astype(jnp.int32)
    g = lax.axis_index("group").astype(jnp.int32)
    ids = jnp.stack([z, g % 2, g // 2])

    def ring(x, d):
        return lax.ppermute(x, "expert", [(i, (i + d) % owners) for i in range(owners)])

    def swap_cores(x):
        return lax.ppermute(x, "group", [(i, i ^ 1) for i in range(groups)])

    def swap(x, stage):
        return lax.ppermute(
            x, "group", [(i, i ^ (1 << (steps - stage if i % 2 else 1 + stage))) for i in range(groups)]
        )

    def near(x):
        return [ring(x, 1), ring(x, -1)] if owners == 4 else [ring(x, d) for d in range(1, owners)]

    def far(x, got):
        if owners != 4:
            return [x, *got]
        before, after = got
        up = lax.ppermute(before, "expert", [(1, 2), (2, 3)])
        down = lax.ppermute(after, "expert", [(1, 0), (2, 1)])
        return [x, before, jnp.where(z >= 2, up, down), after]

    def halve(keep, recv, stage, name, deps=()):
        pieces, *rest = keep.shape
        half = pieces // 2
        tile = rest[0] // 2
        core, mine = g % 2, g // 2
        index = jnp.arange(half, dtype=jnp.int32)
        low = (mine >> stage) & 1
        high = (mine >> (steps - 1 - stage)) & 1
        stay = jnp.where(core == 0, 2 * index + low, index + high * half)
        go = jnp.where(core == 0, 2 * index + 1 - low, index + (1 - high) * half)
        block = (1, tile, rest[1])
        here = pl.BlockSpec(block, lambda i, t, which: (which[0, i], t, 0))
        there = pl.BlockSpec(block, lambda i, t, which: (which[1, i], t, 0))
        made = pl.BlockSpec(block, lambda i, t, which: (i, t, 0))
        return call(
            halve_kernel, [((half, *rest), f32), ((half, *rest), bf16)],
            jnp.stack([stay, go]), keep, recv, keep, recv,
            prefetch=1, grid=(half, 2), specs=[here, here, there, there], out_specs=[made, made], deps=deps, vmem=16, name=name,
        )

    def last(keep, recv, name, deps=()):
        _, rows, cols = keep.shape
        spec = pl.BlockSpec((1, rows // 2, cols), lambda t: (0, t, 0))
        (made,) = call(
            last_kernel, [(keep.shape, bf16)], keep, recv,
            grid=(2,), specs=[spec, spec], out_specs=[spec], deps=deps, vmem=16, name=name,
        )
        return made

    def behind(arrays, deps, name):
        shapes = [(a.shape, a.dtype) for a in arrays]
        return call(
            nothing_kernel, shapes, *arrays, specs=[ANY] * len(arrays), out_specs=[ANY] * len(arrays), deps=deps,
            alias={i: i for i in range(len(arrays))}, us=1, name=name,
        )

    cot_got = near(cotangent)
    gain_one = gain_one.reshape(1, width)
    gain_two = gain_two.reshape(1, width)
    router = w_router.T
    extra = -(-3 * experts * seq // width // 16) * 16

    n1, q, kk, vv, lse, mixed, residual, pack, gates = call(
        functools.partial(dense_forward, capacity),
        [((seq, width), bf16)] * 4
        + [((seq, LANES), f32), ((seq, width), bf16), ((seq, width), f32), ((seq + extra, width), bf16), ((experts, seq), f32)],
        lengths, inputs, gain_one, query_matrix, key_matrix, value_matrix, w_attn_out, gain_two, router, routes.T, ranks.T,
        smem=1, us=9, name="dense_forward",
    )
    (pack,) = behind([pack], tuple(cot_got), "tokens_go")
    packs = far(pack, near(pack))
    cot_got = behind(cot_got, (packs[owners // 2],), "cotangents_go")
    cots = far(cotangent, cot_got)
    piece = (width + half) // groups

    def rows_of(n):
        return pl.BlockSpec((1, places, n), lambda i: (i, 0, 0))

    def weights(first):
        return [
            pl.BlockSpec((1, width, 2 * half), lambda i: (first + i, 0, 0)),
            pl.BlockSpec((1, half, width), lambda i: (first + i, 0, 0)),
        ]

    sent, hidden, slope, silu, wret = call(
        functools.partial(expert_forward, local, capacity, owners),
        [
            ((local, places, width), bf16),
            ((local, places, half), bf16),
            ((local, places, half), f32),
            ((local, places, half), f32),
            ((local, places, width), bf16),
        ],
        ids, *packs, expert_in, expert_out,
        grid=(local,), specs=[SMEM] + [VMEM] * owners + weights(0),
        out_specs=[rows_of(width), rows_of(half), rows_of(half), rows_of(half), rows_of(width)],
        scratch=[pltpu.VMEM((places, 1), f32)], us=17, name="expert_forward",
    )

    grad_sums, grow, dots = call(
        functools.partial(expert_backward, local, capacity, owners),
        [
            ((groups, local * piece, width), bf16),
            ((local, places, width), bf16),
            ((local, owners, seq), f32),
        ],
        ids, *packs, *cots, sent, hidden, slope, silu, expert_in, expert_out,
        grid=(local,),
        specs=[SMEM] + [VMEM] * (2 * owners) + [rows_of(width), rows_of(half), rows_of(half), rows_of(half)] + weights(0),
        out_specs=[
            pl.BlockSpec((groups, piece, width), lambda i: (0, i, 0)),
            rows_of(width),
            pl.BlockSpec((1, owners, seq), lambda i: (i, 0, 0)),
        ],
        scratch=[
            pltpu.VMEM((places, width), bf16),
            pltpu.VMEM((places, 1), f32),
            pltpu.VMEM((places, width), bf16),
            pltpu.VMEM((places, 2 * half), bf16),
        ],
        us=36, name="expert_backward",
    )
    mine = lax.psum_scatter(grad_sums, "group", scatter_dimension=0, tiled=False)

    def combine(rows, dots, deps, name):
        tail = -(-2 * owners // 16) * 16 if dots else 0
        (made,) = call(
            functools.partial(combine_kernel, local, capacity, owners, (len(rows), len(dots))),
            [((owners, seq + tail, width), bf16)], ids, *packs, *rows, *dots, grid=(owners,), prefetch=1,
            specs=[VMEM] * owners
            + [pl.BlockSpec((r.shape[0], capacity, width), lambda d, ids: (0, d, 0)) for r in rows]
            + [VMEM] * len(dots),
            out_specs=[pl.BlockSpec((1, seq + tail, width), lambda d, ids: (lax.rem(ids[0] + owners - d, owners), 0, 0))],
            scratch=[pltpu.VMEM((owners, seq, LANES), jnp.int32)],
            deps=deps, us=5, name=name,
        )
        return made

    def to_owners(x):
        return lax.all_to_all(x, "expert", split_axis=0, concat_axis=0, tiled=True)

    parts = combine([grow], [dots], (), "combine_grad")
    grad_part = to_owners(parts)
    owned = combine([wret], [], (parts,), "combine_out")

    columns = 2 * width + key_matrix.shape[1] + value_matrix.shape[1] + LANES
    grad_inputs, keep, send = call(
        functools.partial(dense_backward, owners, local),
        [((seq, width), f32)] + [((groups // 2, width // groups, columns), bf16)] * 2,
        ids, lengths, grad_part, gates, inputs, cotangent, residual, n1, pack, q, kk, vv, lse, mixed,
        query_matrix, key_matrix, value_matrix, w_attn_out, router, gain_one, gain_two,
        smem=2, deps=(owned,), us=18, name="dense_backward",
        scratch=[
            pltpu.VMEM((experts, seq), f32),
            pltpu.VMEM((seq, width), bf16),
            pltpu.VMEM((seq, width), bf16),
            pltpu.VMEM((seq, key_matrix.shape[1]), bf16),
            pltpu.VMEM((seq, value_matrix.shape[1]), bf16),
            pltpu.VMEM((width, width), f32),
        ],
    )
    recv = swap_cores(send)
    (owned,) = behind([owned], (send,), "returned_go")
    out_parts = to_owners(owned)
    deps = (owned,)
    for stage in range(steps):
        keep, send = halve(keep, recv, stage, f"dense_halve{stage}", deps)
        recv = swap(send, stage)
        deps = (send,)
        if stage == 0:
            (mine,) = behind([mine], deps, "gather_go")
            gathered = lax.all_gather(mine, "group", axis=0, tiled=False)
            deps = (mine,)
    spec = pl.BlockSpec((seq // 4, width), lambda t: (t, 0))
    (output,) = call(
        add_kernel, [((seq, width), f32)], residual, out_parts, grid=(4,),
        specs=[spec, pl.BlockSpec((owners, seq // 4, width), lambda t: (0, t, 0))], out_specs=[spec],
        deps=deps, us=3, name="output",
    )
    rows = width // groups
    block = rows // owners
    summed = last(keep, recv, "dense_last", (output,))
    blocks = to_owners(summed.reshape(owners, block, columns))
    (block_sum,) = call(sum_kernel, [((block, columns), bf16)], blocks, vmem=16, us=2, name="dense_sum")
    shares = [block_sum] + [ring(block_sum, d) for d in range(1, owners)]
    full = call(
        widen_kernel,
        [((local, width, 2 * half), f32), ((local, half, width), f32)],
        gathered,
        grid=(groups,),
        specs=[pl.BlockSpec((1, local * piece, width), lambda i: (i, 0, 0))],
        out_specs=[
            pl.BlockSpec((local, width // groups, 2 * half), lambda i: (0, i, 0)),
            pl.BlockSpec((local, half // groups, width), lambda i: (0, i, 0)),
        ],
        deps=(block_sum,), us=12, name="widen",
    )
    outs = call(
        functools.partial(finish_kernel, owners),
        [((rows, c), f32) for c in (width, key_matrix.shape[1], value_matrix.shape[1], width, LANES)],
        ids, *shares, smem=1, deps=(full[1],), vmem=16, us=3, name="finish",
        scratch=[pltpu.VMEM((owners, block, columns), f32)],
    )
    small = outs[4]
    return (
        output,
        grad_inputs,
        small[:, experts],
        outs[0],
        outs[1],
        outs[2],
        outs[3],
        small[:, experts + 1],
        small[:, :experts],
        *full,
    )


def solution(mesh):
    tokens = P(("group", "expert"), None)
    experts = P("expert", None, None)
    shares = P("group", None)
    return jax.shard_map(
        on_device,
        mesh=mesh,
        in_specs=(
            tokens, P(), P(), P(), P(), P(), P(), P(), experts, experts,
            P(("group", "expert")), tokens, tokens, tokens,
        ),
        out_specs=(
            tokens, tokens, P("group"), shares, shares, shares, shares, P("group"), shares,
            experts, experts,
        ),
        check_vma=False,
    )
```

time: 487 us -> 359 us (0.74)
  waiting for transfers between devices: 248 us -> 161 us
  starting transfers between devices: 95.8 us -> 28.4 us
  other arithmetic: 29.3 us -> 2.46 us
  blocking collectives: 0 us -> 23.5 us
  Pallas kernels: 94.7 us -> 113 us
  between operations: 3.07 us -> 14.9 us
    ppermute x76 -> x14, waiting for transfers between devices: 248 us -> 115 us  [the longest x2 57.9 us: swap(): lax.ppermute(x, 'group', [(i, i ^ 1 << (steps - stage if i % 2 else 1 + s...]
    ppermute x76 -> x14, starting transfers between devices: 95.8 us -> 19.4 us  [the longest x7 12.9 us: ring(): lax.ppermute(x, 'expert', [(i, (i + d) % owners) for i in range(owners)])]
    all_to_all x0 -> x2, waiting for transfers between devices: none -> 44.8 us  [to_owners(): return lax.all_to_all(x, 'expert', split_axis=0, concat_axis=0, tiled=True)]
    all_to_all x0 -> x1, blocking collectives: none -> 23.5 us  [to_owners(): return lax.all_to_all(x, 'expert', split_axis=0, concat_axis=0, tiled=True)]
    pallas_call x9 -> x17, Pallas kernels: 94.7 us -> 113 us  [call(): pl.pallas_call(body, out_shape=outs, compiler_params=pltpu.CompilerParams...]
    unnamed x64 -> x35, local copies, waits for them, and re-layouts: 3.81 us -> 14.7 us
    another operation x16 -> x3, other arithmetic: 11.4 us -> 0.69 us  [the longest x1 0.67 us: on_device(): ids = jnp.stack([z, g % 2, g // 2])]
    add x16 -> x0, other arithmetic: 10 us -> none  [the longest x5 6.08 us: reduce_group(): total = keep.astype(f32) + exchange(send, 0).astype(f32)]
  transfers between devices with their start and end apart: 76 -> 18, of which waited for: 39 -> 11; matrix products, arithmetic and copies ran while one was open for 6% -> 0% of each run, Pallas kernels for 17% -> 23%
where the time goes in v2:
time: 359 us; the launch traced here: 358 us
  waiting for transfers between devices  161 us (45%)
  Pallas kernels  113 us (31%)
  starting transfers between devices  28.4 us (8%)
  blocking collectives  23.5 us (7%)
  local copies, waits for them, and re-layouts  15.4 us (4%)
  between operations  14.9 us (4%)
    pallas_call x17, Pallas kernels, call(): pl.pallas_call(body, out_shape=outs, compiler_params=pltpu.CompilerParams...  113 us
    ppermute x2, waiting for transfers between devices, swap(): lax.ppermute(x, 'group', [(i, i ^ 1 << (steps - stage if i % 2 else 1 + s...  57.9 us
    all_to_all x2, waiting for transfers between devices, to_owners(): return lax.all_to_all(x, 'expert', split_axis=0, concat_axis=0, tiled=True)  44.8 us
    ppermute x7, waiting for transfers between devices, ring(): lax.ppermute(x, 'expert', [(i, (i + d) % owners) for i in range(owners)])  36.6 us
    all_to_all x1, blocking collectives, to_owners(): return lax.all_to_all(x, 'expert', split_axis=0, concat_axis=0, tiled=True)  23.5 us
    ppermute x2, waiting for transfers between devices, far(): down = lax.ppermute(after, 'expert', [(1, 0), (2, 1)])  14.7 us
    unnamed x35, local copies, waits for them, and re-layouts  14.7 us
    ppermute x7, starting transfers between devices, ring(): lax.ppermute(x, 'expert', [(i, (i + d) % owners) for i in range(owners)])  12.9 us
  transfers between devices with their start and end apart: 18, of which 11 were waited for; matrix products, arithmetic and copies ran while one was open for 0% of the time, Pallas kernels for 23%

profile of v2, /device:TPU:0, one launch (start us, length us, event | category | flops | bytes accessed | tf_op | source)
XLA Modules:
  0.0 358.5 jit_solution(13392494052333610811)
XLA Ops:
  7.2 3.1 collective-permute-start
  10.3 2.1 collective-permute-start.1
  13.0 8.5 %dense_forward.1 = (bf16[256,1024]{1,0:T(8,128)(2,1)}, bf16[256,1024]{1,0:T(8,128)(2,1)}, bf16[256,1024]{1,0:T(8,128)(2,1)}, bf16[256,1024]{1,0:T(8,128)(2,1)}, ...) custom-call(s32[1]{0:T(128)S(6)} %copy.37.refs_0_.refs_1_, ...), custom_call_target="tpu_custom_call" | custom-call | bytes 32400000 | tf_op jit(solution)/shard_map/dense_forward/pallas_call | solution.py:50
  21.6 3.8 %collective-permute-done.refs_1_.refs_0_ = bf16[256,1024]{1,0:T(8,128)(2,1)S(1)} collective-permute-done((bf16[256,1024]{1,0:T(8,128)(2,1)}, bf16[256,1024]{1,0:T(8,128)(2,1)S(1)}, u32[]{:S(2)}, u32[]{:S(2)}) %collective-permute-start) | collective-permute-done | bytes 524320 | tf_op jit(solution)/shard_map/ppermute | solution.py:444
  25.3 9.8 %collective-permute-done.1.refs_2_.refs_1_ = bf16[256,1024]{1,0:T(8,128)(2,1)S(1)} collective-permute-done((bf16[256,1024]{1,0:T(8,128)(2,1)}, bf16[256,1024]{1,0:T(8,128)(2,1)S(1)}, u32[]{:S(2)}, u32[]{:S(2)}) %collective-permute-start.1) | collective-permute-done | bytes 524320 | tf_op jit(solution)/shard_map/ppermute | solution.py:444
  35.1 0.8 copy-done.16
  35.9 1.1 collective-permute-start.2
  37.1 2.7 collective-permute-start.4
  39.8 13.7 %collective-permute-done.2.refs_2_ = bf16[272,1024]{1,0:T(8,128)(2,1)S(1)} collective-permute-done((bf16[272,1024]{1,0:T(8,128)(2,1)}, bf16[272,1024]{1,0:T(8,128)(2,1)S(1)}, u32[]{:S(2)}, u32[]{:S(2)}) %collective-permute-start.2) | collective-permute-done | bytes 557088 | tf_op jit(solution)/shard_map/ppermute | solution.py:444
  53.5 0.7 collective-permute-start.3
  54.2 9.3 %collective-permute-done.4.refs_4_ = bf16[272,1024]{1,0:T(8,128)(2,1)S(1)} collective-permute-done((bf16[272,1024]{1,0:T(8,128)(2,1)}, bf16[272,1024]{1,0:T(8,128)(2,1)S(1)}, u32[]{:S(2)}, u32[]{:S(2)}) %collective-permute-start.4) | collective-permute-done | bytes 557088 | tf_op jit(solution)/shard_map/ppermute | solution.py:444
  63.5 1.3 collective-permute-start.5
  64.8 14.7 %collective-permute-done.5 = bf16[272,1024]{1,0:T(8,128)(2,1)S(1)} collective-permute-done((bf16[272,1024]{1,0:T(8,128)(2,1)S(1)}, bf16[272,1024]{1,0:T(8,128)(2,1)S(1)}, u32[]{:S(2)}, u32[]{:S(2)}) %collective-permute-start.5) | collective-permute-done | bytes 557088 | tf_op jit(solution)/shard_map/ppermute | solution.py:462
  79.5 0.9 broadcast_select_fusion.refs_3_.refs_2_
  81.1 1.5 collective-permute-start.7
  83.3 17.0 %expert_forward.1 = (bf16[4,640,1024]{2,1,0:T(8,128)(2,1)}, bf16[4,640,512]{2,1,0:T(8,128)(2,1)}, f32[4,640,512]{2,1,0:T(8,128)}, f32[4,640,512]{2,1,0:T(8,128)}, bf16[4,640,1024]{2,1,0:T(8,128)(2,1)}) custom-call(s32[3]{0:T(128)} %pad_add_fusion.2.refs_0_, bf16[272,1024]{1,0:T(8,128)(2,1)} %tokens_go.1.refs_1_.refs_8_, bf16[272,1024]{1,0:T(8,128)(2,1)} %copy-done.12, ...), custom_call_target="tpu_custom_call" | custom-call | bytes 61200000 | tf_op jit(solution)/shard_map/expert_forward/pallas_call | solution.py:50
  100.3 0.9 broadcast_select_fusion.1.refs_7_
  101.2 28.6 %expert_backward.1 = (bf16[8,768,1024]{2,1,0:T(8,128)(2,1)}, bf16[4,640,1024]{2,1,0:T(8,128)(2,1)}, f32[4,4,256]{2,1,0:T(4,128)}) custom-call(s32[3]{0:T(128)} %pad_add_fusion.2.refs_0_, bf16[272,1024]{1,0:T(8,128)(2,1)} %tokens_go.1.refs_1_.refs_8_, bf16[272,1024]{1,0:T(8,128)(2,1)} %copy-done.12, bf16[272,1024]{1,0:T(8,128)(2,1)} %broadcast_select_fusion.refs_3_.refs_2_, ...), custom_call_target="tpu_custom_call" | custom-call | bytes 129600000 | tf_op jit(solution)/shard_map/expert_backward/pallas_call | solution.py:50
  129.8 8.0 %combine_grad.1.refs_6_ = bf16[4,272,1024]{2,1,0:T(8,128)(2,1)} custom-call(s32[3]{0:T(128)} %pad_add_fusion.2.refs_0_, bf16[272,1024]{1,0:T(8,128)(2,1)} %tokens_go.1.refs_1_.refs_8_, bf16[272,1024]{1,0:T(8,128)(2,1)} %copy-done.12, bf16[272,1024]{1,0:T(8,128)(2,1)} %broadcast_select_fusion.refs_3_.refs_2_, bf16[272,1024]{1,0:T(8,128)(2,1)} %copy-done.13, ...), custom_call_target="tpu_custom_call" | custom-call | bytes 18000000 | tf_op jit(solution)/shard_map/combine_grad/pallas_call | solution.py:50
  137.9 4.3 %all-to-all-start = ((bf16[4,272,1024]{2,1,0:T(8,128)(2,1)}), bf16[4,272,1024]{2,1,0:T(8,128)(2,1)S(1)}, u32[]{:S(2)}, u32[]{:S(2)}) async-start(bf16[4,272,1024]{2,1,0:T(8,128)(2,1)} %combine_grad.1.refs_6_), calls=%async_computation | async-start | bytes 4456448 | tf_op jit(solution)/shard_map/all_to_all | solution.py:584
  142.2 8.9 %combine_out.1.refs_21_.refs_0_ = bf16[4,256,1024]{2,1,0:T(8,128)(2,1)} custom-call(s32[3]{0:T(128)} %pad_add_fusion.2.refs_0_, bf16[272,1024]{1,0:T(8,128)(2,1)} %tokens_go.1.refs_1_.refs_8_, bf16[272,1024]{1,0:T(8,128)(2,1)} %copy-done.12, bf16[272,1024]{1,0:T(8,128)(2,1)} %broadcast_select_fusion.refs_3_.refs_2_, bf16[272,1024]{1,0:T(8,128)(2,1)} %copy-done.13, ...), custom_call_target="tpu_custom_call" | custom-call | bytes 18000000 | tf_op jit(solution)/shard_map/combine_out/pallas_call | solution.py:50
  151.1 40.6 %all-to-all-done.refs_2_ = bf16[4,272,1024]{2,1,0:T(8,128)(2,1)S(1)} async-done(((bf16[4,272,1024]{2,1,0:T(8,128)(2,1)}), bf16[4,272,1024]{2,1,0:T(8,128)(2,1)S(1)}, u32[]{:S(2)}, u32[]{:S(2)}) %all-to-all-start) | async-done | bytes 2228256 | tf_op jit(solution)/shard_map/all_to_all | solution.py:584
  191.7 1.4 copy-done.14
  193.1 18.7 %dense_backward.1 = (f32[256,1024]{1,0:T(8,128)}, bf16[4,128,3200]{2,1,0:T(8,128)(2,1)}, bf16[4,128,3200]{2,1,0:T(8,128)(2,1)}) custom-call(s32[3]{0:T(128)} %pad_add_fusion.2.refs_0_, s32[1]{0:T(128)S(6)} %copy.37.refs_0_.refs_1_, bf16[4,272,1024]{2,1,0:T(8,128)(2,1)} %copy-done.14, f32[16,256]{1,0:T(8,128)} %get-tuple-element.55.refs_3_, ...), custom_call_target="tpu_custom_call" | custom-call | bytes 64800000 | tf_op jit(solution)/shard_map/dense_backward/pallas_call | solution.py:50
  211.9 6.0 %collective-permute-done.8.refs_2_.refs_4_ = bf16[4,128,3200]{2,1,0:T(8,128)(2,1)S(1)} collective-permute-done((bf16[4,128,3200]{2,1,0:T(8,128)(2,1)}, bf16[4,128,3200]{2,1,0:T(8,128)(2,1)S(1)}, u32[]{:S(2)}, u32[]{:S(2)}) %collective-permute-start.8) | collective-permute-done | bytes 3276832 | tf_op jit(solution)/shard_map/ppermute | solution.py:447
  217.9 1.3 dense_halve0.1
  219.2 1.7 copy-done.1
  220.9 1.2 copy-done.8
  222.1 0.8 reduce-scatter.2.cloned.1.call-done
  223.0 4.7 %all-to-all-start.1 = ((bf16[4,256,1024]{2,1,0:T(8,128)(2,1)}), bf16[4,256,1024]{2,1,0:T(8,128)(2,1)}, u32[]{:S(2)}, u32[]{:S(2)}) async-start(bf16[4,256,1024]{2,1,0:T(8,128)(2,1)} %returned_go.1.refs_5_), calls=%async_computation.1 | async-start | bytes 4194304 | tf_op jit(solution)/shard_map/all_to_all | solution.py:584
  227.7 1.3 collective-permute-start.9
  229.0 36.8 %collective-permute-done.9.refs_2_.refs_4_ = bf16[2,128,3200]{2,1,0:T(8,128)(2,1)S(1)} collective-permute-done((bf16[2,128,3200]{2,1,0:T(8,128)(2,1)}, bf16[2,128,3200]{2,1,0:T(8,128)(2,1)S(1)}, u32[]{:S(2)}, u32[]{:S(2)}) %collective-permute-start.9) | collective-permute-done | bytes 1638432 | tf_op jit(solution)/shard_map/ppermute | solution.py:450
  265.9 2.2 copy-done.2
  268.1 1.7 dense_halve1.1
  269.8 1.2 copy-done.9
  270.9 1.1 collective-permute-start.10
  272.0 4.1 %all-to-all-done.1.refs_1_ = bf16[4,256,1024]{2,1,0:T(8,128)(2,1)} async-done(((bf16[4,256,1024]{2,1,0:T(8,128)(2,1)}), bf16[4,256,1024]{2,1,0:T(8,128)(2,1)}, u32[]{:S(2)}, u32[]{:S(2)}) %all-to-all-start.1) | async-done | bytes 2097184 | tf_op jit(solution)/shard_map/all_to_all | solution.py:584
  276.1 3.9 %output.1.refs_2_ = f32[256,1024]{1,0:T(8,128)} custom-call(f32[256,1024]{1,0:T(8,128)} %get-tuple-element.44.refs_6_.refs_0_, bf16[4,256,1024]{2,1,0:T(8,128)(2,1)} %all-to-all-done.1.refs_1_, bf16[1,128,3200]{2,1,0:T(8,128)(2,1)} %get-tuple-element.67.refs_2_), custom_call_target="tpu_custom_call" | custom-call | bytes 10800000 | tf_op jit(solution)/shard_map/output/pallas_call | solution.py:50
  280.0 21.0 %collective-permute-done.10.refs_1_ = bf16[1,128,3200]{2,1,0:T(8,128)(2,1)S(1)} collective-permute-done((bf16[1,128,3200]{2,1,0:T(8,128)(2,1)}, bf16[1,128,3200]{2,1,0:T(8,128)(2,1)S(1)}, u32[]{:S(2)}, u32[]{:S(2)}) %collective-permute-start.10) | collective-permute-done | bytes 819232 | tf_op jit(solution)/shard_map/ppermute | solution.py:450
  301.0 1.2 copy-done.5
  302.4 23.5 %all_to_all.15.refs_0_ = bf16[4,32,3200]{2,1,0:T(8,128)(2,1)S(1)} all-to-all(bf16[4,32,3200]{2,1,0:T(8,128)(2,1)S(1)} %bitcast.19), channel_id=1, replica_groups=mesh['group'=8,'expert'=4] {'expert'}, dimensions={0} | all-to-all | bytes 1638400 | tf_op jit(solution)/shard_map/all_to_all | solution.py:584
  326.5 1.5 collective-permute-start.12
  328.1 1.8 collective-permute-start.13
  329.9 14.2 %widen.1 = (f32[4,1024,1024]{2,1,0:T(8,128)}, f32[4,512,1024]{2,1,0:T(8,128)}) custom-call(bf16[8,768,1024]{2,1,0:T(8,128)(2,1)} %bitcast.21, bf16[32,3200]{1,0:T(8,128)(2,1)} %copy-done.6), custom_call_target="tpu_custom_call" | custom-call | bytes 43200000 | tf_op jit(solution)/shard_map/widen/pallas_call | solution.py:50
  344.1 3.4 copy-done.4
  347.5 0.9 copy-done.7
  348.4 1.8 finish.1
  350.3 0.7 slice_reduce_fusion
  (50 shorter events, 3.0 us)
Async XLA Ops:
  7.2 215.8 %reduce-scatter.2.cloned.1.call-start = ((), (), s32[]{:S(2)}) async-start(), calls=%async_computation.4 | async-start | bytes 14155776 | tf_op jit(solution)/shard_map/reduce_scatter | solution.py:567
  7.2 18.1 %collective-permute-start = (bf16[256,1024]{1,0:T(8,128)(2,1)}, bf16[256,1024]{1,0:T(8,128)(2,1)S(1)}, u32[]{:S(2)}, u32[]{:S(2)}) collective-permute-start(bf16[256,1024]{1,0:T(8,128)(2,1)} %refs_5_.7), channel_id=1, source_target_pairs={{0,1},{1,2},{2,3},{3,0},{4,5},{5,6},{6,7},{7,4},{8,9},{9,10},{10,1... | collective-permute-start | bytes 1572872 | tf_op jit(solution)/shard_map/ppermute | solution.py:444
  10.3 24.8 %collective-permute-start.1 = (bf16[256,1024]{1,0:T(8,128)(2,1)}, bf16[256,1024]{1,0:T(8,128)(2,1)S(1)}, u32[]{:S(2)}, u32[]{:S(2)}) collective-permute-start(bf16[256,1024]{1,0:T(8,128)(2,1)} %refs_5_.7), channel_id=1, source_target_pairs={{0,3},{1,0},{2,1},{3,2},{4,7},{5,4},{6,5},{7,6},{8,11},{9,8},{10,9... | collective-permute-start | bytes 1572872 | tf_op jit(solution)/shard_map/ppermute | solution.py:444
  25.3 9.8 %copy-start.15 = (bf16[256,1024]{1,0:T(8,128)(2,1)}, bf16[256,1024]{1,0:T(8,128)(2,1)S(1)}, u32[]{:S(2)}) copy-start(bf16[256,1024]{1,0:T(8,128)(2,1)S(1)} %collective-permute-done.refs_1_.refs_0_) | copy-start | bytes 1572868
  35.1 0.8 copy-start.16
  35.9 17.6 %collective-permute-start.2 = (bf16[272,1024]{1,0:T(8,128)(2,1)}, bf16[272,1024]{1,0:T(8,128)(2,1)S(1)}, u32[]{:S(2)}, u32[]{:S(2)}) collective-permute-start(bf16[272,1024]{1,0:T(8,128)(2,1)} %tokens_go.1.refs_1_.refs_8_), channel_id=1, source_target_pairs={{0,1},{1,2},{2,3},{3,0},{4,5},{5,6},{6,7},{7,4},{8,9},{9,10},{10,1... | collective-permute-start | bytes 1671176 | tf_op jit(solution)/shard_map/ppermute | solution.py:444
  37.1 26.4 %collective-permute-start.4 = (bf16[272,1024]{1,0:T(8,128)(2,1)}, bf16[272,1024]{1,0:T(8,128)(2,1)S(1)}, u32[]{:S(2)}, u32[]{:S(2)}) collective-permute-start(bf16[272,1024]{1,0:T(8,128)(2,1)} %tokens_go.1.refs_1_.refs_8_), channel_id=1, source_target_pairs={{0,3},{1,0},{2,1},{3,2},{4,7},{5,4},{6,5},{7,6},{8,11},{9,8},{10,9... | collective-permute-start | bytes 1671176 | tf_op jit(solution)/shard_map/ppermute | solution.py:444
  53.5 29.8 %copy-start.12 = (bf16[272,1024]{1,0:T(8,128)(2,1)}, bf16[272,1024]{1,0:T(8,128)(2,1)S(1)}, u32[]{:S(2)}) copy-start(bf16[272,1024]{1,0:T(8,128)(2,1)S(1)} %collective-permute-done.2.refs_2_) | copy-start | bytes 1671172
  53.5 11.3 %collective-permute-start.3 = (bf16[272,1024]{1,0:T(8,128)(2,1)S(1)}, bf16[272,1024]{1,0:T(8,128)(2,1)S(1)}, u32[]{:S(2)}, u32[]{:S(2)}) collective-permute-start(bf16[272,1024]{1,0:T(8,128)(2,1)S(1)} %collective-permute-done.2.refs_2_), channel_id=1, source_target_pairs={{1,2},{2,3},{5,6},{6,7},{9,10},{10,11},{13,14},{14,15},{17,18},{18... | collective-permute-start | bytes 1671176 | tf_op jit(solution)/shard_map/ppermute | solution.py:461
  63.5 19.8 %copy-start.13 = (bf16[272,1024]{1,0:T(8,128)(2,1)}, bf16[272,1024]{1,0:T(8,128)(2,1)S(1)}, u32[]{:S(2)}) copy-start(bf16[272,1024]{1,0:T(8,128)(2,1)S(1)} %collective-permute-done.4.refs_4_) | copy-start | bytes 1671172
  63.5 16.0 %collective-permute-start.5 = (bf16[272,1024]{1,0:T(8,128)(2,1)S(1)}, bf16[272,1024]{1,0:T(8,128)(2,1)S(1)}, u32[]{:S(2)}, u32[]{:S(2)}) collective-permute-start(bf16[272,1024]{1,0:T(8,128)(2,1)S(1)} %collective-permute-done.4.refs_4_), channel_id=1, source_target_pairs={{1,0},{2,1},{5,4},{6,5},{9,8},{10,9},{13,12},{14,13},{17,16},{18,1... | collective-permute-start | bytes 1671176 | tf_op jit(solution)/shard_map/ppermute | solution.py:462
  80.4 19.9 %collective-permute-start.6 = (bf16[256,1024]{1,0:T(8,128)(2,1)}, bf16[256,1024]{1,0:T(8,128)(2,1)S(1)}, u32[]{:S(2)}, u32[]{:S(2)}) collective-permute-start(bf16[256,1024]{1,0:T(8,128)(2,1)} %get-tuple-element.47.refs_6_), channel_id=1, source_target_pairs={{1,2},{2,3},{5,6},{6,7},{9,10},{10,11},{13,14},{14,15},{17,18},{18... | collective-permute-start | bytes 1572872 | tf_op jit(solution)/shard_map/ppermute | solution.py:461
  81.1 19.2 %collective-permute-start.7 = (bf16[256,1024]{1,0:T(8,128)(2,1)}, bf16[256,1024]{1,0:T(8,128)(2,1)S(1)}, u32[]{:S(2)}, u32[]{:S(2)}) collective-permute-start(bf16[256,1024]{1,0:T(8,128)(2,1)} %get-tuple-element.48.refs_8_), channel_id=1, source_target_pairs={{1,0},{2,1},{5,4},{6,5},{9,8},{10,9},{13,12},{14,13},{17,16},{18,1... | collective-permute-start | bytes 1572872 | tf_op jit(solution)/shard_map/ppermute | solution.py:462
  137.9 53.8 %all-to-all-start = ((bf16[4,272,1024]{2,1,0:T(8,128)(2,1)}), bf16[4,272,1024]{2,1,0:T(8,128)(2,1)S(1)}, u32[]{:S(2)}, u32[]{:S(2)}) async-start(bf16[4,272,1024]{2,1,0:T(8,128)(2,1)} %combine_grad.1.refs_6_), calls=%async_computation | async-start | bytes 4456448 | tf_op jit(solution)/shard_map/all_to_all | solution.py:584
  142.2 187.7 %all-gather.3.cloned.1.call-start = ((), (), s32[]{:S(2)}) async-start(), calls=%async_computation.5 | async-start | bytes 14155776 | tf_op jit(solution)/shard_map/all_gather | solution.py:616
  191.7 1.4 copy-start.14
  211.8 6.1 %collective-permute-start.8 = (bf16[4,128,3200]{2,1,0:T(8,128)(2,1)}, bf16[4,128,3200]{2,1,0:T(8,128)(2,1)S(1)}, u32[]{:S(2)}, u32[]{:S(2)}) collective-permute-start(bf16[4,128,3200]{2,1,0:T(8,128)(2,1)} %get-tuple-element.62.refs_1_), channel_id=1, source_target_pairs={{0,4},{4,0},{8,12},{12,8},{16,20},{20,16},{24,28},{28,24},{1,5},{5... | collective-permute-start | bytes 9830408 | tf_op jit(solution)/shard_map/ppermute | solution.py:447
  211.9 6.0 %copy-start.3 = (bf16[4,128,3200]{2,1,0:T(8,128)(2,1)S(1)}, bf16[4,128,3200]{2,1,0:T(8,128)(2,1)}, u32[]{:S(2)}) copy-start(bf16[4,128,3200]{2,1,0:T(8,128)(2,1)} %get-tuple-element.63.refs_1_.refs_3_) | copy-start | bytes 9830404
  219.2 1.7 copy-start.1
  220.9 1.2 copy-start.8
  222.9 42.9 %copy-start = (bf16[768,1024]{1,0:T(8,128)(2,1)S(1)}, bf16[768,1024]{1,0:T(8,128)(2,1)}, u32[]{:S(2)}) copy-start(bf16[768,1024]{1,0:T(8,128)(2,1)} %gather_go.1.refs_5_) | copy-start | bytes 4718596
  223.0 53.1 %all-to-all-start.1 = ((bf16[4,256,1024]{2,1,0:T(8,128)(2,1)}), bf16[4,256,1024]{2,1,0:T(8,128)(2,1)}, u32[]{:S(2)}, u32[]{:S(2)}) async-start(bf16[4,256,1024]{2,1,0:T(8,128)(2,1)} %returned_go.1.refs_5_), calls=%async_computation.1 | async-start | bytes 4194304 | tf_op jit(solution)/shard_map/all_to_all | solution.py:584
  227.7 38.2 %collective-permute-start.9 = (bf16[2,128,3200]{2,1,0:T(8,128)(2,1)}, bf16[2,128,3200]{2,1,0:T(8,128)(2,1)S(1)}, u32[]{:S(2)}, u32[]{:S(2)}) collective-permute-start(bf16[2,128,3200]{2,1,0:T(8,128)(2,1)} %copy-done.8), channel_id=1, source_target_pairs={{0,8},{4,20},{8,0},{12,28},{16,24},{20,4},{24,16},{28,12},{1,9},{5... | collective-permute-start | bytes 4915208 | tf_op jit(solution)/shard_map/ppermute | solution.py:450
  265.9 2.2 copy-start.2
  269.8 1.2 copy-start.9
  270.9 30.1 %copy-start.10 = (f32[1,128,3200]{2,1,0:T(8,128)S(1)}, f32[1,128,3200]{2,1,0:T(8,128)}, u32[]{:S(2)}) copy-start(f32[1,128,3200]{2,1,0:T(8,128)} %copy-done.9) | copy-start | bytes 4915204
  270.9 30.1 %collective-permute-start.10 = (bf16[1,128,3200]{2,1,0:T(8,128)(2,1)}, bf16[1,128,3200]{2,1,0:T(8,128)(2,1)S(1)}, u32[]{:S(2)}, u32[]{:S(2)}) collective-permute-start(bf16[1,128,3200]{2,1,0:T(8,128)(2,1)} %get-tuple-element.67.refs_2_), channel_id=1, source_target_pairs={{0,16},{4,12},{8,24},{12,4},{16,0},{20,28},{24,8},{28,20},{1,17},{... | collective-permute-start | bytes 2457608 | tf_op jit(solution)/shard_map/ppermute | solution.py:450
  301.0 1.2 copy-start.5
  326.0 3.9 %copy-start.6 = (bf16[32,3200]{1,0:T(8,128)(2,1)}, bf16[32,3200]{1,0:T(8,128)(2,1)S(1)}, u32[]{:S(2)}) copy-start(bf16[32,3200]{1,0:T(8,128)(2,1)S(1)} %dense_sum.1.refs_1_) | copy-start | bytes 614404
  326.0 18.1 %collective-permute-start.11 = (bf16[32,3200]{1,0:T(8,128)(2,1)S(1)}, bf16[32,3200]{1,0:T(8,128)(2,1)S(1)}, u32[]{:S(2)}, u32[]{:S(2)}) collective-permute-start(bf16[32,3200]{1,0:T(8,128)(2,1)S(1)} %dense_sum.1.refs_1_), channel_id=1, source_target_pairs={{0,1},{1,2},{2,3},{3,0},{4,5},{5,6},{6,7},{7,4},{8,9},{9,10},{10,1... | collective-permute-start | bytes 614408 | tf_op jit(solution)/shard_map/ppermute | solution.py:444
  326.5 17.6 %collective-permute-start.12 = (bf16[32,3200]{1,0:T(8,128)(2,1)S(1)}, bf16[32,3200]{1,0:T(8,128)(2,1)S(1)}, u32[]{:S(2)}, u32[]{:S(2)}) collective-permute-start(bf16[32,3200]{1,0:T(8,128)(2,1)S(1)} %dense_sum.1.refs_1_), channel_id=1, source_target_pairs={{0,2},{1,3},{2,0},{3,1},{4,6},{5,7},{6,4},{7,5},{8,10},{9,11},{10,... | collective-permute-start | bytes 614408 | tf_op jit(solution)/shard_map/ppermute | solution.py:444
  328.1 16.0 %collective-permute-start.13 = (bf16[32,3200]{1,0:T(8,128)(2,1)S(1)}, bf16[32,3200]{1,0:T(8,128)(2,1)S(1)}, u32[]{:S(2)}, u32[]{:S(2)}) collective-permute-start(bf16[32,3200]{1,0:T(8,128)(2,1)S(1)} %dense_sum.1.refs_1_), channel_id=1, source_target_pairs={{0,3},{1,0},{2,1},{3,2},{4,7},{5,4},{6,5},{7,6},{8,11},{9,8},{10,9... | collective-permute-start | bytes 614408 | tf_op jit(solution)/shard_map/ppermute | solution.py:444
  329.9 14.2 %copy-start.11 = (s32[3]{0:T(128)S(1)}, s32[3]{0:T(128)}, u32[]{:S(2)}) copy-start(s32[3]{0:T(128)} %pad_add_fusion.2.refs_0_) | copy-start | bytes 40
  344.1 3.4 copy-start.4
  347.5 0.9 copy-start.7
Sparse Core Ops, SparseCore 0:
  129.9 92.9 reduce-scatter.1
  224.8 89.3 all-gather.2

commit v3 on v2

--- a/solution.py
+++ b/solution.py
@@ -21,7 +21,9 @@
 VMEM = pl.BlockSpec(memory_space=pltpu.VMEM)
 SMEM = pl.BlockSpec(memory_space=pltpu.SMEM)
 ANY = pl.BlockSpec(memory_space=pl.ANY)
+HELD = pl.BlockSpec(memory_space=pltpu.HBM)
 COST = 3600000
+TOKEN = ((8, LANES), f32)
 
 
 def mm(left, right, dims=((1,), (0,))):
@@ -35,7 +37,7 @@
     def body(*refs):
         kernel(*refs[:taken], *refs[taken + len(deps) :])
 
-    in_specs = (specs or [SMEM] * smem + [VMEM] * (taken - smem)) + [ANY] * len(deps)
+    in_specs = (specs or [SMEM] * smem + [VMEM] * (taken - smem)) + [HELD] * len(deps)
     out_specs = out_specs or [VMEM] * len(outs)
     if prefetch:
         placed = dict(
@@ -196,13 +198,14 @@
         wret_ref[0, :, cols] = (weight[...] * returned).astype(bf16)
 
 
-def expert_backward(local, capacity, owners, id_ref, *refs):
+def expert_backward(first, split, local, capacity, owners, id_ref, *refs):
     tokens, cots = refs[:owners], refs[owners : 2 * owners]
-    (sent_ref, hidden_ref, slope_ref, silu_ref, win_ref, wout_ref,
-     sums_ref, grow_ref, gg_ref, crow, weight, gret, gpre) = refs[2 * owners :]
+    rest = refs[2 * owners :]
+    sent_ref, hidden_ref, slope_ref, silu_ref, win_ref, wout_ref = rest[:6]
+    sums, (grow_ref, gg_ref, crow, weight, gret, gpre) = rest[6:-6], rest[-6:]
     width, half = win_ref.shape[1], wout_ref.shape[1]
     seq = cots[0].shape[0]
-    expert = id_ref[0] * local + pl.program_id(0)
+    expert = id_ref[0] * local + first + pl.program_id(0)
     place = lax.broadcasted_iota(jnp.int32, (capacity, seq), 0).astype(f32)
     places = []
     for d in range(owners):
@@ -229,15 +232,22 @@
         gg_ref[0, d : d + 1, :] = jnp.sum(jnp.where(place == places[d], part, 0.0), 0, keepdims=True)
     for t in range(0, width, tile):
         grow_ref[0, :, t : t + tile] = mm(gpre[...], win_ref[0, t : t + tile, :], ((1,), (1,))).astype(bf16)
-    pieces = sums_ref.shape[0]
+    pieces = sums[0].shape[0] * len(sums)
     base = 0
     for left, right in ((sent_ref, gpre), (hidden_ref, gret)):
         size = left.shape[2]
         step = size // pieces
         for t in range(0, width, tile):
-            made = mm(left[0], right[:, t : t + tile], ((0,), (0,))).astype(bf16)
-            for q in range(pieces):
-                sums_ref[q, base : base + step, t : t + tile] = made[q * step : (q + 1) * step]
+            made = mm(left[0], right[:, t : t + tile], ((0,), (0,)))
+            for q in range(pieces // len(sums)):
+                if split:
+                    low = made[2 * q * step : (2 * q + 1) * step]
+                    high = made[(2 * q + 1) * step : (2 * q + 2) * step]
+                    mine = id_ref[1] == 0
+                    sums[0][q, base : base + step, t : t + tile] = jnp.where(mine, low, high).astype(bf16)
+                    sums[1][q, base : base + step, t : t + tile] = jnp.where(mine, high, low).astype(bf16)
+                else:
+                    sums[0][q, base : base + step, t : t + tile] = made[q * step : (q + 1) * step].astype(bf16)
         base += step
 
 
@@ -246,8 +256,8 @@
     rest = refs[owners:]
     rows_in = [(r, i) for r in rest[: counts[0]] for i in range(r.shape[0])]
     dots = [(r, i) for r in rest[counts[0] : counts[0] + counts[1]] for i in range(r.shape[0])]
-    part_ref, columns = rest[-2:]
-    width = part_ref.shape[2]
+    parts, columns = rest[sum(counts) : -1], rest[-1]
+    width = parts[0].shape[-1]
     seq = width // local
     d = pl.program_id(0)
 
@@ -267,44 +277,69 @@
         hit = same if hit is None else hit | same
     one = jnp.where(hit, 1.0, 0.0).astype(bf16)
     stacked = jnp.concatenate([r[i] for r, i in rows_in], 0)
-    part_ref[0, :seq, :] = mm(one, stacked).astype(bf16)
+    made = mm(one, stacked).astype(bf16)
     if dots:
         line = jnp.concatenate([r[i, pl.ds(d, 1), :] for r, i in dots], 1)
         high = line.astype(bf16).astype(f32)
-        index = lax.broadcasted_iota(jnp.int32, (part_ref.shape[1] - seq, width), 0)
+        index = lax.broadcasted_iota(jnp.int32, (parts[0].shape[0] - seq, width), 0)
         mine = jnp.where(index == id_ref[0], high, 0.0)
         mine = jnp.where(index == owners + id_ref[0], line - high, mine)
-        part_ref[0, seq:, :] = mine.astype(bf16)
-
-
-def halve_kernel(id_ref, keep_ref, recv_ref, keep_go_ref, recv_go_ref, own_ref, send_ref):
-    own_ref[...] = keep_ref[...].astype(f32) + recv_ref[...].astype(f32)
+    if len(parts) == 1:
+        parts[0][lax.rem(id_ref[0] + owners - d, owners)] = made
+    for t in range(len(parts) if dots else 0):
+
+        @pl.when(d == t)
+        def _():
+            parts[t][:seq, :] = made
+            parts[t][seq:, :] = mine.astype(bf16)
+
+
+def hop_kernel(*refs):
+    pairs = len(refs) // 3
+    for i in range(pairs):
+        total = refs[i][...].astype(f32) + refs[pairs + i][...].astype(f32)
+        refs[2 * pairs + i][...] = total.astype(bf16)
+
+
+def halve_kernel(id_ref, keep_ref, recv_ref, keep_go_ref, recv_go_ref, own_ref, send_ref, token_ref):
+    token_ref[...] = jnp.zeros_like(token_ref)
+    own_ref[...] = (keep_ref[...].astype(f32) + recv_ref[...].astype(f32)).astype(own_ref.dtype)
     send_ref[...] = (keep_go_ref[...].astype(f32) + recv_go_ref[...].astype(f32)).astype(bf16)
-
-
-def last_kernel(keep_ref, recv_ref, out_ref):
-    out_ref[...] = (keep_ref[...].astype(f32) + recv_ref[...].astype(f32)).astype(bf16)
 
 
 def nothing_kernel(*refs):
     pass
 
 
-def add_kernel(base_ref, parts_ref, out_ref):
+def add_kernel(base_ref, parts_ref, out_ref, token_ref):
     total = base_ref[...]
     for i in range(parts_ref.shape[0]):
         total = total + parts_ref[i].astype(f32)
     out_ref[...] = total
-
-
-def sum_kernel(in_ref, out_ref):
-    total = in_ref[0].astype(f32)
-    for i in range(1, in_ref.shape[0]):
-        total = total + in_ref[i].astype(f32)
-    out_ref[...] = total.astype(out_ref.dtype)
-
-
-def widen_kernel(in_ref, first_ref, second_ref):
+    token_ref[...] = jnp.zeros_like(token_ref)
+
+
+def spread_kernel(owners, id_ref, keep_ref, recv_ref, *refs):
+    outs, token_ref, total = refs[:owners], refs[owners], refs[owners + 1]
+    token_ref[...] = jnp.zeros_like(token_ref)
+    block = outs[0].shape[0]
+    for i in range(owners):
+        span = slice(i * block, (i + 1) * block)
+        total[i] = keep_ref[0, span, :].astype(f32) + recv_ref[0, span, :].astype(f32)
+    for d in range(owners):
+        outs[d][...] = total[lax.rem(id_ref[0] + d, owners)].astype(bf16)
+
+
+def sum_kernel(*refs):
+    total = refs[0][...].astype(f32)
+    for ref in refs[1:-1]:
+        total = total + ref[...].astype(f32)
+    refs[-1][...] = total.astype(refs[-1].dtype)
+
+
+def widen_kernel(in_ref, *refs):
+    first_ref, second_ref, token_ref = refs[-3:]
+    token_ref[...] = jnp.zeros_like(token_ref)
     count, rows, _ = first_ref.shape
     size = in_ref.shape[1] // count
     for j in range(count):
@@ -325,32 +360,34 @@
             col += cols
 
 
-def dense_backward(owners, local, id_ref, len_ref, *refs):
-    (part_ref, gate_ref, x_ref, cot_ref, res_ref, n1_ref, pack_ref, q_ref, kk_ref, vv_ref, lse_ref, mixed_ref,
+def dense_backward(parts, owners, local, id_ref, len_ref, *refs):
+    part_refs, refs = refs[:parts], refs[parts:]
+    (gate_ref, x_ref, cot_ref, res_ref, n1_ref, pack_ref, q_ref, kk_ref, vv_ref, lse_ref, mixed_ref,
      wq_ref, wk_ref, wv_ref, wo_ref, wr_ref, g1_ref, g2_ref,
-     gin_ref, keep_ref, send_ref, gg_all, gmix, gq, gk, gv, acc) = refs
+     gin_ref, keep_one, send_one, keep_two, send_two, gg_all, gmix, gq, gk, gv, acc) = refs
     rows, width = x_ref.shape
     core = id_ref[1]
-    pieces = 2 * keep_ref.shape[0]
+    pieces = 2 * keep_one.shape[0]
     step = width // pieces
 
-    def put(offset, size):
+    def put(stream, offset, size):
+        keep_ref, send_ref = stream
         for q in range(pieces // 2):
             lo = pl.multiple_of((2 * q + core) * step, step)
             hi = pl.multiple_of((2 * q + 1 - core) * step, step)
             keep_ref[q, :, offset : offset + size] = acc[pl.ds(lo, step), :size].astype(bf16)
             send_ref[q, :, offset : offset + size] = acc[pl.ds(hi, step), :size].astype(bf16)
 
-    def weight_gradient(left, right, offset):
+    def weight_gradient(left, right, stream, offset):
         size = right.shape[1]
         tile = 256
         for t in range(0, size, tile):
             acc[:, t : t + tile] = mm(left[...], right[:, t : t + tile], ((0,), (0,)))
-        put(offset, size)
-
-    tail = part_ref[0, rows:, :].astype(f32)
-    for owner in range(1, owners):
-        tail = tail + part_ref[owner, rows:, :].astype(f32)
+        put(stream, offset, size)
+
+    tail = part_refs[0][rows:, :].astype(f32)
+    for part_ref in part_refs[1:]:
+        tail = tail + part_ref[rows:, :].astype(f32)
     lines = tail[:owners] + tail[owners : 2 * owners]
     for owner in range(owners):
         for j in range(local):
@@ -359,9 +396,9 @@
     grad_gates = gg_all[...]
     mean = jnp.sum(gates * grad_gates, 0, keepdims=True)
     glog = (gates * (grad_gates - mean)).astype(bf16)
-    grad = part_ref[0, :rows, :].astype(f32)
-    for owner in range(1, owners):
-        grad = grad + part_ref[owner, :rows, :].astype(f32)
+    grad = part_refs[0][:rows, :].astype(f32)
+    for part_ref in part_refs[1:]:
+        grad = grad + part_ref[:rows, :].astype(f32)
     grad = grad + mm(glog, wr_ref[...], ((0,), (0,)))
     grouter = mm(glog, pack_ref[:rows, :])
     residual = res_ref[...]
@@ -375,8 +412,11 @@
     gmix[...] = mm(branch, wo_ref[...], ((1,), (1,))).astype(bf16)
     gin_ref[...] = gres
     gq[...] = branch
-    col = wq_ref.shape[1] + wk_ref.shape[1] + wv_ref.shape[1]
-    weight_gradient(mixed_ref, gq, col)
+    one, two = (keep_one, send_one), (keep_two, send_two)
+    weight_gradient(mixed_ref, gq, one, 0)
+    rest = LANES - 1 - grouter.shape[0]
+    acc[:, :LANES] = jnp.concatenate([grouter, ggain_two, jnp.zeros((rest, width), f32)], 0).T
+    put(one, width, LANES)
     low = low_lanes(rows)
     allowed = allowed_keys(rows, len_ref[0])
     held = None
@@ -402,9 +442,10 @@
             both = slice((h // 2) * PAIR, (h // 2 + 1) * PAIR)
             gk[:, both] = jnp.where(low, held[0], gkey).astype(bf16)
             gv[:, both] = jnp.where(low, held[1], gvalue).astype(bf16)
-    weight_gradient(n1_ref, gq, 0)
-    weight_gradient(n1_ref, gk, wq_ref.shape[1])
-    weight_gradient(n1_ref, gv, wq_ref.shape[1] + wk_ref.shape[1])
+    col = 0
+    for right in (gq, gk, gv):
+        weight_gradient(n1_ref, right, two, col)
+        col += right.shape[1]
     grad = mm(gq[...], wq_ref[...], ((1,), (1,)))
     grad = grad + mm(gk[...], wk_ref[...], ((1,), (1,)))
     grad = grad + mm(gv[...], wv_ref[...], ((1,), (1,)))
@@ -415,11 +456,8 @@
     gin_ref[...] = gin_ref[...] + inverse * scaled - x * inverse**3 * jnp.mean(
         scaled * x, -1, keepdims=True
     )
-    small = jnp.concatenate(
-        [grouter, ggain_one, ggain_two, jnp.zeros((LANES - 2 - grouter.shape[0], width), f32)], 0
-    )
-    acc[:, :LANES] = small.T
-    put(col + width, LANES)
+    acc[:, :LANES] = jnp.concatenate([ggain_one, jnp.zeros((LANES - 1, width), f32)], 0).T
+    put(two, col, LANES)
 
 
 def on_device(
@@ -462,7 +500,7 @@
         down = lax.ppermute(after, "expert", [(1, 0), (2, 1)])
         return [x, before, jnp.where(z >= 2, up, down), after]
 
-    def halve(keep, recv, stage, name, deps=()):
+    def halve(keep, recv, stage, name, deps=(), us=4):
         pieces, *rest = keep.shape
         half = pieces // 2
         tile = rest[0] // 2
@@ -477,25 +515,16 @@
         there = pl.BlockSpec(block, lambda i, t, which: (which[1, i], t, 0))
         made = pl.BlockSpec(block, lambda i, t, which: (i, t, 0))
         return call(
-            halve_kernel, [((half, *rest), f32), ((half, *rest), bf16)],
+            halve_kernel, [((half, *rest), bf16), ((half, *rest), bf16), TOKEN],
             jnp.stack([stay, go]), keep, recv, keep, recv,
-            prefetch=1, grid=(half, 2), specs=[here, here, there, there], out_specs=[made, made], deps=deps, vmem=16, name=name,
+            prefetch=1, grid=(half, 2), specs=[here, here, there, there], out_specs=[made, made, VMEM], deps=deps, vmem=16, us=us, name=name,
         )
-
-    def last(keep, recv, name, deps=()):
-        _, rows, cols = keep.shape
-        spec = pl.BlockSpec((1, rows // 2, cols), lambda t: (0, t, 0))
-        (made,) = call(
-            last_kernel, [(keep.shape, bf16)], keep, recv,
-            grid=(2,), specs=[spec, spec], out_specs=[spec], deps=deps, vmem=16, name=name,
-        )
-        return made
 
     def behind(arrays, deps, name):
         shapes = [(a.shape, a.dtype) for a in arrays]
         return call(
             nothing_kernel, shapes, *arrays, specs=[ANY] * len(arrays), out_specs=[ANY] * len(arrays), deps=deps,
-            alias={i: i for i in range(len(arrays))}, us=1, name=name,
+            alias={i: i for i in range(len(arrays))}, us=0, name=name,
         )
 
     cot_got = near(cotangent)
@@ -541,59 +570,72 @@
         scratch=[pltpu.VMEM((places, 1), f32)], us=17, name="expert_forward",
     )
 
-    grad_sums, grow, dots = call(
-        functools.partial(expert_backward, local, capacity, owners),
-        [
-            ((groups, local * piece, width), bf16),
-            ((local, places, width), bf16),
-            ((local, owners, seq), f32),
-        ],
-        ids, *packs, *cots, sent, hidden, slope, silu, expert_in, expert_out,
-        grid=(local,),
-        specs=[SMEM] + [VMEM] * (2 * owners) + [rows_of(width), rows_of(half), rows_of(half), rows_of(half)] + weights(0),
-        out_specs=[
-            pl.BlockSpec((groups, piece, width), lambda i: (0, i, 0)),
-            rows_of(width),
-            pl.BlockSpec((1, owners, seq), lambda i: (i, 0, 0)),
-        ],
-        scratch=[
-            pltpu.VMEM((places, width), bf16),
-            pltpu.VMEM((places, 1), f32),
-            pltpu.VMEM((places, width), bf16),
-            pltpu.VMEM((places, 2 * half), bf16),
-        ],
-        us=36, name="expert_backward",
-    )
-    mine = lax.psum_scatter(grad_sums, "group", scatter_dimension=0, tiled=False)
-
-    def combine(rows, dots, deps, name):
-        tail = -(-2 * owners // 16) * 16 if dots else 0
-        (made,) = call(
+    tail = -(-2 * owners // 16) * 16
+
+    def backward(first, count, split, deps=()):
+        def of(n):
+            return pl.BlockSpec((1, places, n), lambda i: (first + i, 0, 0))
+
+        if split:
+            sums = [((groups // 2, count * piece, width), bf16)] * 2
+            sum_specs = [pl.BlockSpec((groups // 2, piece, width), lambda i: (0, i, 0))] * 2
+        else:
+            sums = [((groups, count * piece, width), bf16)]
+            sum_specs = [pl.BlockSpec((groups, piece, width), lambda i: (0, i, 0))]
+        return call(
+            functools.partial(expert_backward, first, split, local, capacity, owners),
+            sums + [((count, places, width), bf16), ((count, owners, seq), f32)],
+            ids, *packs, *cots, sent, hidden, slope, silu, expert_in, expert_out,
+            grid=(count,),
+            specs=[SMEM] + [VMEM] * (2 * owners) + [of(width), of(half), of(half), of(half)] + weights(first),
+            out_specs=sum_specs + [rows_of(width), pl.BlockSpec((1, owners, seq), lambda i: (i, 0, 0))],
+            scratch=[
+                pltpu.VMEM((places, width), bf16),
+                pltpu.VMEM((places, 1), f32),
+                pltpu.VMEM((places, width), bf16),
+                pltpu.VMEM((places, 2 * half), bf16),
+            ],
+            deps=deps, us=8 * count, name=f"expert_backward{first}",
+        )
+
+    def combine(rows, dots, deps, name, us=8):
+        outs = [((seq + tail, width), bf16)] * owners if dots else [((owners, seq, width), bf16)]
+        return call(
             functools.partial(combine_kernel, local, capacity, owners, (len(rows), len(dots))),
-            [((owners, seq + tail, width), bf16)], ids, *packs, *rows, *dots, grid=(owners,), prefetch=1,
-            specs=[VMEM] * owners
-            + [pl.BlockSpec((r.shape[0], capacity, width), lambda d, ids: (0, d, 0)) for r in rows]
+            outs, ids, *packs, *rows, *dots, grid=(owners,),
+            specs=[SMEM] + [VMEM] * owners
+            + [pl.BlockSpec((r.shape[0], capacity, width), lambda d: (0, d, 0)) for r in rows]
             + [VMEM] * len(dots),
-            out_specs=[pl.BlockSpec((1, seq + tail, width), lambda d, ids: (lax.rem(ids[0] + owners - d, owners), 0, 0))],
             scratch=[pltpu.VMEM((owners, seq, LANES), jnp.int32)],
-            deps=deps, us=5, name=name,
+            deps=deps, us=us, name=name,
         )
-        return made
+
+    sums, *grads = backward(0, local, False)
+    mine = lax.psum_scatter(sums, "group", scatter_dimension=0, tiled=False)
+    parts = combine([grads[0]], [grads[1]], (), "combine_grad")
+    if owners == 4:
+        near_by = [
+            lax.ppermute(parts[2], "expert", [(2, 1), (3, 2)]),
+            lax.ppermute(parts[2], "expert", [(0, 1), (1, 2)]),
+        ]
+        joined = call(hop_kernel, [(parts[0].shape, bf16)] * 2, parts[1], parts[3], *near_by, us=2, name="hop")
+        grad_parts = [parts[0], ring(joined[0], -1), ring(joined[1], 1)]
+    else:
+        joined = parts
+        grad_parts = [parts[0]] + [ring(parts[d], -d) for d in range(1, owners)]
+    (owned,) = combine([wret], [], (joined[0],), "combine_out")
+    deps = (owned,)
 
     def to_owners(x):
         return lax.all_to_all(x, "expert", split_axis=0, concat_axis=0, tiled=True)
 
-    parts = combine([grow], [dots], (), "combine_grad")
-    grad_part = to_owners(parts)
-    owned = combine([wret], [], (parts,), "combine_out")
-
-    columns = 2 * width + key_matrix.shape[1] + value_matrix.shape[1] + LANES
-    grad_inputs, keep, send = call(
-        functools.partial(dense_backward, owners, local),
-        [((seq, width), f32)] + [((groups // 2, width // groups, columns), bf16)] * 2,
-        ids, lengths, grad_part, gates, inputs, cotangent, residual, n1, pack, q, kk, vv, lse, mixed,
+    sizes = ((width, LANES), (width, key_matrix.shape[1], value_matrix.shape[1], LANES))
+    grad_inputs, keep_one, send_one, keep_two, send_two = call(
+        functools.partial(dense_backward, len(grad_parts), owners, local),
+        [((seq, width), f32)] + [((groups // 2, width // groups, sum(cols)), bf16) for cols in sizes for _ in range(2)],
+        ids, lengths, *grad_parts, gates, inputs, cotangent, residual, n1, pack, q, kk, vv, lse, mixed,
         query_matrix, key_matrix, value_matrix, w_attn_out, router, gain_one, gain_two,
-        smem=2, deps=(owned,), us=18, name="dense_backward",
+        smem=2, deps=deps, us=18, name="dense_backward",
         scratch=[
             pltpu.VMEM((experts, seq), f32),
             pltpu.VMEM((seq, width), bf16),
@@ -603,59 +645,79 @@
             pltpu.VMEM((width, width), f32),
         ],
     )
-    recv = swap_cores(send)
-    (owned,) = behind([owned], (send,), "returned_go")
-    out_parts = to_owners(owned)
-    deps = (owned,)
-    for stage in range(steps):
-        keep, send = halve(keep, recv, stage, f"dense_halve{stage}", deps)
-        recv = swap(send, stage)
-        deps = (send,)
-        if stage == 0:
-            (mine,) = behind([mine], deps, "gather_go")
-            gathered = lax.all_gather(mine, "group", axis=0, tiled=False)
-            deps = (mine,)
-    spec = pl.BlockSpec((seq // 4, width), lambda t: (t, 0))
-    (output,) = call(
-        add_kernel, [((seq, width), f32)], residual, out_parts, grid=(4,),
-        specs=[spec, pl.BlockSpec((owners, seq // 4, width), lambda t: (0, t, 0))], out_specs=[spec],
-        deps=deps, us=3, name="output",
-    )
     rows = width // groups
     block = rows // owners
-    summed = last(keep, recv, "dense_last", (output,))
-    blocks = to_owners(summed.reshape(owners, block, columns))
-    (block_sum,) = call(sum_kernel, [((block, columns), bf16)], blocks, vmem=16, us=2, name="dense_sum")
-    shares = [block_sum] + [ring(block_sum, d) for d in range(1, owners)]
-    full = call(
+    recv_one, recv_two = swap_cores(send_one), swap_cores(send_two)
+    (owned,) = behind([owned], (send_one,), "returned_go")
+    out_parts = to_owners(owned)
+    keep_one, send_one, token = halve(keep_one, recv_one, 0, "one_halve0", (owned,))
+    recv_one = swap(send_one, 0)
+    keep_two, send_two, token = halve(keep_two, recv_two, 0, "two_halve0", (token,))
+    recv_two = swap(send_two, 0)
+    (mine,) = behind([mine], (recv_one, token), "gather_go")
+    gathered = lax.all_gather(mine, "group", axis=0, tiled=False)
+    token = mine
+    def spread(keep, recv, name, deps):
+        cols = keep.shape[2]
+        return call(
+            functools.partial(spread_kernel, owners), [((block, cols), bf16)] * owners + [TOKEN], ids, keep, recv,
+            smem=1, deps=deps, vmem=16, us=2, name=name, scratch=[pltpu.VMEM((owners, block, cols), f32)],
+        )
+
+    def total(blocks, name, deps):
+        (made,) = call(sum_kernel, [(blocks[0].shape, bf16)], *blocks, deps=deps, vmem=16, us=2, name=name)
+        return [made] + [ring(made, d) for d in range(1, owners)]
+
+    def finish(shares, cols, name, deps):
+        return call(
+            functools.partial(finish_kernel, owners), [((rows, c), f32) for c in cols],
+            ids, *shares, smem=1, deps=deps, vmem=16, us=2, name=name,
+            scratch=[pltpu.VMEM((owners, block, sum(cols)), f32)],
+        )
+
+    for stage in range(1, steps):
+        keep_one, send_one, token = halve(keep_one, recv_one, stage, f"one_halve{stage}", (token,))
+        recv_one = swap(send_one, stage)
+    *blocks_one, token = spread(keep_one, recv_one, "one_spread", (token,))
+    blocks_one = [blocks_one[0]] + [ring(blocks_one[d], d) for d in range(1, owners)]
+    for stage in range(1, steps):
+        keep_two, send_two, token = halve(keep_two, recv_two, stage, f"two_halve{stage}", (token,))
+        recv_two = swap(send_two, stage)
+    shares_one = total(blocks_one, "one_sum", (token,))
+    spec = pl.BlockSpec((seq // 4, width), lambda t: (t, 0))
+    output, token = call(
+        add_kernel, [((seq, width), f32), TOKEN], residual, out_parts, grid=(4,),
+        specs=[spec, pl.BlockSpec((owners, seq // 4, width), lambda t: (0, t, 0))], out_specs=[spec, VMEM],
+        deps=(shares_one[0],), us=4, name="output",
+    )
+    *one, small_one = finish(shares_one, sizes[0], "one_finish", (token,))
+    *blocks_two, token = spread(keep_two, recv_two, "two_spread", (small_one,))
+    blocks_two = [blocks_two[0]] + [ring(blocks_two[d], d) for d in range(1, owners)]
+
+    shares_two = total(blocks_two, "two_sum", (token,))
+    token = shares_two[0]
+    *full, token = call(
         widen_kernel,
-        [((local, width, 2 * half), f32), ((local, half, width), f32)],
+        [((local, width, 2 * half), f32), ((local, half, width), f32), TOKEN],
         gathered,
         grid=(groups,),
         specs=[pl.BlockSpec((1, local * piece, width), lambda i: (i, 0, 0))],
         out_specs=[
             pl.BlockSpec((local, width // groups, 2 * half), lambda i: (0, i, 0)),
             pl.BlockSpec((local, half // groups, width), lambda i: (0, i, 0)),
+            VMEM,
         ],
-        deps=(block_sum,), us=12, name="widen",
-    )
-    outs = call(
-        functools.partial(finish_kernel, owners),
-        [((rows, c), f32) for c in (width, key_matrix.shape[1], value_matrix.shape[1], width, LANES)],
-        ids, *shares, smem=1, deps=(full[1],), vmem=16, us=3, name="finish",
-        scratch=[pltpu.VMEM((owners, block, columns), f32)],
-    )
-    small = outs[4]
+        deps=(token,), us=12, name="widen",
+    )
+    *two, small_two = finish(shares_two, sizes[1], "two_finish", (token,))
     return (
         output,
         grad_inputs,
-        small[:, experts],
-        outs[0],
-        outs[1],
-        outs[2],
-        outs[3],
-        small[:, experts + 1],
-        small[:, :experts],
+        small_two[:, 0],
+        *two,
+        *one,
+        small_one[:, experts],
+        small_one[:, :experts],
         *full,
     )
 

time: 359 us -> 344 us (0.958)
  starting transfers between devices: 28.4 us -> 53.8 us
  blocking collectives: 23.5 us -> 0 us
  waiting for transfers between devices: 161 us -> 142 us
  Pallas kernels: 113 us -> 117 us
    all_to_all x2 -> x1, waiting for transfers between devices: 44.8 us -> 0.01 us  [to_owners(): return lax.all_to_all(x, 'expert', split_axis=0, concat_axis=0, tiled=True)]
    ppermute x7 -> x18, waiting for transfers between devices: 36.6 us -> 70.9 us  [ring(): lax.ppermute(x, 'expert', [(i, (i + d) % owners) for i in range(owners)])]
    all_to_all x1 -> x0, blocking collectives: 23.5 us -> none  [to_owners(): return lax.all_to_all(x, 'expert', split_axis=0, concat_axis=0, tiled=True)]
    ppermute x7 -> x18, starting transfers between devices: 12.9 us -> 32.1 us  [ring(): lax.ppermute(x, 'expert', [(i, (i + d) % owners) for i in range(owners)])]
    ppermute x2 -> x4, waiting for transfers between devices: 57.9 us -> 40.2 us  [swap(): lax.ppermute(x, 'group', [(i, i ^ 1 << (steps - stage if i % 2 else 1 + s...]
    ppermute x0 -> x2, waiting for transfers between devices: none -> 10.5 us  [the longest x1 10.5 us: on_device(): lax.ppermute(parts[2], 'expert', [(0, 1), (1, 2)])]
    ppermute x0 -> x2, starting transfers between devices: none -> 6.15 us  [the longest x1 5.47 us: on_device(): lax.ppermute(parts[2], 'expert', [(0, 1), (1, 2)])]
    pallas_call x17 -> x23, Pallas kernels: 113 us -> 117 us  [call(): pl.pallas_call(body, out_shape=outs, compiler_params=pltpu.CompilerParams...]
  transfers between devices with their start and end apart: 18 -> 33, of which waited for: 11 -> 17; matrix products, arithmetic and copies ran while one was open for 0% -> 1% of each run, Pallas kernels for 23% -> 25%
where the time goes in v3:
time: 344 us
  waiting for transfers between devices  142 us (41%)
  Pallas kernels  117 us (34%)
  starting transfers between devices  53.8 us (16%)
  between operations  15 us (4%)
  local copies, waits for them, and re-layouts  13 us (4%)
    pallas_call x23, Pallas kernels, call(): pl.pallas_call(body, out_shape=outs, compiler_params=pltpu.CompilerParams...  117 us
    ppermute x18, waiting for transfers between devices, ring(): lax.ppermute(x, 'expert', [(i, (i + d) % owners) for i in range(owners)])  70.9 us
    ppermute x4, waiting for transfers between devices, swap(): lax.ppermute(x, 'group', [(i, i ^ 1 << (steps - stage if i % 2 else 1 + s...  40.2 us
    ppermute x18, starting transfers between devices, ring(): lax.ppermute(x, 'expert', [(i, (i + d) % owners) for i in range(owners)])  32.1 us
    ppermute x2, waiting for transfers between devices, far(): down = lax.ppermute(after, 'expert', [(1, 0), (2, 1)])  14.7 us
    unnamed x53, local copies, waits for them, and re-layouts  11.7 us
    ppermute x1, waiting for transfers between devices, on_device(): lax.ppermute(parts[2], 'expert', [(0, 1), (1, 2)])  10.5 us
  transfers between devices with their start and end apart: 33, of which 17 were waited for; matrix products, arithmetic and copies ran while one was open for 1% of the time, Pallas kernels for 25%

profile of v3, /device:TPU:0, one launch (start us, length us, event | category | flops | bytes accessed | tf_op | source)
XLA Modules:
  0.0 343.6 jit_solution(10430191790858443373)
XLA Ops:
  7.2 3.1 collective-permute-start
  10.3 2.1 collective-permute-start.1
  13.0 8.5 %dense_forward.1 = (bf16[256,1024]{1,0:T(8,128)(2,1)}, bf16[256,1024]{1,0:T(8,128)(2,1)}, bf16[256,1024]{1,0:T(8,128)(2,1)}, bf16[256,1024]{1,0:T(8,128)(2,1)}, ...) custom-call(s32[1]{0:T(128)S(6)} %copy.37.refs_0_.refs_1_, ...), custom_call_target="tpu_custom_call" | custom-call | bytes 32400000 | tf_op jit(solution)/shard_map/dense_forward/pallas_call | solution.py:52
  21.6 3.8 %collective-permute-done.refs_1_.refs_0_ = bf16[256,1024]{1,0:T(8,128)(2,1)S(1)} collective-permute-done((bf16[256,1024]{1,0:T(8,128)(2,1)}, bf16[256,1024]{1,0:T(8,128)(2,1)S(1)}, u32[]{:S(2)}, u32[]{:S(2)}) %collective-permute-start) | collective-permute-done | bytes 524320 | tf_op jit(solution)/shard_map/ppermute | solution.py:482
  25.3 9.8 %collective-permute-done.1.refs_2_.refs_1_ = bf16[256,1024]{1,0:T(8,128)(2,1)S(1)} collective-permute-done((bf16[256,1024]{1,0:T(8,128)(2,1)}, bf16[256,1024]{1,0:T(8,128)(2,1)S(1)}, u32[]{:S(2)}, u32[]{:S(2)}) %collective-permute-start.1) | collective-permute-done | bytes 524320 | tf_op jit(solution)/shard_map/ppermute | solution.py:482
  37.1 2.7 collective-permute-start.4
  39.8 13.7 %collective-permute-done.2.refs_2_ = bf16[272,1024]{1,0:T(8,128)(2,1)S(1)} collective-permute-done((bf16[272,1024]{1,0:T(8,128)(2,1)}, bf16[272,1024]{1,0:T(8,128)(2,1)S(1)}, u32[]{:S(2)}, u32[]{:S(2)}) %collective-permute-start.2) | collective-permute-done | bytes 557088 | tf_op jit(solution)/shard_map/ppermute | solution.py:482
  54.2 9.3 %collective-permute-done.4.refs_4_ = bf16[272,1024]{1,0:T(8,128)(2,1)S(1)} collective-permute-done((bf16[272,1024]{1,0:T(8,128)(2,1)}, bf16[272,1024]{1,0:T(8,128)(2,1)S(1)}, u32[]{:S(2)}, u32[]{:S(2)}) %collective-permute-start.4) | collective-permute-done | bytes 557088 | tf_op jit(solution)/shard_map/ppermute | solution.py:482
  63.5 1.3 collective-permute-start.5
  64.8 14.7 %collective-permute-done.5 = bf16[272,1024]{1,0:T(8,128)(2,1)S(1)} collective-permute-done((bf16[272,1024]{1,0:T(8,128)(2,1)S(1)}, bf16[272,1024]{1,0:T(8,128)(2,1)S(1)}, u32[]{:S(2)}, u32[]{:S(2)}) %collective-permute-start.5) | collective-permute-done | bytes 557088 | tf_op jit(solution)/shard_map/ppermute | solution.py:500
  81.1 1.5 collective-permute-start.7
  83.3 17.0 %expert_forward.1 = (bf16[4,640,1024]{2,1,0:T(8,128)(2,1)}, bf16[4,640,512]{2,1,0:T(8,128)(2,1)}, f32[4,640,512]{2,1,0:T(8,128)}, f32[4,640,512]{2,1,0:T(8,128)}, bf16[4,640,1024]{2,1,0:T(8,128)(2,1)}) custom-call(s32[3]{0:T(128)} %pad_add_fusion.2.refs_0_, bf16[272,1024]{1,0:T(8,128)(2,1)} %tokens_go.1.refs_1_.refs_10_, bf16[272,1024]{1,0:T(8,128)(2,1)} %copy-done.18, ...), custom_call_target="tpu_custom_call" | custom-call | bytes 61200000 | tf_op jit(solution)/shard_map/expert_forward/pallas_call | solution.py:52
  101.2 28.6 %expert_backward0.1 = (bf16[8,768,1024]{2,1,0:T(8,128)(2,1)}, bf16[4,640,1024]{2,1,0:T(8,128)(2,1)}, f32[4,4,256]{2,1,0:T(4,128)}) custom-call(s32[3]{0:T(128)} %pad_add_fusion.2.refs_0_, bf16[272,1024]{1,0:T(8,128)(2,1)} %tokens_go.1.refs_1_.refs_10_, bf16[272,1024]{1,0:T(8,128)(2,1)} %copy-done.18, bf16[272,1024]{1,0:T(8,128)(2,1)} %broadcast_select_fusion.refs_3_.refs_2_, ...), custom_call_target="tpu_custom_call" | custom-call | bytes 115200000 | tf_op jit(solution)/shard_map/expert_backward0/pallas_call | solution.py:52
  129.9 7.8 %combine_grad.1 = (bf16[272,1024]{1,0:T(8,128)(2,1)}, bf16[272,1024]{1,0:T(8,128)(2,1)}, bf16[272,1024]{1,0:T(8,128)(2,1)}, bf16[272,1024]{1,0:T(8,128)(2,1)}) custom-call(s32[3]{0:T(128)} %pad_add_fusion.2.refs_0_, bf16[272,1024]{1,0:T(8,128)(2,1)} %tokens_go.1.refs_1_.refs_10_, bf16[272,1024]{1,0:T(8,128)(2,1)} %copy-done.18, ...), custom_call_target="tpu_custom_call" | custom-call | bytes 28800000 | tf_op jit(solution)/shard_map/combine_grad/pallas_call | solution.py:52
  138.4 5.5 %collective-permute-start.9 = (bf16[272,1024]{1,0:T(8,128)(2,1)}, bf16[272,1024]{1,0:T(8,128)(2,1)S(1)}, u32[]{:S(2)}, u32[]{:S(2)}) collective-permute-start(bf16[272,1024]{1,0:T(8,128)(2,1)} %get-tuple-element.87), channel_id=1, source_target_pairs={{0,1},{1,2},{4,5},{5,6},{8,9},{9,10},{12,13},{13,14},{16,17},{17,1... | collective-permute-start | bytes 1671176 | tf_op jit(solution)/shard_map/ppermute | solution.py:619
  143.9 10.5 %collective-permute-done.9.refs_3_ = bf16[272,1024]{1,0:T(8,128)(2,1)S(1)} collective-permute-done((bf16[272,1024]{1,0:T(8,128)(2,1)}, bf16[272,1024]{1,0:T(8,128)(2,1)S(1)}, u32[]{:S(2)}, u32[]{:S(2)}) %collective-permute-start.9) | collective-permute-done | bytes 557088 | tf_op jit(solution)/shard_map/ppermute | solution.py:619
  155.2 2.7 hop.1
  158.1 2.2 collective-permute-start.11
  160.3 7.5 %combine_out.1.refs_23_.refs_0_ = bf16[4,256,1024]{2,1,0:T(8,128)(2,1)} custom-call(s32[3]{0:T(128)} %pad_add_fusion.2.refs_0_, bf16[272,1024]{1,0:T(8,128)(2,1)} %tokens_go.1.refs_1_.refs_10_, bf16[272,1024]{1,0:T(8,128)(2,1)} %copy-done.18, bf16[272,1024]{1,0:T(8,128)(2,1)} %broadcast_select_fusion.refs_3_.refs_2_, bf16[272,1024]{1,0:T(8,128)(2,1)} %copy-done.19, ...), custom_call_target="tpu_custom_call" | custom-call | bytes 28800000 | tf_op jit(solution)/shard_map/combine_out/pallas_call | solution.py:52
  167.9 4.1 %collective-permute-done.10.refs_3_ = bf16[272,1024]{1,0:T(8,128)(2,1)S(1)} collective-permute-done((bf16[272,1024]{1,0:T(8,128)(2,1)}, bf16[272,1024]{1,0:T(8,128)(2,1)S(1)}, u32[]{:S(2)}, u32[]{:S(2)}) %collective-permute-start.10) | collective-permute-done | bytes 557088 | tf_op jit(solution)/shard_map/ppermute | solution.py:482
  171.9 13.3 %collective-permute-done.11.refs_4_ = bf16[272,1024]{1,0:T(8,128)(2,1)S(1)} collective-permute-done((bf16[272,1024]{1,0:T(8,128)(2,1)}, bf16[272,1024]{1,0:T(8,128)(2,1)S(1)}, u32[]{:S(2)}, u32[]{:S(2)}) %collective-permute-start.11) | collective-permute-done | bytes 557088 | tf_op jit(solution)/shard_map/ppermute | solution.py:482
  186.0 18.5 %dense_backward.1 = (f32[256,1024]{1,0:T(8,128)}, bf16[4,128,1152]{2,1,0:T(8,128)(2,1)}, bf16[4,128,1152]{2,1,0:T(8,128)(2,1)}, bf16[4,128,2176]{2,1,0:T(8,128)(2,1)}, bf16[4,128,2176]{2,1,0:T(8,128)(2,1)}) custom-call(s32[3]{0:T(128)} %pad_add_fusion.2.refs_0_, s32[1]{0:T(128)S(6)} %copy.37.refs_0_.refs_1_, bf16[272,1024]{1,0:T(8,128)(2,1)} %get-tuple-element.89.refs_2_, ...), custom_call_target="tpu_custom_call" | custom-call | bytes 64800000 | tf_op jit(solution)/shard_map/dense_backward/pallas_call | solution.py:52
  205.1 5.7 %collective-permute-done.12.refs_2_.refs_4_ = bf16[4,128,1152]{2,1,0:T(8,128)(2,1)S(1)} collective-permute-done((bf16[4,128,1152]{2,1,0:T(8,128)(2,1)}, bf16[4,128,1152]{2,1,0:T(8,128)(2,1)S(1)}, u32[]{:S(2)}, u32[]{:S(2)}) %collective-permute-start.12) | collective-permute-done | bytes 1179680 | tf_op jit(solution)/shard_map/ppermute | solution.py:485
  210.8 1.2 one_halve0.1
  212.8 1.7 collective-permute-start.13
  218.3 9.1 %collective-permute-done.13.refs_1_.refs_2_.refs_4_ = bf16[2,128,1152]{2,1,0:T(8,128)(2,1)S(1)} collective-permute-done((bf16[2,128,1152]{2,1,0:T(8,128)(2,1)S(1)}, bf16[2,128,1152]{2,1,0:T(8,128)(2,1)S(1)}, u32[]{:S(2)}, u32[]{:S(2)}) %collective-permute-start.13) | collective-permute-done | bytes 589856 | tf_op jit(solution)/shard_map/ppermute | solution.py:488
  228.3 4.7 %all-to-all-start = ((bf16[4,256,1024]{2,1,0:T(8,128)(2,1)}), bf16[4,256,1024]{2,1,0:T(8,128)(2,1)}, u32[]{:S(2)}, u32[]{:S(2)}) async-start(bf16[4,256,1024]{2,1,0:T(8,128)(2,1)} %returned_go.1.refs_5_), calls=%async_computation | async-start | bytes 4194304 | tf_op jit(solution)/shard_map/all_to_all | solution.py:630
  235.7 1.3 collective-permute-start.15
  237.0 13.2 %collective-permute-done.15.refs_2_ = bf16[1,128,1152]{2,1,0:T(8,128)(2,1)S(1)} collective-permute-done((bf16[1,128,1152]{2,1,0:T(8,128)(2,1)S(1)}, bf16[1,128,1152]{2,1,0:T(8,128)(2,1)S(1)}, u32[]{:S(2)}, u32[]{:S(2)}) %collective-permute-start.15) | collective-permute-done | bytes 294944 | tf_op jit(solution)/shard_map/ppermute | solution.py:488
  250.8 17.9 %collective-permute-done.19.refs_2_.refs_4_ = bf16[2,128,2176]{2,1,0:T(8,128)(2,1)S(1)} collective-permute-done((bf16[2,128,2176]{2,1,0:T(8,128)(2,1)}, bf16[2,128,2176]{2,1,0:T(8,128)(2,1)S(1)}, u32[]{:S(2)}, u32[]{:S(2)}) %collective-permute-start.19) | collective-permute-done | bytes 1114144 | tf_op jit(solution)/shard_map/ppermute | solution.py:488
  269.6 2.3 collective-permute-start.20
  271.9 2.6 collective-permute-start.16
  274.6 2.5 collective-permute-start.17
  277.0 1.4 collective-permute-start.18
  279.0 8.2 %collective-permute-done.17.refs_2_ = bf16[32,1152]{1,0:T(8,128)(2,1)S(1)} collective-permute-done((bf16[32,1152]{1,0:T(8,128)(2,1)S(1)}, bf16[32,1152]{1,0:T(8,128)(2,1)S(1)}, u32[]{:S(2)}, u32[]{:S(2)}) %collective-permute-start.17) | collective-permute-done | bytes 73760 | tf_op jit(solution)/shard_map/ppermute | solution.py:482
  287.3 1.4 collective-permute-start.21
  288.7 1.5 collective-permute-start.22
  291.2 3.9 %output.1 = (f32[256,1024]{1,0:T(8,128)}, f32[8,128]{1,0:T(8,128)}) custom-call(f32[256,1024]{1,0:T(8,128)} %get-tuple-element.74.refs_8_.refs_0_, bf16[4,256,1024]{2,1,0:T(8,128)(2,1)} %all-to-all-done.refs_1_, bf16[32,1152]{1,0:T(8,128)(2,1)} %copy-done.11), custom_call_target="tpu_custom_call" | custom-call | bytes 14400000 | tf_op jit(solution)/shard_map/output/pallas_call | solution.py:52
  297.2 1.4 one_finish.1
  299.4 1.4 collective-permute-start.24
  300.8 1.7 collective-permute-start.25
  302.5 1.3 collective-permute-start.26
  303.8 4.2 %collective-permute-done.24.refs_1_ = bf16[32,2176]{1,0:T(8,128)(2,1)S(1)} collective-permute-done((bf16[32,2176]{1,0:T(8,128)(2,1)S(1)}, bf16[32,2176]{1,0:T(8,128)(2,1)S(1)}, u32[]{:S(2)}, u32[]{:S(2)}) %collective-permute-start.24) | collective-permute-done | bytes 139296 | tf_op jit(solution)/shard_map/ppermute | solution.py:482
  307.9 3.3 collective-permute-done.25.refs_2_
  311.4 3.5 %collective-permute-start.27 = (bf16[32,2176]{1,0:T(8,128)(2,1)S(1)}, bf16[32,2176]{1,0:T(8,128)(2,1)S(1)}, u32[]{:S(2)}, u32[]{:S(2)}) collective-permute-start(bf16[32,2176]{1,0:T(8,128)(2,1)S(1)} %two_sum.1.refs_1_), channel_id=1, source_target_pairs={{0,1},{1,2},{2,3},{3,0},{4,5},{5,6},{6,7},{7,4},{8,9},{9,10},{10,1... | collective-permute-start | bytes 417800 | tf_op jit(solution)/shard_map/ppermute | solution.py:482
  316.0 1.3 collective-permute-start.29
  318.7 14.2 %widen.1 = (f32[4,1024,1024]{2,1,0:T(8,128)}, f32[4,512,1024]{2,1,0:T(8,128)}, f32[8,128]{1,0:T(8,128)}) custom-call(bf16[8,768,1024]{2,1,0:T(8,128)(2,1)} %bitcast.19, bf16[32,2176]{1,0:T(8,128)(2,1)} %copy-done.9), custom_call_target="tpu_custom_call" | custom-call | bytes 43200000 | tf_op jit(solution)/shard_map/widen/pallas_call | solution.py:52
  334.5 1.6 two_finish.1
  (104 shorter events, 27.9 us)
Async XLA Ops:
  7.2 220.2 %reduce-scatter.2.cloned.1.call-start = ((), (), s32[]{:S(2)}) async-start(), calls=%async_computation.2 | async-start | bytes 14155776 | tf_op jit(solution)/shard_map/reduce_scatter | solution.py:614
  7.2 18.1 %collective-permute-start = (bf16[256,1024]{1,0:T(8,128)(2,1)}, bf16[256,1024]{1,0:T(8,128)(2,1)S(1)}, u32[]{:S(2)}, u32[]{:S(2)}) collective-permute-start(bf16[256,1024]{1,0:T(8,128)(2,1)} %refs_7_.1), channel_id=1, source_target_pairs={{0,1},{1,2},{2,3},{3,0},{4,5},{5,6},{6,7},{7,4},{8,9},{9,10},{10,1... | collective-permute-start | bytes 1572872 | tf_op jit(solution)/shard_map/ppermute | solution.py:482
  10.3 24.8 %collective-permute-start.1 = (bf16[256,1024]{1,0:T(8,128)(2,1)}, bf16[256,1024]{1,0:T(8,128)(2,1)S(1)}, u32[]{:S(2)}, u32[]{:S(2)}) collective-permute-start(bf16[256,1024]{1,0:T(8,128)(2,1)} %refs_7_.1), channel_id=1, source_target_pairs={{0,3},{1,0},{2,1},{3,2},{4,7},{5,4},{6,5},{7,6},{8,11},{9,8},{10,9... | collective-permute-start | bytes 1572872 | tf_op jit(solution)/shard_map/ppermute | solution.py:482
  25.3 9.8 %copy-start.20 = (bf16[256,1024]{1,0:T(8,128)(2,1)}, bf16[256,1024]{1,0:T(8,128)(2,1)S(1)}, u32[]{:S(2)}) copy-start(bf16[256,1024]{1,0:T(8,128)(2,1)S(1)} %collective-permute-done.refs_1_.refs_0_) | copy-start | bytes 1572868
  36.0 17.6 %collective-permute-start.2 = (bf16[272,1024]{1,0:T(8,128)(2,1)}, bf16[272,1024]{1,0:T(8,128)(2,1)S(1)}, u32[]{:S(2)}, u32[]{:S(2)}) collective-permute-start(bf16[272,1024]{1,0:T(8,128)(2,1)} %tokens_go.1.refs_1_.refs_10_), channel_id=1, source_target_pairs={{0,1},{1,2},{2,3},{3,0},{4,5},{5,6},{6,7},{7,4},{8,9},{9,10},{10,1... | collective-permute-start | bytes 1671176 | tf_op jit(solution)/shard_map/ppermute | solution.py:482
  37.1 26.4 %collective-permute-start.4 = (bf16[272,1024]{1,0:T(8,128)(2,1)}, bf16[272,1024]{1,0:T(8,128)(2,1)S(1)}, u32[]{:S(2)}, u32[]{:S(2)}) collective-permute-start(bf16[272,1024]{1,0:T(8,128)(2,1)} %tokens_go.1.refs_1_.refs_10_), channel_id=1, source_target_pairs={{0,3},{1,0},{2,1},{3,2},{4,7},{5,4},{6,5},{7,6},{8,11},{9,8},{10,9... | collective-permute-start | bytes 1671176 | tf_op jit(solution)/shard_map/ppermute | solution.py:482
  53.5 29.8 %copy-start.18 = (bf16[272,1024]{1,0:T(8,128)(2,1)}, bf16[272,1024]{1,0:T(8,128)(2,1)S(1)}, u32[]{:S(2)}) copy-start(bf16[272,1024]{1,0:T(8,128)(2,1)S(1)} %collective-permute-done.2.refs_2_) | copy-start | bytes 1671172
  53.5 11.3 %collective-permute-start.3 = (bf16[272,1024]{1,0:T(8,128)(2,1)S(1)}, bf16[272,1024]{1,0:T(8,128)(2,1)S(1)}, u32[]{:S(2)}, u32[]{:S(2)}) collective-permute-start(bf16[272,1024]{1,0:T(8,128)(2,1)S(1)} %collective-permute-done.2.refs_2_), channel_id=1, source_target_pairs={{1,2},{2,3},{5,6},{6,7},{9,10},{10,11},{13,14},{14,15},{17,18},{18... | collective-permute-start | bytes 1671176 | tf_op jit(solution)/shard_map/ppermute | solution.py:499
  63.5 19.8 %copy-start.19 = (bf16[272,1024]{1,0:T(8,128)(2,1)}, bf16[272,1024]{1,0:T(8,128)(2,1)S(1)}, u32[]{:S(2)}) copy-start(bf16[272,1024]{1,0:T(8,128)(2,1)S(1)} %collective-permute-done.4.refs_4_) | copy-start | bytes 1671172
  63.5 16.0 %collective-permute-start.5 = (bf16[272,1024]{1,0:T(8,128)(2,1)S(1)}, bf16[272,1024]{1,0:T(8,128)(2,1)S(1)}, u32[]{:S(2)}, u32[]{:S(2)}) collective-permute-start(bf16[272,1024]{1,0:T(8,128)(2,1)S(1)} %collective-permute-done.4.refs_4_), channel_id=1, source_target_pairs={{1,0},{2,1},{5,4},{6,5},{9,8},{10,9},{13,12},{14,13},{17,16},{18,1... | collective-permute-start | bytes 1671176 | tf_op jit(solution)/shard_map/ppermute | solution.py:500
  80.4 19.9 %collective-permute-start.6 = (bf16[256,1024]{1,0:T(8,128)(2,1)}, bf16[256,1024]{1,0:T(8,128)(2,1)S(1)}, u32[]{:S(2)}, u32[]{:S(2)}) collective-permute-start(bf16[256,1024]{1,0:T(8,128)(2,1)} %get-tuple-element.77.refs_6_), channel_id=1, source_target_pairs={{1,2},{2,3},{5,6},{6,7},{9,10},{10,11},{13,14},{14,15},{17,18},{18... | collective-permute-start | bytes 1572872 | tf_op jit(solution)/shard_map/ppermute | solution.py:499
  81.1 19.2 %collective-permute-start.7 = (bf16[256,1024]{1,0:T(8,128)(2,1)}, bf16[256,1024]{1,0:T(8,128)(2,1)S(1)}, u32[]{:S(2)}, u32[]{:S(2)}) collective-permute-start(bf16[256,1024]{1,0:T(8,128)(2,1)} %get-tuple-element.78.refs_8_), channel_id=1, source_target_pairs={{1,0},{2,1},{5,4},{6,5},{9,8},{10,9},{13,12},{14,13},{17,16},{18,1... | collective-permute-start | bytes 1572872 | tf_op jit(solution)/shard_map/ppermute | solution.py:500
  129.8 188.8 %all-gather.3.cloned.1.call-start = ((), (), s32[]{:S(2)}) async-start(), calls=%async_computation.3 | async-start | bytes 14155776 | tf_op jit(solution)/shard_map/all_gather | solution.py:658
  137.7 6.2 %collective-permute-start.8 = (bf16[272,1024]{1,0:T(8,128)(2,1)}, bf16[272,1024]{1,0:T(8,128)(2,1)S(1)}, u32[]{:S(2)}, u32[]{:S(2)}) collective-permute-start(bf16[272,1024]{1,0:T(8,128)(2,1)} %get-tuple-element.87), channel_id=1, source_target_pairs={{2,1},{3,2},{6,5},{7,6},{10,9},{11,10},{14,13},{15,14},{18,17},{19... | collective-permute-start | bytes 1671176 | tf_op jit(solution)/shard_map/ppermute | solution.py:618
  138.4 16.0 %collective-permute-start.9 = (bf16[272,1024]{1,0:T(8,128)(2,1)}, bf16[272,1024]{1,0:T(8,128)(2,1)S(1)}, u32[]{:S(2)}, u32[]{:S(2)}) collective-permute-start(bf16[272,1024]{1,0:T(8,128)(2,1)} %get-tuple-element.87), channel_id=1, source_target_pairs={{0,1},{1,2},{4,5},{5,6},{8,9},{9,10},{12,13},{13,14},{16,17},{17,1... | collective-permute-start | bytes 1671176 | tf_op jit(solution)/shard_map/ppermute | solution.py:619
  143.9 10.5 %copy-start.24 = (bf16[272,1024]{1,0:T(8,128)(2,1)}, bf16[272,1024]{1,0:T(8,128)(2,1)S(1)}, u32[]{:S(2)}) copy-start(bf16[272,1024]{1,0:T(8,128)(2,1)S(1)} %collective-permute-done.8.refs_2_) | copy-start | bytes 1671172
  157.9 14.0 %collective-permute-start.10 = (bf16[272,1024]{1,0:T(8,128)(2,1)}, bf16[272,1024]{1,0:T(8,128)(2,1)S(1)}, u32[]{:S(2)}, u32[]{:S(2)}) collective-permute-start(bf16[272,1024]{1,0:T(8,128)(2,1)} %get-tuple-element.88.refs_6_), channel_id=1, source_target_pairs={{0,3},{1,0},{2,1},{3,2},{4,7},{5,4},{6,5},{7,6},{8,11},{9,8},{10,9... | collective-permute-start | bytes 1671176 | tf_op jit(solution)/shard_map/ppermute | solution.py:482
  158.1 27.1 %collective-permute-start.11 = (bf16[272,1024]{1,0:T(8,128)(2,1)}, bf16[272,1024]{1,0:T(8,128)(2,1)S(1)}, u32[]{:S(2)}, u32[]{:S(2)}) collective-permute-start(bf16[272,1024]{1,0:T(8,128)(2,1)} %get-tuple-element.90), channel_id=1, source_target_pairs={{0,1},{1,2},{2,3},{3,0},{4,5},{5,6},{6,7},{7,4},{8,9},{9,10},{10,1... | collective-permute-start | bytes 1671176 | tf_op jit(solution)/shard_map/ppermute | solution.py:482
  171.9 13.3 %copy-start.22 = (bf16[272,1024]{1,0:T(8,128)(2,1)}, bf16[272,1024]{1,0:T(8,128)(2,1)S(1)}, u32[]{:S(2)}) copy-start(bf16[272,1024]{1,0:T(8,128)(2,1)S(1)} %collective-permute-done.10.refs_3_) | copy-start | bytes 1671172
  204.6 10.0 %collective-permute-start.14 = (bf16[4,128,2176]{2,1,0:T(8,128)(2,1)}, bf16[4,128,2176]{2,1,0:T(8,128)(2,1)S(1)}, u32[]{:S(2)}, u32[]{:S(2)}) collective-permute-start(bf16[4,128,2176]{2,1,0:T(8,128)(2,1)} %get-tuple-element.104), channel_id=1, source_target_pairs={{0,4},{4,0},{8,12},{12,8},{16,20},{20,16},{24,28},{28,24},{1,5},{5... | collective-permute-start | bytes 6684680 | tf_op jit(solution)/shard_map/ppermute | solution.py:485
  204.6 6.2 %collective-permute-start.12 = (bf16[4,128,1152]{2,1,0:T(8,128)(2,1)}, bf16[4,128,1152]{2,1,0:T(8,128)(2,1)S(1)}, u32[]{:S(2)}, u32[]{:S(2)}) collective-permute-start(bf16[4,128,1152]{2,1,0:T(8,128)(2,1)} %get-tuple-element.98.refs_1_), channel_id=1, source_target_pairs={{0,4},{4,0},{8,12},{12,8},{16,20},{20,16},{24,28},{28,24},{1,5},{5... | collective-permute-start | bytes 3538952 | tf_op jit(solution)/shard_map/ppermute | solution.py:485
  205.1 5.7 %copy-start.4 = (bf16[4,128,1152]{2,1,0:T(8,128)(2,1)S(1)}, bf16[4,128,1152]{2,1,0:T(8,128)(2,1)}, u32[]{:S(2)}) copy-start(bf16[4,128,1152]{2,1,0:T(8,128)(2,1)} %get-tuple-element.99.refs_1_.refs_3_) | copy-start | bytes 3538948
  210.8 3.7 %copy-start.1 = (bf16[4,128,2176]{2,1,0:T(8,128)(2,1)S(1)}, bf16[4,128,2176]{2,1,0:T(8,128)(2,1)}, u32[]{:S(2)}) copy-start(bf16[4,128,2176]{2,1,0:T(8,128)(2,1)} %get-tuple-element.103.refs_1_.refs_3_) | copy-start | bytes 6684676
  212.8 14.6 %collective-permute-start.13 = (bf16[2,128,1152]{2,1,0:T(8,128)(2,1)S(1)}, bf16[2,128,1152]{2,1,0:T(8,128)(2,1)S(1)}, u32[]{:S(2)}, u32[]{:S(2)}) collective-permute-start(bf16[2,128,1152]{2,1,0:T(8,128)(2,1)S(1)} %get-tuple-element.101), channel_id=1, source_target_pairs={{0,8},{4,20},{8,0},{12,28},{16,24},{20,4},{24,16},{28,12},{1,9},{5... | collective-permute-start | bytes 1769480 | tf_op jit(solution)/shard_map/ppermute | solution.py:488
  217.3 1.0 copy-start.17
  228.3 5.6 %copy-start = (bf16[768,1024]{1,0:T(8,128)(2,1)S(1)}, bf16[768,1024]{1,0:T(8,128)(2,1)}, u32[]{:S(2)}) copy-start(bf16[768,1024]{1,0:T(8,128)(2,1)} %gather_go.1.refs_5_) | copy-start | bytes 4718596
  228.3 5.6 %copy-start.3 = (bf16[2,128,1152]{2,1,0:T(8,128)(2,1)S(1)}, bf16[2,128,1152]{2,1,0:T(8,128)(2,1)}, u32[]{:S(2)}) copy-start(bf16[2,128,1152]{2,1,0:T(8,128)(2,1)} %copy-done.2) | copy-start | bytes 1769476
  228.3 62.9 %all-to-all-start = ((bf16[4,256,1024]{2,1,0:T(8,128)(2,1)}), bf16[4,256,1024]{2,1,0:T(8,128)(2,1)}, u32[]{:S(2)}, u32[]{:S(2)}) async-start(bf16[4,256,1024]{2,1,0:T(8,128)(2,1)} %returned_go.1.refs_5_), calls=%async_computation | async-start | bytes 4194304 | tf_op jit(solution)/shard_map/all_to_all | solution.py:630
  233.0 17.1 %copy-start.13 = (s32[3]{0:T(128)S(1)}, s32[3]{0:T(128)}, u32[]{:S(2)}) copy-start(s32[3]{0:T(128)} %pad_add_fusion.2.refs_0_) | copy-start | bytes 40
  233.0 35.7 %collective-permute-start.19 = (bf16[2,128,2176]{2,1,0:T(8,128)(2,1)}, bf16[2,128,2176]{2,1,0:T(8,128)(2,1)S(1)}, u32[]{:S(2)}, u32[]{:S(2)}) collective-permute-start(bf16[2,128,2176]{2,1,0:T(8,128)(2,1)} %copy-done.17), channel_id=1, source_target_pairs={{0,8},{4,20},{8,0},{12,28},{16,24},{20,4},{24,16},{28,12},{1,9},{5... | collective-permute-start | bytes 3342344 | tf_op jit(solution)/shard_map/ppermute | solution.py:488
  233.9 1.1 copy-start.8
  235.0 33.8 %copy-start.6 = (bf16[2,128,2176]{2,1,0:T(8,128)(2,1)S(1)}, bf16[2,128,2176]{2,1,0:T(8,128)(2,1)}, u32[]{:S(2)}) copy-start(bf16[2,128,2176]{2,1,0:T(8,128)(2,1)} %copy-done.5) | copy-start | bytes 3342340
  235.7 14.5 %collective-permute-start.15 = (bf16[1,128,1152]{2,1,0:T(8,128)(2,1)S(1)}, bf16[1,128,1152]{2,1,0:T(8,128)(2,1)S(1)}, u32[]{:S(2)}, u32[]{:S(2)}) collective-permute-start(bf16[1,128,1152]{2,1,0:T(8,128)(2,1)S(1)} %get-tuple-element.108), channel_id=1, source_target_pairs={{0,16},{4,12},{8,24},{12,4},{16,0},{20,28},{24,8},{28,20},{1,17},{... | collective-permute-start | bytes 884744 | tf_op jit(solution)/shard_map/ppermute | solution.py:488
  269.6 29.0 %collective-permute-start.20 = (bf16[1,128,2176]{2,1,0:T(8,128)(2,1)S(1)}, bf16[1,128,2176]{2,1,0:T(8,128)(2,1)S(1)}, u32[]{:S(2)}, u32[]{:S(2)}) collective-permute-start(bf16[1,128,2176]{2,1,0:T(8,128)(2,1)S(1)} %get-tuple-element.121), channel_id=1, source_target_pairs={{0,16},{4,12},{8,24},{12,4},{16,0},{20,28},{24,8},{28,20},{1,17},{... | collective-permute-start | bytes 1671176 | tf_op jit(solution)/shard_map/ppermute | solution.py:488
  271.9 7.0 %collective-permute-start.16 = (bf16[32,1152]{1,0:T(8,128)(2,1)S(1)}, bf16[32,1152]{1,0:T(8,128)(2,1)S(1)}, u32[]{:S(2)}, u32[]{:S(2)}) collective-permute-start(bf16[32,1152]{1,0:T(8,128)(2,1)S(1)} %get-tuple-element.111), channel_id=1, source_target_pairs={{0,1},{1,2},{2,3},{3,0},{4,5},{5,6},{6,7},{7,4},{8,9},{9,10},{10,1... | collective-permute-start | bytes 221192 | tf_op jit(solution)/shard_map/ppermute | solution.py:482
  274.6 12.6 %collective-permute-start.17 = (bf16[32,1152]{1,0:T(8,128)(2,1)S(1)}, bf16[32,1152]{1,0:T(8,128)(2,1)S(1)}, u32[]{:S(2)}, u32[]{:S(2)}) collective-permute-start(bf16[32,1152]{1,0:T(8,128)(2,1)S(1)} %get-tuple-element.112), channel_id=1, source_target_pairs={{0,2},{1,3},{2,0},{3,1},{4,6},{5,7},{6,4},{7,5},{8,10},{9,11},{10,... | collective-permute-start | bytes 221192 | tf_op jit(solution)/shard_map/ppermute | solution.py:482
  277.0 10.2 %collective-permute-start.18 = (bf16[32,1152]{1,0:T(8,128)(2,1)S(1)}, bf16[32,1152]{1,0:T(8,128)(2,1)S(1)}, u32[]{:S(2)}, u32[]{:S(2)}) collective-permute-start(bf16[32,1152]{1,0:T(8,128)(2,1)S(1)} %get-tuple-element.113), channel_id=1, source_target_pairs={{0,3},{1,0},{2,1},{3,2},{4,7},{5,4},{6,5},{7,6},{8,11},{9,8},{10,9... | collective-permute-start | bytes 221192 | tf_op jit(solution)/shard_map/ppermute | solution.py:482
  287.3 3.9 %copy-start.11 = (bf16[32,1152]{1,0:T(8,128)(2,1)}, bf16[32,1152]{1,0:T(8,128)(2,1)S(1)}, u32[]{:S(2)}) copy-start(bf16[32,1152]{1,0:T(8,128)(2,1)S(1)} %one_sum.1.refs_2_.refs_1_) | copy-start | bytes 221188
  287.3 7.7 %collective-permute-start.21 = (bf16[32,1152]{1,0:T(8,128)(2,1)S(1)}, bf16[32,1152]{1,0:T(8,128)(2,1)S(1)}, u32[]{:S(2)}, u32[]{:S(2)}) collective-permute-start(bf16[32,1152]{1,0:T(8,128)(2,1)S(1)} %one_sum.1.refs_2_.refs_1_), channel_id=1, source_target_pairs={{0,1},{1,2},{2,3},{3,0},{4,5},{5,6},{6,7},{7,4},{8,9},{9,10},{10,1... | collective-permute-start | bytes 221192 | tf_op jit(solution)/shard_map/ppermute | solution.py:482
  288.7 7.0 %collective-permute-start.22 = (bf16[32,1152]{1,0:T(8,128)(2,1)S(1)}, bf16[32,1152]{1,0:T(8,128)(2,1)S(1)}, u32[]{:S(2)}, u32[]{:S(2)}) collective-permute-start(bf16[32,1152]{1,0:T(8,128)(2,1)S(1)} %one_sum.1.refs_2_.refs_1_), channel_id=1, source_target_pairs={{0,2},{1,3},{2,0},{3,1},{4,6},{5,7},{6,4},{7,5},{8,10},{9,11},{10,... | collective-permute-start | bytes 221192 | tf_op jit(solution)/shard_map/ppermute | solution.py:482
  290.1 5.5 %collective-permute-start.23 = (bf16[32,1152]{1,0:T(8,128)(2,1)S(1)}, bf16[32,1152]{1,0:T(8,128)(2,1)S(1)}, u32[]{:S(2)}, u32[]{:S(2)}) collective-permute-start(bf16[32,1152]{1,0:T(8,128)(2,1)S(1)} %one_sum.1.refs_2_.refs_1_), channel_id=1, source_target_pairs={{0,3},{1,0},{2,1},{3,2},{4,7},{5,4},{6,5},{7,6},{8,11},{9,8},{10,9... | collective-permute-start | bytes 221192 | tf_op jit(solution)/shard_map/ppermute | solution.py:482
  299.4 8.5 %collective-permute-start.24 = (bf16[32,2176]{1,0:T(8,128)(2,1)S(1)}, bf16[32,2176]{1,0:T(8,128)(2,1)S(1)}, u32[]{:S(2)}, u32[]{:S(2)}) collective-permute-start(bf16[32,2176]{1,0:T(8,128)(2,1)S(1)} %get-tuple-element.125), channel_id=1, source_target_pairs={{0,1},{1,2},{2,3},{3,0},{4,5},{5,6},{6,7},{7,4},{8,9},{9,10},{10,1... | collective-permute-start | bytes 417800 | tf_op jit(solution)/shard_map/ppermute | solution.py:482
  300.8 10.5 %collective-permute-start.25 = (bf16[32,2176]{1,0:T(8,128)(2,1)S(1)}, bf16[32,2176]{1,0:T(8,128)(2,1)S(1)}, u32[]{:S(2)}, u32[]{:S(2)}) collective-permute-start(bf16[32,2176]{1,0:T(8,128)(2,1)S(1)} %get-tuple-element.126), channel_id=1, source_target_pairs={{0,2},{1,3},{2,0},{3,1},{4,6},{5,7},{6,4},{7,5},{8,10},{9,11},{10,... | collective-permute-start | bytes 417800 | tf_op jit(solution)/shard_map/ppermute | solution.py:482
  302.5 8.8 %collective-permute-start.26 = (bf16[32,2176]{1,0:T(8,128)(2,1)S(1)}, bf16[32,2176]{1,0:T(8,128)(2,1)S(1)}, u32[]{:S(2)}, u32[]{:S(2)}) collective-permute-start(bf16[32,2176]{1,0:T(8,128)(2,1)S(1)} %get-tuple-element.127), channel_id=1, source_target_pairs={{0,3},{1,0},{2,1},{3,2},{4,7},{5,4},{6,5},{7,6},{8,11},{9,8},{10,9... | collective-permute-start | bytes 417800 | tf_op jit(solution)/shard_map/ppermute | solution.py:482
  311.4 7.3 %copy-start.9 = (bf16[32,2176]{1,0:T(8,128)(2,1)}, bf16[32,2176]{1,0:T(8,128)(2,1)S(1)}, u32[]{:S(2)}) copy-start(bf16[32,2176]{1,0:T(8,128)(2,1)S(1)} %two_sum.1.refs_1_) | copy-start | bytes 417796
  311.4 21.5 %collective-permute-start.27 = (bf16[32,2176]{1,0:T(8,128)(2,1)S(1)}, bf16[32,2176]{1,0:T(8,128)(2,1)S(1)}, u32[]{:S(2)}, u32[]{:S(2)}) collective-permute-start(bf16[32,2176]{1,0:T(8,128)(2,1)S(1)} %two_sum.1.refs_1_), channel_id=1, source_target_pairs={{0,1},{1,2},{2,3},{3,0},{4,5},{5,6},{6,7},{7,4},{8,9},{9,10},{10,1... | collective-permute-start | bytes 417800 | tf_op jit(solution)/shard_map/ppermute | solution.py:482
  314.9 18.0 %collective-permute-start.28 = (bf16[32,2176]{1,0:T(8,128)(2,1)S(1)}, bf16[32,2176]{1,0:T(8,128)(2,1)S(1)}, u32[]{:S(2)}, u32[]{:S(2)}) collective-permute-start(bf16[32,2176]{1,0:T(8,128)(2,1)S(1)} %two_sum.1.refs_1_), channel_id=1, source_target_pairs={{0,2},{1,3},{2,0},{3,1},{4,6},{5,7},{6,4},{7,5},{8,10},{9,11},{10,... | collective-permute-start | bytes 417800 | tf_op jit(solution)/shard_map/ppermute | solution.py:482
  316.0 16.9 %collective-permute-start.29 = (bf16[32,2176]{1,0:T(8,128)(2,1)S(1)}, bf16[32,2176]{1,0:T(8,128)(2,1)S(1)}, u32[]{:S(2)}, u32[]{:S(2)}) collective-permute-start(bf16[32,2176]{1,0:T(8,128)(2,1)S(1)} %two_sum.1.refs_1_), channel_id=1, source_target_pairs={{0,3},{1,0},{2,1},{3,2},{4,7},{5,4},{6,5},{7,6},{8,11},{9,8},{10,9... | collective-permute-start | bytes 417800 | tf_op jit(solution)/shard_map/ppermute | solution.py:482
  (11 other events, 8.9 us)
Sparse Core Ops, SparseCore 0:
  130.0 95.7 reduce-scatter.1
  228.4 87.0 all-gather.2

commit v4 on v3

--- a/solution.py
+++ b/solution.py
@@ -189,8 +189,8 @@
         up = mm(sent_ref[0], win_ref[0, :, half + t : half + t + tile])
         sig = jax.nn.sigmoid(gate)
         act = gate * sig
-        silu_ref[0, :, t : t + tile] = act
-        slope_ref[0, :, t : t + tile] = up * sig * (1.0 + gate * (1.0 - sig))
+        silu_ref[0, :, t : t + tile] = act.astype(bf16)
+        slope_ref[0, :, t : t + tile] = (up * sig * (1.0 + gate * (1.0 - sig))).astype(bf16)
         hidden_ref[0, :, t : t + tile] = (act * up).astype(bf16)
     for t in range(0, width, tile):
         cols = slice(t, t + tile)
@@ -225,8 +225,8 @@
         ghid = mm(crow[...], wout_ref[0, cols, :], ((1,), (1,)))
         dots = dots + jnp.sum(ghid * hidden_ref[0, :, cols].astype(f32), 1, keepdims=True)
         ghid = ghid * weight[...]
-        gpre[:, cols] = (ghid * slope_ref[0, :, cols]).astype(bf16)
-        gpre[:, half + t : half + t + tile] = (ghid * silu_ref[0, :, cols]).astype(bf16)
+        gpre[:, cols] = (ghid * slope_ref[0, :, cols].astype(f32)).astype(bf16)
+        gpre[:, half + t : half + t + tile] = (ghid * silu_ref[0, :, cols].astype(f32)).astype(bf16)
     for d in range(owners):
         part = dots[d * capacity : (d + 1) * capacity]
         gg_ref[0, d : d + 1, :] = jnp.sum(jnp.where(place == places[d], part, 0.0), 0, keepdims=True)
@@ -560,8 +560,8 @@
         [
             ((local, places, width), bf16),
             ((local, places, half), bf16),
-            ((local, places, half), f32),
-            ((local, places, half), f32),
+            ((local, places, half), bf16),
+            ((local, places, half), bf16),
             ((local, places, width), bf16),
         ],
         ids, *packs, expert_in, expert_out,
@@ -684,19 +684,19 @@
         keep_two, send_two, token = halve(keep_two, recv_two, stage, f"two_halve{stage}", (token,))
         recv_two = swap(send_two, stage)
     shares_one = total(blocks_one, "one_sum", (token,))
+    *blocks_two, token = spread(keep_two, recv_two, "two_spread", (shares_one[0],))
+    blocks_two = [blocks_two[0]] + [ring(blocks_two[d], d) for d in range(1, owners)]
     spec = pl.BlockSpec((seq // 4, width), lambda t: (t, 0))
     output, token = call(
         add_kernel, [((seq, width), f32), TOKEN], residual, out_parts, grid=(4,),
         specs=[spec, pl.BlockSpec((owners, seq // 4, width), lambda t: (0, t, 0))], out_specs=[spec, VMEM],
-        deps=(shares_one[0],), us=4, name="output",
-    )
-    *one, small_one = finish(shares_one, sizes[0], "one_finish", (token,))
-    *blocks_two, token = spread(keep_two, recv_two, "two_spread", (small_one,))
-    blocks_two = [blocks_two[0]] + [ring(blocks_two[d], d) for d in range(1, owners)]
-
+        deps=(token,), us=4, name="output",
+    )
     shares_two = total(blocks_two, "two_sum", (token,))
-    token = shares_two[0]
-    *full, token = call(
+    *one, small_one = finish(shares_one, sizes[0], "one_finish", (shares_two[0],))
+    *two, small_two = finish(shares_two, sizes[1], "two_finish", (small_one,))
+    token = small_two
+    *full, _ = call(
         widen_kernel,
         [((local, width, 2 * half), f32), ((local, half, width), f32), TOKEN],
         gathered,
@@ -709,7 +709,6 @@
         ],
         deps=(token,), us=12, name="widen",
     )
-    *two, small_two = finish(shares_two, sizes[1], "two_finish", (token,))
     return (
         output,
         grad_inputs,

time: 344 us -> 342 us (level)
    ppermute x18, waiting for transfers between devices: 70.9 us -> 67.3 us  [ring(): lax.ppermute(x, 'expert', [(i, (i + d) % owners) for i in range(owners)])]
    unnamed x53 -> x47, local copies, waits for them, and re-layouts: 11.7 us -> 9.13 us
  transfers between devices with their start and end apart: 33 -> 33, of which waited for: 17 -> 18; matrix products, arithmetic and copies ran while one was open for 1% -> 1% of each run, Pallas kernels for 25% -> 21%
where the time goes in v4:
time: 342 us; the launch traced here: 341 us
  waiting for transfers between devices  141 us (41%)
  Pallas kernels  115 us (34%)
  starting transfers between devices  56.9 us (17%)
  between operations  15 us (4%)
  local copies, waits for them, and re-layouts  10.5 us (3%)
    pallas_call x23, Pallas kernels, call(): pl.pallas_call(body, out_shape=outs, compiler_params=pltpu.CompilerParams...  115 us
    ppermute x18, waiting for transfers between devices, ring(): lax.ppermute(x, 'expert', [(i, (i + d) % owners) for i in range(owners)])  67.3 us
    ppermute x4, waiting for transfers between devices, swap(): lax.ppermute(x, 'group', [(i, i ^ 1 << (steps - stage if i % 2 else 1 + s...  42.8 us
    ppermute x18, starting transfers between devices, ring(): lax.ppermute(x, 'expert', [(i, (i + d) % owners) for i in range(owners)])  35.3 us
    ppermute x2, waiting for transfers between devices, far(): down = lax.ppermute(after, 'expert', [(1, 0), (2, 1)])  14.7 us
    ppermute x1, waiting for transfers between devices, on_device(): lax.ppermute(parts[2], 'expert', [(0, 1), (1, 2)])  10.5 us
    unnamed x47, local copies, waits for them, and re-layouts  9.13 us
  transfers between devices with their start and end apart: 33, of which 18 were waited for; matrix products, arithmetic and copies ran while one was open for 1% of the time, Pallas kernels for 21%

profile of v4, /device:TPU:0, one launch (start us, length us, event | category | flops | bytes accessed | tf_op | source)
XLA Modules:
  0.0 341.1 jit_solution(7397151925382196408)
XLA Ops:
  7.2 3.1 collective-permute-start
  10.3 2.1 collective-permute-start.1
  13.0 8.5 %dense_forward.1 = (bf16[256,1024]{1,0:T(8,128)(2,1)}, bf16[256,1024]{1,0:T(8,128)(2,1)}, bf16[256,1024]{1,0:T(8,128)(2,1)}, bf16[256,1024]{1,0:T(8,128)(2,1)}, ...) custom-call(s32[1]{0:T(128)S(6)} %copy.37.refs_0_.refs_1_, ...), custom_call_target="tpu_custom_call" | custom-call | bytes 32400000 | tf_op jit(solution)/shard_map/dense_forward/pallas_call | solution.py:52
  21.6 3.8 %collective-permute-done.refs_1_.refs_0_ = bf16[256,1024]{1,0:T(8,128)(2,1)S(1)} collective-permute-done((bf16[256,1024]{1,0:T(8,128)(2,1)}, bf16[256,1024]{1,0:T(8,128)(2,1)S(1)}, u32[]{:S(2)}, u32[]{:S(2)}) %collective-permute-start) | collective-permute-done | bytes 524320 | tf_op jit(solution)/shard_map/ppermute | solution.py:482
  25.3 9.8 %collective-permute-done.1.refs_2_.refs_1_ = bf16[256,1024]{1,0:T(8,128)(2,1)S(1)} collective-permute-done((bf16[256,1024]{1,0:T(8,128)(2,1)}, bf16[256,1024]{1,0:T(8,128)(2,1)S(1)}, u32[]{:S(2)}, u32[]{:S(2)}) %collective-permute-start.1) | collective-permute-done | bytes 524320 | tf_op jit(solution)/shard_map/ppermute | solution.py:482
  37.1 2.7 collective-permute-start.4
  39.7 13.7 %collective-permute-done.2.refs_2_ = bf16[272,1024]{1,0:T(8,128)(2,1)S(1)} collective-permute-done((bf16[272,1024]{1,0:T(8,128)(2,1)}, bf16[272,1024]{1,0:T(8,128)(2,1)S(1)}, u32[]{:S(2)}, u32[]{:S(2)}) %collective-permute-start.2) | collective-permute-done | bytes 557088 | tf_op jit(solution)/shard_map/ppermute | solution.py:482
  54.2 9.3 %collective-permute-done.4.refs_4_ = bf16[272,1024]{1,0:T(8,128)(2,1)S(1)} collective-permute-done((bf16[272,1024]{1,0:T(8,128)(2,1)}, bf16[272,1024]{1,0:T(8,128)(2,1)S(1)}, u32[]{:S(2)}, u32[]{:S(2)}) %collective-permute-start.4) | collective-permute-done | bytes 557088 | tf_op jit(solution)/shard_map/ppermute | solution.py:482
  63.5 1.3 collective-permute-start.5
  64.8 14.7 %collective-permute-done.5 = bf16[272,1024]{1,0:T(8,128)(2,1)S(1)} collective-permute-done((bf16[272,1024]{1,0:T(8,128)(2,1)S(1)}, bf16[272,1024]{1,0:T(8,128)(2,1)S(1)}, u32[]{:S(2)}, u32[]{:S(2)}) %collective-permute-start.5) | collective-permute-done | bytes 557088 | tf_op jit(solution)/shard_map/ppermute | solution.py:500
  81.1 1.5 collective-permute-start.7
  83.2 15.7 %expert_forward.1 = (bf16[4,640,1024]{2,1,0:T(8,128)(2,1)}, bf16[4,640,512]{2,1,0:T(8,128)(2,1)}, bf16[4,640,512]{2,1,0:T(8,128)(2,1)}, bf16[4,640,512]{2,1,0:T(8,128)(2,1)}, bf16[4,640,1024]{2,1,0:T(8,128)(2,1)}) custom-call(s32[3]{0:T(128)} %pad_add_fusion.2.refs_0_, bf16[272,1024]{1,0:T(8,128)(2,1)} %tokens_go.1.refs_1_.refs_10_, ...), custom_call_target="tpu_custom_call" | custom-call | bytes 61200000 | tf_op jit(solution)/shard_map/expert_forward/pallas_call | solution.py:52
  99.8 28.0 %expert_backward0.1 = (bf16[8,768,1024]{2,1,0:T(8,128)(2,1)}, bf16[4,640,1024]{2,1,0:T(8,128)(2,1)}, f32[4,4,256]{2,1,0:T(4,128)}) custom-call(s32[3]{0:T(128)} %pad_add_fusion.2.refs_0_, bf16[272,1024]{1,0:T(8,128)(2,1)} %tokens_go.1.refs_1_.refs_10_, bf16[272,1024]{1,0:T(8,128)(2,1)} %copy-done.15, bf16[272,1024]{1,0:T(8,128)(2,1)} %broadcast_select_fusion.refs_3_.refs_2_, ...), custom_call_target="tpu_custom_call" | custom-call | bytes 115200000 | tf_op jit(solution)/shard_map/expert_backward0/pallas_call | solution.py:52
  127.8 7.8 %combine_grad.1 = (bf16[272,1024]{1,0:T(8,128)(2,1)}, bf16[272,1024]{1,0:T(8,128)(2,1)}, bf16[272,1024]{1,0:T(8,128)(2,1)}, bf16[272,1024]{1,0:T(8,128)(2,1)}) custom-call(s32[3]{0:T(128)} %pad_add_fusion.2.refs_0_, bf16[272,1024]{1,0:T(8,128)(2,1)} %tokens_go.1.refs_1_.refs_10_, bf16[272,1024]{1,0:T(8,128)(2,1)} %copy-done.15, ...), custom_call_target="tpu_custom_call" | custom-call | bytes 28800000 | tf_op jit(solution)/shard_map/combine_grad/pallas_call | solution.py:52
  136.3 5.4 %collective-permute-start.9 = (bf16[272,1024]{1,0:T(8,128)(2,1)}, bf16[272,1024]{1,0:T(8,128)(2,1)S(1)}, u32[]{:S(2)}, u32[]{:S(2)}) collective-permute-start(bf16[272,1024]{1,0:T(8,128)(2,1)} %get-tuple-element.86), channel_id=1, source_target_pairs={{0,1},{1,2},{4,5},{5,6},{8,9},{9,10},{12,13},{13,14},{16,17},{17,1... | collective-permute-start | bytes 1671176 | tf_op jit(solution)/shard_map/ppermute | solution.py:619
  141.8 10.5 %collective-permute-done.9.refs_3_ = bf16[272,1024]{1,0:T(8,128)(2,1)S(1)} collective-permute-done((bf16[272,1024]{1,0:T(8,128)(2,1)}, bf16[272,1024]{1,0:T(8,128)(2,1)S(1)}, u32[]{:S(2)}, u32[]{:S(2)}) %collective-permute-start.9) | collective-permute-done | bytes 557088 | tf_op jit(solution)/shard_map/ppermute | solution.py:619
  153.1 2.7 hop.1
  155.9 2.2 collective-permute-start.11
  158.2 7.5 %combine_out.1.refs_23_.refs_0_ = bf16[4,256,1024]{2,1,0:T(8,128)(2,1)} custom-call(s32[3]{0:T(128)} %pad_add_fusion.2.refs_0_, bf16[272,1024]{1,0:T(8,128)(2,1)} %tokens_go.1.refs_1_.refs_10_, bf16[272,1024]{1,0:T(8,128)(2,1)} %copy-done.15, bf16[272,1024]{1,0:T(8,128)(2,1)} %broadcast_select_fusion.refs_3_.refs_2_, bf16[272,1024]{1,0:T(8,128)(2,1)} %copy-done.16, ...), custom_call_target="tpu_custom_call" | custom-call | bytes 28800000 | tf_op jit(solution)/shard_map/combine_out/pallas_call | solution.py:52
  165.7 4.1 %collective-permute-done.10.refs_3_ = bf16[272,1024]{1,0:T(8,128)(2,1)S(1)} collective-permute-done((bf16[272,1024]{1,0:T(8,128)(2,1)}, bf16[272,1024]{1,0:T(8,128)(2,1)S(1)}, u32[]{:S(2)}, u32[]{:S(2)}) %collective-permute-start.10) | collective-permute-done | bytes 557088 | tf_op jit(solution)/shard_map/ppermute | solution.py:482
  169.8 13.3 %collective-permute-done.11.refs_4_ = bf16[272,1024]{1,0:T(8,128)(2,1)S(1)} collective-permute-done((bf16[272,1024]{1,0:T(8,128)(2,1)}, bf16[272,1024]{1,0:T(8,128)(2,1)S(1)}, u32[]{:S(2)}, u32[]{:S(2)}) %collective-permute-start.11) | collective-permute-done | bytes 557088 | tf_op jit(solution)/shard_map/ppermute | solution.py:482
  183.9 18.5 %dense_backward.1 = (f32[256,1024]{1,0:T(8,128)}, bf16[4,128,1152]{2,1,0:T(8,128)(2,1)}, bf16[4,128,1152]{2,1,0:T(8,128)(2,1)}, bf16[4,128,2176]{2,1,0:T(8,128)(2,1)}, bf16[4,128,2176]{2,1,0:T(8,128)(2,1)}) custom-call(s32[3]{0:T(128)} %pad_add_fusion.2.refs_0_, s32[1]{0:T(128)S(6)} %copy.37.refs_0_.refs_1_, bf16[272,1024]{1,0:T(8,128)(2,1)} %get-tuple-element.88.refs_2_, ...), custom_call_target="tpu_custom_call" | custom-call | bytes 64800000 | tf_op jit(solution)/shard_map/dense_backward/pallas_call | solution.py:52
  203.0 5.7 %collective-permute-done.13.refs_2_.refs_4_ = bf16[4,128,1152]{2,1,0:T(8,128)(2,1)S(1)} collective-permute-done((bf16[4,128,1152]{2,1,0:T(8,128)(2,1)}, bf16[4,128,1152]{2,1,0:T(8,128)(2,1)S(1)}, u32[]{:S(2)}, u32[]{:S(2)}) %collective-permute-start.13) | collective-permute-done | bytes 1179680 | tf_op jit(solution)/shard_map/ppermute | solution.py:485
  208.7 1.2 one_halve0.1
  210.7 1.7 collective-permute-start.15
  216.2 9.1 %collective-permute-done.15.refs_1_.refs_2_.refs_4_ = bf16[2,128,1152]{2,1,0:T(8,128)(2,1)S(1)} collective-permute-done((bf16[2,128,1152]{2,1,0:T(8,128)(2,1)S(1)}, bf16[2,128,1152]{2,1,0:T(8,128)(2,1)S(1)}, u32[]{:S(2)}, u32[]{:S(2)}) %collective-permute-start.15) | collective-permute-done | bytes 589856 | tf_op jit(solution)/shard_map/ppermute | solution.py:488
  226.2 4.7 %all-to-all-start = ((bf16[4,256,1024]{2,1,0:T(8,128)(2,1)}), bf16[4,256,1024]{2,1,0:T(8,128)(2,1)}, u32[]{:S(2)}, u32[]{:S(2)}) async-start(bf16[4,256,1024]{2,1,0:T(8,128)(2,1)} %returned_go.1.refs_5_), calls=%async_computation | async-start | bytes 4194304 | tf_op jit(solution)/shard_map/all_to_all | solution.py:630
  233.6 1.3 collective-permute-start.16
  234.9 13.2 %collective-permute-done.16.refs_2_ = bf16[1,128,1152]{2,1,0:T(8,128)(2,1)S(1)} collective-permute-done((bf16[1,128,1152]{2,1,0:T(8,128)(2,1)S(1)}, bf16[1,128,1152]{2,1,0:T(8,128)(2,1)S(1)}, u32[]{:S(2)}, u32[]{:S(2)}) %collective-permute-start.16) | collective-permute-done | bytes 294944 | tf_op jit(solution)/shard_map/ppermute | solution.py:488
  248.7 17.9 %collective-permute-done.14.refs_2_.refs_4_ = bf16[2,128,2176]{2,1,0:T(8,128)(2,1)S(1)} collective-permute-done((bf16[2,128,2176]{2,1,0:T(8,128)(2,1)}, bf16[2,128,2176]{2,1,0:T(8,128)(2,1)S(1)}, u32[]{:S(2)}, u32[]{:S(2)}) %collective-permute-start.14) | collective-permute-done | bytes 1114144 | tf_op jit(solution)/shard_map/ppermute | solution.py:488
  267.5 2.3 collective-permute-start.17
  269.8 2.7 collective-permute-start.18
  272.5 2.5 collective-permute-start.19
  274.9 1.4 collective-permute-start.20
  276.9 8.2 %collective-permute-done.19.refs_2_ = bf16[32,1152]{1,0:T(8,128)(2,1)S(1)} collective-permute-done((bf16[32,1152]{1,0:T(8,128)(2,1)S(1)}, bf16[32,1152]{1,0:T(8,128)(2,1)S(1)}, u32[]{:S(2)}, u32[]{:S(2)}) %collective-permute-start.19) | collective-permute-done | bytes 73760 | tf_op jit(solution)/shard_map/ppermute | solution.py:482
  285.2 2.5 collective-permute-done.17.refs_2_
  288.5 3.6 %collective-permute-start.21 = (bf16[32,2176]{1,0:T(8,128)(2,1)S(1)}, bf16[32,2176]{1,0:T(8,128)(2,1)S(1)}, u32[]{:S(2)}, u32[]{:S(2)}) collective-permute-start(bf16[32,2176]{1,0:T(8,128)(2,1)S(1)} %get-tuple-element.123), channel_id=1, source_target_pairs={{0,1},{1,2},{2,3},{3,0},{4,5},{5,6},{6,7},{7,4},{8,9},{9,10},{10,1... | collective-permute-start | bytes 417800 | tf_op jit(solution)/shard_map/ppermute | solution.py:482
  292.1 2.5 collective-permute-start.22
  294.5 1.3 collective-permute-start.23
  297.3 2.8 collective-permute-start.29
  300.1 3.9 %output.1 = (f32[256,1024]{1,0:T(8,128)}, f32[8,128]{1,0:T(8,128)}) custom-call(f32[256,1024]{1,0:T(8,128)} %get-tuple-element.73.refs_8_.refs_0_, bf16[4,256,1024]{2,1,0:T(8,128)(2,1)} %all-to-all-done.refs_1_, f32[8,128]{1,0:T(8,128)} %copy-done.11), custom_call_target="tpu_custom_call" | custom-call | bytes 14400000 | tf_op jit(solution)/shard_map/output/pallas_call | solution.py:52
  304.0 2.5 collective-permute-done.22.refs_2_
  307.2 3.6 %collective-permute-start.24 = (bf16[32,2176]{1,0:T(8,128)(2,1)S(1)}, bf16[32,2176]{1,0:T(8,128)(2,1)S(1)}, u32[]{:S(2)}, u32[]{:S(2)}) collective-permute-start(bf16[32,2176]{1,0:T(8,128)(2,1)S(1)} %two_sum.1.refs_5_.refs_1_), channel_id=1, source_target_pairs={{0,1},{1,2},{2,3},{3,0},{4,5},{5,6},{6,7},{7,4},{8,9},{9,10},{10,1... | collective-permute-start | bytes 417800 | tf_op jit(solution)/shard_map/ppermute | solution.py:482
  310.8 2.4 collective-permute-start.26
  313.3 1.4 one_finish.1
  316.1 1.7 collective-permute-done.25.refs_3_
  317.8 1.6 two_finish.1
  320.0 14.2 %widen.1 = (f32[4,1024,1024]{2,1,0:T(8,128)}, f32[4,512,1024]{2,1,0:T(8,128)}, f32[8,128]{1,0:T(8,128)}) custom-call(bf16[8,768,1024]{2,1,0:T(8,128)(2,1)} %bitcast.19, f32[128,128]{1,0:T(8,128)} %copy-done.9), custom_call_target="tpu_custom_call" | custom-call | bytes 43200000 | tf_op jit(solution)/shard_map/widen/pallas_call | solution.py:52
  (98 shorter events, 23.9 us)
Async XLA Ops:
  7.2 218.1 %reduce-scatter.2.cloned.1.call-start = ((), (), s32[]{:S(2)}) async-start(), calls=%async_computation.2 | async-start | bytes 14155776 | tf_op jit(solution)/shard_map/reduce_scatter | solution.py:614
  7.2 18.1 %collective-permute-start = (bf16[256,1024]{1,0:T(8,128)(2,1)}, bf16[256,1024]{1,0:T(8,128)(2,1)S(1)}, u32[]{:S(2)}, u32[]{:S(2)}) collective-permute-start(bf16[256,1024]{1,0:T(8,128)(2,1)} %refs_7_.1), channel_id=1, source_target_pairs={{0,1},{1,2},{2,3},{3,0},{4,5},{5,6},{6,7},{7,4},{8,9},{9,10},{10,1... | collective-permute-start | bytes 1572872 | tf_op jit(solution)/shard_map/ppermute | solution.py:482
  10.3 24.8 %collective-permute-start.1 = (bf16[256,1024]{1,0:T(8,128)(2,1)}, bf16[256,1024]{1,0:T(8,128)(2,1)S(1)}, u32[]{:S(2)}, u32[]{:S(2)}) collective-permute-start(bf16[256,1024]{1,0:T(8,128)(2,1)} %refs_7_.1), channel_id=1, source_target_pairs={{0,3},{1,0},{2,1},{3,2},{4,7},{5,4},{6,5},{7,6},{8,11},{9,8},{10,9... | collective-permute-start | bytes 1572872 | tf_op jit(solution)/shard_map/ppermute | solution.py:482
  25.3 9.8 %copy-start.17 = (bf16[256,1024]{1,0:T(8,128)(2,1)}, bf16[256,1024]{1,0:T(8,128)(2,1)S(1)}, u32[]{:S(2)}) copy-start(bf16[256,1024]{1,0:T(8,128)(2,1)S(1)} %collective-permute-done.refs_1_.refs_0_) | copy-start | bytes 1572868
  35.9 17.6 %collective-permute-start.2 = (bf16[272,1024]{1,0:T(8,128)(2,1)}, bf16[272,1024]{1,0:T(8,128)(2,1)S(1)}, u32[]{:S(2)}, u32[]{:S(2)}) collective-permute-start(bf16[272,1024]{1,0:T(8,128)(2,1)} %tokens_go.1.refs_1_.refs_10_), channel_id=1, source_target_pairs={{0,1},{1,2},{2,3},{3,0},{4,5},{5,6},{6,7},{7,4},{8,9},{9,10},{10,1... | collective-permute-start | bytes 1671176 | tf_op jit(solution)/shard_map/ppermute | solution.py:482
  37.1 26.4 %collective-permute-start.4 = (bf16[272,1024]{1,0:T(8,128)(2,1)}, bf16[272,1024]{1,0:T(8,128)(2,1)S(1)}, u32[]{:S(2)}, u32[]{:S(2)}) collective-permute-start(bf16[272,1024]{1,0:T(8,128)(2,1)} %tokens_go.1.refs_1_.refs_10_), channel_id=1, source_target_pairs={{0,3},{1,0},{2,1},{3,2},{4,7},{5,4},{6,5},{7,6},{8,11},{9,8},{10,9... | collective-permute-start | bytes 1671176 | tf_op jit(solution)/shard_map/ppermute | solution.py:482
  53.5 29.7 %copy-start.15 = (bf16[272,1024]{1,0:T(8,128)(2,1)}, bf16[272,1024]{1,0:T(8,128)(2,1)S(1)}, u32[]{:S(2)}) copy-start(bf16[272,1024]{1,0:T(8,128)(2,1)S(1)} %collective-permute-done.2.refs_2_) | copy-start | bytes 1671172
  53.5 11.3 %collective-permute-start.3 = (bf16[272,1024]{1,0:T(8,128)(2,1)S(1)}, bf16[272,1024]{1,0:T(8,128)(2,1)S(1)}, u32[]{:S(2)}, u32[]{:S(2)}) collective-permute-start(bf16[272,1024]{1,0:T(8,128)(2,1)S(1)} %collective-permute-done.2.refs_2_), channel_id=1, source_target_pairs={{1,2},{2,3},{5,6},{6,7},{9,10},{10,11},{13,14},{14,15},{17,18},{18... | collective-permute-start | bytes 1671176 | tf_op jit(solution)/shard_map/ppermute | solution.py:499
  63.5 19.7 %copy-start.16 = (bf16[272,1024]{1,0:T(8,128)(2,1)}, bf16[272,1024]{1,0:T(8,128)(2,1)S(1)}, u32[]{:S(2)}) copy-start(bf16[272,1024]{1,0:T(8,128)(2,1)S(1)} %collective-permute-done.4.refs_4_) | copy-start | bytes 1671172
  63.5 16.0 %collective-permute-start.5 = (bf16[272,1024]{1,0:T(8,128)(2,1)S(1)}, bf16[272,1024]{1,0:T(8,128)(2,1)S(1)}, u32[]{:S(2)}, u32[]{:S(2)}) collective-permute-start(bf16[272,1024]{1,0:T(8,128)(2,1)S(1)} %collective-permute-done.4.refs_4_), channel_id=1, source_target_pairs={{1,0},{2,1},{5,4},{6,5},{9,8},{10,9},{13,12},{14,13},{17,16},{18,1... | collective-permute-start | bytes 1671176 | tf_op jit(solution)/shard_map/ppermute | solution.py:500
  80.4 18.5 %collective-permute-start.6 = (bf16[256,1024]{1,0:T(8,128)(2,1)}, bf16[256,1024]{1,0:T(8,128)(2,1)S(1)}, u32[]{:S(2)}, u32[]{:S(2)}) collective-permute-start(bf16[256,1024]{1,0:T(8,128)(2,1)} %get-tuple-element.76.refs_6_), channel_id=1, source_target_pairs={{1,2},{2,3},{5,6},{6,7},{9,10},{10,11},{13,14},{14,15},{17,18},{18... | collective-permute-start | bytes 1572872 | tf_op jit(solution)/shard_map/ppermute | solution.py:499
  81.1 17.8 %collective-permute-start.7 = (bf16[256,1024]{1,0:T(8,128)(2,1)}, bf16[256,1024]{1,0:T(8,128)(2,1)S(1)}, u32[]{:S(2)}, u32[]{:S(2)}) collective-permute-start(bf16[256,1024]{1,0:T(8,128)(2,1)} %get-tuple-element.77.refs_8_), channel_id=1, source_target_pairs={{1,0},{2,1},{5,4},{6,5},{9,8},{10,9},{13,12},{14,13},{17,16},{18,1... | collective-permute-start | bytes 1572872 | tf_op jit(solution)/shard_map/ppermute | solution.py:500
  127.8 192.3 %all-gather.3.cloned.1.call-start = ((), (), s32[]{:S(2)}) async-start(), calls=%async_computation.3 | async-start | bytes 14155776 | tf_op jit(solution)/shard_map/all_gather | solution.py:658
  135.6 6.1 %collective-permute-start.8 = (bf16[272,1024]{1,0:T(8,128)(2,1)}, bf16[272,1024]{1,0:T(8,128)(2,1)S(1)}, u32[]{:S(2)}, u32[]{:S(2)}) collective-permute-start(bf16[272,1024]{1,0:T(8,128)(2,1)} %get-tuple-element.86), channel_id=1, source_target_pairs={{2,1},{3,2},{6,5},{7,6},{10,9},{11,10},{14,13},{15,14},{18,17},{19... | collective-permute-start | bytes 1671176 | tf_op jit(solution)/shard_map/ppermute | solution.py:618
  136.3 16.0 %collective-permute-start.9 = (bf16[272,1024]{1,0:T(8,128)(2,1)}, bf16[272,1024]{1,0:T(8,128)(2,1)S(1)}, u32[]{:S(2)}, u32[]{:S(2)}) collective-permute-start(bf16[272,1024]{1,0:T(8,128)(2,1)} %get-tuple-element.86), channel_id=1, source_target_pairs={{0,1},{1,2},{4,5},{5,6},{8,9},{9,10},{12,13},{13,14},{16,17},{17,1... | collective-permute-start | bytes 1671176 | tf_op jit(solution)/shard_map/ppermute | solution.py:619
  141.8 10.5 %copy-start.21 = (bf16[272,1024]{1,0:T(8,128)(2,1)}, bf16[272,1024]{1,0:T(8,128)(2,1)S(1)}, u32[]{:S(2)}) copy-start(bf16[272,1024]{1,0:T(8,128)(2,1)S(1)} %collective-permute-done.8.refs_2_) | copy-start | bytes 1671172
  155.8 14.0 %collective-permute-start.10 = (bf16[272,1024]{1,0:T(8,128)(2,1)}, bf16[272,1024]{1,0:T(8,128)(2,1)S(1)}, u32[]{:S(2)}, u32[]{:S(2)}) collective-permute-start(bf16[272,1024]{1,0:T(8,128)(2,1)} %get-tuple-element.87.refs_6_), channel_id=1, source_target_pairs={{0,3},{1,0},{2,1},{3,2},{4,7},{5,4},{6,5},{7,6},{8,11},{9,8},{10,9... | collective-permute-start | bytes 1671176 | tf_op jit(solution)/shard_map/ppermute | solution.py:482
  155.9 27.2 %collective-permute-start.11 = (bf16[272,1024]{1,0:T(8,128)(2,1)}, bf16[272,1024]{1,0:T(8,128)(2,1)S(1)}, u32[]{:S(2)}, u32[]{:S(2)}) collective-permute-start(bf16[272,1024]{1,0:T(8,128)(2,1)} %get-tuple-element.89), channel_id=1, source_target_pairs={{0,1},{1,2},{2,3},{3,0},{4,5},{5,6},{6,7},{7,4},{8,9},{9,10},{10,1... | collective-permute-start | bytes 1671176 | tf_op jit(solution)/shard_map/ppermute | solution.py:482
  169.8 13.3 %copy-start.19 = (bf16[272,1024]{1,0:T(8,128)(2,1)}, bf16[272,1024]{1,0:T(8,128)(2,1)S(1)}, u32[]{:S(2)}) copy-start(bf16[272,1024]{1,0:T(8,128)(2,1)S(1)} %collective-permute-done.10.refs_3_) | copy-start | bytes 1671172
  202.5 10.0 %collective-permute-start.12 = (bf16[4,128,2176]{2,1,0:T(8,128)(2,1)}, bf16[4,128,2176]{2,1,0:T(8,128)(2,1)S(1)}, u32[]{:S(2)}, u32[]{:S(2)}) collective-permute-start(bf16[4,128,2176]{2,1,0:T(8,128)(2,1)} %get-tuple-element.99), channel_id=1, source_target_pairs={{0,4},{4,0},{8,12},{12,8},{16,20},{20,16},{24,28},{28,24},{1,5},{5... | collective-permute-start | bytes 6684680 | tf_op jit(solution)/shard_map/ppermute | solution.py:485
  202.5 6.2 %collective-permute-start.13 = (bf16[4,128,1152]{2,1,0:T(8,128)(2,1)}, bf16[4,128,1152]{2,1,0:T(8,128)(2,1)S(1)}, u32[]{:S(2)}, u32[]{:S(2)}) collective-permute-start(bf16[4,128,1152]{2,1,0:T(8,128)(2,1)} %get-tuple-element.97.refs_1_), channel_id=1, source_target_pairs={{0,4},{4,0},{8,12},{12,8},{16,20},{20,16},{24,28},{28,24},{1,5},{5... | collective-permute-start | bytes 3538952 | tf_op jit(solution)/shard_map/ppermute | solution.py:485
  203.0 5.7 %copy-start.4 = (bf16[4,128,1152]{2,1,0:T(8,128)(2,1)S(1)}, bf16[4,128,1152]{2,1,0:T(8,128)(2,1)}, u32[]{:S(2)}) copy-start(bf16[4,128,1152]{2,1,0:T(8,128)(2,1)} %get-tuple-element.100.refs_1_.refs_3_) | copy-start | bytes 3538948
  208.7 3.7 %copy-start.1 = (bf16[4,128,2176]{2,1,0:T(8,128)(2,1)S(1)}, bf16[4,128,2176]{2,1,0:T(8,128)(2,1)}, u32[]{:S(2)}) copy-start(bf16[4,128,2176]{2,1,0:T(8,128)(2,1)} %get-tuple-element.98.refs_1_.refs_3_) | copy-start | bytes 6684676
  210.7 14.6 %collective-permute-start.15 = (bf16[2,128,1152]{2,1,0:T(8,128)(2,1)S(1)}, bf16[2,128,1152]{2,1,0:T(8,128)(2,1)S(1)}, u32[]{:S(2)}, u32[]{:S(2)}) collective-permute-start(bf16[2,128,1152]{2,1,0:T(8,128)(2,1)S(1)} %get-tuple-element.105), channel_id=1, source_target_pairs={{0,8},{4,20},{8,0},{12,28},{16,24},{20,4},{24,16},{28,12},{1,9},{5... | collective-permute-start | bytes 1769480 | tf_op jit(solution)/shard_map/ppermute | solution.py:488
  213.6 1.0 copy-start.5
  215.2 1.0 copy-start.14
  226.2 5.6 %copy-start = (bf16[768,1024]{1,0:T(8,128)(2,1)S(1)}, bf16[768,1024]{1,0:T(8,128)(2,1)}, u32[]{:S(2)}) copy-start(bf16[768,1024]{1,0:T(8,128)(2,1)} %gather_go.1.refs_5_) | copy-start | bytes 4718596
  226.2 5.6 %copy-start.3 = (bf16[2,128,1152]{2,1,0:T(8,128)(2,1)S(1)}, bf16[2,128,1152]{2,1,0:T(8,128)(2,1)}, u32[]{:S(2)}) copy-start(bf16[2,128,1152]{2,1,0:T(8,128)(2,1)} %copy-done.2) | copy-start | bytes 1769476
  226.2 74.0 %all-to-all-start = ((bf16[4,256,1024]{2,1,0:T(8,128)(2,1)}), bf16[4,256,1024]{2,1,0:T(8,128)(2,1)}, u32[]{:S(2)}, u32[]{:S(2)}) async-start(bf16[4,256,1024]{2,1,0:T(8,128)(2,1)} %returned_go.1.refs_5_), calls=%async_computation | async-start | bytes 4194304 | tf_op jit(solution)/shard_map/all_to_all | solution.py:630
  230.9 17.1 %copy-start.10 = (s32[3]{0:T(128)S(1)}, s32[3]{0:T(128)}, u32[]{:S(2)}) copy-start(s32[3]{0:T(128)} %pad_add_fusion.2.refs_0_) | copy-start | bytes 40
  230.9 35.7 %collective-permute-start.14 = (bf16[2,128,2176]{2,1,0:T(8,128)(2,1)}, bf16[2,128,2176]{2,1,0:T(8,128)(2,1)S(1)}, u32[]{:S(2)}, u32[]{:S(2)}) collective-permute-start(bf16[2,128,2176]{2,1,0:T(8,128)(2,1)} %copy-done.14), channel_id=1, source_target_pairs={{0,8},{4,20},{8,0},{12,28},{16,24},{20,4},{24,16},{28,12},{1,9},{5... | collective-permute-start | bytes 3342344 | tf_op jit(solution)/shard_map/ppermute | solution.py:488
  231.8 1.1 copy-start.8
  232.8 33.8 %copy-start.6 = (bf16[2,128,2176]{2,1,0:T(8,128)(2,1)S(1)}, bf16[2,128,2176]{2,1,0:T(8,128)(2,1)}, u32[]{:S(2)}) copy-start(bf16[2,128,2176]{2,1,0:T(8,128)(2,1)} %copy-done.5) | copy-start | bytes 3342340
  233.6 14.5 %collective-permute-start.16 = (bf16[1,128,1152]{2,1,0:T(8,128)(2,1)S(1)}, bf16[1,128,1152]{2,1,0:T(8,128)(2,1)S(1)}, u32[]{:S(2)}, u32[]{:S(2)}) collective-permute-start(bf16[1,128,1152]{2,1,0:T(8,128)(2,1)S(1)} %get-tuple-element.109), channel_id=1, source_target_pairs={{0,16},{4,12},{8,24},{12,4},{16,0},{20,28},{24,8},{28,20},{1,17},{... | collective-permute-start | bytes 884744 | tf_op jit(solution)/shard_map/ppermute | solution.py:488
  267.5 20.2 %collective-permute-start.17 = (bf16[1,128,2176]{2,1,0:T(8,128)(2,1)S(1)}, bf16[1,128,2176]{2,1,0:T(8,128)(2,1)S(1)}, u32[]{:S(2)}, u32[]{:S(2)}) collective-permute-start(bf16[1,128,2176]{2,1,0:T(8,128)(2,1)S(1)} %get-tuple-element.113), channel_id=1, source_target_pairs={{0,16},{4,12},{8,24},{12,4},{16,0},{20,28},{24,8},{28,20},{1,17},{... | collective-permute-start | bytes 1671176 | tf_op jit(solution)/shard_map/ppermute | solution.py:488
  269.8 7.0 %collective-permute-start.18 = (bf16[32,1152]{1,0:T(8,128)(2,1)S(1)}, bf16[32,1152]{1,0:T(8,128)(2,1)S(1)}, u32[]{:S(2)}, u32[]{:S(2)}) collective-permute-start(bf16[32,1152]{1,0:T(8,128)(2,1)S(1)} %get-tuple-element.115), channel_id=1, source_target_pairs={{0,1},{1,2},{2,3},{3,0},{4,5},{5,6},{6,7},{7,4},{8,9},{9,10},{10,1... | collective-permute-start | bytes 221192 | tf_op jit(solution)/shard_map/ppermute | solution.py:482
  272.5 12.6 %collective-permute-start.19 = (bf16[32,1152]{1,0:T(8,128)(2,1)S(1)}, bf16[32,1152]{1,0:T(8,128)(2,1)S(1)}, u32[]{:S(2)}, u32[]{:S(2)}) collective-permute-start(bf16[32,1152]{1,0:T(8,128)(2,1)S(1)} %get-tuple-element.116), channel_id=1, source_target_pairs={{0,2},{1,3},{2,0},{3,1},{4,6},{5,7},{6,4},{7,5},{8,10},{9,11},{10,... | collective-permute-start | bytes 221192 | tf_op jit(solution)/shard_map/ppermute | solution.py:482
  274.9 10.2 %collective-permute-start.20 = (bf16[32,1152]{1,0:T(8,128)(2,1)S(1)}, bf16[32,1152]{1,0:T(8,128)(2,1)S(1)}, u32[]{:S(2)}, u32[]{:S(2)}) collective-permute-start(bf16[32,1152]{1,0:T(8,128)(2,1)S(1)} %get-tuple-element.117), channel_id=1, source_target_pairs={{0,3},{1,0},{2,1},{3,2},{4,7},{5,4},{6,5},{7,6},{8,11},{9,8},{10,9... | collective-permute-start | bytes 221192 | tf_op jit(solution)/shard_map/ppermute | solution.py:482
  288.5 8.9 %copy-start.11 = (f32[8,128]{1,0:T(8,128)}, f32[8,128]{1,0:T(8,128)S(1)}, u32[]{:S(2)}) copy-start(f32[8,128]{1,0:T(8,128)S(1)} %get-tuple-element.119.refs_2_) | copy-start | bytes 12292
  288.5 8.9 %collective-permute-start.21 = (bf16[32,2176]{1,0:T(8,128)(2,1)S(1)}, bf16[32,2176]{1,0:T(8,128)(2,1)S(1)}, u32[]{:S(2)}, u32[]{:S(2)}) collective-permute-start(bf16[32,2176]{1,0:T(8,128)(2,1)S(1)} %get-tuple-element.123), channel_id=1, source_target_pairs={{0,1},{1,2},{2,3},{3,0},{4,5},{5,6},{6,7},{7,4},{8,9},{9,10},{10,1... | collective-permute-start | bytes 417800 | tf_op jit(solution)/shard_map/ppermute | solution.py:482
  292.1 14.4 %collective-permute-start.22 = (bf16[32,2176]{1,0:T(8,128)(2,1)S(1)}, bf16[32,2176]{1,0:T(8,128)(2,1)S(1)}, u32[]{:S(2)}, u32[]{:S(2)}) collective-permute-start(bf16[32,2176]{1,0:T(8,128)(2,1)S(1)} %get-tuple-element.124), channel_id=1, source_target_pairs={{0,2},{1,3},{2,0},{3,1},{4,6},{5,7},{6,4},{7,5},{8,10},{9,11},{10,... | collective-permute-start | bytes 417800 | tf_op jit(solution)/shard_map/ppermute | solution.py:482
  294.5 11.9 %collective-permute-start.23 = (bf16[32,2176]{1,0:T(8,128)(2,1)S(1)}, bf16[32,2176]{1,0:T(8,128)(2,1)S(1)}, u32[]{:S(2)}, u32[]{:S(2)}) collective-permute-start(bf16[32,2176]{1,0:T(8,128)(2,1)S(1)} %get-tuple-element.125), channel_id=1, source_target_pairs={{0,3},{1,0},{2,1},{3,2},{4,7},{5,4},{6,5},{7,6},{8,11},{9,8},{10,9... | collective-permute-start | bytes 417800 | tf_op jit(solution)/shard_map/ppermute | solution.py:482
  295.9 15.0 %collective-permute-start.27 = (bf16[32,1152]{1,0:T(8,128)(2,1)S(1)}, bf16[32,1152]{1,0:T(8,128)(2,1)S(1)}, u32[]{:S(2)}, u32[]{:S(2)}) collective-permute-start(bf16[32,1152]{1,0:T(8,128)(2,1)S(1)} %one_sum.1.refs_3_.refs_1_), channel_id=1, source_target_pairs={{0,1},{1,2},{2,3},{3,0},{4,5},{5,6},{6,7},{7,4},{8,9},{9,10},{10,1... | collective-permute-start | bytes 221192 | tf_op jit(solution)/shard_map/ppermute | solution.py:482
  296.6 16.7 %collective-permute-start.28 = (bf16[32,1152]{1,0:T(8,128)(2,1)S(1)}, bf16[32,1152]{1,0:T(8,128)(2,1)S(1)}, u32[]{:S(2)}, u32[]{:S(2)}) collective-permute-start(bf16[32,1152]{1,0:T(8,128)(2,1)S(1)} %one_sum.1.refs_3_.refs_1_), channel_id=1, source_target_pairs={{0,2},{1,3},{2,0},{3,1},{4,6},{5,7},{6,4},{7,5},{8,10},{9,11},{10,... | collective-permute-start | bytes 221192 | tf_op jit(solution)/shard_map/ppermute | solution.py:482
  297.3 16.0 %collective-permute-start.29 = (bf16[32,1152]{1,0:T(8,128)(2,1)S(1)}, bf16[32,1152]{1,0:T(8,128)(2,1)S(1)}, u32[]{:S(2)}, u32[]{:S(2)}) collective-permute-start(bf16[32,1152]{1,0:T(8,128)(2,1)S(1)} %one_sum.1.refs_3_.refs_1_), channel_id=1, source_target_pairs={{0,3},{1,0},{2,1},{3,2},{4,7},{5,4},{6,5},{7,6},{8,11},{9,8},{10,9... | collective-permute-start | bytes 221192 | tf_op jit(solution)/shard_map/ppermute | solution.py:482
  307.2 8.8 %collective-permute-start.24 = (bf16[32,2176]{1,0:T(8,128)(2,1)S(1)}, bf16[32,2176]{1,0:T(8,128)(2,1)S(1)}, u32[]{:S(2)}, u32[]{:S(2)}) collective-permute-start(bf16[32,2176]{1,0:T(8,128)(2,1)S(1)} %two_sum.1.refs_5_.refs_1_), channel_id=1, source_target_pairs={{0,1},{1,2},{2,3},{3,0},{4,5},{5,6},{6,7},{7,4},{8,9},{9,10},{10,1... | collective-permute-start | bytes 417800 | tf_op jit(solution)/shard_map/ppermute | solution.py:482
  310.8 7.0 %collective-permute-start.25 = (bf16[32,2176]{1,0:T(8,128)(2,1)S(1)}, bf16[32,2176]{1,0:T(8,128)(2,1)S(1)}, u32[]{:S(2)}, u32[]{:S(2)}) collective-permute-start(bf16[32,2176]{1,0:T(8,128)(2,1)S(1)} %two_sum.1.refs_5_.refs_1_), channel_id=1, source_target_pairs={{0,2},{1,3},{2,0},{3,1},{4,6},{5,7},{6,4},{7,5},{8,10},{9,11},{10,... | collective-permute-start | bytes 417800 | tf_op jit(solution)/shard_map/ppermute | solution.py:482
  310.8 7.0 %collective-permute-start.26 = (bf16[32,2176]{1,0:T(8,128)(2,1)S(1)}, bf16[32,2176]{1,0:T(8,128)(2,1)S(1)}, u32[]{:S(2)}, u32[]{:S(2)}) collective-permute-start(bf16[32,2176]{1,0:T(8,128)(2,1)S(1)} %two_sum.1.refs_5_.refs_1_), channel_id=1, source_target_pairs={{0,3},{1,0},{2,1},{3,2},{4,7},{5,4},{6,5},{7,6},{8,11},{9,8},{10,9... | collective-permute-start | bytes 417800 | tf_op jit(solution)/shard_map/ppermute | solution.py:482
  (8 other events, 6.0 us)
Sparse Core Ops, SparseCore 0:
  127.9 95.6 reduce-scatter.1
  226.3 87.0 all-gather.2

commit v5 on v4

--- a/solution.py
+++ b/solution.py
@@ -202,7 +202,8 @@
     tokens, cots = refs[:owners], refs[owners : 2 * owners]
     rest = refs[2 * owners :]
     sent_ref, hidden_ref, slope_ref, silu_ref, win_ref, wout_ref = rest[:6]
-    sums, (grow_ref, gg_ref, crow, weight, gret, gpre) = rest[6:-6], rest[-6:]
+    sums, (gpre_ref, gg_ref, crow, weight, gret) = rest[6:-5], rest[-5:]
+    gpre = gpre_ref.at[0]
     width, half = win_ref.shape[1], wout_ref.shape[1]
     seq = cots[0].shape[0]
     expert = id_ref[0] * local + first + pl.program_id(0)
@@ -230,8 +231,6 @@
     for d in range(owners):
         part = dots[d * capacity : (d + 1) * capacity]
         gg_ref[0, d : d + 1, :] = jnp.sum(jnp.where(place == places[d], part, 0.0), 0, keepdims=True)
-    for t in range(0, width, tile):
-        grow_ref[0, :, t : t + tile] = mm(gpre[...], win_ref[0, t : t + tile, :], ((1,), (1,))).astype(bf16)
     pieces = sums[0].shape[0] * len(sums)
     base = 0
     for left, right in ((sent_ref, gpre), (hidden_ref, gret)):
@@ -292,6 +291,41 @@
         def _():
             parts[t][:seq, :] = made
             parts[t][seq:, :] = mine.astype(bf16)
+
+
+def rows_kernel(local, capacity, owners, id_ref, *refs):
+    tokens, (gpre_ref, win_ref, dots_ref), parts, rows = (
+        refs[:owners], refs[owners : owners + 3], refs[owners + 3 : -1], refs[-1]
+    )
+    width = win_ref.shape[1]
+    seq = width // local
+    step = pl.program_id(0)
+    for t in range(0, width, 256):
+        rows[step, :, t : t + 256] = mm(gpre_ref[0], win_ref[0, t : t + 256, :], ((1,), (1,))).astype(bf16)
+
+    @pl.when(step == local - 1)
+    def _():
+        first = id_ref[0] * local
+        lane = lax.broadcasted_iota(jnp.int32, (seq, local * capacity), 1)
+        index = lax.broadcasted_iota(jnp.int32, (parts[0].shape[0] - seq, width), 0)
+        for d in range(owners):
+            table = [unpack(tokens[d], first + j, owners * local, seq)[0] for j in range(local)]
+            table.append(jnp.zeros((LANES - local, seq), f32))
+            columns = jnp.concatenate(table, 0).T.astype(jnp.int32)
+            hit = None
+            for j in range(local):
+                col = columns[:, j : j + 1]
+                same = lane == jnp.where(col < 0, -1, col + j * capacity)
+                hit = same if hit is None else hit | same
+            one = jnp.where(hit, 1.0, 0.0).astype(bf16)
+            span = slice(d * capacity, (d + 1) * capacity)
+            stacked = jnp.concatenate([rows[j, span, :] for j in range(local)], 0)
+            parts[d][:seq, :] = mm(one, stacked).astype(bf16)
+            line = jnp.concatenate([dots_ref[j, d : d + 1, :] for j in range(local)], 1)
+            high = line.astype(bf16).astype(f32)
+            mine = jnp.where(index == id_ref[0], high, 0.0)
+            mine = jnp.where(index == owners + id_ref[0], line - high, mine)
+            parts[d][seq:, :] = mine.astype(bf16)
 
 
 def hop_kernel(*refs):
@@ -584,16 +618,15 @@
             sum_specs = [pl.BlockSpec((groups, piece, width), lambda i: (0, i, 0))]
         return call(
             functools.partial(expert_backward, first, split, local, capacity, owners),
-            sums + [((count, places, width), bf16), ((count, owners, seq), f32)],
+            sums + [((count, places, 2 * half), bf16), ((count, owners, seq), f32)],
             ids, *packs, *cots, sent, hidden, slope, silu, expert_in, expert_out,
             grid=(count,),
             specs=[SMEM] + [VMEM] * (2 * owners) + [of(width), of(half), of(half), of(half)] + weights(first),
-            out_specs=sum_specs + [rows_of(width), pl.BlockSpec((1, owners, seq), lambda i: (i, 0, 0))],
+            out_specs=sum_specs + [rows_of(2 * half), pl.BlockSpec((1, owners, seq), lambda i: (i, 0, 0))],
             scratch=[
                 pltpu.VMEM((places, width), bf16),
                 pltpu.VMEM((places, 1), f32),
                 pltpu.VMEM((places, width), bf16),
-                pltpu.VMEM((places, 2 * half), bf16),
             ],
             deps=deps, us=8 * count, name=f"expert_backward{first}",
         )
@@ -612,7 +645,13 @@
 
     sums, *grads = backward(0, local, False)
     mine = lax.psum_scatter(sums, "group", scatter_dimension=0, tiled=False)
-    parts = combine([grads[0]], [grads[1]], (), "combine_grad")
+    parts = call(
+        functools.partial(rows_kernel, local, capacity, owners),
+        [((seq + tail, width), bf16)] * owners,
+        ids, *packs, grads[0], expert_in, grads[1],
+        grid=(local,), specs=[SMEM] + [VMEM] * owners + [rows_of(2 * half), weights(0)[0], VMEM],
+        scratch=[pltpu.VMEM((local, places, width), bf16)], us=14, name="expert_rows",
+    )
     if owners == 4:
         near_by = [
             lax.ppermute(parts[2], "expert", [(2, 1), (3, 2)]),

time: 342 us -> 338 us (0.988)
  waiting for transfers between devices: 141 us -> 136 us
    ppermute x4, waiting for transfers between devices: 42.8 us -> 38.4 us  [swap(): lax.ppermute(x, 'group', [(i, i ^ 1 << (steps - stage if i % 2 else 1 + s...]
  transfers between devices with their start and end apart: 33 -> 33, of which waited for: 18 -> 18; matrix products, arithmetic and copies ran while one was open for 1% -> 1% of each run, Pallas kernels for 21% -> 24%
where the time goes in v5:
time: 338 us; the launch traced here: 337 us
  waiting for transfers between devices  136 us (40%)
  Pallas kernels  117 us (35%)
  starting transfers between devices  55.4 us (16%)
  between operations  15 us (4%)
  local copies, waits for them, and re-layouts  10.5 us (3%)
    pallas_call x23, Pallas kernels, call(): pl.pallas_call(body, out_shape=outs, compiler_params=pltpu.CompilerParams...  117 us
    ppermute x18, waiting for transfers between devices, ring(): lax.ppermute(x, 'expert', [(i, (i + d) % owners) for i in range(owners)])  66.9 us
    ppermute x4, waiting for transfers between devices, swap(): lax.ppermute(x, 'group', [(i, i ^ 1 << (steps - stage if i % 2 else 1 + s...  38.4 us
    ppermute x18, starting transfers between devices, ring(): lax.ppermute(x, 'expert', [(i, (i + d) % owners) for i in range(owners)])  33.6 us
    ppermute x2, waiting for transfers between devices, far(): down = lax.ppermute(after, 'expert', [(1, 0), (2, 1)])  14.7 us
    ppermute x1, waiting for transfers between devices, on_device(): lax.ppermute(parts[2], 'expert', [(0, 1), (1, 2)])  10.7 us
    unnamed x47, local copies, waits for them, and re-layouts  9.22 us
  transfers between devices with their start and end apart: 33, of which 18 were waited for; matrix products, arithmetic and copies ran while one was open for 1% of the time, Pallas kernels for 24%

profile of v5, /device:TPU:0, one launch (start us, length us, event | category | flops | bytes accessed | tf_op | source)
XLA Modules:
  0.0 337.1 jit_solution(6754153988036335459)
XLA Ops:
  7.2 3.1 collective-permute-start
  10.3 2.1 collective-permute-start.1
  13.0 8.5 %dense_forward.1 = (bf16[256,1024]{1,0:T(8,128)(2,1)}, bf16[256,1024]{1,0:T(8,128)(2,1)}, bf16[256,1024]{1,0:T(8,128)(2,1)}, bf16[256,1024]{1,0:T(8,128)(2,1)}, ...) custom-call(s32[1]{0:T(128)S(6)} %copy.37.refs_0_.refs_1_, ...), custom_call_target="tpu_custom_call" | custom-call | bytes 32400000 | tf_op jit(solution)/shard_map/dense_forward/pallas_call | solution.py:52
  21.6 3.8 %collective-permute-done.refs_1_.refs_0_ = bf16[256,1024]{1,0:T(8,128)(2,1)S(1)} collective-permute-done((bf16[256,1024]{1,0:T(8,128)(2,1)}, bf16[256,1024]{1,0:T(8,128)(2,1)S(1)}, u32[]{:S(2)}, u32[]{:S(2)}) %collective-permute-start) | collective-permute-done | bytes 524320 | tf_op jit(solution)/shard_map/ppermute | solution.py:516
  25.3 9.8 %collective-permute-done.1.refs_2_.refs_1_ = bf16[256,1024]{1,0:T(8,128)(2,1)S(1)} collective-permute-done((bf16[256,1024]{1,0:T(8,128)(2,1)}, bf16[256,1024]{1,0:T(8,128)(2,1)S(1)}, u32[]{:S(2)}, u32[]{:S(2)}) %collective-permute-start.1) | collective-permute-done | bytes 524320 | tf_op jit(solution)/shard_map/ppermute | solution.py:516
  37.1 2.7 collective-permute-start.4
  39.7 13.7 %collective-permute-done.2.refs_2_ = bf16[272,1024]{1,0:T(8,128)(2,1)S(1)} collective-permute-done((bf16[272,1024]{1,0:T(8,128)(2,1)}, bf16[272,1024]{1,0:T(8,128)(2,1)S(1)}, u32[]{:S(2)}, u32[]{:S(2)}) %collective-permute-start.2) | collective-permute-done | bytes 557088 | tf_op jit(solution)/shard_map/ppermute | solution.py:516
  54.2 9.3 %collective-permute-done.4.refs_4_ = bf16[272,1024]{1,0:T(8,128)(2,1)S(1)} collective-permute-done((bf16[272,1024]{1,0:T(8,128)(2,1)}, bf16[272,1024]{1,0:T(8,128)(2,1)S(1)}, u32[]{:S(2)}, u32[]{:S(2)}) %collective-permute-start.4) | collective-permute-done | bytes 557088 | tf_op jit(solution)/shard_map/ppermute | solution.py:516
  63.5 1.3 collective-permute-start.5
  64.8 14.7 %collective-permute-done.5 = bf16[272,1024]{1,0:T(8,128)(2,1)S(1)} collective-permute-done((bf16[272,1024]{1,0:T(8,128)(2,1)S(1)}, bf16[272,1024]{1,0:T(8,128)(2,1)S(1)}, u32[]{:S(2)}, u32[]{:S(2)}) %collective-permute-start.5) | collective-permute-done | bytes 557088 | tf_op jit(solution)/shard_map/ppermute | solution.py:534
  81.1 1.5 collective-permute-start.7
  83.2 15.7 %expert_forward.1 = (bf16[4,640,1024]{2,1,0:T(8,128)(2,1)}, bf16[4,640,512]{2,1,0:T(8,128)(2,1)}, bf16[4,640,512]{2,1,0:T(8,128)(2,1)}, bf16[4,640,512]{2,1,0:T(8,128)(2,1)}, bf16[4,640,1024]{2,1,0:T(8,128)(2,1)}) custom-call(s32[3]{0:T(128)} %pad_add_fusion.2.refs_0_, bf16[272,1024]{1,0:T(8,128)(2,1)} %tokens_go.1.refs_1_.refs_10_, ...), custom_call_target="tpu_custom_call" | custom-call | bytes 61200000 | tf_op jit(solution)/shard_map/expert_forward/pallas_call | solution.py:52
  99.8 23.3 %expert_backward0.1 = (bf16[8,768,1024]{2,1,0:T(8,128)(2,1)}, bf16[4,640,1024]{2,1,0:T(8,128)(2,1)}, f32[4,4,256]{2,1,0:T(4,128)}) custom-call(s32[3]{0:T(128)} %pad_add_fusion.2.refs_0_, bf16[272,1024]{1,0:T(8,128)(2,1)} %tokens_go.1.refs_1_.refs_10_, bf16[272,1024]{1,0:T(8,128)(2,1)} %copy-done.15, bf16[272,1024]{1,0:T(8,128)(2,1)} %broadcast_select_fusion.refs_3_.refs_2_, ...), custom_call_target="tpu_custom_call" | custom-call | bytes 115200000 | tf_op jit(solution)/shard_map/expert_backward0/pallas_call | solution.py:52
  123.1 14.1 %expert_rows.1 = (bf16[272,1024]{1,0:T(8,128)(2,1)}, bf16[272,1024]{1,0:T(8,128)(2,1)}, bf16[272,1024]{1,0:T(8,128)(2,1)}, bf16[272,1024]{1,0:T(8,128)(2,1)}) custom-call(s32[3]{0:T(128)} %pad_add_fusion.2.refs_0_, bf16[272,1024]{1,0:T(8,128)(2,1)} %tokens_go.1.refs_1_.refs_10_, bf16[272,1024]{1,0:T(8,128)(2,1)} %copy-done.15, ...), custom_call_target="tpu_custom_call" | custom-call | bytes 50400000 | tf_op jit(solution)/shard_map/expert_rows/pallas_call | solution.py:52
  137.9 5.5 %collective-permute-start.9 = (bf16[272,1024]{1,0:T(8,128)(2,1)}, bf16[272,1024]{1,0:T(8,128)(2,1)S(1)}, u32[]{:S(2)}, u32[]{:S(2)}) collective-permute-start(bf16[272,1024]{1,0:T(8,128)(2,1)} %get-tuple-element.86), channel_id=1, source_target_pairs={{0,1},{1,2},{4,5},{5,6},{8,9},{9,10},{12,13},{13,14},{16,17},{17,1... | collective-permute-start | bytes 1671176 | tf_op jit(solution)/shard_map/ppermute | solution.py:658
  143.4 10.7 %collective-permute-done.9.refs_3_ = bf16[272,1024]{1,0:T(8,128)(2,1)S(1)} collective-permute-done((bf16[272,1024]{1,0:T(8,128)(2,1)}, bf16[272,1024]{1,0:T(8,128)(2,1)S(1)}, u32[]{:S(2)}, u32[]{:S(2)}) %collective-permute-start.9) | collective-permute-done | bytes 557088 | tf_op jit(solution)/shard_map/ppermute | solution.py:658
  154.9 2.7 hop.1
  157.6 2.4 collective-permute-start.11
  160.0 8.1 %combine_out.1.refs_23_.refs_0_ = bf16[4,256,1024]{2,1,0:T(8,128)(2,1)} custom-call(s32[3]{0:T(128)} %pad_add_fusion.2.refs_0_, bf16[272,1024]{1,0:T(8,128)(2,1)} %tokens_go.1.refs_1_.refs_10_, bf16[272,1024]{1,0:T(8,128)(2,1)} %copy-done.15, bf16[272,1024]{1,0:T(8,128)(2,1)} %broadcast_select_fusion.refs_3_.refs_2_, bf16[272,1024]{1,0:T(8,128)(2,1)} %copy-done.16, ...), custom_call_target="tpu_custom_call" | custom-call | bytes 28800000 | tf_op jit(solution)/shard_map/combine_out/pallas_call | solution.py:52
  168.1 3.8 %collective-permute-done.10.refs_3_ = bf16[272,1024]{1,0:T(8,128)(2,1)S(1)} collective-permute-done((bf16[272,1024]{1,0:T(8,128)(2,1)}, bf16[272,1024]{1,0:T(8,128)(2,1)S(1)}, u32[]{:S(2)}, u32[]{:S(2)}) %collective-permute-start.10) | collective-permute-done | bytes 557088 | tf_op jit(solution)/shard_map/ppermute | solution.py:516
  171.9 13.2 %collective-permute-done.11.refs_4_ = bf16[272,1024]{1,0:T(8,128)(2,1)S(1)} collective-permute-done((bf16[272,1024]{1,0:T(8,128)(2,1)}, bf16[272,1024]{1,0:T(8,128)(2,1)S(1)}, u32[]{:S(2)}, u32[]{:S(2)}) %collective-permute-start.11) | collective-permute-done | bytes 557088 | tf_op jit(solution)/shard_map/ppermute | solution.py:516
  185.9 18.5 %dense_backward.1 = (f32[256,1024]{1,0:T(8,128)}, bf16[4,128,1152]{2,1,0:T(8,128)(2,1)}, bf16[4,128,1152]{2,1,0:T(8,128)(2,1)}, bf16[4,128,2176]{2,1,0:T(8,128)(2,1)}, bf16[4,128,2176]{2,1,0:T(8,128)(2,1)}) custom-call(s32[3]{0:T(128)} %pad_add_fusion.2.refs_0_, s32[1]{0:T(128)S(6)} %copy.37.refs_0_.refs_1_, bf16[272,1024]{1,0:T(8,128)(2,1)} %get-tuple-element.88.refs_2_, ...), custom_call_target="tpu_custom_call" | custom-call | bytes 64800000 | tf_op jit(solution)/shard_map/dense_backward/pallas_call | solution.py:52
  204.9 5.7 %collective-permute-done.13.refs_2_.refs_4_ = bf16[4,128,1152]{2,1,0:T(8,128)(2,1)S(1)} collective-permute-done((bf16[4,128,1152]{2,1,0:T(8,128)(2,1)}, bf16[4,128,1152]{2,1,0:T(8,128)(2,1)S(1)}, u32[]{:S(2)}, u32[]{:S(2)}) %collective-permute-start.13) | collective-permute-done | bytes 1179680 | tf_op jit(solution)/shard_map/ppermute | solution.py:519
  212.6 1.5 collective-permute-start.15
  217.9 4.6 %collective-permute-done.15.refs_1_.refs_2_.refs_4_ = bf16[2,128,1152]{2,1,0:T(8,128)(2,1)S(1)} collective-permute-done((bf16[2,128,1152]{2,1,0:T(8,128)(2,1)S(1)}, bf16[2,128,1152]{2,1,0:T(8,128)(2,1)S(1)}, u32[]{:S(2)}, u32[]{:S(2)}) %collective-permute-start.15) | collective-permute-done | bytes 589856 | tf_op jit(solution)/shard_map/ppermute | solution.py:522
  223.4 4.6 %all-to-all-start = ((bf16[4,256,1024]{2,1,0:T(8,128)(2,1)}), bf16[4,256,1024]{2,1,0:T(8,128)(2,1)}, u32[]{:S(2)}, u32[]{:S(2)}) async-start(bf16[4,256,1024]{2,1,0:T(8,128)(2,1)} %returned_go.1.refs_5_), calls=%async_computation | async-start | bytes 4194304 | tf_op jit(solution)/shard_map/all_to_all | solution.py:669
  228.0 1.5 collective-permute-start.14
  231.5 1.6 collective-permute-start.16
  233.1 14.5 %collective-permute-done.16.refs_2_ = bf16[1,128,1152]{2,1,0:T(8,128)(2,1)S(1)} collective-permute-done((bf16[1,128,1152]{2,1,0:T(8,128)(2,1)S(1)}, bf16[1,128,1152]{2,1,0:T(8,128)(2,1)S(1)}, u32[]{:S(2)}, u32[]{:S(2)}) %collective-permute-start.16) | collective-permute-done | bytes 294944 | tf_op jit(solution)/shard_map/ppermute | solution.py:522
  248.2 15.6 %collective-permute-done.14.refs_2_.refs_4_ = bf16[2,128,2176]{2,1,0:T(8,128)(2,1)S(1)} collective-permute-done((bf16[2,128,2176]{2,1,0:T(8,128)(2,1)}, bf16[2,128,2176]{2,1,0:T(8,128)(2,1)S(1)}, u32[]{:S(2)}, u32[]{:S(2)}) %collective-permute-start.14) | collective-permute-done | bytes 1114144 | tf_op jit(solution)/shard_map/ppermute | solution.py:522
  264.7 1.6 collective-permute-start.17
  266.3 1.9 collective-permute-start.18
  268.2 2.4 collective-permute-start.19
  270.6 1.5 collective-permute-start.20
  272.8 8.7 %collective-permute-done.19.refs_2_ = bf16[32,1152]{1,0:T(8,128)(2,1)S(1)} collective-permute-done((bf16[32,1152]{1,0:T(8,128)(2,1)S(1)}, bf16[32,1152]{1,0:T(8,128)(2,1)S(1)}, u32[]{:S(2)}, u32[]{:S(2)}) %collective-permute-start.19) | collective-permute-done | bytes 73760 | tf_op jit(solution)/shard_map/ppermute | solution.py:516
  281.5 3.8 %collective-permute-done.17.refs_2_ = bf16[1,128,2176]{2,1,0:T(8,128)(2,1)S(1)} collective-permute-done((bf16[1,128,2176]{2,1,0:T(8,128)(2,1)S(1)}, bf16[1,128,2176]{2,1,0:T(8,128)(2,1)S(1)}, u32[]{:S(2)}, u32[]{:S(2)}) %collective-permute-start.17) | collective-permute-done | bytes 557088 | tf_op jit(solution)/shard_map/ppermute | solution.py:522
  286.0 1.8 collective-permute-start.21
  287.8 2.4 collective-permute-start.22
  290.2 1.5 collective-permute-start.23
  293.5 2.4 collective-permute-start.29
  295.9 3.9 %output.1 = (f32[256,1024]{1,0:T(8,128)}, f32[8,128]{1,0:T(8,128)}) custom-call(f32[256,1024]{1,0:T(8,128)} %get-tuple-element.73.refs_8_.refs_0_, bf16[4,256,1024]{2,1,0:T(8,128)(2,1)} %all-to-all-done.refs_1_, f32[8,128]{1,0:T(8,128)} %copy-done.11), custom_call_target="tpu_custom_call" | custom-call | bytes 14400000 | tf_op jit(solution)/shard_map/output/pallas_call | solution.py:52
  299.8 1.3 collective-permute-done.22.refs_2_
  301.9 5.0 %collective-permute-start.24 = (bf16[32,2176]{1,0:T(8,128)(2,1)S(1)}, bf16[32,2176]{1,0:T(8,128)(2,1)S(1)}, u32[]{:S(2)}, u32[]{:S(2)}) collective-permute-start(bf16[32,2176]{1,0:T(8,128)(2,1)S(1)} %two_sum.1.refs_5_.refs_1_), channel_id=1, source_target_pairs={{0,1},{1,2},{2,3},{3,0},{4,5},{5,6},{6,7},{7,4},{8,9},{9,10},{10,1... | collective-permute-start | bytes 417800 | tf_op jit(solution)/shard_map/ppermute | solution.py:516
  306.9 2.4 collective-permute-start.26
  309.3 1.4 one_finish.1
  312.1 1.7 collective-permute-done.25.refs_3_
  313.8 1.6 two_finish.1
  316.1 14.2 %widen.1 = (f32[4,1024,1024]{2,1,0:T(8,128)}, f32[4,512,1024]{2,1,0:T(8,128)}, f32[8,128]{1,0:T(8,128)}) custom-call(bf16[8,768,1024]{2,1,0:T(8,128)(2,1)} %bitcast.19, f32[128,128]{1,0:T(8,128)} %copy-done.9), custom_call_target="tpu_custom_call" | custom-call | bytes 43200000 | tf_op jit(solution)/shard_map/widen/pallas_call | solution.py:52
  (98 shorter events, 24.8 us)
Async XLA Ops:
  7.2 215.3 %reduce-scatter.2.cloned.1.call-start = ((), (), s32[]{:S(2)}) async-start(), calls=%async_computation.2 | async-start | bytes 14155776 | tf_op jit(solution)/shard_map/reduce_scatter | solution.py:647
  7.2 18.1 %collective-permute-start = (bf16[256,1024]{1,0:T(8,128)(2,1)}, bf16[256,1024]{1,0:T(8,128)(2,1)S(1)}, u32[]{:S(2)}, u32[]{:S(2)}) collective-permute-start(bf16[256,1024]{1,0:T(8,128)(2,1)} %refs_7_.1), channel_id=1, source_target_pairs={{0,1},{1,2},{2,3},{3,0},{4,5},{5,6},{6,7},{7,4},{8,9},{9,10},{10,1... | collective-permute-start | bytes 1572872 | tf_op jit(solution)/shard_map/ppermute | solution.py:516
  10.3 24.8 %collective-permute-start.1 = (bf16[256,1024]{1,0:T(8,128)(2,1)}, bf16[256,1024]{1,0:T(8,128)(2,1)S(1)}, u32[]{:S(2)}, u32[]{:S(2)}) collective-permute-start(bf16[256,1024]{1,0:T(8,128)(2,1)} %refs_7_.1), channel_id=1, source_target_pairs={{0,3},{1,0},{2,1},{3,2},{4,7},{5,4},{6,5},{7,6},{8,11},{9,8},{10,9... | collective-permute-start | bytes 1572872 | tf_op jit(solution)/shard_map/ppermute | solution.py:516
  25.3 9.8 %copy-start.17 = (bf16[256,1024]{1,0:T(8,128)(2,1)}, bf16[256,1024]{1,0:T(8,128)(2,1)S(1)}, u32[]{:S(2)}) copy-start(bf16[256,1024]{1,0:T(8,128)(2,1)S(1)} %collective-permute-done.refs_1_.refs_0_) | copy-start | bytes 1572868
  35.9 17.6 %collective-permute-start.2 = (bf16[272,1024]{1,0:T(8,128)(2,1)}, bf16[272,1024]{1,0:T(8,128)(2,1)S(1)}, u32[]{:S(2)}, u32[]{:S(2)}) collective-permute-start(bf16[272,1024]{1,0:T(8,128)(2,1)} %tokens_go.1.refs_1_.refs_10_), channel_id=1, source_target_pairs={{0,1},{1,2},{2,3},{3,0},{4,5},{5,6},{6,7},{7,4},{8,9},{9,10},{10,1... | collective-permute-start | bytes 1671176 | tf_op jit(solution)/shard_map/ppermute | solution.py:516
  37.1 26.4 %collective-permute-start.4 = (bf16[272,1024]{1,0:T(8,128)(2,1)}, bf16[272,1024]{1,0:T(8,128)(2,1)S(1)}, u32[]{:S(2)}, u32[]{:S(2)}) collective-permute-start(bf16[272,1024]{1,0:T(8,128)(2,1)} %tokens_go.1.refs_1_.refs_10_), channel_id=1, source_target_pairs={{0,3},{1,0},{2,1},{3,2},{4,7},{5,4},{6,5},{7,6},{8,11},{9,8},{10,9... | collective-permute-start | bytes 1671176 | tf_op jit(solution)/shard_map/ppermute | solution.py:516
  53.5 29.7 %copy-start.15 = (bf16[272,1024]{1,0:T(8,128)(2,1)}, bf16[272,1024]{1,0:T(8,128)(2,1)S(1)}, u32[]{:S(2)}) copy-start(bf16[272,1024]{1,0:T(8,128)(2,1)S(1)} %collective-permute-done.2.refs_2_) | copy-start | bytes 1671172
  53.5 11.3 %collective-permute-start.3 = (bf16[272,1024]{1,0:T(8,128)(2,1)S(1)}, bf16[272,1024]{1,0:T(8,128)(2,1)S(1)}, u32[]{:S(2)}, u32[]{:S(2)}) collective-permute-start(bf16[272,1024]{1,0:T(8,128)(2,1)S(1)} %collective-permute-done.2.refs_2_), channel_id=1, source_target_pairs={{1,2},{2,3},{5,6},{6,7},{9,10},{10,11},{13,14},{14,15},{17,18},{18... | collective-permute-start | bytes 1671176 | tf_op jit(solution)/shard_map/ppermute | solution.py:533
  63.5 19.7 %copy-start.16 = (bf16[272,1024]{1,0:T(8,128)(2,1)}, bf16[272,1024]{1,0:T(8,128)(2,1)S(1)}, u32[]{:S(2)}) copy-start(bf16[272,1024]{1,0:T(8,128)(2,1)S(1)} %collective-permute-done.4.refs_4_) | copy-start | bytes 1671172
  63.5 16.0 %collective-permute-start.5 = (bf16[272,1024]{1,0:T(8,128)(2,1)S(1)}, bf16[272,1024]{1,0:T(8,128)(2,1)S(1)}, u32[]{:S(2)}, u32[]{:S(2)}) collective-permute-start(bf16[272,1024]{1,0:T(8,128)(2,1)S(1)} %collective-permute-done.4.refs_4_), channel_id=1, source_target_pairs={{1,0},{2,1},{5,4},{6,5},{9,8},{10,9},{13,12},{14,13},{17,16},{18,1... | collective-permute-start | bytes 1671176 | tf_op jit(solution)/shard_map/ppermute | solution.py:534
  80.4 18.5 %collective-permute-start.6 = (bf16[256,1024]{1,0:T(8,128)(2,1)}, bf16[256,1024]{1,0:T(8,128)(2,1)S(1)}, u32[]{:S(2)}, u32[]{:S(2)}) collective-permute-start(bf16[256,1024]{1,0:T(8,128)(2,1)} %get-tuple-element.76.refs_6_), channel_id=1, source_target_pairs={{1,2},{2,3},{5,6},{6,7},{9,10},{10,11},{13,14},{14,15},{17,18},{18... | collective-permute-start | bytes 1572872 | tf_op jit(solution)/shard_map/ppermute | solution.py:533
  81.1 17.8 %collective-permute-start.7 = (bf16[256,1024]{1,0:T(8,128)(2,1)}, bf16[256,1024]{1,0:T(8,128)(2,1)S(1)}, u32[]{:S(2)}, u32[]{:S(2)}) collective-permute-start(bf16[256,1024]{1,0:T(8,128)(2,1)} %get-tuple-element.77.refs_8_), channel_id=1, source_target_pairs={{1,0},{2,1},{5,4},{6,5},{9,8},{10,9},{13,12},{14,13},{17,16},{18,1... | collective-permute-start | bytes 1572872 | tf_op jit(solution)/shard_map/ppermute | solution.py:534
  123.1 193.0 %all-gather.3.cloned.1.call-start = ((), (), s32[]{:S(2)}) async-start(), calls=%async_computation.3 | async-start | bytes 14155776 | tf_op jit(solution)/shard_map/all_gather | solution.py:697
  137.2 6.2 %collective-permute-start.8 = (bf16[272,1024]{1,0:T(8,128)(2,1)}, bf16[272,1024]{1,0:T(8,128)(2,1)S(1)}, u32[]{:S(2)}, u32[]{:S(2)}) collective-permute-start(bf16[272,1024]{1,0:T(8,128)(2,1)} %get-tuple-element.86), channel_id=1, source_target_pairs={{2,1},{3,2},{6,5},{7,6},{10,9},{11,10},{14,13},{15,14},{18,17},{19... | collective-permute-start | bytes 1671176 | tf_op jit(solution)/shard_map/ppermute | solution.py:657
  137.9 16.2 %collective-permute-start.9 = (bf16[272,1024]{1,0:T(8,128)(2,1)}, bf16[272,1024]{1,0:T(8,128)(2,1)S(1)}, u32[]{:S(2)}, u32[]{:S(2)}) collective-permute-start(bf16[272,1024]{1,0:T(8,128)(2,1)} %get-tuple-element.86), channel_id=1, source_target_pairs={{0,1},{1,2},{4,5},{5,6},{8,9},{9,10},{12,13},{13,14},{16,17},{17,1... | collective-permute-start | bytes 1671176 | tf_op jit(solution)/shard_map/ppermute | solution.py:658
  143.4 10.7 %copy-start.21 = (bf16[272,1024]{1,0:T(8,128)(2,1)}, bf16[272,1024]{1,0:T(8,128)(2,1)S(1)}, u32[]{:S(2)}) copy-start(bf16[272,1024]{1,0:T(8,128)(2,1)S(1)} %collective-permute-done.8.refs_2_) | copy-start | bytes 1671172
  157.6 14.3 %collective-permute-start.10 = (bf16[272,1024]{1,0:T(8,128)(2,1)}, bf16[272,1024]{1,0:T(8,128)(2,1)S(1)}, u32[]{:S(2)}, u32[]{:S(2)}) collective-permute-start(bf16[272,1024]{1,0:T(8,128)(2,1)} %get-tuple-element.87.refs_6_), channel_id=1, source_target_pairs={{0,3},{1,0},{2,1},{3,2},{4,7},{5,4},{6,5},{7,6},{8,11},{9,8},{10,9... | collective-permute-start | bytes 1671176 | tf_op jit(solution)/shard_map/ppermute | solution.py:516
  157.6 27.5 %collective-permute-start.11 = (bf16[272,1024]{1,0:T(8,128)(2,1)}, bf16[272,1024]{1,0:T(8,128)(2,1)S(1)}, u32[]{:S(2)}, u32[]{:S(2)}) collective-permute-start(bf16[272,1024]{1,0:T(8,128)(2,1)} %get-tuple-element.89), channel_id=1, source_target_pairs={{0,1},{1,2},{2,3},{3,0},{4,5},{5,6},{6,7},{7,4},{8,9},{9,10},{10,1... | collective-permute-start | bytes 1671176 | tf_op jit(solution)/shard_map/ppermute | solution.py:516
  171.9 13.2 %copy-start.19 = (bf16[272,1024]{1,0:T(8,128)(2,1)}, bf16[272,1024]{1,0:T(8,128)(2,1)S(1)}, u32[]{:S(2)}) copy-start(bf16[272,1024]{1,0:T(8,128)(2,1)S(1)} %collective-permute-done.10.refs_3_) | copy-start | bytes 1671172
  204.4 9.7 %collective-permute-start.12 = (bf16[4,128,2176]{2,1,0:T(8,128)(2,1)}, bf16[4,128,2176]{2,1,0:T(8,128)(2,1)S(1)}, u32[]{:S(2)}, u32[]{:S(2)}) collective-permute-start(bf16[4,128,2176]{2,1,0:T(8,128)(2,1)} %get-tuple-element.99), channel_id=1, source_target_pairs={{0,4},{4,0},{8,12},{12,8},{16,20},{20,16},{24,28},{28,24},{1,5},{5... | collective-permute-start | bytes 6684680 | tf_op jit(solution)/shard_map/ppermute | solution.py:519
  204.4 6.2 %collective-permute-start.13 = (bf16[4,128,1152]{2,1,0:T(8,128)(2,1)}, bf16[4,128,1152]{2,1,0:T(8,128)(2,1)S(1)}, u32[]{:S(2)}, u32[]{:S(2)}) collective-permute-start(bf16[4,128,1152]{2,1,0:T(8,128)(2,1)} %get-tuple-element.97.refs_1_), channel_id=1, source_target_pairs={{0,4},{4,0},{8,12},{12,8},{16,20},{20,16},{24,28},{28,24},{1,5},{5... | collective-permute-start | bytes 3538952 | tf_op jit(solution)/shard_map/ppermute | solution.py:519
  204.9 5.7 %copy-start.4 = (bf16[4,128,1152]{2,1,0:T(8,128)(2,1)S(1)}, bf16[4,128,1152]{2,1,0:T(8,128)(2,1)}, u32[]{:S(2)}) copy-start(bf16[4,128,1152]{2,1,0:T(8,128)(2,1)} %get-tuple-element.100.refs_1_.refs_3_) | copy-start | bytes 3538948
  210.6 3.5 %copy-start.1 = (bf16[4,128,2176]{2,1,0:T(8,128)(2,1)S(1)}, bf16[4,128,2176]{2,1,0:T(8,128)(2,1)}, u32[]{:S(2)}) copy-start(bf16[4,128,2176]{2,1,0:T(8,128)(2,1)} %get-tuple-element.98.refs_1_.refs_3_) | copy-start | bytes 6684676
  212.6 9.9 %collective-permute-start.15 = (bf16[2,128,1152]{2,1,0:T(8,128)(2,1)S(1)}, bf16[2,128,1152]{2,1,0:T(8,128)(2,1)S(1)}, u32[]{:S(2)}, u32[]{:S(2)}) collective-permute-start(bf16[2,128,1152]{2,1,0:T(8,128)(2,1)S(1)} %get-tuple-element.105), channel_id=1, source_target_pairs={{0,8},{4,20},{8,0},{12,28},{16,24},{20,4},{24,16},{28,12},{1,9},{5... | collective-permute-start | bytes 1769480 | tf_op jit(solution)/shard_map/ppermute | solution.py:522
  215.3 1.0 copy-start.5
  216.9 1.0 copy-start.14
  223.4 6.2 %copy-start = (bf16[768,1024]{1,0:T(8,128)(2,1)S(1)}, bf16[768,1024]{1,0:T(8,128)(2,1)}, u32[]{:S(2)}) copy-start(bf16[768,1024]{1,0:T(8,128)(2,1)} %gather_go.1.refs_5_) | copy-start | bytes 4718596
  223.4 6.2 %copy-start.3 = (bf16[2,128,1152]{2,1,0:T(8,128)(2,1)S(1)}, bf16[2,128,1152]{2,1,0:T(8,128)(2,1)}, u32[]{:S(2)}) copy-start(bf16[2,128,1152]{2,1,0:T(8,128)(2,1)} %copy-done.2) | copy-start | bytes 1769476
  223.4 72.5 %all-to-all-start = ((bf16[4,256,1024]{2,1,0:T(8,128)(2,1)}), bf16[4,256,1024]{2,1,0:T(8,128)(2,1)}, u32[]{:S(2)}, u32[]{:S(2)}) async-start(bf16[4,256,1024]{2,1,0:T(8,128)(2,1)} %returned_go.1.refs_5_), calls=%async_computation | async-start | bytes 4194304 | tf_op jit(solution)/shard_map/all_to_all | solution.py:669
  228.0 19.6 %copy-start.10 = (s32[3]{0:T(128)S(1)}, s32[3]{0:T(128)}, u32[]{:S(2)}) copy-start(s32[3]{0:T(128)} %pad_add_fusion.2.refs_0_) | copy-start | bytes 40
  228.0 35.8 %collective-permute-start.14 = (bf16[2,128,2176]{2,1,0:T(8,128)(2,1)}, bf16[2,128,2176]{2,1,0:T(8,128)(2,1)S(1)}, u32[]{:S(2)}, u32[]{:S(2)}) collective-permute-start(bf16[2,128,2176]{2,1,0:T(8,128)(2,1)} %copy-done.14), channel_id=1, source_target_pairs={{0,8},{4,20},{8,0},{12,28},{16,24},{20,4},{24,16},{28,12},{1,9},{5... | collective-permute-start | bytes 3342344 | tf_op jit(solution)/shard_map/ppermute | solution.py:522
  229.6 1.2 copy-start.8
  230.7 33.1 %copy-start.6 = (bf16[2,128,2176]{2,1,0:T(8,128)(2,1)S(1)}, bf16[2,128,2176]{2,1,0:T(8,128)(2,1)}, u32[]{:S(2)}) copy-start(bf16[2,128,2176]{2,1,0:T(8,128)(2,1)} %copy-done.5) | copy-start | bytes 3342340
  231.5 16.1 %collective-permute-start.16 = (bf16[1,128,1152]{2,1,0:T(8,128)(2,1)S(1)}, bf16[1,128,1152]{2,1,0:T(8,128)(2,1)S(1)}, u32[]{:S(2)}, u32[]{:S(2)}) collective-permute-start(bf16[1,128,1152]{2,1,0:T(8,128)(2,1)S(1)} %get-tuple-element.109), channel_id=1, source_target_pairs={{0,16},{4,12},{8,24},{12,4},{16,0},{20,28},{24,8},{28,20},{1,17},{... | collective-permute-start | bytes 884744 | tf_op jit(solution)/shard_map/ppermute | solution.py:522
  264.7 20.6 %collective-permute-start.17 = (bf16[1,128,2176]{2,1,0:T(8,128)(2,1)S(1)}, bf16[1,128,2176]{2,1,0:T(8,128)(2,1)S(1)}, u32[]{:S(2)}, u32[]{:S(2)}) collective-permute-start(bf16[1,128,2176]{2,1,0:T(8,128)(2,1)S(1)} %get-tuple-element.113), channel_id=1, source_target_pairs={{0,16},{4,12},{8,24},{12,4},{16,0},{20,28},{24,8},{28,20},{1,17},{... | collective-permute-start | bytes 1671176 | tf_op jit(solution)/shard_map/ppermute | solution.py:522
  266.3 6.5 %collective-permute-start.18 = (bf16[32,1152]{1,0:T(8,128)(2,1)S(1)}, bf16[32,1152]{1,0:T(8,128)(2,1)S(1)}, u32[]{:S(2)}, u32[]{:S(2)}) collective-permute-start(bf16[32,1152]{1,0:T(8,128)(2,1)S(1)} %get-tuple-element.115), channel_id=1, source_target_pairs={{0,1},{1,2},{2,3},{3,0},{4,5},{5,6},{6,7},{7,4},{8,9},{9,10},{10,1... | collective-permute-start | bytes 221192 | tf_op jit(solution)/shard_map/ppermute | solution.py:516
  268.2 13.3 %collective-permute-start.19 = (bf16[32,1152]{1,0:T(8,128)(2,1)S(1)}, bf16[32,1152]{1,0:T(8,128)(2,1)S(1)}, u32[]{:S(2)}, u32[]{:S(2)}) collective-permute-start(bf16[32,1152]{1,0:T(8,128)(2,1)S(1)} %get-tuple-element.116), channel_id=1, source_target_pairs={{0,2},{1,3},{2,0},{3,1},{4,6},{5,7},{6,4},{7,5},{8,10},{9,11},{10,... | collective-permute-start | bytes 221192 | tf_op jit(solution)/shard_map/ppermute | solution.py:516
  270.6 10.9 %collective-permute-start.20 = (bf16[32,1152]{1,0:T(8,128)(2,1)S(1)}, bf16[32,1152]{1,0:T(8,128)(2,1)S(1)}, u32[]{:S(2)}, u32[]{:S(2)}) collective-permute-start(bf16[32,1152]{1,0:T(8,128)(2,1)S(1)} %get-tuple-element.117), channel_id=1, source_target_pairs={{0,3},{1,0},{2,1},{3,2},{4,7},{5,4},{6,5},{7,6},{8,11},{9,8},{10,9... | collective-permute-start | bytes 221192 | tf_op jit(solution)/shard_map/ppermute | solution.py:516
  286.0 7.5 %copy-start.11 = (f32[8,128]{1,0:T(8,128)}, f32[8,128]{1,0:T(8,128)S(1)}, u32[]{:S(2)}) copy-start(f32[8,128]{1,0:T(8,128)S(1)} %get-tuple-element.119.refs_2_) | copy-start | bytes 12292
  286.0 7.5 %collective-permute-start.21 = (bf16[32,2176]{1,0:T(8,128)(2,1)S(1)}, bf16[32,2176]{1,0:T(8,128)(2,1)S(1)}, u32[]{:S(2)}, u32[]{:S(2)}) collective-permute-start(bf16[32,2176]{1,0:T(8,128)(2,1)S(1)} %get-tuple-element.123), channel_id=1, source_target_pairs={{0,1},{1,2},{2,3},{3,0},{4,5},{5,6},{6,7},{7,4},{8,9},{9,10},{10,1... | collective-permute-start | bytes 417800 | tf_op jit(solution)/shard_map/ppermute | solution.py:516
  287.8 13.3 %collective-permute-start.22 = (bf16[32,2176]{1,0:T(8,128)(2,1)S(1)}, bf16[32,2176]{1,0:T(8,128)(2,1)S(1)}, u32[]{:S(2)}, u32[]{:S(2)}) collective-permute-start(bf16[32,2176]{1,0:T(8,128)(2,1)S(1)} %get-tuple-element.124), channel_id=1, source_target_pairs={{0,2},{1,3},{2,0},{3,1},{4,6},{5,7},{6,4},{7,5},{8,10},{9,11},{10,... | collective-permute-start | bytes 417800 | tf_op jit(solution)/shard_map/ppermute | solution.py:516
  290.2 10.9 %collective-permute-start.23 = (bf16[32,2176]{1,0:T(8,128)(2,1)S(1)}, bf16[32,2176]{1,0:T(8,128)(2,1)S(1)}, u32[]{:S(2)}, u32[]{:S(2)}) collective-permute-start(bf16[32,2176]{1,0:T(8,128)(2,1)S(1)} %get-tuple-element.125), channel_id=1, source_target_pairs={{0,3},{1,0},{2,1},{3,2},{4,7},{5,4},{6,5},{7,6},{8,11},{9,8},{10,9... | collective-permute-start | bytes 417800 | tf_op jit(solution)/shard_map/ppermute | solution.py:516
  291.7 15.2 %collective-permute-start.27 = (bf16[32,1152]{1,0:T(8,128)(2,1)S(1)}, bf16[32,1152]{1,0:T(8,128)(2,1)S(1)}, u32[]{:S(2)}, u32[]{:S(2)}) collective-permute-start(bf16[32,1152]{1,0:T(8,128)(2,1)S(1)} %one_sum.1.refs_3_.refs_1_), channel_id=1, source_target_pairs={{0,1},{1,2},{2,3},{3,0},{4,5},{5,6},{6,7},{7,4},{8,9},{9,10},{10,1... | collective-permute-start | bytes 221192 | tf_op jit(solution)/shard_map/ppermute | solution.py:516
  292.2 17.1 %collective-permute-start.28 = (bf16[32,1152]{1,0:T(8,128)(2,1)S(1)}, bf16[32,1152]{1,0:T(8,128)(2,1)S(1)}, u32[]{:S(2)}, u32[]{:S(2)}) collective-permute-start(bf16[32,1152]{1,0:T(8,128)(2,1)S(1)} %one_sum.1.refs_3_.refs_1_), channel_id=1, source_target_pairs={{0,2},{1,3},{2,0},{3,1},{4,6},{5,7},{6,4},{7,5},{8,10},{9,11},{10,... | collective-permute-start | bytes 221192 | tf_op jit(solution)/shard_map/ppermute | solution.py:516
  293.5 15.8 %collective-permute-start.29 = (bf16[32,1152]{1,0:T(8,128)(2,1)S(1)}, bf16[32,1152]{1,0:T(8,128)(2,1)S(1)}, u32[]{:S(2)}, u32[]{:S(2)}) collective-permute-start(bf16[32,1152]{1,0:T(8,128)(2,1)S(1)} %one_sum.1.refs_3_.refs_1_), channel_id=1, source_target_pairs={{0,3},{1,0},{2,1},{3,2},{4,7},{5,4},{6,5},{7,6},{8,11},{9,8},{10,9... | collective-permute-start | bytes 221192 | tf_op jit(solution)/shard_map/ppermute | solution.py:516
  301.9 10.2 %collective-permute-start.24 = (bf16[32,2176]{1,0:T(8,128)(2,1)S(1)}, bf16[32,2176]{1,0:T(8,128)(2,1)S(1)}, u32[]{:S(2)}, u32[]{:S(2)}) collective-permute-start(bf16[32,2176]{1,0:T(8,128)(2,1)S(1)} %two_sum.1.refs_5_.refs_1_), channel_id=1, source_target_pairs={{0,1},{1,2},{2,3},{3,0},{4,5},{5,6},{6,7},{7,4},{8,9},{9,10},{10,1... | collective-permute-start | bytes 417800 | tf_op jit(solution)/shard_map/ppermute | solution.py:516
  306.9 7.0 %collective-permute-start.25 = (bf16[32,2176]{1,0:T(8,128)(2,1)S(1)}, bf16[32,2176]{1,0:T(8,128)(2,1)S(1)}, u32[]{:S(2)}, u32[]{:S(2)}) collective-permute-start(bf16[32,2176]{1,0:T(8,128)(2,1)S(1)} %two_sum.1.refs_5_.refs_1_), channel_id=1, source_target_pairs={{0,2},{1,3},{2,0},{3,1},{4,6},{5,7},{6,4},{7,5},{8,10},{9,11},{10,... | collective-permute-start | bytes 417800 | tf_op jit(solution)/shard_map/ppermute | solution.py:516
  306.9 7.0 %collective-permute-start.26 = (bf16[32,2176]{1,0:T(8,128)(2,1)S(1)}, bf16[32,2176]{1,0:T(8,128)(2,1)S(1)}, u32[]{:S(2)}, u32[]{:S(2)}) collective-permute-start(bf16[32,2176]{1,0:T(8,128)(2,1)S(1)} %two_sum.1.refs_5_.refs_1_), channel_id=1, source_target_pairs={{0,3},{1,0},{2,1},{3,2},{4,7},{5,4},{6,5},{7,6},{8,11},{9,8},{10,9... | collective-permute-start | bytes 417800 | tf_op jit(solution)/shard_map/ppermute | solution.py:516
  (8 other events, 6.0 us)
Sparse Core Ops, SparseCore 0:
  123.2 92.9 reduce-scatter.1
  223.5 86.7 all-gather.2

commit v6 on v5

--- a/solution.py
+++ b/solution.py
@@ -674,7 +674,7 @@
         [((seq, width), f32)] + [((groups // 2, width // groups, sum(cols)), bf16) for cols in sizes for _ in range(2)],
         ids, lengths, *grad_parts, gates, inputs, cotangent, residual, n1, pack, q, kk, vv, lse, mixed,
         query_matrix, key_matrix, value_matrix, w_attn_out, router, gain_one, gain_two,
-        smem=2, deps=deps, us=18, name="dense_backward",
+        smem=2, deps=deps, us=18, vmem=44, name="dense_backward",
         scratch=[
             pltpu.VMEM((experts, seq), f32),
             pltpu.VMEM((seq, width), bf16),

time: 338 us -> 337 us (level)
    unnamed x47 -> x77, local copies, waits for them, and re-layouts: 9.22 us -> 10.6 us
  transfers between devices with their start and end apart: 33 -> 33, of which waited for: 18 -> 18; matrix products, arithmetic and copies ran while one was open for 1% -> 1% of each run, Pallas kernels for 24% -> 23%
where the time goes in v6:
time: 337 us; the launch traced here: 336 us
  waiting for transfers between devices  137 us (41%)
  Pallas kernels  116 us (34%)
  starting transfers between devices  54.3 us (16%)
  between operations  15.2 us (5%)
  local copies, waits for them, and re-layouts  11.9 us (4%)
    pallas_call x23, Pallas kernels, call(): pl.pallas_call(body, out_shape=outs, compiler_params=pltpu.CompilerParams...  116 us
    ppermute x18, waiting for transfers between devices, ring(): lax.ppermute(x, 'expert', [(i, (i + d) % owners) for i in range(owners)])  68.6 us
    ppermute x4, waiting for transfers between devices, swap(): lax.ppermute(x, 'group', [(i, i ^ 1 << (steps - stage if i % 2 else 1 + s...  37.4 us
    ppermute x18, starting transfers between devices, ring(): lax.ppermute(x, 'expert', [(i, (i + d) % owners) for i in range(owners)])  32.3 us
    ppermute x2, waiting for transfers between devices, far(): down = lax.ppermute(after, 'expert', [(1, 0), (2, 1)])  14.7 us
    ppermute x1, waiting for transfers between devices, on_device(): lax.ppermute(parts[2], 'expert', [(0, 1), (1, 2)])  10.6 us
    unnamed x77, local copies, waits for them, and re-layouts  10.6 us
  transfers between devices with their start and end apart: 33, of which 18 were waited for; matrix products, arithmetic and copies ran while one was open for 1% of the time, Pallas kernels for 23%

profile of v6, /device:TPU:0, one launch (start us, length us, event | category | flops | bytes accessed | tf_op | source)
XLA Modules:
  0.0 336.4 jit_solution(1457773384279760449)
XLA Ops:
  7.2 3.1 collective-permute-start
  10.3 2.1 collective-permute-start.1
  13.0 8.5 %dense_forward.1 = (bf16[256,1024]{1,0:T(8,128)(2,1)}, bf16[256,1024]{1,0:T(8,128)(2,1)}, bf16[256,1024]{1,0:T(8,128)(2,1)}, bf16[256,1024]{1,0:T(8,128)(2,1)}, ...) custom-call(s32[1]{0:T(128)S(6)} %copy.37.refs_0_.refs_1_, ...), custom_call_target="tpu_custom_call" | custom-call | bytes 32400000 | tf_op jit(solution)/shard_map/dense_forward/pallas_call | solution.py:52
  21.6 3.8 %collective-permute-done.refs_1_.refs_0_ = bf16[256,1024]{1,0:T(8,128)(2,1)S(1)} collective-permute-done((bf16[256,1024]{1,0:T(8,128)(2,1)}, bf16[256,1024]{1,0:T(8,128)(2,1)S(1)}, u32[]{:S(2)}, u32[]{:S(2)}) %collective-permute-start) | collective-permute-done | bytes 524320 | tf_op jit(solution)/shard_map/ppermute | solution.py:516
  25.3 9.8 %collective-permute-done.1.refs_2_.refs_1_ = bf16[256,1024]{1,0:T(8,128)(2,1)S(1)} collective-permute-done((bf16[256,1024]{1,0:T(8,128)(2,1)}, bf16[256,1024]{1,0:T(8,128)(2,1)S(1)}, u32[]{:S(2)}, u32[]{:S(2)}) %collective-permute-start.1) | collective-permute-done | bytes 524320 | tf_op jit(solution)/shard_map/ppermute | solution.py:516
  37.0 2.7 collective-permute-start.4
  39.7 13.7 %collective-permute-done.2.refs_2_ = bf16[272,1024]{1,0:T(8,128)(2,1)S(1)} collective-permute-done((bf16[272,1024]{1,0:T(8,128)(2,1)}, bf16[272,1024]{1,0:T(8,128)(2,1)S(1)}, u32[]{:S(2)}, u32[]{:S(2)}) %collective-permute-start.2) | collective-permute-done | bytes 557088 | tf_op jit(solution)/shard_map/ppermute | solution.py:516
  54.2 9.3 %collective-permute-done.4.refs_4_ = bf16[272,1024]{1,0:T(8,128)(2,1)S(1)} collective-permute-done((bf16[272,1024]{1,0:T(8,128)(2,1)}, bf16[272,1024]{1,0:T(8,128)(2,1)S(1)}, u32[]{:S(2)}, u32[]{:S(2)}) %collective-permute-start.4) | collective-permute-done | bytes 557088 | tf_op jit(solution)/shard_map/ppermute | solution.py:516
  64.8 14.7 %collective-permute-done.5 = bf16[272,1024]{1,0:T(8,128)(2,1)S(1)} collective-permute-done((bf16[272,1024]{1,0:T(8,128)(2,1)S(1)}, bf16[272,1024]{1,0:T(8,128)(2,1)S(1)}, u32[]{:S(2)}, u32[]{:S(2)}) %collective-permute-start.5) | collective-permute-done | bytes 557088 | tf_op jit(solution)/shard_map/ppermute | solution.py:534
  81.0 1.5 collective-permute-start.7
  83.2 15.7 %expert_forward.1 = (bf16[4,640,1024]{2,1,0:T(8,128)(2,1)}, bf16[4,640,512]{2,1,0:T(8,128)(2,1)}, bf16[4,640,512]{2,1,0:T(8,128)(2,1)}, bf16[4,640,512]{2,1,0:T(8,128)(2,1)}, bf16[4,640,1024]{2,1,0:T(8,128)(2,1)}) custom-call(s32[3]{0:T(128)} %pad_add_fusion.2.refs_0_, bf16[272,1024]{1,0:T(8,128)(2,1)} %tokens_go.1.refs_1_.refs_10_, ...), custom_call_target="tpu_custom_call" | custom-call | bytes 61200000 | tf_op jit(solution)/shard_map/expert_forward/pallas_call | solution.py:52
  99.7 23.3 %expert_backward0.1 = (bf16[8,768,1024]{2,1,0:T(8,128)(2,1)}, bf16[4,640,1024]{2,1,0:T(8,128)(2,1)}, f32[4,4,256]{2,1,0:T(4,128)}) custom-call(s32[3]{0:T(128)} %pad_add_fusion.2.refs_0_, bf16[272,1024]{1,0:T(8,128)(2,1)} %tokens_go.1.refs_1_.refs_10_, bf16[272,1024]{1,0:T(8,128)(2,1)} %copy-done.32, bf16[272,1024]{1,0:T(8,128)(2,1)} %broadcast_select_fusion.refs_3_.refs_2_, ...), custom_call_target="tpu_custom_call" | custom-call | bytes 115200000 | tf_op jit(solution)/shard_map/expert_backward0/pallas_call | solution.py:52
  123.1 14.1 %expert_rows.1 = (bf16[272,1024]{1,0:T(8,128)(2,1)}, bf16[272,1024]{1,0:T(8,128)(2,1)}, bf16[272,1024]{1,0:T(8,128)(2,1)}, bf16[272,1024]{1,0:T(8,128)(2,1)}) custom-call(s32[3]{0:T(128)} %pad_add_fusion.2.refs_0_, bf16[272,1024]{1,0:T(8,128)(2,1)} %tokens_go.1.refs_1_.refs_10_, bf16[272,1024]{1,0:T(8,128)(2,1)} %copy-done.32, ...), custom_call_target="tpu_custom_call" | custom-call | bytes 50400000 | tf_op jit(solution)/shard_map/expert_rows/pallas_call | solution.py:52
  137.9 5.5 %collective-permute-start.9 = (bf16[272,1024]{1,0:T(8,128)(2,1)}, bf16[272,1024]{1,0:T(8,128)(2,1)S(1)}, u32[]{:S(2)}, u32[]{:S(2)}) collective-permute-start(bf16[272,1024]{1,0:T(8,128)(2,1)} %get-tuple-element.86), channel_id=1, source_target_pairs={{0,1},{1,2},{4,5},{5,6},{8,9},{9,10},{12,13},{13,14},{16,17},{17,1... | collective-permute-start | bytes 1671176 | tf_op jit(solution)/shard_map/ppermute | solution.py:658
  143.4 10.6 %collective-permute-done.9.refs_3_ = bf16[272,1024]{1,0:T(8,128)(2,1)S(1)} collective-permute-done((bf16[272,1024]{1,0:T(8,128)(2,1)}, bf16[272,1024]{1,0:T(8,128)(2,1)S(1)}, u32[]{:S(2)}, u32[]{:S(2)}) %collective-permute-start.9) | collective-permute-done | bytes 557088 | tf_op jit(solution)/shard_map/ppermute | solution.py:658
  154.9 2.7 hop.1
  157.6 2.4 collective-permute-start.11
  160.2 8.4 %combine_out.1.refs_23_.refs_0_ = bf16[4,256,1024]{2,1,0:T(8,128)(2,1)} custom-call(s32[3]{0:T(128)} %pad_add_fusion.2.refs_0_, bf16[272,1024]{1,0:T(8,128)(2,1)} %tokens_go.1.refs_1_.refs_10_, bf16[272,1024]{1,0:T(8,128)(2,1)} %copy-done.32, bf16[272,1024]{1,0:T(8,128)(2,1)} %broadcast_select_fusion.refs_3_.refs_2_, bf16[272,1024]{1,0:T(8,128)(2,1)} %copy-done.33, ...), custom_call_target="tpu_custom_call" | custom-call | bytes 28800000 | tf_op jit(solution)/shard_map/combine_out/pallas_call | solution.py:52
  168.6 3.3 collective-permute-done.10.refs_3_
  171.9 13.2 %collective-permute-done.11.refs_4_ = bf16[272,1024]{1,0:T(8,128)(2,1)S(1)} collective-permute-done((bf16[272,1024]{1,0:T(8,128)(2,1)}, bf16[272,1024]{1,0:T(8,128)(2,1)S(1)}, u32[]{:S(2)}, u32[]{:S(2)}) %collective-permute-start.11) | collective-permute-done | bytes 557088 | tf_op jit(solution)/shard_map/ppermute | solution.py:516
  187.3 16.3 %dense_backward.1 = (f32[256,1024]{1,0:T(8,128)}, bf16[4,128,1152]{2,1,0:T(8,128)(2,1)}, bf16[4,128,1152]{2,1,0:T(8,128)(2,1)}, bf16[4,128,2176]{2,1,0:T(8,128)(2,1)}, bf16[4,128,2176]{2,1,0:T(8,128)(2,1)}) custom-call(s32[3]{0:T(128)S(1)} %copy-done.24, s32[1]{0:T(128)S(6)} %copy.37.refs_0_.refs_1_, bf16[272,1024]{1,0:T(8,128)(2,1)S(1)} %copy-done.15, ...), custom_call_target="tpu_custom_call" | custom-call | bytes 64800000 | tf_op jit(solution)/shard_map/dense_backward/pallas_call | solution.py:52
  204.2 5.7 %collective-permute-done.13.refs_2_.refs_4_ = bf16[4,128,1152]{2,1,0:T(8,128)(2,1)S(1)} collective-permute-done((bf16[4,128,1152]{2,1,0:T(8,128)(2,1)}, bf16[4,128,1152]{2,1,0:T(8,128)(2,1)S(1)}, u32[]{:S(2)}, u32[]{:S(2)}) %collective-permute-start.13) | collective-permute-done | bytes 1179680 | tf_op jit(solution)/shard_map/ppermute | solution.py:519
  211.9 1.5 collective-permute-start.15
  217.2 4.6 %collective-permute-done.15.refs_1_.refs_2_.refs_4_ = bf16[2,128,1152]{2,1,0:T(8,128)(2,1)S(1)} collective-permute-done((bf16[2,128,1152]{2,1,0:T(8,128)(2,1)S(1)}, bf16[2,128,1152]{2,1,0:T(8,128)(2,1)S(1)}, u32[]{:S(2)}, u32[]{:S(2)}) %collective-permute-start.15) | collective-permute-done | bytes 589856 | tf_op jit(solution)/shard_map/ppermute | solution.py:522
  222.7 4.6 %all-to-all-start = ((bf16[4,256,1024]{2,1,0:T(8,128)(2,1)}), bf16[4,256,1024]{2,1,0:T(8,128)(2,1)}, u32[]{:S(2)}, u32[]{:S(2)}) async-start(bf16[4,256,1024]{2,1,0:T(8,128)(2,1)} %returned_go.1.refs_5_), calls=%async_computation | async-start | bytes 4194304 | tf_op jit(solution)/shard_map/all_to_all | solution.py:669
  227.3 1.6 collective-permute-start.14
  230.8 1.8 collective-permute-start.16
  232.6 14.1 %collective-permute-done.16.refs_2_ = bf16[1,128,1152]{2,1,0:T(8,128)(2,1)S(1)} collective-permute-done((bf16[1,128,1152]{2,1,0:T(8,128)(2,1)S(1)}, bf16[1,128,1152]{2,1,0:T(8,128)(2,1)S(1)}, u32[]{:S(2)}, u32[]{:S(2)}) %collective-permute-start.16) | collective-permute-done | bytes 294944 | tf_op jit(solution)/shard_map/ppermute | solution.py:522
  247.3 15.7 %collective-permute-done.14.refs_2_.refs_4_ = bf16[2,128,2176]{2,1,0:T(8,128)(2,1)S(1)} collective-permute-done((bf16[2,128,2176]{2,1,0:T(8,128)(2,1)}, bf16[2,128,2176]{2,1,0:T(8,128)(2,1)S(1)}, u32[]{:S(2)}, u32[]{:S(2)}) %collective-permute-start.14) | collective-permute-done | bytes 1114144 | tf_op jit(solution)/shard_map/ppermute | solution.py:522
  264.0 1.6 collective-permute-start.17
  265.6 1.8 collective-permute-start.18
  267.4 2.4 collective-permute-start.19
  269.8 1.5 collective-permute-start.20
  272.0 8.8 %collective-permute-done.19.refs_2_ = bf16[32,1152]{1,0:T(8,128)(2,1)S(1)} collective-permute-done((bf16[32,1152]{1,0:T(8,128)(2,1)S(1)}, bf16[32,1152]{1,0:T(8,128)(2,1)S(1)}, u32[]{:S(2)}, u32[]{:S(2)}) %collective-permute-start.19) | collective-permute-done | bytes 73760 | tf_op jit(solution)/shard_map/ppermute | solution.py:516
  280.8 2.9 collective-permute-done.17.refs_2_
  284.5 2.0 collective-permute-start.21
  286.5 2.3 collective-permute-start.22
  288.8 1.5 collective-permute-start.23
  291.5 1.4 collective-permute-done.21.refs_1_
  292.9 1.3 collective-permute-start.29
  294.2 3.9 %output.1 = (f32[256,1024]{1,0:T(8,128)}, f32[8,128]{1,0:T(8,128)}) custom-call(f32[256,1024]{1,0:T(8,128)} %get-tuple-element.73.refs_8_.refs_0_, bf16[4,256,1024]{2,1,0:T(8,128)(2,1)} %all-to-all-done.refs_1_, f32[8,128]{1,0:T(8,128)} %copy-done.28), custom_call_target="tpu_custom_call" | custom-call | bytes 14400000 | tf_op jit(solution)/shard_map/output/pallas_call | solution.py:52
  298.1 1.7 collective-permute-done.22.refs_2_
  300.5 3.5 %collective-permute-start.24 = (bf16[32,2176]{1,0:T(8,128)(2,1)S(1)}, bf16[32,2176]{1,0:T(8,128)(2,1)S(1)}, u32[]{:S(2)}, u32[]{:S(2)}) collective-permute-start(bf16[32,2176]{1,0:T(8,128)(2,1)S(1)} %two_sum.1.refs_5_.refs_1_), channel_id=1, source_target_pairs={{0,1},{1,2},{2,3},{3,0},{4,5},{5,6},{6,7},{7,4},{8,9},{9,10},{10,1... | collective-permute-start | bytes 417800 | tf_op jit(solution)/shard_map/ppermute | solution.py:516
  304.0 2.6 collective-permute-start.25
  307.5 1.4 one_finish.1
  310.3 2.9 collective-permute-done.25.refs_3_
  313.2 1.6 two_finish.1
  315.4 14.2 %widen.1 = (f32[4,1024,1024]{2,1,0:T(8,128)}, f32[4,512,1024]{2,1,0:T(8,128)}, f32[8,128]{1,0:T(8,128)}) custom-call(bf16[8,768,1024]{2,1,0:T(8,128)(2,1)} %bitcast.25, f32[128,128]{1,0:T(8,128)} %copy-done.21), custom_call_target="tpu_custom_call" | custom-call | bytes 43200000 | tf_op jit(solution)/shard_map/widen/pallas_call | solution.py:52
  (128 shorter events, 27.7 us)
Async XLA Ops:
  7.2 214.6 %reduce-scatter.2.cloned.1.call-start = ((), (), s32[]{:S(2)}) async-start(), calls=%async_computation.2 | async-start | bytes 14155776 | tf_op jit(solution)/shard_map/reduce_scatter | solution.py:647
  7.2 18.1 %collective-permute-start = (bf16[256,1024]{1,0:T(8,128)(2,1)}, bf16[256,1024]{1,0:T(8,128)(2,1)S(1)}, u32[]{:S(2)}, u32[]{:S(2)}) collective-permute-start(bf16[256,1024]{1,0:T(8,128)(2,1)} %refs_7_.1), channel_id=1, source_target_pairs={{0,1},{1,2},{2,3},{3,0},{4,5},{5,6},{6,7},{7,4},{8,9},{9,10},{10,1... | collective-permute-start | bytes 1572872 | tf_op jit(solution)/shard_map/ppermute | solution.py:516
  10.3 24.8 %collective-permute-start.1 = (bf16[256,1024]{1,0:T(8,128)(2,1)}, bf16[256,1024]{1,0:T(8,128)(2,1)S(1)}, u32[]{:S(2)}, u32[]{:S(2)}) collective-permute-start(bf16[256,1024]{1,0:T(8,128)(2,1)} %refs_7_.1), channel_id=1, source_target_pairs={{0,3},{1,0},{2,1},{3,2},{4,7},{5,4},{6,5},{7,6},{8,11},{9,8},{10,9... | collective-permute-start | bytes 1572872 | tf_op jit(solution)/shard_map/ppermute | solution.py:516
  35.9 17.6 %collective-permute-start.2 = (bf16[272,1024]{1,0:T(8,128)(2,1)}, bf16[272,1024]{1,0:T(8,128)(2,1)S(1)}, u32[]{:S(2)}, u32[]{:S(2)}) collective-permute-start(bf16[272,1024]{1,0:T(8,128)(2,1)} %tokens_go.1.refs_1_.refs_10_), channel_id=1, source_target_pairs={{0,1},{1,2},{2,3},{3,0},{4,5},{5,6},{6,7},{7,4},{8,9},{9,10},{10,1... | collective-permute-start | bytes 1671176 | tf_op jit(solution)/shard_map/ppermute | solution.py:516
  37.0 26.4 %collective-permute-start.4 = (bf16[272,1024]{1,0:T(8,128)(2,1)}, bf16[272,1024]{1,0:T(8,128)(2,1)S(1)}, u32[]{:S(2)}, u32[]{:S(2)}) collective-permute-start(bf16[272,1024]{1,0:T(8,128)(2,1)} %tokens_go.1.refs_1_.refs_10_), channel_id=1, source_target_pairs={{0,3},{1,0},{2,1},{3,2},{4,7},{5,4},{6,5},{7,6},{8,11},{9,8},{10,9... | collective-permute-start | bytes 1671176 | tf_op jit(solution)/shard_map/ppermute | solution.py:516
  53.5 29.7 %copy-start.32 = (bf16[272,1024]{1,0:T(8,128)(2,1)}, bf16[272,1024]{1,0:T(8,128)(2,1)S(1)}, u32[]{:S(2)}) copy-start(bf16[272,1024]{1,0:T(8,128)(2,1)S(1)} %collective-permute-done.2.refs_2_) | copy-start | bytes 1671172
  53.5 11.3 %collective-permute-start.3 = (bf16[272,1024]{1,0:T(8,128)(2,1)S(1)}, bf16[272,1024]{1,0:T(8,128)(2,1)S(1)}, u32[]{:S(2)}, u32[]{:S(2)}) collective-permute-start(bf16[272,1024]{1,0:T(8,128)(2,1)S(1)} %collective-permute-done.2.refs_2_), channel_id=1, source_target_pairs={{1,2},{2,3},{5,6},{6,7},{9,10},{10,11},{13,14},{14,15},{17,18},{18... | collective-permute-start | bytes 1671176 | tf_op jit(solution)/shard_map/ppermute | solution.py:533
  63.5 16.0 %collective-permute-start.5 = (bf16[272,1024]{1,0:T(8,128)(2,1)S(1)}, bf16[272,1024]{1,0:T(8,128)(2,1)S(1)}, u32[]{:S(2)}, u32[]{:S(2)}) collective-permute-start(bf16[272,1024]{1,0:T(8,128)(2,1)S(1)} %collective-permute-done.4.refs_4_), channel_id=1, source_target_pairs={{1,0},{2,1},{5,4},{6,5},{9,8},{10,9},{13,12},{14,13},{17,16},{18,1... | collective-permute-start | bytes 1671176 | tf_op jit(solution)/shard_map/ppermute | solution.py:534
  80.4 18.5 %collective-permute-start.6 = (bf16[256,1024]{1,0:T(8,128)(2,1)}, bf16[256,1024]{1,0:T(8,128)(2,1)S(1)}, u32[]{:S(2)}, u32[]{:S(2)}) collective-permute-start(bf16[256,1024]{1,0:T(8,128)(2,1)} %get-tuple-element.76.refs_6_), channel_id=1, source_target_pairs={{1,2},{2,3},{5,6},{6,7},{9,10},{10,11},{13,14},{14,15},{17,18},{18... | collective-permute-start | bytes 1572872 | tf_op jit(solution)/shard_map/ppermute | solution.py:533
  81.0 17.8 %collective-permute-start.7 = (bf16[256,1024]{1,0:T(8,128)(2,1)}, bf16[256,1024]{1,0:T(8,128)(2,1)S(1)}, u32[]{:S(2)}, u32[]{:S(2)}) collective-permute-start(bf16[256,1024]{1,0:T(8,128)(2,1)} %get-tuple-element.77.refs_8_), channel_id=1, source_target_pairs={{1,0},{2,1},{5,4},{6,5},{9,8},{10,9},{13,12},{14,13},{17,16},{18,1... | collective-permute-start | bytes 1572872 | tf_op jit(solution)/shard_map/ppermute | solution.py:534
  123.1 192.3 %all-gather.3.cloned.1.call-start = ((), (), s32[]{:S(2)}) async-start(), calls=%async_computation.3 | async-start | bytes 14155776 | tf_op jit(solution)/shard_map/all_gather | solution.py:697
  137.2 6.2 %collective-permute-start.8 = (bf16[272,1024]{1,0:T(8,128)(2,1)}, bf16[272,1024]{1,0:T(8,128)(2,1)S(1)}, u32[]{:S(2)}, u32[]{:S(2)}) collective-permute-start(bf16[272,1024]{1,0:T(8,128)(2,1)} %get-tuple-element.86), channel_id=1, source_target_pairs={{2,1},{3,2},{6,5},{7,6},{10,9},{11,10},{14,13},{15,14},{18,17},{19... | collective-permute-start | bytes 1671176 | tf_op jit(solution)/shard_map/ppermute | solution.py:657
  137.9 16.2 %collective-permute-start.9 = (bf16[272,1024]{1,0:T(8,128)(2,1)}, bf16[272,1024]{1,0:T(8,128)(2,1)S(1)}, u32[]{:S(2)}, u32[]{:S(2)}) collective-permute-start(bf16[272,1024]{1,0:T(8,128)(2,1)} %get-tuple-element.86), channel_id=1, source_target_pairs={{0,1},{1,2},{4,5},{5,6},{8,9},{9,10},{12,13},{13,14},{16,17},{17,1... | collective-permute-start | bytes 1671176 | tf_op jit(solution)/shard_map/ppermute | solution.py:658
  157.6 14.2 %collective-permute-start.10 = (bf16[272,1024]{1,0:T(8,128)(2,1)}, bf16[272,1024]{1,0:T(8,128)(2,1)S(1)}, u32[]{:S(2)}, u32[]{:S(2)}) collective-permute-start(bf16[272,1024]{1,0:T(8,128)(2,1)} %get-tuple-element.87.refs_6_), channel_id=1, source_target_pairs={{0,3},{1,0},{2,1},{3,2},{4,7},{5,4},{6,5},{7,6},{8,11},{9,8},{10,9... | collective-permute-start | bytes 1671176 | tf_op jit(solution)/shard_map/ppermute | solution.py:516
  157.6 27.4 %collective-permute-start.11 = (bf16[272,1024]{1,0:T(8,128)(2,1)}, bf16[272,1024]{1,0:T(8,128)(2,1)S(1)}, u32[]{:S(2)}, u32[]{:S(2)}) collective-permute-start(bf16[272,1024]{1,0:T(8,128)(2,1)} %get-tuple-element.89), channel_id=1, source_target_pairs={{0,1},{1,2},{2,3},{3,0},{4,5},{5,6},{6,7},{7,4},{8,9},{9,10},{10,1... | collective-permute-start | bytes 1671176 | tf_op jit(solution)/shard_map/ppermute | solution.py:516
  160.0 25.1 %copy-start = (bf16[272,1024]{1,0:T(8,128)(2,1)S(1)}, bf16[272,1024]{1,0:T(8,128)(2,1)}, u32[]{:S(2)}) copy-start(bf16[272,1024]{1,0:T(8,128)(2,1)} %tokens_go.1.refs_1_.refs_10_) | copy-start | bytes 1671172
  160.0 25.1 %copy-start.8 = (f32[256,1024]{1,0:T(8,128)S(1)}, f32[256,1024]{1,0:T(8,128)}, u32[]{:S(2)}) copy-start(f32[256,1024]{1,0:T(8,128)} %get-tuple-element.73.refs_8_.refs_0_) | copy-start | bytes 3145732
  160.0 25.1 %copy-start.9 = (bf16[1024,512]{1,0:T(8,128)(2,1)S(1)}, bf16[1024,512]{1,0:T(8,128)(2,1)}, u32[]{:S(2)}) copy-start(bf16[1024,512]{1,0:T(8,128)(2,1)} %refs_17_.1) | copy-start | bytes 3145732
  160.0 25.1 %copy-start.10 = (bf16[1024,512]{1,0:T(8,128)(2,1)S(1)}, bf16[1024,512]{1,0:T(8,128)(2,1)}, u32[]{:S(2)}) copy-start(bf16[1024,512]{1,0:T(8,128)(2,1)} %refs_18_.1) | copy-start | bytes 3145732
  160.0 25.1 %copy-start.13 = (bf16[256,1024]{1,0:T(8,128)(2,1)S(1)}, bf16[256,1024]{1,0:T(8,128)(2,1)}, u32[]{:S(2)}) copy-start(bf16[256,1024]{1,0:T(8,128)(2,1)} %refs_7_.1) | copy-start | bytes 1572868
  160.0 25.1 %copy-start.14 = (bf16[256,1024]{1,0:T(8,128)(2,1)S(1)}, bf16[256,1024]{1,0:T(8,128)(2,1)}, u32[]{:S(2)}) copy-start(bf16[256,1024]{1,0:T(8,128)(2,1)} %refs_6_.7) | copy-start | bytes 1572868
  160.0 25.1 %copy-start.15 = (bf16[272,1024]{1,0:T(8,128)(2,1)S(1)}, bf16[272,1024]{1,0:T(8,128)(2,1)}, u32[]{:S(2)}) copy-start(bf16[272,1024]{1,0:T(8,128)(2,1)} %get-tuple-element.88.refs_2_) | copy-start | bytes 1671172
  160.0 25.1 %copy-start.16 = (bf16[256,1024]{1,0:T(8,128)(2,1)S(1)}, bf16[256,1024]{1,0:T(8,128)(2,1)}, u32[]{:S(2)}) copy-start(bf16[256,1024]{1,0:T(8,128)(2,1)} %get-tuple-element.91.refs_9_) | copy-start | bytes 1572868
  160.1 25.1 %copy-start.17 = (bf16[256,1024]{1,0:T(8,128)(2,1)S(1)}, bf16[256,1024]{1,0:T(8,128)(2,1)}, u32[]{:S(2)}) copy-start(bf16[256,1024]{1,0:T(8,128)(2,1)} %get-tuple-element.92.refs_11_) | copy-start | bytes 1572868
  160.1 25.1 %copy-start.18 = (bf16[256,1024]{1,0:T(8,128)(2,1)S(1)}, bf16[256,1024]{1,0:T(8,128)(2,1)}, u32[]{:S(2)}) copy-start(bf16[256,1024]{1,0:T(8,128)(2,1)} %get-tuple-element.93.refs_12_) | copy-start | bytes 1572868
  160.1 25.1 %copy-start.22 = (f32[256,128]{1,0:T(8,128)S(1)}, f32[256,128]{1,0:T(8,128)}, u32[]{:S(2)}) copy-start(f32[256,128]{1,0:T(8,128)} %get-tuple-element.95.refs_14_) | copy-start | bytes 393220
  160.1 25.1 %copy-start.23 = (bf16[1024,16]{0,1:T(8,128)(2,1)S(1)}, bf16[1024,16]{0,1:T(8,128)(2,1)}, u32[]{:S(2)}) copy-start(bf16[1024,16]{0,1:T(8,128)(2,1)} %param.21) | copy-start | bytes 98308
  160.1 25.1 %copy-start.24 = (s32[3]{0:T(128)S(1)}, s32[3]{0:T(128)}, u32[]{:S(2)}) copy-start(s32[3]{0:T(128)} %pad_add_fusion.2.refs_0_) | copy-start | bytes 40
  203.7 9.8 %collective-permute-start.12 = (bf16[4,128,2176]{2,1,0:T(8,128)(2,1)}, bf16[4,128,2176]{2,1,0:T(8,128)(2,1)S(1)}, u32[]{:S(2)}, u32[]{:S(2)}) collective-permute-start(bf16[4,128,2176]{2,1,0:T(8,128)(2,1)} %get-tuple-element.99), channel_id=1, source_target_pairs={{0,4},{4,0},{8,12},{12,8},{16,20},{20,16},{24,28},{28,24},{1,5},{5... | collective-permute-start | bytes 6684680 | tf_op jit(solution)/shard_map/ppermute | solution.py:519
  203.7 6.2 %collective-permute-start.13 = (bf16[4,128,1152]{2,1,0:T(8,128)(2,1)}, bf16[4,128,1152]{2,1,0:T(8,128)(2,1)S(1)}, u32[]{:S(2)}, u32[]{:S(2)}) collective-permute-start(bf16[4,128,1152]{2,1,0:T(8,128)(2,1)} %get-tuple-element.97.refs_1_), channel_id=1, source_target_pairs={{0,4},{4,0},{8,12},{12,8},{16,20},{20,16},{24,28},{28,24},{1,5},{5... | collective-permute-start | bytes 3538952 | tf_op jit(solution)/shard_map/ppermute | solution.py:519
  211.9 9.9 %collective-permute-start.15 = (bf16[2,128,1152]{2,1,0:T(8,128)(2,1)S(1)}, bf16[2,128,1152]{2,1,0:T(8,128)(2,1)S(1)}, u32[]{:S(2)}, u32[]{:S(2)}) collective-permute-start(bf16[2,128,1152]{2,1,0:T(8,128)(2,1)S(1)} %get-tuple-element.105), channel_id=1, source_target_pairs={{0,8},{4,20},{8,0},{12,28},{16,24},{20,4},{24,16},{28,12},{1,9},{5... | collective-permute-start | bytes 1769480 | tf_op jit(solution)/shard_map/ppermute | solution.py:522
  222.7 71.5 %all-to-all-start = ((bf16[4,256,1024]{2,1,0:T(8,128)(2,1)}), bf16[4,256,1024]{2,1,0:T(8,128)(2,1)}, u32[]{:S(2)}, u32[]{:S(2)}) async-start(bf16[4,256,1024]{2,1,0:T(8,128)(2,1)} %returned_go.1.refs_5_), calls=%async_computation | async-start | bytes 4194304 | tf_op jit(solution)/shard_map/all_to_all | solution.py:669
  227.3 35.8 %collective-permute-start.14 = (bf16[2,128,2176]{2,1,0:T(8,128)(2,1)}, bf16[2,128,2176]{2,1,0:T(8,128)(2,1)S(1)}, u32[]{:S(2)}, u32[]{:S(2)}) collective-permute-start(bf16[2,128,2176]{2,1,0:T(8,128)(2,1)} %copy-done.31), channel_id=1, source_target_pairs={{0,8},{4,20},{8,0},{12,28},{16,24},{20,4},{24,16},{28,12},{1,9},{5... | collective-permute-start | bytes 3342344 | tf_op jit(solution)/shard_map/ppermute | solution.py:522
  230.0 33.0 %copy-start.7 = (bf16[2,128,2176]{2,1,0:T(8,128)(2,1)S(1)}, bf16[2,128,2176]{2,1,0:T(8,128)(2,1)}, u32[]{:S(2)}) copy-start(bf16[2,128,2176]{2,1,0:T(8,128)(2,1)} %copy-done.6) | copy-start | bytes 3342340
  230.8 15.9 %collective-permute-start.16 = (bf16[1,128,1152]{2,1,0:T(8,128)(2,1)S(1)}, bf16[1,128,1152]{2,1,0:T(8,128)(2,1)S(1)}, u32[]{:S(2)}, u32[]{:S(2)}) collective-permute-start(bf16[1,128,1152]{2,1,0:T(8,128)(2,1)S(1)} %get-tuple-element.109), channel_id=1, source_target_pairs={{0,16},{4,12},{8,24},{12,4},{16,0},{20,28},{24,8},{28,20},{1,17},{... | collective-permute-start | bytes 884744 | tf_op jit(solution)/shard_map/ppermute | solution.py:522
  264.0 19.8 %collective-permute-start.17 = (bf16[1,128,2176]{2,1,0:T(8,128)(2,1)S(1)}, bf16[1,128,2176]{2,1,0:T(8,128)(2,1)S(1)}, u32[]{:S(2)}, u32[]{:S(2)}) collective-permute-start(bf16[1,128,2176]{2,1,0:T(8,128)(2,1)S(1)} %get-tuple-element.113), channel_id=1, source_target_pairs={{0,16},{4,12},{8,24},{12,4},{16,0},{20,28},{24,8},{28,20},{1,17},{... | collective-permute-start | bytes 1671176 | tf_op jit(solution)/shard_map/ppermute | solution.py:522
  265.6 6.4 %collective-permute-start.18 = (bf16[32,1152]{1,0:T(8,128)(2,1)S(1)}, bf16[32,1152]{1,0:T(8,128)(2,1)S(1)}, u32[]{:S(2)}, u32[]{:S(2)}) collective-permute-start(bf16[32,1152]{1,0:T(8,128)(2,1)S(1)} %get-tuple-element.115), channel_id=1, source_target_pairs={{0,1},{1,2},{2,3},{3,0},{4,5},{5,6},{6,7},{7,4},{8,9},{9,10},{10,1... | collective-permute-start | bytes 221192 | tf_op jit(solution)/shard_map/ppermute | solution.py:516
  267.4 13.4 %collective-permute-start.19 = (bf16[32,1152]{1,0:T(8,128)(2,1)S(1)}, bf16[32,1152]{1,0:T(8,128)(2,1)S(1)}, u32[]{:S(2)}, u32[]{:S(2)}) collective-permute-start(bf16[32,1152]{1,0:T(8,128)(2,1)S(1)} %get-tuple-element.116), channel_id=1, source_target_pairs={{0,2},{1,3},{2,0},{3,1},{4,6},{5,7},{6,4},{7,5},{8,10},{9,11},{10,... | collective-permute-start | bytes 221192 | tf_op jit(solution)/shard_map/ppermute | solution.py:516
  269.8 11.0 %collective-permute-start.20 = (bf16[32,1152]{1,0:T(8,128)(2,1)S(1)}, bf16[32,1152]{1,0:T(8,128)(2,1)S(1)}, u32[]{:S(2)}, u32[]{:S(2)}) collective-permute-start(bf16[32,1152]{1,0:T(8,128)(2,1)S(1)} %get-tuple-element.117), channel_id=1, source_target_pairs={{0,3},{1,0},{2,1},{3,2},{4,7},{5,4},{6,5},{7,6},{8,11},{9,8},{10,9... | collective-permute-start | bytes 221192 | tf_op jit(solution)/shard_map/ppermute | solution.py:516
  284.5 8.4 %collective-permute-start.21 = (bf16[32,2176]{1,0:T(8,128)(2,1)S(1)}, bf16[32,2176]{1,0:T(8,128)(2,1)S(1)}, u32[]{:S(2)}, u32[]{:S(2)}) collective-permute-start(bf16[32,2176]{1,0:T(8,128)(2,1)S(1)} %get-tuple-element.123), channel_id=1, source_target_pairs={{0,1},{1,2},{2,3},{3,0},{4,5},{5,6},{6,7},{7,4},{8,9},{9,10},{10,1... | collective-permute-start | bytes 417800 | tf_op jit(solution)/shard_map/ppermute | solution.py:516
  286.5 13.2 %collective-permute-start.22 = (bf16[32,2176]{1,0:T(8,128)(2,1)S(1)}, bf16[32,2176]{1,0:T(8,128)(2,1)S(1)}, u32[]{:S(2)}, u32[]{:S(2)}) collective-permute-start(bf16[32,2176]{1,0:T(8,128)(2,1)S(1)} %get-tuple-element.124), channel_id=1, source_target_pairs={{0,2},{1,3},{2,0},{3,1},{4,6},{5,7},{6,4},{7,5},{8,10},{9,11},{10,... | collective-permute-start | bytes 417800 | tf_op jit(solution)/shard_map/ppermute | solution.py:516
  288.8 10.9 %collective-permute-start.23 = (bf16[32,2176]{1,0:T(8,128)(2,1)S(1)}, bf16[32,2176]{1,0:T(8,128)(2,1)S(1)}, u32[]{:S(2)}, u32[]{:S(2)}) collective-permute-start(bf16[32,2176]{1,0:T(8,128)(2,1)S(1)} %get-tuple-element.125), channel_id=1, source_target_pairs={{0,3},{1,0},{2,1},{3,2},{4,7},{5,4},{6,5},{7,6},{8,11},{9,8},{10,9... | collective-permute-start | bytes 417800 | tf_op jit(solution)/shard_map/ppermute | solution.py:516
  290.3 16.3 %collective-permute-start.27 = (bf16[32,1152]{1,0:T(8,128)(2,1)S(1)}, bf16[32,1152]{1,0:T(8,128)(2,1)S(1)}, u32[]{:S(2)}, u32[]{:S(2)}) collective-permute-start(bf16[32,1152]{1,0:T(8,128)(2,1)S(1)} %one_sum.1.refs_3_.refs_1_), channel_id=1, source_target_pairs={{0,1},{1,2},{2,3},{3,0},{4,5},{5,6},{6,7},{7,4},{8,9},{9,10},{10,1... | collective-permute-start | bytes 221192 | tf_op jit(solution)/shard_map/ppermute | solution.py:516
  290.8 16.7 %collective-permute-start.28 = (bf16[32,1152]{1,0:T(8,128)(2,1)S(1)}, bf16[32,1152]{1,0:T(8,128)(2,1)S(1)}, u32[]{:S(2)}, u32[]{:S(2)}) collective-permute-start(bf16[32,1152]{1,0:T(8,128)(2,1)S(1)} %one_sum.1.refs_3_.refs_1_), channel_id=1, source_target_pairs={{0,2},{1,3},{2,0},{3,1},{4,6},{5,7},{6,4},{7,5},{8,10},{9,11},{10,... | collective-permute-start | bytes 221192 | tf_op jit(solution)/shard_map/ppermute | solution.py:516
  292.9 14.6 %collective-permute-start.29 = (bf16[32,1152]{1,0:T(8,128)(2,1)S(1)}, bf16[32,1152]{1,0:T(8,128)(2,1)S(1)}, u32[]{:S(2)}, u32[]{:S(2)}) collective-permute-start(bf16[32,1152]{1,0:T(8,128)(2,1)S(1)} %one_sum.1.refs_3_.refs_1_), channel_id=1, source_target_pairs={{0,3},{1,0},{2,1},{3,2},{4,7},{5,4},{6,5},{7,6},{8,11},{9,8},{10,9... | collective-permute-start | bytes 221192 | tf_op jit(solution)/shard_map/ppermute | solution.py:516
  300.5 9.8 %collective-permute-start.24 = (bf16[32,2176]{1,0:T(8,128)(2,1)S(1)}, bf16[32,2176]{1,0:T(8,128)(2,1)S(1)}, u32[]{:S(2)}, u32[]{:S(2)}) collective-permute-start(bf16[32,2176]{1,0:T(8,128)(2,1)S(1)} %two_sum.1.refs_5_.refs_1_), channel_id=1, source_target_pairs={{0,1},{1,2},{2,3},{3,0},{4,5},{5,6},{6,7},{7,4},{8,9},{9,10},{10,1... | collective-permute-start | bytes 417800 | tf_op jit(solution)/shard_map/ppermute | solution.py:516
  304.0 9.2 %collective-permute-start.25 = (bf16[32,2176]{1,0:T(8,128)(2,1)S(1)}, bf16[32,2176]{1,0:T(8,128)(2,1)S(1)}, u32[]{:S(2)}, u32[]{:S(2)}) collective-permute-start(bf16[32,2176]{1,0:T(8,128)(2,1)S(1)} %two_sum.1.refs_5_.refs_1_), channel_id=1, source_target_pairs={{0,2},{1,3},{2,0},{3,1},{4,6},{5,7},{6,4},{7,5},{8,10},{9,11},{10,... | collective-permute-start | bytes 417800 | tf_op jit(solution)/shard_map/ppermute | solution.py:516
  306.6 6.6 %collective-permute-start.26 = (bf16[32,2176]{1,0:T(8,128)(2,1)S(1)}, bf16[32,2176]{1,0:T(8,128)(2,1)S(1)}, u32[]{:S(2)}, u32[]{:S(2)}) collective-permute-start(bf16[32,2176]{1,0:T(8,128)(2,1)S(1)} %two_sum.1.refs_5_.refs_1_), channel_id=1, source_target_pairs={{0,3},{1,0},{2,1},{3,2},{4,7},{5,4},{6,5},{7,6},{8,11},{9,8},{10,9... | collective-permute-start | bytes 417800 | tf_op jit(solution)/shard_map/ppermute | solution.py:516
  (23 other events, 155.8 us)
Sparse Core Ops, SparseCore 0:
  123.2 92.9 reduce-scatter.1
  222.8 86.7 all-gather.2

commit v7 on v5

--- a/solution.py
+++ b/solution.py
@@ -733,9 +733,8 @@
     )
     shares_two = total(blocks_two, "two_sum", (token,))
     *one, small_one = finish(shares_one, sizes[0], "one_finish", (shares_two[0],))
-    *two, small_two = finish(shares_two, sizes[1], "two_finish", (small_one,))
-    token = small_two
-    *full, _ = call(
+    token = small_one
+    *full, token = call(
         widen_kernel,
         [((local, width, 2 * half), f32), ((local, half, width), f32), TOKEN],
         gathered,
@@ -748,6 +747,7 @@
         ],
         deps=(token,), us=12, name="widen",
     )
+    *two, small_two = finish(shares_two, sizes[1], "two_finish", (token,))
     return (
         output,
         grad_inputs,

time: 338 us -> 337 us (level)
    unnamed x47 -> x49, local copies, waits for them, and re-layouts: 9.22 us -> 9.9 us
  transfers between devices with their start and end apart: 33 -> 33, of which waited for: 18 -> 17; matrix products, arithmetic and copies ran while one was open for 1% -> 1% of each run, Pallas kernels for 24% -> 28%
where the time goes in v7:
time: 337 us; the launch traced here: 336 us
  waiting for transfers between devices  134 us (40%)
  Pallas kernels  117 us (35%)
  starting transfers between devices  55.8 us (17%)
  between operations  15 us (4%)
  local copies, waits for them, and re-layouts  11.2 us (3%)
    pallas_call x23, Pallas kernels, call(): pl.pallas_call(body, out_shape=outs, compiler_params=pltpu.CompilerParams...  117 us
    ppermute x18, waiting for transfers between devices, ring(): lax.ppermute(x, 'expert', [(i, (i + d) % owners) for i in range(owners)])  65 us
    ppermute x4, waiting for transfers between devices, swap(): lax.ppermute(x, 'group', [(i, i ^ 1 << (steps - stage if i % 2 else 1 + s...  38.2 us
    ppermute x18, starting transfers between devices, ring(): lax.ppermute(x, 'expert', [(i, (i + d) % owners) for i in range(owners)])  33.8 us
    ppermute x2, waiting for transfers between devices, far(): down = lax.ppermute(after, 'expert', [(1, 0), (2, 1)])  14.7 us
    ppermute x1, waiting for transfers between devices, on_device(): lax.ppermute(parts[2], 'expert', [(0, 1), (1, 2)])  10.6 us
    unnamed x49, local copies, waits for them, and re-layouts  9.9 us
  transfers between devices with their start and end apart: 33, of which 17 were waited for; matrix products, arithmetic and copies ran while one was open for 1% of the time, Pallas kernels for 28%

profile of v7, /device:TPU:0, one launch (start us, length us, event | category | flops | bytes accessed | tf_op | source)
XLA Modules:
  0.0 336.1 jit_solution(6402917652699378738)
XLA Ops:
  7.2 3.1 collective-permute-start
  10.3 2.1 collective-permute-start.1
  13.0 8.5 %dense_forward.1 = (bf16[256,1024]{1,0:T(8,128)(2,1)}, bf16[256,1024]{1,0:T(8,128)(2,1)}, bf16[256,1024]{1,0:T(8,128)(2,1)}, bf16[256,1024]{1,0:T(8,128)(2,1)}, ...) custom-call(s32[1]{0:T(128)S(6)} %copy.37.refs_0_.refs_1_, ...), custom_call_target="tpu_custom_call" | custom-call | bytes 32400000 | tf_op jit(solution)/shard_map/dense_forward/pallas_call | solution.py:52
  21.6 3.8 %collective-permute-done.refs_1_.refs_0_ = bf16[256,1024]{1,0:T(8,128)(2,1)S(1)} collective-permute-done((bf16[256,1024]{1,0:T(8,128)(2,1)}, bf16[256,1024]{1,0:T(8,128)(2,1)S(1)}, u32[]{:S(2)}, u32[]{:S(2)}) %collective-permute-start) | collective-permute-done | bytes 524320 | tf_op jit(solution)/shard_map/ppermute | solution.py:516
  25.3 9.8 %collective-permute-done.1.refs_2_.refs_1_ = bf16[256,1024]{1,0:T(8,128)(2,1)S(1)} collective-permute-done((bf16[256,1024]{1,0:T(8,128)(2,1)}, bf16[256,1024]{1,0:T(8,128)(2,1)S(1)}, u32[]{:S(2)}, u32[]{:S(2)}) %collective-permute-start.1) | collective-permute-done | bytes 524320 | tf_op jit(solution)/shard_map/ppermute | solution.py:516
  37.0 2.7 collective-permute-start.4
  39.7 13.7 %collective-permute-done.2.refs_2_ = bf16[272,1024]{1,0:T(8,128)(2,1)S(1)} collective-permute-done((bf16[272,1024]{1,0:T(8,128)(2,1)}, bf16[272,1024]{1,0:T(8,128)(2,1)S(1)}, u32[]{:S(2)}, u32[]{:S(2)}) %collective-permute-start.2) | collective-permute-done | bytes 557088 | tf_op jit(solution)/shard_map/ppermute | solution.py:516
  54.2 9.3 %collective-permute-done.4.refs_4_ = bf16[272,1024]{1,0:T(8,128)(2,1)S(1)} collective-permute-done((bf16[272,1024]{1,0:T(8,128)(2,1)}, bf16[272,1024]{1,0:T(8,128)(2,1)S(1)}, u32[]{:S(2)}, u32[]{:S(2)}) %collective-permute-start.4) | collective-permute-done | bytes 557088 | tf_op jit(solution)/shard_map/ppermute | solution.py:516
  63.5 1.3 collective-permute-start.5
  64.8 14.7 %collective-permute-done.5 = bf16[272,1024]{1,0:T(8,128)(2,1)S(1)} collective-permute-done((bf16[272,1024]{1,0:T(8,128)(2,1)S(1)}, bf16[272,1024]{1,0:T(8,128)(2,1)S(1)}, u32[]{:S(2)}, u32[]{:S(2)}) %collective-permute-start.5) | collective-permute-done | bytes 557088 | tf_op jit(solution)/shard_map/ppermute | solution.py:534
  81.1 1.5 collective-permute-start.7
  83.2 15.7 %expert_forward.1 = (bf16[4,640,1024]{2,1,0:T(8,128)(2,1)}, bf16[4,640,512]{2,1,0:T(8,128)(2,1)}, bf16[4,640,512]{2,1,0:T(8,128)(2,1)}, bf16[4,640,512]{2,1,0:T(8,128)(2,1)}, bf16[4,640,1024]{2,1,0:T(8,128)(2,1)}) custom-call(s32[3]{0:T(128)} %pad_add_fusion.2.refs_0_, bf16[272,1024]{1,0:T(8,128)(2,1)} %tokens_go.1.refs_1_.refs_10_, ...), custom_call_target="tpu_custom_call" | custom-call | bytes 61200000 | tf_op jit(solution)/shard_map/expert_forward/pallas_call | solution.py:52
  99.8 23.3 %expert_backward0.1 = (bf16[8,768,1024]{2,1,0:T(8,128)(2,1)}, bf16[4,640,1024]{2,1,0:T(8,128)(2,1)}, f32[4,4,256]{2,1,0:T(4,128)}) custom-call(s32[3]{0:T(128)} %pad_add_fusion.2.refs_0_, bf16[272,1024]{1,0:T(8,128)(2,1)} %tokens_go.1.refs_1_.refs_10_, bf16[272,1024]{1,0:T(8,128)(2,1)} %copy-done.16, bf16[272,1024]{1,0:T(8,128)(2,1)} %broadcast_select_fusion.refs_3_.refs_2_, ...), custom_call_target="tpu_custom_call" | custom-call | bytes 115200000 | tf_op jit(solution)/shard_map/expert_backward0/pallas_call | solution.py:52
  123.2 14.1 %expert_rows.1 = (bf16[272,1024]{1,0:T(8,128)(2,1)}, bf16[272,1024]{1,0:T(8,128)(2,1)}, bf16[272,1024]{1,0:T(8,128)(2,1)}, bf16[272,1024]{1,0:T(8,128)(2,1)}) custom-call(s32[3]{0:T(128)} %pad_add_fusion.2.refs_0_, bf16[272,1024]{1,0:T(8,128)(2,1)} %tokens_go.1.refs_1_.refs_10_, bf16[272,1024]{1,0:T(8,128)(2,1)} %copy-done.16, ...), custom_call_target="tpu_custom_call" | custom-call | bytes 50400000 | tf_op jit(solution)/shard_map/expert_rows/pallas_call | solution.py:52
  137.9 5.5 %collective-permute-start.9 = (bf16[272,1024]{1,0:T(8,128)(2,1)}, bf16[272,1024]{1,0:T(8,128)(2,1)S(1)}, u32[]{:S(2)}, u32[]{:S(2)}) collective-permute-start(bf16[272,1024]{1,0:T(8,128)(2,1)} %get-tuple-element.87), channel_id=1, source_target_pairs={{0,1},{1,2},{4,5},{5,6},{8,9},{9,10},{12,13},{13,14},{16,17},{17,1... | collective-permute-start | bytes 1671176 | tf_op jit(solution)/shard_map/ppermute | solution.py:658
  143.5 10.6 %collective-permute-done.9.refs_3_ = bf16[272,1024]{1,0:T(8,128)(2,1)S(1)} collective-permute-done((bf16[272,1024]{1,0:T(8,128)(2,1)}, bf16[272,1024]{1,0:T(8,128)(2,1)S(1)}, u32[]{:S(2)}, u32[]{:S(2)}) %collective-permute-start.9) | collective-permute-done | bytes 557088 | tf_op jit(solution)/shard_map/ppermute | solution.py:658
  155.0 2.7 hop.1
  157.7 2.4 collective-permute-start.11
  160.0 8.1 %combine_out.1.refs_23_.refs_0_ = bf16[4,256,1024]{2,1,0:T(8,128)(2,1)} custom-call(s32[3]{0:T(128)} %pad_add_fusion.2.refs_0_, bf16[272,1024]{1,0:T(8,128)(2,1)} %tokens_go.1.refs_1_.refs_10_, bf16[272,1024]{1,0:T(8,128)(2,1)} %copy-done.16, bf16[272,1024]{1,0:T(8,128)(2,1)} %broadcast_select_fusion.refs_3_.refs_2_, bf16[272,1024]{1,0:T(8,128)(2,1)} %copy-done.17, ...), custom_call_target="tpu_custom_call" | custom-call | bytes 28800000 | tf_op jit(solution)/shard_map/combine_out/pallas_call | solution.py:52
  168.1 3.8 %collective-permute-done.10.refs_3_ = bf16[272,1024]{1,0:T(8,128)(2,1)S(1)} collective-permute-done((bf16[272,1024]{1,0:T(8,128)(2,1)}, bf16[272,1024]{1,0:T(8,128)(2,1)S(1)}, u32[]{:S(2)}, u32[]{:S(2)}) %collective-permute-start.10) | collective-permute-done | bytes 557088 | tf_op jit(solution)/shard_map/ppermute | solution.py:516
  172.0 13.2 %collective-permute-done.11.refs_4_ = bf16[272,1024]{1,0:T(8,128)(2,1)S(1)} collective-permute-done((bf16[272,1024]{1,0:T(8,128)(2,1)}, bf16[272,1024]{1,0:T(8,128)(2,1)S(1)}, u32[]{:S(2)}, u32[]{:S(2)}) %collective-permute-start.11) | collective-permute-done | bytes 557088 | tf_op jit(solution)/shard_map/ppermute | solution.py:516
  186.0 18.5 %dense_backward.1 = (f32[256,1024]{1,0:T(8,128)}, bf16[4,128,1152]{2,1,0:T(8,128)(2,1)}, bf16[4,128,1152]{2,1,0:T(8,128)(2,1)}, bf16[4,128,2176]{2,1,0:T(8,128)(2,1)}, bf16[4,128,2176]{2,1,0:T(8,128)(2,1)}) custom-call(s32[3]{0:T(128)} %pad_add_fusion.2.refs_0_, s32[1]{0:T(128)S(6)} %copy.37.refs_0_.refs_1_, bf16[272,1024]{1,0:T(8,128)(2,1)} %get-tuple-element.89.refs_2_, ...), custom_call_target="tpu_custom_call" | custom-call | bytes 64800000 | tf_op jit(solution)/shard_map/dense_backward/pallas_call | solution.py:52
  205.0 5.7 %collective-permute-done.13.refs_2_.refs_4_ = bf16[4,128,1152]{2,1,0:T(8,128)(2,1)S(1)} collective-permute-done((bf16[4,128,1152]{2,1,0:T(8,128)(2,1)}, bf16[4,128,1152]{2,1,0:T(8,128)(2,1)S(1)}, u32[]{:S(2)}, u32[]{:S(2)}) %collective-permute-start.13) | collective-permute-done | bytes 1179680 | tf_op jit(solution)/shard_map/ppermute | solution.py:519
  210.7 1.2 one_halve0.1
  212.7 1.5 collective-permute-start.15
  218.0 4.6 %collective-permute-done.15.refs_1_.refs_2_.refs_4_ = bf16[2,128,1152]{2,1,0:T(8,128)(2,1)S(1)} collective-permute-done((bf16[2,128,1152]{2,1,0:T(8,128)(2,1)S(1)}, bf16[2,128,1152]{2,1,0:T(8,128)(2,1)S(1)}, u32[]{:S(2)}, u32[]{:S(2)}) %collective-permute-start.15) | collective-permute-done | bytes 589856 | tf_op jit(solution)/shard_map/ppermute | solution.py:522
  223.5 4.6 %all-to-all-start = ((bf16[4,256,1024]{2,1,0:T(8,128)(2,1)}), bf16[4,256,1024]{2,1,0:T(8,128)(2,1)}, u32[]{:S(2)}, u32[]{:S(2)}) async-start(bf16[4,256,1024]{2,1,0:T(8,128)(2,1)} %returned_go.1.refs_5_), calls=%async_computation | async-start | bytes 4194304 | tf_op jit(solution)/shard_map/all_to_all | solution.py:669
  228.1 1.6 collective-permute-start.14
  231.6 1.6 collective-permute-start.16
  233.2 14.4 %collective-permute-done.16.refs_2_ = bf16[1,128,1152]{2,1,0:T(8,128)(2,1)S(1)} collective-permute-done((bf16[1,128,1152]{2,1,0:T(8,128)(2,1)S(1)}, bf16[1,128,1152]{2,1,0:T(8,128)(2,1)S(1)}, u32[]{:S(2)}, u32[]{:S(2)}) %collective-permute-start.16) | collective-permute-done | bytes 294944 | tf_op jit(solution)/shard_map/ppermute | solution.py:522
  248.3 15.5 %collective-permute-done.14.refs_2_.refs_4_ = bf16[2,128,2176]{2,1,0:T(8,128)(2,1)S(1)} collective-permute-done((bf16[2,128,2176]{2,1,0:T(8,128)(2,1)}, bf16[2,128,2176]{2,1,0:T(8,128)(2,1)S(1)}, u32[]{:S(2)}, u32[]{:S(2)}) %collective-permute-start.14) | collective-permute-done | bytes 1114144 | tf_op jit(solution)/shard_map/ppermute | solution.py:522
  264.7 1.7 collective-permute-start.17
  266.4 1.9 collective-permute-start.18
  268.2 2.3 collective-permute-start.19
  270.6 1.5 collective-permute-start.20
  272.9 8.7 %collective-permute-done.19.refs_2_ = bf16[32,1152]{1,0:T(8,128)(2,1)S(1)} collective-permute-done((bf16[32,1152]{1,0:T(8,128)(2,1)S(1)}, bf16[32,1152]{1,0:T(8,128)(2,1)S(1)}, u32[]{:S(2)}, u32[]{:S(2)}) %collective-permute-start.19) | collective-permute-done | bytes 73760 | tf_op jit(solution)/shard_map/ppermute | solution.py:516
  281.6 3.7 %collective-permute-done.17.refs_2_ = bf16[1,128,2176]{2,1,0:T(8,128)(2,1)S(1)} collective-permute-done((bf16[1,128,2176]{2,1,0:T(8,128)(2,1)S(1)}, bf16[1,128,2176]{2,1,0:T(8,128)(2,1)S(1)}, u32[]{:S(2)}, u32[]{:S(2)}) %collective-permute-start.17) | collective-permute-done | bytes 557088 | tf_op jit(solution)/shard_map/ppermute | solution.py:522
  286.0 1.9 collective-permute-start.21
  287.9 2.4 collective-permute-start.22
  290.3 1.4 collective-permute-start.23
  293.6 2.5 collective-permute-start.29
  296.1 3.9 %output.1 = (f32[256,1024]{1,0:T(8,128)}, f32[8,128]{1,0:T(8,128)}) custom-call(f32[256,1024]{1,0:T(8,128)} %get-tuple-element.74.refs_8_.refs_0_, bf16[4,256,1024]{2,1,0:T(8,128)(2,1)} %all-to-all-done.refs_1_, f32[8,128]{1,0:T(8,128)} %copy-done.11), custom_call_target="tpu_custom_call" | custom-call | bytes 14400000 | tf_op jit(solution)/shard_map/output/pallas_call | solution.py:52
  299.9 1.2 collective-permute-done.22.refs_2_
  301.9 5.0 %collective-permute-start.24 = (bf16[32,2176]{1,0:T(8,128)(2,1)S(1)}, bf16[32,2176]{1,0:T(8,128)(2,1)S(1)}, u32[]{:S(2)}, u32[]{:S(2)}) collective-permute-start(bf16[32,2176]{1,0:T(8,128)(2,1)S(1)} %two_sum.1.refs_5_.refs_1_), channel_id=1, source_target_pairs={{0,1},{1,2},{2,3},{3,0},{4,5},{5,6},{6,7},{7,4},{8,9},{9,10},{10,1... | collective-permute-start | bytes 417800 | tf_op jit(solution)/shard_map/ppermute | solution.py:516
  306.9 2.4 collective-permute-start.26
  309.3 1.4 one_finish.1
  312.1 14.2 %widen.1 = (f32[4,1024,1024]{2,1,0:T(8,128)}, f32[4,512,1024]{2,1,0:T(8,128)}, f32[8,128]{1,0:T(8,128)}) custom-call(bf16[8,768,1024]{2,1,0:T(8,128)(2,1)} %bitcast.19, f32[128,128]{1,0:T(8,128)} %copy-done.9), custom_call_target="tpu_custom_call" | custom-call | bytes 43200000 | tf_op jit(solution)/shard_map/widen/pallas_call | solution.py:52
  327.0 1.6 two_finish.1
  (100 shorter events, 24.4 us)
Async XLA Ops:
  7.2 215.4 %reduce-scatter.2.cloned.1.call-start = ((), (), s32[]{:S(2)}) async-start(), calls=%async_computation.2 | async-start | bytes 14155776 | tf_op jit(solution)/shard_map/reduce_scatter | solution.py:647
  7.2 18.1 %collective-permute-start = (bf16[256,1024]{1,0:T(8,128)(2,1)}, bf16[256,1024]{1,0:T(8,128)(2,1)S(1)}, u32[]{:S(2)}, u32[]{:S(2)}) collective-permute-start(bf16[256,1024]{1,0:T(8,128)(2,1)} %refs_7_.1), channel_id=1, source_target_pairs={{0,1},{1,2},{2,3},{3,0},{4,5},{5,6},{6,7},{7,4},{8,9},{9,10},{10,1... | collective-permute-start | bytes 1572872 | tf_op jit(solution)/shard_map/ppermute | solution.py:516
  10.3 24.8 %collective-permute-start.1 = (bf16[256,1024]{1,0:T(8,128)(2,1)}, bf16[256,1024]{1,0:T(8,128)(2,1)S(1)}, u32[]{:S(2)}, u32[]{:S(2)}) collective-permute-start(bf16[256,1024]{1,0:T(8,128)(2,1)} %refs_7_.1), channel_id=1, source_target_pairs={{0,3},{1,0},{2,1},{3,2},{4,7},{5,4},{6,5},{7,6},{8,11},{9,8},{10,9... | collective-permute-start | bytes 1572872 | tf_op jit(solution)/shard_map/ppermute | solution.py:516
  25.3 9.8 %copy-start.18 = (bf16[256,1024]{1,0:T(8,128)(2,1)}, bf16[256,1024]{1,0:T(8,128)(2,1)S(1)}, u32[]{:S(2)}) copy-start(bf16[256,1024]{1,0:T(8,128)(2,1)S(1)} %collective-permute-done.refs_1_.refs_0_) | copy-start | bytes 1572868
  35.9 17.6 %collective-permute-start.2 = (bf16[272,1024]{1,0:T(8,128)(2,1)}, bf16[272,1024]{1,0:T(8,128)(2,1)S(1)}, u32[]{:S(2)}, u32[]{:S(2)}) collective-permute-start(bf16[272,1024]{1,0:T(8,128)(2,1)} %tokens_go.1.refs_1_.refs_10_), channel_id=1, source_target_pairs={{0,1},{1,2},{2,3},{3,0},{4,5},{5,6},{6,7},{7,4},{8,9},{9,10},{10,1... | collective-permute-start | bytes 1671176 | tf_op jit(solution)/shard_map/ppermute | solution.py:516
  37.0 26.4 %collective-permute-start.4 = (bf16[272,1024]{1,0:T(8,128)(2,1)}, bf16[272,1024]{1,0:T(8,128)(2,1)S(1)}, u32[]{:S(2)}, u32[]{:S(2)}) collective-permute-start(bf16[272,1024]{1,0:T(8,128)(2,1)} %tokens_go.1.refs_1_.refs_10_), channel_id=1, source_target_pairs={{0,3},{1,0},{2,1},{3,2},{4,7},{5,4},{6,5},{7,6},{8,11},{9,8},{10,9... | collective-permute-start | bytes 1671176 | tf_op jit(solution)/shard_map/ppermute | solution.py:516
  53.5 29.7 %copy-start.16 = (bf16[272,1024]{1,0:T(8,128)(2,1)}, bf16[272,1024]{1,0:T(8,128)(2,1)S(1)}, u32[]{:S(2)}) copy-start(bf16[272,1024]{1,0:T(8,128)(2,1)S(1)} %collective-permute-done.2.refs_2_) | copy-start | bytes 1671172
  53.5 11.3 %collective-permute-start.3 = (bf16[272,1024]{1,0:T(8,128)(2,1)S(1)}, bf16[272,1024]{1,0:T(8,128)(2,1)S(1)}, u32[]{:S(2)}, u32[]{:S(2)}) collective-permute-start(bf16[272,1024]{1,0:T(8,128)(2,1)S(1)} %collective-permute-done.2.refs_2_), channel_id=1, source_target_pairs={{1,2},{2,3},{5,6},{6,7},{9,10},{10,11},{13,14},{14,15},{17,18},{18... | collective-permute-start | bytes 1671176 | tf_op jit(solution)/shard_map/ppermute | solution.py:533
  63.5 19.7 %copy-start.17 = (bf16[272,1024]{1,0:T(8,128)(2,1)}, bf16[272,1024]{1,0:T(8,128)(2,1)S(1)}, u32[]{:S(2)}) copy-start(bf16[272,1024]{1,0:T(8,128)(2,1)S(1)} %collective-permute-done.4.refs_4_) | copy-start | bytes 1671172
  63.5 16.0 %collective-permute-start.5 = (bf16[272,1024]{1,0:T(8,128)(2,1)S(1)}, bf16[272,1024]{1,0:T(8,128)(2,1)S(1)}, u32[]{:S(2)}, u32[]{:S(2)}) collective-permute-start(bf16[272,1024]{1,0:T(8,128)(2,1)S(1)} %collective-permute-done.4.refs_4_), channel_id=1, source_target_pairs={{1,0},{2,1},{5,4},{6,5},{9,8},{10,9},{13,12},{14,13},{17,16},{18,1... | collective-permute-start | bytes 1671176 | tf_op jit(solution)/shard_map/ppermute | solution.py:534
  80.4 18.5 %collective-permute-start.6 = (bf16[256,1024]{1,0:T(8,128)(2,1)}, bf16[256,1024]{1,0:T(8,128)(2,1)S(1)}, u32[]{:S(2)}, u32[]{:S(2)}) collective-permute-start(bf16[256,1024]{1,0:T(8,128)(2,1)} %get-tuple-element.77.refs_6_), channel_id=1, source_target_pairs={{1,2},{2,3},{5,6},{6,7},{9,10},{10,11},{13,14},{14,15},{17,18},{18... | collective-permute-start | bytes 1572872 | tf_op jit(solution)/shard_map/ppermute | solution.py:533
  81.1 17.8 %collective-permute-start.7 = (bf16[256,1024]{1,0:T(8,128)(2,1)}, bf16[256,1024]{1,0:T(8,128)(2,1)S(1)}, u32[]{:S(2)}, u32[]{:S(2)}) collective-permute-start(bf16[256,1024]{1,0:T(8,128)(2,1)} %get-tuple-element.78.refs_8_), channel_id=1, source_target_pairs={{1,0},{2,1},{5,4},{6,5},{9,8},{10,9},{13,12},{14,13},{17,16},{18,1... | collective-permute-start | bytes 1572872 | tf_op jit(solution)/shard_map/ppermute | solution.py:534
  123.1 189.0 %all-gather.3.cloned.1.call-start = ((), (), s32[]{:S(2)}) async-start(), calls=%async_computation.3 | async-start | bytes 14155776 | tf_op jit(solution)/shard_map/all_gather | solution.py:697
  137.2 6.2 %collective-permute-start.8 = (bf16[272,1024]{1,0:T(8,128)(2,1)}, bf16[272,1024]{1,0:T(8,128)(2,1)S(1)}, u32[]{:S(2)}, u32[]{:S(2)}) collective-permute-start(bf16[272,1024]{1,0:T(8,128)(2,1)} %get-tuple-element.87), channel_id=1, source_target_pairs={{2,1},{3,2},{6,5},{7,6},{10,9},{11,10},{14,13},{15,14},{18,17},{19... | collective-permute-start | bytes 1671176 | tf_op jit(solution)/shard_map/ppermute | solution.py:657
  137.9 16.2 %collective-permute-start.9 = (bf16[272,1024]{1,0:T(8,128)(2,1)}, bf16[272,1024]{1,0:T(8,128)(2,1)S(1)}, u32[]{:S(2)}, u32[]{:S(2)}) collective-permute-start(bf16[272,1024]{1,0:T(8,128)(2,1)} %get-tuple-element.87), channel_id=1, source_target_pairs={{0,1},{1,2},{4,5},{5,6},{8,9},{9,10},{12,13},{13,14},{16,17},{17,1... | collective-permute-start | bytes 1671176 | tf_op jit(solution)/shard_map/ppermute | solution.py:658
  143.5 10.7 %copy-start.22 = (bf16[272,1024]{1,0:T(8,128)(2,1)}, bf16[272,1024]{1,0:T(8,128)(2,1)S(1)}, u32[]{:S(2)}) copy-start(bf16[272,1024]{1,0:T(8,128)(2,1)S(1)} %collective-permute-done.8.refs_2_) | copy-start | bytes 1671172
  157.7 14.3 %collective-permute-start.10 = (bf16[272,1024]{1,0:T(8,128)(2,1)}, bf16[272,1024]{1,0:T(8,128)(2,1)S(1)}, u32[]{:S(2)}, u32[]{:S(2)}) collective-permute-start(bf16[272,1024]{1,0:T(8,128)(2,1)} %get-tuple-element.88.refs_6_), channel_id=1, source_target_pairs={{0,3},{1,0},{2,1},{3,2},{4,7},{5,4},{6,5},{7,6},{8,11},{9,8},{10,9... | collective-permute-start | bytes 1671176 | tf_op jit(solution)/shard_map/ppermute | solution.py:516
  157.7 27.5 %collective-permute-start.11 = (bf16[272,1024]{1,0:T(8,128)(2,1)}, bf16[272,1024]{1,0:T(8,128)(2,1)S(1)}, u32[]{:S(2)}, u32[]{:S(2)}) collective-permute-start(bf16[272,1024]{1,0:T(8,128)(2,1)} %get-tuple-element.90), channel_id=1, source_target_pairs={{0,1},{1,2},{2,3},{3,0},{4,5},{5,6},{6,7},{7,4},{8,9},{9,10},{10,1... | collective-permute-start | bytes 1671176 | tf_op jit(solution)/shard_map/ppermute | solution.py:516
  172.0 13.2 %copy-start.20 = (bf16[272,1024]{1,0:T(8,128)(2,1)}, bf16[272,1024]{1,0:T(8,128)(2,1)S(1)}, u32[]{:S(2)}) copy-start(bf16[272,1024]{1,0:T(8,128)(2,1)S(1)} %collective-permute-done.10.refs_3_) | copy-start | bytes 1671172
  204.4 9.8 %collective-permute-start.12 = (bf16[4,128,2176]{2,1,0:T(8,128)(2,1)}, bf16[4,128,2176]{2,1,0:T(8,128)(2,1)S(1)}, u32[]{:S(2)}, u32[]{:S(2)}) collective-permute-start(bf16[4,128,2176]{2,1,0:T(8,128)(2,1)} %get-tuple-element.100), channel_id=1, source_target_pairs={{0,4},{4,0},{8,12},{12,8},{16,20},{20,16},{24,28},{28,24},{1,5},{5... | collective-permute-start | bytes 6684680 | tf_op jit(solution)/shard_map/ppermute | solution.py:519
  204.4 6.2 %collective-permute-start.13 = (bf16[4,128,1152]{2,1,0:T(8,128)(2,1)}, bf16[4,128,1152]{2,1,0:T(8,128)(2,1)S(1)}, u32[]{:S(2)}, u32[]{:S(2)}) collective-permute-start(bf16[4,128,1152]{2,1,0:T(8,128)(2,1)} %get-tuple-element.98.refs_1_), channel_id=1, source_target_pairs={{0,4},{4,0},{8,12},{12,8},{16,20},{20,16},{24,28},{28,24},{1,5},{5... | collective-permute-start | bytes 3538952 | tf_op jit(solution)/shard_map/ppermute | solution.py:519
  205.0 5.7 %copy-start.4 = (bf16[4,128,1152]{2,1,0:T(8,128)(2,1)S(1)}, bf16[4,128,1152]{2,1,0:T(8,128)(2,1)}, u32[]{:S(2)}) copy-start(bf16[4,128,1152]{2,1,0:T(8,128)(2,1)} %get-tuple-element.101.refs_1_.refs_3_) | copy-start | bytes 3538948
  210.7 3.6 %copy-start.1 = (bf16[4,128,2176]{2,1,0:T(8,128)(2,1)S(1)}, bf16[4,128,2176]{2,1,0:T(8,128)(2,1)}, u32[]{:S(2)}) copy-start(bf16[4,128,2176]{2,1,0:T(8,128)(2,1)} %get-tuple-element.99.refs_1_.refs_3_) | copy-start | bytes 6684676
  212.7 9.9 %collective-permute-start.15 = (bf16[2,128,1152]{2,1,0:T(8,128)(2,1)S(1)}, bf16[2,128,1152]{2,1,0:T(8,128)(2,1)S(1)}, u32[]{:S(2)}, u32[]{:S(2)}) collective-permute-start(bf16[2,128,1152]{2,1,0:T(8,128)(2,1)S(1)} %get-tuple-element.106), channel_id=1, source_target_pairs={{0,8},{4,20},{8,0},{12,28},{16,24},{20,4},{24,16},{28,12},{1,9},{5... | collective-permute-start | bytes 1769480 | tf_op jit(solution)/shard_map/ppermute | solution.py:522
  217.0 1.0 copy-start.15
  223.4 6.2 %copy-start = (bf16[768,1024]{1,0:T(8,128)(2,1)S(1)}, bf16[768,1024]{1,0:T(8,128)(2,1)}, u32[]{:S(2)}) copy-start(bf16[768,1024]{1,0:T(8,128)(2,1)} %gather_go.1.refs_5_) | copy-start | bytes 4718596
  223.4 6.2 %copy-start.3 = (bf16[2,128,1152]{2,1,0:T(8,128)(2,1)S(1)}, bf16[2,128,1152]{2,1,0:T(8,128)(2,1)}, u32[]{:S(2)}) copy-start(bf16[2,128,1152]{2,1,0:T(8,128)(2,1)} %copy-done.2) | copy-start | bytes 1769476
  223.5 72.6 %all-to-all-start = ((bf16[4,256,1024]{2,1,0:T(8,128)(2,1)}), bf16[4,256,1024]{2,1,0:T(8,128)(2,1)}, u32[]{:S(2)}, u32[]{:S(2)}) async-start(bf16[4,256,1024]{2,1,0:T(8,128)(2,1)} %returned_go.1.refs_5_), calls=%async_computation | async-start | bytes 4194304 | tf_op jit(solution)/shard_map/all_to_all | solution.py:669
  228.0 19.6 %copy-start.10 = (s32[3]{0:T(128)S(1)}, s32[3]{0:T(128)}, u32[]{:S(2)}) copy-start(s32[3]{0:T(128)} %pad_add_fusion.2.refs_0_) | copy-start | bytes 40
  228.1 35.8 %collective-permute-start.14 = (bf16[2,128,2176]{2,1,0:T(8,128)(2,1)}, bf16[2,128,2176]{2,1,0:T(8,128)(2,1)S(1)}, u32[]{:S(2)}, u32[]{:S(2)}) collective-permute-start(bf16[2,128,2176]{2,1,0:T(8,128)(2,1)} %copy-done.15), channel_id=1, source_target_pairs={{0,8},{4,20},{8,0},{12,28},{16,24},{20,4},{24,16},{28,12},{1,9},{5... | collective-permute-start | bytes 3342344 | tf_op jit(solution)/shard_map/ppermute | solution.py:522
  229.7 1.2 copy-start.8
  230.8 33.0 %copy-start.6 = (bf16[2,128,2176]{2,1,0:T(8,128)(2,1)S(1)}, bf16[2,128,2176]{2,1,0:T(8,128)(2,1)}, u32[]{:S(2)}) copy-start(bf16[2,128,2176]{2,1,0:T(8,128)(2,1)} %copy-done.5) | copy-start | bytes 3342340
  231.6 16.1 %collective-permute-start.16 = (bf16[1,128,1152]{2,1,0:T(8,128)(2,1)S(1)}, bf16[1,128,1152]{2,1,0:T(8,128)(2,1)S(1)}, u32[]{:S(2)}, u32[]{:S(2)}) collective-permute-start(bf16[1,128,1152]{2,1,0:T(8,128)(2,1)S(1)} %get-tuple-element.110), channel_id=1, source_target_pairs={{0,16},{4,12},{8,24},{12,4},{16,0},{20,28},{24,8},{28,20},{1,17},{... | collective-permute-start | bytes 884744 | tf_op jit(solution)/shard_map/ppermute | solution.py:522
  264.7 20.5 %collective-permute-start.17 = (bf16[1,128,2176]{2,1,0:T(8,128)(2,1)S(1)}, bf16[1,128,2176]{2,1,0:T(8,128)(2,1)S(1)}, u32[]{:S(2)}, u32[]{:S(2)}) collective-permute-start(bf16[1,128,2176]{2,1,0:T(8,128)(2,1)S(1)} %get-tuple-element.114), channel_id=1, source_target_pairs={{0,16},{4,12},{8,24},{12,4},{16,0},{20,28},{24,8},{28,20},{1,17},{... | collective-permute-start | bytes 1671176 | tf_op jit(solution)/shard_map/ppermute | solution.py:522
  266.4 6.5 %collective-permute-start.18 = (bf16[32,1152]{1,0:T(8,128)(2,1)S(1)}, bf16[32,1152]{1,0:T(8,128)(2,1)S(1)}, u32[]{:S(2)}, u32[]{:S(2)}) collective-permute-start(bf16[32,1152]{1,0:T(8,128)(2,1)S(1)} %get-tuple-element.116), channel_id=1, source_target_pairs={{0,1},{1,2},{2,3},{3,0},{4,5},{5,6},{6,7},{7,4},{8,9},{9,10},{10,1... | collective-permute-start | bytes 221192 | tf_op jit(solution)/shard_map/ppermute | solution.py:516
  268.2 13.3 %collective-permute-start.19 = (bf16[32,1152]{1,0:T(8,128)(2,1)S(1)}, bf16[32,1152]{1,0:T(8,128)(2,1)S(1)}, u32[]{:S(2)}, u32[]{:S(2)}) collective-permute-start(bf16[32,1152]{1,0:T(8,128)(2,1)S(1)} %get-tuple-element.117), channel_id=1, source_target_pairs={{0,2},{1,3},{2,0},{3,1},{4,6},{5,7},{6,4},{7,5},{8,10},{9,11},{10,... | collective-permute-start | bytes 221192 | tf_op jit(solution)/shard_map/ppermute | solution.py:516
  270.6 10.9 %collective-permute-start.20 = (bf16[32,1152]{1,0:T(8,128)(2,1)S(1)}, bf16[32,1152]{1,0:T(8,128)(2,1)S(1)}, u32[]{:S(2)}, u32[]{:S(2)}) collective-permute-start(bf16[32,1152]{1,0:T(8,128)(2,1)S(1)} %get-tuple-element.118), channel_id=1, source_target_pairs={{0,3},{1,0},{2,1},{3,2},{4,7},{5,4},{6,5},{7,6},{8,11},{9,8},{10,9... | collective-permute-start | bytes 221192 | tf_op jit(solution)/shard_map/ppermute | solution.py:516
  286.0 7.6 %copy-start.11 = (f32[8,128]{1,0:T(8,128)}, f32[8,128]{1,0:T(8,128)S(1)}, u32[]{:S(2)}) copy-start(f32[8,128]{1,0:T(8,128)S(1)} %get-tuple-element.120.refs_2_) | copy-start | bytes 12292
  286.0 7.6 %collective-permute-start.21 = (bf16[32,2176]{1,0:T(8,128)(2,1)S(1)}, bf16[32,2176]{1,0:T(8,128)(2,1)S(1)}, u32[]{:S(2)}, u32[]{:S(2)}) collective-permute-start(bf16[32,2176]{1,0:T(8,128)(2,1)S(1)} %get-tuple-element.124), channel_id=1, source_target_pairs={{0,1},{1,2},{2,3},{3,0},{4,5},{5,6},{6,7},{7,4},{8,9},{9,10},{10,1... | collective-permute-start | bytes 417800 | tf_op jit(solution)/shard_map/ppermute | solution.py:516
  287.9 13.2 %collective-permute-start.22 = (bf16[32,2176]{1,0:T(8,128)(2,1)S(1)}, bf16[32,2176]{1,0:T(8,128)(2,1)S(1)}, u32[]{:S(2)}, u32[]{:S(2)}) collective-permute-start(bf16[32,2176]{1,0:T(8,128)(2,1)S(1)} %get-tuple-element.125), channel_id=1, source_target_pairs={{0,2},{1,3},{2,0},{3,1},{4,6},{5,7},{6,4},{7,5},{8,10},{9,11},{10,... | collective-permute-start | bytes 417800 | tf_op jit(solution)/shard_map/ppermute | solution.py:516
  290.3 10.8 %collective-permute-start.23 = (bf16[32,2176]{1,0:T(8,128)(2,1)S(1)}, bf16[32,2176]{1,0:T(8,128)(2,1)S(1)}, u32[]{:S(2)}, u32[]{:S(2)}) collective-permute-start(bf16[32,2176]{1,0:T(8,128)(2,1)S(1)} %get-tuple-element.126), channel_id=1, source_target_pairs={{0,3},{1,0},{2,1},{3,2},{4,7},{5,4},{6,5},{7,6},{8,11},{9,8},{10,9... | collective-permute-start | bytes 417800 | tf_op jit(solution)/shard_map/ppermute | solution.py:516
  291.8 15.1 %collective-permute-start.27 = (bf16[32,1152]{1,0:T(8,128)(2,1)S(1)}, bf16[32,1152]{1,0:T(8,128)(2,1)S(1)}, u32[]{:S(2)}, u32[]{:S(2)}) collective-permute-start(bf16[32,1152]{1,0:T(8,128)(2,1)S(1)} %one_sum.1.refs_3_.refs_1_), channel_id=1, source_target_pairs={{0,1},{1,2},{2,3},{3,0},{4,5},{5,6},{6,7},{7,4},{8,9},{9,10},{10,1... | collective-permute-start | bytes 221192 | tf_op jit(solution)/shard_map/ppermute | solution.py:516
  292.4 17.0 %collective-permute-start.28 = (bf16[32,1152]{1,0:T(8,128)(2,1)S(1)}, bf16[32,1152]{1,0:T(8,128)(2,1)S(1)}, u32[]{:S(2)}, u32[]{:S(2)}) collective-permute-start(bf16[32,1152]{1,0:T(8,128)(2,1)S(1)} %one_sum.1.refs_3_.refs_1_), channel_id=1, source_target_pairs={{0,2},{1,3},{2,0},{3,1},{4,6},{5,7},{6,4},{7,5},{8,10},{9,11},{10,... | collective-permute-start | bytes 221192 | tf_op jit(solution)/shard_map/ppermute | solution.py:516
  293.6 15.8 %collective-permute-start.29 = (bf16[32,1152]{1,0:T(8,128)(2,1)S(1)}, bf16[32,1152]{1,0:T(8,128)(2,1)S(1)}, u32[]{:S(2)}, u32[]{:S(2)}) collective-permute-start(bf16[32,1152]{1,0:T(8,128)(2,1)S(1)} %one_sum.1.refs_3_.refs_1_), channel_id=1, source_target_pairs={{0,3},{1,0},{2,1},{3,2},{4,7},{5,4},{6,5},{7,6},{8,11},{9,8},{10,9... | collective-permute-start | bytes 221192 | tf_op jit(solution)/shard_map/ppermute | solution.py:516
  301.9 24.4 %collective-permute-start.24 = (bf16[32,2176]{1,0:T(8,128)(2,1)S(1)}, bf16[32,2176]{1,0:T(8,128)(2,1)S(1)}, u32[]{:S(2)}, u32[]{:S(2)}) collective-permute-start(bf16[32,2176]{1,0:T(8,128)(2,1)S(1)} %two_sum.1.refs_5_.refs_1_), channel_id=1, source_target_pairs={{0,1},{1,2},{2,3},{3,0},{4,5},{5,6},{6,7},{7,4},{8,9},{9,10},{10,1... | collective-permute-start | bytes 417800 | tf_op jit(solution)/shard_map/ppermute | solution.py:516
  306.9 19.4 %collective-permute-start.25 = (bf16[32,2176]{1,0:T(8,128)(2,1)S(1)}, bf16[32,2176]{1,0:T(8,128)(2,1)S(1)}, u32[]{:S(2)}, u32[]{:S(2)}) collective-permute-start(bf16[32,2176]{1,0:T(8,128)(2,1)S(1)} %two_sum.1.refs_5_.refs_1_), channel_id=1, source_target_pairs={{0,2},{1,3},{2,0},{3,1},{4,6},{5,7},{6,4},{7,5},{8,10},{9,11},{10,... | collective-permute-start | bytes 417800 | tf_op jit(solution)/shard_map/ppermute | solution.py:516
  306.9 19.4 %collective-permute-start.26 = (bf16[32,2176]{1,0:T(8,128)(2,1)S(1)}, bf16[32,2176]{1,0:T(8,128)(2,1)S(1)}, u32[]{:S(2)}, u32[]{:S(2)}) collective-permute-start(bf16[32,2176]{1,0:T(8,128)(2,1)S(1)} %two_sum.1.refs_5_.refs_1_), channel_id=1, source_target_pairs={{0,3},{1,0},{2,1},{3,2},{4,7},{5,4},{6,5},{7,6},{8,11},{9,8},{10,9... | collective-permute-start | bytes 417800 | tf_op jit(solution)/shard_map/ppermute | solution.py:516
  310.8 1.4 copy-start.9
  (9 other events, 7.1 us)
Sparse Core Ops, SparseCore 0:
  123.2 92.9 reduce-scatter.1
  223.6 86.7 all-gather.2
